TPU v7x, 128 devices: a whole 4x4x4 slice. The times are simulated.
128 devices in a mesh: seq: 16 (over y, z_lo, core), batch: 8 (over z_hi, x).
Axes of the slice: x: 4, y: 4, z: 4 (z_hi: 2, z_lo: 2; z = z_hi * 2 + z_lo), core: 2. Of those that a mesh axis runs over, the one named last changes fastest.
Arguments:
- tokens: bfloat16 [2048, 16, 768], P('seq', 'batch'), may hold values from -6 to 6
- lengths: int32 [16], P('batch'), may hold values from 64 to 2048, as said below
- gain_one: bfloat16 [768], P(('seq', 'batch')), may hold values from 0.5 to 1.5
- bias_one: bfloat16 [768], P(('seq', 'batch')), may hold values from -3 to 3
- w_qkv: bfloat16 [768, 2304], P(('seq', 'batch')), may hold values from -0.21875 to 0.21875
- w_out: bfloat16 [768, 768], P(('seq', 'batch')), may hold values from -0.875 to 0.875
- gain_two: bfloat16 [768], P(('seq', 'batch')), may hold values from 0.5 to 1.5
- bias_two: bfloat16 [768], P(('seq', 'batch')), may hold values from -3 to 3
- w_up: bfloat16 [768, 3072], P(('seq', 'batch')), may hold values from -0.21875 to 0.21875
- w_down: bfloat16 [3072, 768], P(('seq', 'batch')), may hold values from -0.109375 to 0.109375
- d_out: bfloat16 [2048, 16, 768], P('seq', 'batch'), may hold values from -6 to 6
Outputs:
- output: bfloat16 [2048, 16, 768], P('seq', 'batch')
- d_tokens: bfloat16 [2048, 16, 768], P('seq', 'batch')
- d_gain_one: float32 [768], P(('seq', 'batch'))
- d_bias_one: float32 [768], P(('seq', 'batch'))
- d_w_qkv: float32 [768, 2304], P(('seq', 'batch'))
- d_w_out: float32 [768, 768], P(('seq', 'batch'))
- d_gain_two: float32 [768], P(('seq', 'batch'))
- d_bias_two: float32 [768], P(('seq', 'batch'))
- d_w_up: float32 [768, 3072], P(('seq', 'batch'))
- d_w_down: float32 [3072, 768], P(('seq', 'batch'))
Inputs may be any that keep to these rules, and one draw needn't show every extreme that they name: `lengths`: one sequence has 2048 valid tokens and another 64, in every draw.
All inputs are finite; a program needn't handle non-finite values.
Results may differ from a plain program's by a relative error of at most 0.033.
Values may be sent and summed in bfloat16 or wider, within the bound.
No kernel may reach another device: no remote copies, remote signals or barrier semaphores. Data moves between devices by JAX's collectives and lax.ppermute only.
A program may use at most 192 MiB of HBM per device.

v0:
```python
import math

import jax
import jax.numpy as jnp
from jax import lax
from jax.sharding import PartitionSpec as P

H = 12
HD = 64


EPSILON = 1e-05


def layer_norm(values, gain, bias):
    center = jnp.mean(values, axis=-1, keepdims=True)
    shifted = values - center
    spread = jnp.mean(shifted * shifted, axis=-1, keepdims=True)
    return shifted * lax.rsqrt(spread + EPSILON) * gain + bias


def block_layout(length):
    block_size = math.gcd(length, 256)
    return (block_size, length // block_size)


def allowed_mask(query_pos, key_offset, amount, lengths):
    key_pos = key_offset + jnp.arange(amount, dtype=jnp.int32)
    causal = key_pos[None, :] <= query_pos[:, None]
    inside = key_pos[None, None, :] < lengths[:, None, None]
    return (causal[None, :, :] & inside)[:, None, :, :]


def signed_scores(queries, key_heads, factor):
    scores = (
        jnp.einsum("qbhd,kbhd->bhqk", queries, key_heads, preferred_element_type=jnp.float32)
        * factor
    )
    smooth = jnp.sqrt(scores * scores + 1.0)
    return (smooth, scores / smooth)


def fold_step(carry, key_block, value_block, offset, queries, query_pos, lengths, factor):
    running, totals, accum = carry
    amount = key_block.shape[0]
    sequences = key_block.shape[1]
    key_heads = key_block.reshape(amount, sequences, H, HD)
    value_heads = value_block.reshape(amount, sequences, H, HD)
    smooth, slope = signed_scores(queries, key_heads, factor)
    allowed = allowed_mask(query_pos, offset, amount, lengths)
    fresh = jnp.maximum(running, jnp.max(jnp.where(allowed, smooth, 0.0), axis=-1))
    expo = jnp.where(allowed, jnp.exp(jnp.where(allowed, smooth - fresh[..., None], -30.0)), 0.0)
    rescale = jnp.exp(running - fresh)
    totals = totals * rescale + jnp.sum(expo, axis=-1)
    weights = (slope * expo).astype(jnp.bfloat16)
    accum = accum * rescale[..., None] + jnp.einsum(
        "bhqk,kbhd->bhqd", weights, value_heads, preferred_element_type=jnp.float32
    )
    return (fresh, totals, accum)


def fold_blocks(carry, key_rows, value_rows, queries, query_pos, lengths, factor):
    fold_size, fold_count = block_layout(key_rows.shape[0])

    def inner(number, state):
        start = number * fold_size
        key_block = lax.dynamic_slice_in_dim(key_rows, start, fold_size, 0)
        value_block = lax.dynamic_slice_in_dim(value_rows, start, fold_size, 0)
        return fold_step(state, key_block, value_block, start, queries, query_pos, lengths, factor)

    return lax.fori_loop(0, fold_count, inner, carry)


def signed_grads(
    queries,
    grad_heads,
    log_totals,
    delta,
    query_pos,
    key_block,
    value_block,
    key_offset,
    lengths,
    factor,
):
    amount = key_block.shape[0]
    sequences = key_block.shape[1]
    key_heads = key_block.reshape(amount, sequences, H, HD)
    value_heads = value_block.reshape(amount, sequences, H, HD)
    smooth, slope = signed_scores(queries, key_heads, factor)
    allowed = allowed_mask(query_pos, key_offset, amount, lengths)
    chance = jnp.where(
        allowed, jnp.exp(jnp.where(allowed, smooth - log_totals[..., None], -30.0)), 0.0
    )
    weights = (slope * chance).astype(jnp.bfloat16)
    d_chance = jnp.einsum(
        "qbhd,kbhd->bhqk", grad_heads, value_heads, preferred_element_type=jnp.float32
    )
    cubed = smooth * smooth * smooth
    d_scores = chance * (d_chance * (1.0 / cubed + slope * slope) - slope * delta[..., None])
    return (d_scores.astype(jnp.bfloat16), weights, key_heads)


def body(
    tokens, lengths, gain_one, bias_one, w_qkv, w_out, gain_two, bias_two, w_up, w_down, d_out
):
    local_len, sequences, features = tokens.shape
    row_count = local_len * sequences
    factor = 1.0 / math.sqrt(HD)
    fetched = (
        lax.all_gather(w_qkv, ("seq", "batch"), axis=0, tiled=True),
        lax.all_gather(w_out, ("seq", "batch"), axis=0, tiled=True),
        lax.all_gather(w_up, ("seq", "batch"), axis=0, tiled=True),
        lax.all_gather(w_down, ("seq", "batch"), axis=0, tiled=True),
        lax.all_gather(gain_one, ("seq", "batch"), axis=0, tiled=True),
        lax.all_gather(bias_one, ("seq", "batch"), axis=0, tiled=True),
        lax.all_gather(gain_two, ("seq", "batch"), axis=0, tiled=True),
        lax.all_gather(bias_two, ("seq", "batch"), axis=0, tiled=True),
    )
    qkv_full, out_full, up_full, down_full = (fetched[0], fetched[1], fetched[2], fetched[3])
    gain_first = fetched[4].astype(jnp.float32)
    bias_first = fetched[5].astype(jnp.float32)
    gain_second = fetched[6].astype(jnp.float32)
    bias_second = fetched[7].astype(jnp.float32)
    inputs = tokens.astype(jnp.float32).reshape(row_count, features)
    normed = layer_norm(inputs, gain_first, bias_first).astype(jnp.bfloat16)
    mixed = jnp.dot(normed, qkv_full, preferred_element_type=jnp.float32).astype(jnp.bfloat16)
    queries = mixed[:, :features].reshape(local_len, sequences, H, HD)
    keys = mixed[:, features : 2 * features].reshape(local_len, sequences, features)
    values = mixed[:, 2 * features :].reshape(local_len, sequences, features)
    my_offset = lax.axis_index("seq") * local_len
    query_pos = my_offset + jnp.arange(local_len, dtype=jnp.int32)
    start_state = (
        jnp.zeros((sequences, H, local_len), jnp.float32),
        jnp.zeros((sequences, H, local_len), jnp.float32),
        jnp.zeros((sequences, H, local_len, HD), jnp.float32),
    )
    running, totals, accum = fold_blocks(
        start_state,
        lax.all_gather(keys, "seq", axis=0, tiled=True),
        lax.all_gather(values, "seq", axis=0, tiled=True),
        queries,
        query_pos,
        lengths,
        factor,
    )
    attended = accum / totals[..., None]
    log_totals = running + jnp.log(totals)
    attended_rows = (
        jnp.transpose(attended, (2, 0, 1, 3)).reshape(row_count, features).astype(jnp.bfloat16)
    )
    first = inputs + jnp.dot(attended_rows, out_full, preferred_element_type=jnp.float32)
    normed_two = layer_norm(first, gain_second, bias_second).astype(jnp.bfloat16)
    hidden = jnp.dot(normed_two, up_full, preferred_element_type=jnp.float32)
    active = jax.nn.gelu(hidden).astype(jnp.bfloat16)
    result = first + jnp.dot(active, down_full, preferred_element_type=jnp.float32)
    output = result.astype(jnp.bfloat16).reshape(local_len, sequences, features)
    again = (
        lax.all_gather(w_qkv, ("seq", "batch"), axis=0, tiled=True),
        lax.all_gather(w_out, ("seq", "batch"), axis=0, tiled=True),
        lax.all_gather(w_up, ("seq", "batch"), axis=0, tiled=True),
        lax.all_gather(w_down, ("seq", "batch"), axis=0, tiled=True),
    )
    qkv_full, out_full, up_full, down_full = (again[0], again[1], again[2], again[3])
    grad_rows = d_out.reshape(row_count, features)
    grad_float = grad_rows.astype(jnp.float32)
    d_down = jnp.dot(active.T, grad_rows, preferred_element_type=jnp.float32)
    d_active = jnp.dot(grad_rows, down_full.T, preferred_element_type=jnp.float32)
    unused, gelu_pull = jax.vjp(jax.nn.gelu, hidden)
    d_hidden = gelu_pull(d_active)[0].astype(jnp.bfloat16)
    d_up = jnp.dot(normed_two.T, d_hidden, preferred_element_type=jnp.float32)
    d_normed_two = jnp.dot(d_hidden, up_full.T, preferred_element_type=jnp.float32)
    unused, second_pull = jax.vjp(layer_norm, first, gain_second, bias_second)
    d_first_part, d_gain_two, d_bias_two = second_pull(d_normed_two)
    d_first = grad_float + d_first_part
    d_first_low = d_first.astype(jnp.bfloat16)
    d_out_w = jnp.dot(attended_rows.T, d_first_low, preferred_element_type=jnp.float32)
    d_attended = jnp.dot(d_first_low, out_full.T, preferred_element_type=jnp.float32).astype(
        jnp.bfloat16
    )
    grad_heads = d_attended.reshape(local_len, sequences, H, HD)
    grad_order = jnp.transpose(grad_heads.astype(jnp.float32), (1, 2, 0, 3))
    delta = jnp.sum(grad_order * attended, axis=-1)
    all_keys, all_values = (
        lax.all_gather(keys, "seq", axis=0, tiled=True),
        lax.all_gather(values, "seq", axis=0, tiled=True),
    )
    block_size, block_count = block_layout(all_keys.shape[0])
    numbers = jnp.arange(block_count, dtype=jnp.int32)
    zero_heads = jnp.zeros((local_len, sequences, H, HD), jnp.float32)

    def sender_step(d_query, number):
        offset = number * block_size
        key_block = lax.dynamic_slice_in_dim(all_keys, offset, block_size, 0)
        value_block = lax.dynamic_slice_in_dim(all_values, offset, block_size, 0)
        d_scores, weights, key_heads = signed_grads(
            queries,
            grad_heads,
            log_totals,
            delta,
            query_pos,
            key_block,
            value_block,
            offset,
            lengths,
            factor,
        )
        d_query = (
            d_query
            + jnp.einsum("bhqk,kbhd->qbhd", d_scores, key_heads, preferred_element_type=jnp.float32)
            * factor
        )
        key_part = (
            jnp.einsum("bhqk,qbhd->kbhd", d_scores, queries, preferred_element_type=jnp.float32)
            * factor
        )
        value_part = jnp.einsum(
            "bhqk,qbhd->kbhd", weights, grad_heads, preferred_element_type=jnp.float32
        )
        return (d_query, (key_part, value_part))

    d_query, (key_parts, value_parts) = lax.scan(sender_step, zero_heads, numbers)
    total_keys = all_keys.shape[0]
    term = jnp.concatenate(
        [
            key_parts.reshape(total_keys, sequences, features),
            value_parts.reshape(total_keys, sequences, features),
        ],
        axis=2,
    )
    kv_summed = lax.psum_scatter(term, "seq", scatter_dimension=0, tiled=True)
    d_key = kv_summed[:, :, :features]
    d_value = kv_summed[:, :, features:]
    d_mixed = jnp.concatenate(
        [
            d_query.reshape(row_count, features),
            d_key.reshape(row_count, features),
            d_value.reshape(row_count, features),
        ],
        axis=1,
    ).astype(jnp.bfloat16)
    d_qkv = jnp.dot(normed.T, d_mixed, preferred_element_type=jnp.float32)
    d_normed = jnp.dot(d_mixed, qkv_full.T, preferred_element_type=jnp.float32)
    unused, first_pull = jax.vjp(layer_norm, inputs, gain_first, bias_first)
    d_input_part, d_gain_one, d_bias_one = first_pull(d_normed)
    d_tokens = (d_first + d_input_part).astype(jnp.bfloat16).reshape(local_len, sequences, features)
    summed = (
        lax.psum_scatter(d_qkv, ("seq", "batch"), scatter_dimension=0, tiled=True),
        lax.psum_scatter(d_out_w, ("seq", "batch"), scatter_dimension=0, tiled=True),
        lax.psum_scatter(d_up, ("seq", "batch"), scatter_dimension=0, tiled=True),
        lax.psum_scatter(d_down, ("seq", "batch"), scatter_dimension=0, tiled=True),
        lax.psum_scatter(d_gain_one, ("seq", "batch"), scatter_dimension=0, tiled=True),
        lax.psum_scatter(d_bias_one, ("seq", "batch"), scatter_dimension=0, tiled=True),
        lax.psum_scatter(d_gain_two, ("seq", "batch"), scatter_dimension=0, tiled=True),
        lax.psum_scatter(d_bias_two, ("seq", "batch"), scatter_dimension=0, tiled=True),
    )
    return (
        output,
        d_tokens,
        summed[4],
        summed[5],
        summed[0],
        summed[1],
        summed[6],
        summed[7],
        summed[2],
        summed[3],
    )


def solution(mesh):
    return jax.shard_map(
        body,
        mesh=mesh,
        in_specs=(
            P("seq", "batch", None),
            P("batch"),
            P(("seq", "batch")),
            P(("seq", "batch")),
            P(("seq", "batch"), None),
            P(("seq", "batch"), None),
            P(("seq", "batch")),
            P(("seq", "batch")),
            P(("seq", "batch"), None),
            P(("seq", "batch"), None),
            P("seq", "batch", None),
        ),
        out_specs=(
            P("seq", "batch", None),
            P("seq", "batch", None),
            P(("seq", "batch")),
            P(("seq", "batch")),
            P(("seq", "batch"), None),
            P(("seq", "batch"), None),
            P(("seq", "batch")),
            P(("seq", "batch")),
            P(("seq", "batch"), None),
            P(("seq", "batch"), None),
        ),
        check_vma=False,
    )
```

profile of v0, /device:TPU:64, one launch (start us, length us, event | category | flops | bytes accessed | tf_op | source)
XLA Modules:
  0.0 3401.1 jit_solution(5392109833458117978)
XLA Ops:
  14.6 66.2 %all-reduce.15 = (bf16[768]{0:T(1024)(128)(2,1)S(1)}, bf16[768]{0:T(1024)(128)(2,1)S(1)}, bf16[768]{0:T(1024)(128)(2,1)S(1)}, bf16[768]{0:T(1024)(128)(2,1)S(1)}) all-reduce(bf16[768]{0:T(1024)(128)(2,1)S(1)} %dynamic-update-slice.1, bf16[768]{0:T(1024)(128)(2,1)S(1)} %dynamic-update-slice, ...), channel_id=1, replica_groups=mesh['seq'=16,'batch'=8] {'seq','batch'}, use_global_device_ids=true, to_apply=%add.1 | all-reduce | flops 3072 | bytes 12288
  84.3 234.1 %all-gather.16.cloned.1.call-done = bf16[128,6,2304]{2,1,0:T(8,128)(2,1)} async-done(((bf16[1,6,2304]{2,1,0:T(8,128)(2,1)}), bf16[128,6,2304]{2,1,0:T(8,128)(2,1)}) %all-gather.16.cloned.1.call-update) | async-done | bytes 3538960 | tf_op jit(solution)/shard_map/all_gather | solution.py:111
  318.4 6.6 reshape.328
  332.6 286.5 %all-gather.18.cloned.1.call-done = bf16[128,6,768]{2,1,0:T(8,128)(2,1)} async-done(((bf16[1,6,768]{2,1,0:T(8,128)(2,1)}), bf16[128,6,768]{2,1,0:T(8,128)(2,1)}) %all-gather.18.cloned.1.call-update) | async-done | bytes 1179664 | tf_op jit(solution)/shard_map/all_gather | solution.py:112
  623.9 309.2 %all-gather.20.cloned.1.call-done = bf16[128,6,3072]{2,1,0:T(8,128)(2,1)} async-done(((bf16[1,6,3072]{2,1,0:T(8,128)(2,1)}), bf16[128,6,3072]{2,1,0:T(8,128)(2,1)}) %all-gather.20.cloned.1.call-update) | async-done | bytes 4718608 | tf_op jit(solution)/shard_map/all_gather | solution.py:113
  933.1 7.7 reshape.332
  940.8 302.2 %all-gather.14.cloned.1.call-done = bf16[3072,768]{1,0:T(8,128)(2,1)} async-done(((bf16[24,768]{1,0:T(8,128)(2,1)}), bf16[3072,768]{1,0:T(8,128)(2,1)}) %all-gather.14.cloned.1.call-update) | async-done | bytes 4718608 | tf_op jit(solution)/shard_map/all_gather | solution.py:114
  1243.0 5.5 fusion.75
  1248.4 52.0 %all-gather.10.cloned.1.call-done = bf16[2048,2,768]{0,2,1:T(8,128)(2,1)} async-done(((bf16[128,2,768]{0,2,1:T(8,128)(2,1)}), bf16[2048,2,768]{0,2,1:T(8,128)(2,1)}) %all-gather.10.cloned.1.call-update) | async-done | bytes 6291472 | tf_op jit(solution)/shard_map/all_gather | solution.py:140
  1300.4 54.5 %all-gather.12.cloned.1.call-done = bf16[2048,2,768]{0,2,1:T(8,128)(2,1)} async-done(((bf16[128,2,768]{0,2,1:T(8,128)(2,1)}), bf16[2048,2,768]{0,2,1:T(8,128)(2,1)}) %all-gather.12.cloned.1.call-update) | async-done | bytes 6291472 | tf_op jit(solution)/shard_map/all_gather | solution.py:141
  1354.9 108.5 %while.33 = (s32[]{:T(128)}, f32[2,12,128]{2,1,0:T(8,128)S(1)}, f32[2,12,128]{2,1,0:T(8,128)}, f32[2,12,128,64]{2,3,1,0:T(8,128)}, s32[2]{0:T(128)}, /*index=5*/...) while((s32[]{:T(128)}, f32[2,12,128]{2,1,0:T(8,128)S(1)}, ...), condition=%wide.region_5.6_spmd.clone, body=%wide.region_2.5_spmd.clone.sunk | while | flops 218546048 | bytes 26711444 | solution.py:71
  1473.8 8.0 fusion.59
  1498.3 712.1 %while.34 = (s32[]{:T(128)}, f32[128,2,12,64]{0,3,2,1:T(8,128)S(1)}, f32[8,256,2,12,64]{1,0,4,3,2:T(8,128)}, f32[8,256,2,12,64]{1,0,4,3,2:T(8,128)}, s32[8]{0:T(...) while((s32[]{:T(128)}, ...), condition=%wide.region_12.13_spmd.clone, body=%wide.region_11.12_spmd.clone.sunk | while | flops 524845952 | bytes 55190984 | solution.py:222
  1509.8 35.8 %dynamic_update_slice.11 = f32[8,256,2,12,64]{1,0,4,3,2:T(8,128)} dynamic-update-slice(f32[8,256,2,12,64]{1,0,4,3,2:T(8,128)} %get-tuple-element.680, f32[1,256,2,12,64]{1,0,4,3,2:T(1,128)S(1)} %copy.87, s32[]{:T(128)S(6)} %copy.111, s32[]{:T(128)} %constant.110.clone.1..sunk.1, s32[]{:T(128)} %constant.110.clone.1..sunk.1, s32[]{:T(128)} %constant.110.clone.1..sunk.1, s32[]{:T(128)} %constant.110.clone.1..sunk.1) | dynamic-update-slice | bytes 3145732 | tf_op jit(solution)/shard_map/while/body/jit(dynamic_update_index_in_dim)/dynamic_update_slice | solution.py:222
  1545.7 4.1 fusion.150
  1551.5 35.9 %dynamic_update_slice.12 = f32[8,256,2,12,64]{1,0,4,3,2:T(8,128)} dynamic-update-slice(f32[8,256,2,12,64]{1,0,4,3,2:T(8,128)} %get-tuple-element.681, f32[1,256,2,12,64]{1,0,4,3,2:T(1,128)S(1)} %copy.88, s32[]{:T(128)S(6)} %copy.111, s32[]{:T(128)} %constant.110.clone.1..sunk.1, s32[]{:T(128)} %constant.110.clone.1..sunk.1, s32[]{:T(128)} %constant.110.clone.1..sunk.1, s32[]{:T(128)} %constant.110.clone.1..sunk.1) | dynamic-update-slice | bytes 3145732 | tf_op jit(solution)/shard_map/while/body/jit(dynamic_update_index_in_dim)/dynamic_update_slice | solution.py:222
  1598.9 35.8 %dynamic_update_slice.11 = f32[8,256,2,12,64]{1,0,4,3,2:T(8,128)} dynamic-update-slice(f32[8,256,2,12,64]{1,0,4,3,2:T(8,128)} %get-tuple-element.680, f32[1,256,2,12,64]{1,0,4,3,2:T(1,128)S(1)} %copy.87, s32[]{:T(128)S(6)} %copy.111, s32[]{:T(128)} %constant.110.clone.1..sunk.1, s32[]{:T(128)} %constant.110.clone.1..sunk.1, s32[]{:T(128)} %constant.110.clone.1..sunk.1, s32[]{:T(128)} %constant.110.clone.1..sunk.1) | dynamic-update-slice | bytes 3145732 | tf_op jit(solution)/shard_map/while/body/jit(dynamic_update_index_in_dim)/dynamic_update_slice | solution.py:222
  1634.7 4.1 fusion.150
  1640.5 35.9 %dynamic_update_slice.12 = f32[8,256,2,12,64]{1,0,4,3,2:T(8,128)} dynamic-update-slice(f32[8,256,2,12,64]{1,0,4,3,2:T(8,128)} %get-tuple-element.681, f32[1,256,2,12,64]{1,0,4,3,2:T(1,128)S(1)} %copy.88, s32[]{:T(128)S(6)} %copy.111, s32[]{:T(128)} %constant.110.clone.1..sunk.1, s32[]{:T(128)} %constant.110.clone.1..sunk.1, s32[]{:T(128)} %constant.110.clone.1..sunk.1, s32[]{:T(128)} %constant.110.clone.1..sunk.1) | dynamic-update-slice | bytes 3145732 | tf_op jit(solution)/shard_map/while/body/jit(dynamic_update_index_in_dim)/dynamic_update_slice | solution.py:222
  1687.9 35.8 %dynamic_update_slice.11 = f32[8,256,2,12,64]{1,0,4,3,2:T(8,128)} dynamic-update-slice(f32[8,256,2,12,64]{1,0,4,3,2:T(8,128)} %get-tuple-element.680, f32[1,256,2,12,64]{1,0,4,3,2:T(1,128)S(1)} %copy.87, s32[]{:T(128)S(6)} %copy.111, s32[]{:T(128)} %constant.110.clone.1..sunk.1, s32[]{:T(128)} %constant.110.clone.1..sunk.1, s32[]{:T(128)} %constant.110.clone.1..sunk.1, s32[]{:T(128)} %constant.110.clone.1..sunk.1) | dynamic-update-slice | bytes 3145732 | tf_op jit(solution)/shard_map/while/body/jit(dynamic_update_index_in_dim)/dynamic_update_slice | solution.py:222
  1723.7 4.1 fusion.150
  1729.5 35.9 %dynamic_update_slice.12 = f32[8,256,2,12,64]{1,0,4,3,2:T(8,128)} dynamic-update-slice(f32[8,256,2,12,64]{1,0,4,3,2:T(8,128)} %get-tuple-element.681, f32[1,256,2,12,64]{1,0,4,3,2:T(1,128)S(1)} %copy.88, s32[]{:T(128)S(6)} %copy.111, s32[]{:T(128)} %constant.110.clone.1..sunk.1, s32[]{:T(128)} %constant.110.clone.1..sunk.1, s32[]{:T(128)} %constant.110.clone.1..sunk.1, s32[]{:T(128)} %constant.110.clone.1..sunk.1) | dynamic-update-slice | bytes 3145732 | tf_op jit(solution)/shard_map/while/body/jit(dynamic_update_index_in_dim)/dynamic_update_slice | solution.py:222
  1776.9 35.8 %dynamic_update_slice.11 = f32[8,256,2,12,64]{1,0,4,3,2:T(8,128)} dynamic-update-slice(f32[8,256,2,12,64]{1,0,4,3,2:T(8,128)} %get-tuple-element.680, f32[1,256,2,12,64]{1,0,4,3,2:T(1,128)S(1)} %copy.87, s32[]{:T(128)S(6)} %copy.111, s32[]{:T(128)} %constant.110.clone.1..sunk.1, s32[]{:T(128)} %constant.110.clone.1..sunk.1, s32[]{:T(128)} %constant.110.clone.1..sunk.1, s32[]{:T(128)} %constant.110.clone.1..sunk.1) | dynamic-update-slice | bytes 3145732 | tf_op jit(solution)/shard_map/while/body/jit(dynamic_update_index_in_dim)/dynamic_update_slice | solution.py:222
  1812.7 4.1 fusion.150
  1818.5 35.9 %dynamic_update_slice.12 = f32[8,256,2,12,64]{1,0,4,3,2:T(8,128)} dynamic-update-slice(f32[8,256,2,12,64]{1,0,4,3,2:T(8,128)} %get-tuple-element.681, f32[1,256,2,12,64]{1,0,4,3,2:T(1,128)S(1)} %copy.88, s32[]{:T(128)S(6)} %copy.111, s32[]{:T(128)} %constant.110.clone.1..sunk.1, s32[]{:T(128)} %constant.110.clone.1..sunk.1, s32[]{:T(128)} %constant.110.clone.1..sunk.1, s32[]{:T(128)} %constant.110.clone.1..sunk.1) | dynamic-update-slice | bytes 3145732 | tf_op jit(solution)/shard_map/while/body/jit(dynamic_update_index_in_dim)/dynamic_update_slice | solution.py:222
  1865.9 35.8 %dynamic_update_slice.11 = f32[8,256,2,12,64]{1,0,4,3,2:T(8,128)} dynamic-update-slice(f32[8,256,2,12,64]{1,0,4,3,2:T(8,128)} %get-tuple-element.680, f32[1,256,2,12,64]{1,0,4,3,2:T(1,128)S(1)} %copy.87, s32[]{:T(128)S(6)} %copy.111, s32[]{:T(128)} %constant.110.clone.1..sunk.1, s32[]{:T(128)} %constant.110.clone.1..sunk.1, s32[]{:T(128)} %constant.110.clone.1..sunk.1, s32[]{:T(128)} %constant.110.clone.1..sunk.1) | dynamic-update-slice | bytes 3145732 | tf_op jit(solution)/shard_map/while/body/jit(dynamic_update_index_in_dim)/dynamic_update_slice | solution.py:222
  1901.7 4.1 fusion.150
  1907.5 35.9 %dynamic_update_slice.12 = f32[8,256,2,12,64]{1,0,4,3,2:T(8,128)} dynamic-update-slice(f32[8,256,2,12,64]{1,0,4,3,2:T(8,128)} %get-tuple-element.681, f32[1,256,2,12,64]{1,0,4,3,2:T(1,128)S(1)} %copy.88, s32[]{:T(128)S(6)} %copy.111, s32[]{:T(128)} %constant.110.clone.1..sunk.1, s32[]{:T(128)} %constant.110.clone.1..sunk.1, s32[]{:T(128)} %constant.110.clone.1..sunk.1, s32[]{:T(128)} %constant.110.clone.1..sunk.1) | dynamic-update-slice | bytes 3145732 | tf_op jit(solution)/shard_map/while/body/jit(dynamic_update_index_in_dim)/dynamic_update_slice | solution.py:222
  1954.9 35.8 %dynamic_update_slice.11 = f32[8,256,2,12,64]{1,0,4,3,2:T(8,128)} dynamic-update-slice(f32[8,256,2,12,64]{1,0,4,3,2:T(8,128)} %get-tuple-element.680, f32[1,256,2,12,64]{1,0,4,3,2:T(1,128)S(1)} %copy.87, s32[]{:T(128)S(6)} %copy.111, s32[]{:T(128)} %constant.110.clone.1..sunk.1, s32[]{:T(128)} %constant.110.clone.1..sunk.1, s32[]{:T(128)} %constant.110.clone.1..sunk.1, s32[]{:T(128)} %constant.110.clone.1..sunk.1) | dynamic-update-slice | bytes 3145732 | tf_op jit(solution)/shard_map/while/body/jit(dynamic_update_index_in_dim)/dynamic_update_slice | solution.py:222
  1990.7 4.1 fusion.150
  1996.5 35.9 %dynamic_update_slice.12 = f32[8,256,2,12,64]{1,0,4,3,2:T(8,128)} dynamic-update-slice(f32[8,256,2,12,64]{1,0,4,3,2:T(8,128)} %get-tuple-element.681, f32[1,256,2,12,64]{1,0,4,3,2:T(1,128)S(1)} %copy.88, s32[]{:T(128)S(6)} %copy.111, s32[]{:T(128)} %constant.110.clone.1..sunk.1, s32[]{:T(128)} %constant.110.clone.1..sunk.1, s32[]{:T(128)} %constant.110.clone.1..sunk.1, s32[]{:T(128)} %constant.110.clone.1..sunk.1) | dynamic-update-slice | bytes 3145732 | tf_op jit(solution)/shard_map/while/body/jit(dynamic_update_index_in_dim)/dynamic_update_slice | solution.py:222
  2043.9 35.8 %dynamic_update_slice.11 = f32[8,256,2,12,64]{1,0,4,3,2:T(8,128)} dynamic-update-slice(f32[8,256,2,12,64]{1,0,4,3,2:T(8,128)} %get-tuple-element.680, f32[1,256,2,12,64]{1,0,4,3,2:T(1,128)S(1)} %copy.87, s32[]{:T(128)S(6)} %copy.111, s32[]{:T(128)} %constant.110.clone.1..sunk.1, s32[]{:T(128)} %constant.110.clone.1..sunk.1, s32[]{:T(128)} %constant.110.clone.1..sunk.1, s32[]{:T(128)} %constant.110.clone.1..sunk.1) | dynamic-update-slice | bytes 3145732 | tf_op jit(solution)/shard_map/while/body/jit(dynamic_update_index_in_dim)/dynamic_update_slice | solution.py:222
  2079.7 4.1 fusion.150
  2085.5 35.9 %dynamic_update_slice.12 = f32[8,256,2,12,64]{1,0,4,3,2:T(8,128)} dynamic-update-slice(f32[8,256,2,12,64]{1,0,4,3,2:T(8,128)} %get-tuple-element.681, f32[1,256,2,12,64]{1,0,4,3,2:T(1,128)S(1)} %copy.88, s32[]{:T(128)S(6)} %copy.111, s32[]{:T(128)} %constant.110.clone.1..sunk.1, s32[]{:T(128)} %constant.110.clone.1..sunk.1, s32[]{:T(128)} %constant.110.clone.1..sunk.1, s32[]{:T(128)} %constant.110.clone.1..sunk.1) | dynamic-update-slice | bytes 3145732 | tf_op jit(solution)/shard_map/while/body/jit(dynamic_update_index_in_dim)/dynamic_update_slice | solution.py:222
  2132.9 35.8 %dynamic_update_slice.11 = f32[8,256,2,12,64]{1,0,4,3,2:T(8,128)} dynamic-update-slice(f32[8,256,2,12,64]{1,0,4,3,2:T(8,128)} %get-tuple-element.680, f32[1,256,2,12,64]{1,0,4,3,2:T(1,128)S(1)} %copy.87, s32[]{:T(128)S(6)} %copy.111, s32[]{:T(128)} %constant.110.clone.1..sunk.1, s32[]{:T(128)} %constant.110.clone.1..sunk.1, s32[]{:T(128)} %constant.110.clone.1..sunk.1, s32[]{:T(128)} %constant.110.clone.1..sunk.1) | dynamic-update-slice | bytes 3145732 | tf_op jit(solution)/shard_map/while/body/jit(dynamic_update_index_in_dim)/dynamic_update_slice | solution.py:222
  2168.8 4.1 fusion.150
  2174.5 35.9 %dynamic_update_slice.12 = f32[8,256,2,12,64]{1,0,4,3,2:T(8,128)} dynamic-update-slice(f32[8,256,2,12,64]{1,0,4,3,2:T(8,128)} %get-tuple-element.681, f32[1,256,2,12,64]{1,0,4,3,2:T(1,128)S(1)} %copy.88, s32[]{:T(128)S(6)} %copy.111, s32[]{:T(128)} %constant.110.clone.1..sunk.1, s32[]{:T(128)} %constant.110.clone.1..sunk.1, s32[]{:T(128)} %constant.110.clone.1..sunk.1, s32[]{:T(128)} %constant.110.clone.1..sunk.1) | dynamic-update-slice | bytes 3145732 | tf_op jit(solution)/shard_map/while/body/jit(dynamic_update_index_in_dim)/dynamic_update_slice | solution.py:222
  2210.4 13.6 reshape.315
  2224.0 13.6 reshape.314
  2237.6 18.7 pad_maximum_fusion
  2257.3 7.8 fusion.67
  2271.1 5.2 fusion.65
  2276.4 238.4 %reduce-scatter.9.cloned.1.call-done = f32[128,2,1536]{0,2,1:T(8,128)} async-done(((f32[2048,2,1536]{0,2,1:T(8,128)}), f32[128,2,1536]{0,2,1:T(8,128)}) %reduce-scatter.9.cloned.1.call-update) | async-done | bytes 1572880 | tf_op jit(solution)/shard_map/reduce_scatter | solution.py:231
  2524.2 4.2 fusion.64
  2528.4 402.8 %fusion.68 = (f32[8,2304]{1,0:T(8,128)S(1)}, f32[8,768]{1,0:T(8,128)S(1)}, f32[8,3072]{1,0:T(8,128)S(1)}) fusion(f32[768,2304]{1,0:T(8,128)} %fusion.64, f32[768,768]{1,0:T(8,128)} %fusion.76, f32[768,3072]{1,0:T(8,128)} %fusion.65), kind=kCustom, calls=%all-reduce-scatter.3 | all-reduce-scatter fusion | flops 6291457 | bytes 19070976
  2935.1 12.3 collective-permute-start.60
  2955.3 10.0 collective-permute-start.53
  3001.6 5.1 collective-permute-start.38
  3030.0 6.7 collective-permute-done.33
  3039.3 6.9 collective-permute-done.32
  3061.1 5.6 collective-permute-start.18
  3085.9 4.1 collective-permute-start.9
  3094.6 5.9 collective-permute-start.6
  3107.8 6.0 fusion.61
  3119.2 4.9 collective-permute-start.1
  3149.8 7.6 collective-permute-start.85
  3175.0 4.2 collective-permute-start.77
  3187.4 66.2 %all-reduce.14 = (f32[768]{0:T(1024)S(1)}, f32[768]{0:T(1024)S(1)}, f32[768]{0:T(1024)S(1)}, f32[768]{0:T(1024)S(1)}) all-reduce(f32[768]{0:T(1024)S(1)} %copy-done.129, f32[768]{0:T(1024)S(1)} %copy-done.130, f32[768]{0:T(1024)} %get-tuple-element.385, ...), channel_id=3, replica_groups=mesh['seq'=16,'batch'=8] {'seq','batch'}, use_global_device_ids=true, to_apply=%region_17.18.clone | all-reduce | flops 3072 | bytes 24576
  3256.0 27.2 concatenate.10
  3283.2 4.3 collective-permute-start.73
  3293.4 6.8 collective-permute-start.70
  3303.6 32.6 concatenate.9
  3344.8 6.9 collective-permute-start.65
  3361.9 31.5 concatenate.11
  (944 shorter events, 478.3 us)
Async XLA Ops:
  7.2 311.2 %all-gather.16.cloned.1.call-start = ((), (), s32[]{:S(2)}) async-start(), calls=%async_computation.7 | async-start | bytes 4755456 | tf_op jit(solution)/shard_map/all_gather | solution.py:111
  7.9 611.2 %all-gather.18.cloned.1.call-start = ((), (), s32[]{:S(2)}) async-start(), calls=%async_computation.8 | async-start | bytes 1585152 | tf_op jit(solution)/shard_map/all_gather | solution.py:112
  8.7 924.4 %all-gather.20.cloned.1.call-start = ((), (), s32[]{:S(2)}) async-start(), calls=%async_computation.9 | async-start | bytes 6340608 | tf_op jit(solution)/shard_map/all_gather | solution.py:113
  9.4 1233.6 %all-gather.14.cloned.1.call-start = ((), (), s32[]{:S(2)}) async-start(), calls=%async_computation.4 | async-start | bytes 4755456 | tf_op jit(solution)/shard_map/all_gather | solution.py:114
  10.0 1290.5 %all-gather.10.cloned.1.call-start = ((), (), s32[]{:S(2)}) async-start(), calls=%async_computation.2 | async-start | bytes 6684672 | tf_op jit(solution)/shard_map/all_gather | solution.py:140
  329.6 1025.4 %all-gather.12.cloned.1.call-start = ((), (), s32[]{:S(2)}) async-start(), calls=%async_computation.3 | async-start | bytes 6684672 | tf_op jit(solution)/shard_map/all_gather | solution.py:141
  330.9 2183.8 %reduce-scatter.9.cloned.1.call-start = ((), (), s32[]{:S(2)}) async-start(), calls=%async_computation.5 | async-start | bytes 26738688 | tf_op jit(solution)/shard_map/reduce_scatter | solution.py:231
  2256.3 1137.7 %reduce-scatter.11.cloned.1.call-start = ((), (), s32[]{:S(2)}) async-start(), calls=%async_computation.6 | async-start | bytes 9510912 | tf_op jit(solution)/shard_map/reduce_scatter | solution.py:251
  2931.2 18.8 collective-permute-start.62
  2932.5 18.8 collective-permute-start.61
  2933.8 14.9 collective-permute-start.63
  2935.1 17.5 collective-permute-start.60
  2950.0 15.3 collective-permute-start.57
  2951.4 18.0 collective-permute-start.56
  2952.7 18.4 collective-permute-start.55
  2954.0 20.2 collective-permute-start.54
  2955.3 21.7 collective-permute-start.53
  2971.0 13.8 collective-permute-start.50
  2991.1 15.6 collective-permute-start.42
  2993.7 15.6 collective-permute-start.41
  2996.7 15.7 collective-permute-start.40
  3000.1 14.5 collective-permute-start.39
  3001.6 16.7 collective-permute-start.38
  3009.3 14.3 collective-permute-start.36
  3018.3 30.5 collective-permute-start.30
  3019.7 30.5 collective-permute-start.29
  3024.4 27.1 collective-permute-start.28
  3025.7 21.8 collective-permute-start.31
  3052.8 13.9 collective-permute-start.22
  3061.1 14.4 collective-permute-start.18
  3075.4 14.5 collective-permute-start.13
  3077.7 15.0 collective-permute-start.12
  3083.4 17.1 collective-permute-start.10
  3085.9 16.8 collective-permute-start.9
  3090.0 15.9 collective-permute-start.8
  3092.7 23.0 collective-permute-start.7
  3094.6 24.6 collective-permute-start.6
  3100.5 23.6 collective-permute-start.5
  3102.7 23.4 collective-permute-start.4
  3105.9 22.9 collective-permute-start.3
  3115.7 18.2 collective-permute-start.2
  3119.2 16.6 collective-permute-start.1
  3126.1 16.5 collective-permute-start.94
  3142.6 14.8 collective-permute-start.89
  3143.9 15.1 collective-permute-start.88
  3145.3 15.1 collective-permute-start.87
  3146.6 17.4 collective-permute-start.86
  3149.8 16.4 collective-permute-start.85
  3160.4 14.6 collective-permute-start.82
  3164.0 15.2 collective-permute-start.81
  3166.2 14.9 collective-permute-start.80
  3168.4 14.7 collective-permute-start.79
  3170.9 112.3 %collective-permute-start.78 = (f32[8,3072]{1,0:T(8,128)S(1)}, f32[8,3072]{1,0:T(8,128)}, u32[]{:S(2)}, u32[]{:S(2)}) collective-permute-start(f32[8,3072]{1,0:T(8,128)S(1)} %get-tuple-element.448), channel_id=1, source_target_pairs={{0,15},{1,16},{2,17},{3,18},{4,19},{5,20},{6,21},{7,22},{8,23},{9,... | collective-permute-start | bytes 294920
  3175.0 112.5 %collective-permute-start.77 = (f32[8,3072]{1,0:T(8,128)S(1)}, f32[8,3072]{1,0:T(8,128)}, u32[]{:S(2)}, u32[]{:S(2)}) collective-permute-start(f32[8,3072]{1,0:T(8,128)S(1)} %get-tuple-element.448), channel_id=1, source_target_pairs={{0,14},{1,15},{2,16},{3,17},{4,18},{5,19},{6,20},{7,21},{8,22},{9,... | collective-permute-start | bytes 294920
  3179.2 111.7 %collective-permute-start.76 = (f32[8,3072]{1,0:T(8,128)S(1)}, f32[8,3072]{1,0:T(8,128)}, u32[]{:S(2)}, u32[]{:S(2)}) collective-permute-start(f32[8,3072]{1,0:T(8,128)S(1)} %get-tuple-element.448), channel_id=1, source_target_pairs={{0,13},{1,14},{2,15},{3,16},{4,17},{5,18},{6,19},{7,20},{8,21},{9,... | collective-permute-start | bytes 294920
  3181.1 112.3 %collective-permute-start.75 = (f32[8,3072]{1,0:T(8,128)S(1)}, f32[8,3072]{1,0:T(8,128)}, u32[]{:S(2)}, u32[]{:S(2)}) collective-permute-start(f32[8,3072]{1,0:T(8,128)S(1)} %get-tuple-element.448), channel_id=1, source_target_pairs={{0,12},{1,13},{2,14},{3,15},{4,16},{5,17},{6,18},{7,19},{8,20},{9,... | collective-permute-start | bytes 294920
  3183.0 117.2 %collective-permute-start.74 = (f32[8,3072]{1,0:T(8,128)S(1)}, f32[8,3072]{1,0:T(8,128)}, u32[]{:S(2)}, u32[]{:S(2)}) collective-permute-start(f32[8,3072]{1,0:T(8,128)S(1)} %get-tuple-element.448), channel_id=1, source_target_pairs={{0,11},{1,12},{2,13},{3,14},{4,15},{5,16},{6,17},{7,18},{8,19},{9,... | collective-permute-start | bytes 294920
  3283.2 53.1 %collective-permute-start.73 = (f32[8,3072]{1,0:T(8,128)S(1)}, f32[8,3072]{1,0:T(8,128)}, u32[]{:S(2)}, u32[]{:S(2)}) collective-permute-start(f32[8,3072]{1,0:T(8,128)S(1)} %get-tuple-element.448), channel_id=1, source_target_pairs={{0,10},{1,11},{2,12},{3,13},{4,14},{5,15},{6,16},{7,17},{8,18},{9,... | collective-permute-start | bytes 294920
  3287.5 51.3 %collective-permute-start.72 = (f32[8,3072]{1,0:T(8,128)S(1)}, f32[8,3072]{1,0:T(8,128)}, u32[]{:S(2)}, u32[]{:S(2)}) collective-permute-start(f32[8,3072]{1,0:T(8,128)S(1)} %get-tuple-element.448), channel_id=1, source_target_pairs={{0,9},{1,10},{2,11},{3,12},{4,13},{5,14},{6,15},{7,16},{8,17},{9,1... | collective-permute-start | bytes 294920
  3290.8 51.4 %collective-permute-start.71 = (f32[8,3072]{1,0:T(8,128)S(1)}, f32[8,3072]{1,0:T(8,128)}, u32[]{:S(2)}, u32[]{:S(2)}) collective-permute-start(f32[8,3072]{1,0:T(8,128)S(1)} %get-tuple-element.448), channel_id=1, source_target_pairs={{0,8},{1,9},{2,10},{3,11},{4,12},{5,13},{6,14},{7,15},{8,16},{9,17... | collective-permute-start | bytes 294920
  3293.4 51.3 %collective-permute-start.70 = (f32[8,3072]{1,0:T(8,128)S(1)}, f32[8,3072]{1,0:T(8,128)}, u32[]{:S(2)}, u32[]{:S(2)}) collective-permute-start(f32[8,3072]{1,0:T(8,128)S(1)} %get-tuple-element.448), channel_id=1, source_target_pairs={{0,7},{1,8},{2,9},{3,10},{4,11},{5,12},{6,13},{7,14},{8,15},{9,16}... | collective-permute-start | bytes 294920
  3300.3 51.4 %collective-permute-start.69 = (f32[8,3072]{1,0:T(8,128)S(1)}, f32[8,3072]{1,0:T(8,128)}, u32[]{:S(2)}, u32[]{:S(2)}) collective-permute-start(f32[8,3072]{1,0:T(8,128)S(1)} %get-tuple-element.448), channel_id=1, source_target_pairs={{0,6},{1,7},{2,8},{3,9},{4,10},{5,11},{6,12},{7,13},{8,14},{9,15},... | collective-permute-start | bytes 294920
  3336.3 17.9 collective-permute-start.68
  3338.9 15.4 collective-permute-start.67
  (271 other events, 8412.4 us)
Sparse Core Ops, SparseCore 0:
  9.7 308.6 all-gather.15
  320.1 298.9 all-gather.17
  620.8 312.2 all-gather.19
  934.6 308.2 all-gather.13
  1245.0 55.3 all-gather.9
  1302.5 52.3 all-gather.11
  2256.5 258.2 reduce-scatter.8
  2517.7 677.6 reduce-scatter.10
where the time goes:
time: 3430 us; the launch traced here: 3400 us
  waiting for transfers between devices  1500 us (44%)
  local copies, waits for them, and re-layouts  830 us (24%)
  blocking collectives  535 us (16%)
  starting transfers between devices  264 us (8%)
  matrix products  166 us (5%)
  other arithmetic  81 us (2%)
    dynamic_update_slice x32, local copies, waits for them, and re-layouts, body(): lax.scan(sender_step, zero_heads, numbers)  599 us
    unnamed x3, blocking collectives  535 us
    all_gather x1, waiting for transfers between devices, body(): lax.all_gather(w_up, ('seq', 'batch'), axis=0, tiled=True)  309 us
    all_gather x1, waiting for transfers between devices, body(): lax.all_gather(w_down, ('seq', 'batch'), axis=0, tiled=True)  302 us
    all_gather x1, waiting for transfers between devices, body(): lax.all_gather(w_out, ('seq', 'batch'), axis=0, tiled=True)  286 us
    unnamed x96, starting transfers between devices  263 us
    reduce_scatter x1, waiting for transfers between devices, body(): kv_summed = lax.psum_scatter(term, 'seq', scatter_dimension=0, tiled=True)  238 us
    all_gather x1, waiting for transfers between devices, body(): lax.all_gather(w_qkv, ('seq', 'batch'), axis=0, tiled=True)  234 us
  transfers between devices with their start and end apart: 104, of which 11 were waited for; matrix products, arithmetic and copies ran while one was open for 17% of the time, Pallas kernels for 0%

commit v1 on v0

v1 whole, which is shorter than its diff:
```python
import functools
import math

import jax
import jax.numpy as jnp
import numpy as np
from jax import lax
from jax.experimental import pallas as pl
from jax.experimental.pallas import tpu as pltpu
from jax.sharding import PartitionSpec as P

H = 12
HD = 64
EPSILON = 1e-05
BF = jnp.bfloat16
F32 = jnp.float32
VMEM_LIMIT = 50 * 1024 * 1024
BOTH = ("seq", "batch")
SAME_CORE = [[2 * k + c for k in range(8)] for c in range(2)]
SWAP_CORE = [(i, i ^ 1) for i in range(16)]
TURNS = [(0, 0), (0, 1), (0, 2), (0, 3), (1, 3), (1, 2), (1, 1), (1, 0)]
RING = [(c ^ (i & 1), z, x) for i, (z, x) in enumerate(TURNS) for c in range(2)]
RINGS = [
    [((y * 2 + (low ^ z)) * 2 + c) * 8 + z * 4 + x for c, z, x in RING]
    for y in range(4)
    for low in range(2)
]


def one_hot(rows):
    out = np.zeros((len(rows), len(rows)), np.float32)
    out[np.arange(len(rows)), rows] = 1.0
    return out


def in_order(outer, size):
    natural = np.arange(outer * 16 * size).reshape(outer, 2, 8, size)
    return np.stack([natural[:, c, z * 4 + x] for c, z, x in RING])


QKV_ORDER = one_hot(np.arange(768).reshape(8, 2, 8, 6).transpose(1, 2, 0, 3).reshape(768))
ROW_ORDER = one_hot(in_order(8, 6).reshape(768))
UNIT_ORDER = one_hot(in_order(2, 24).reshape(768))


def regroup_matrix():
    out = np.zeros((480, 512), np.float32)
    for j in range(8):
        for r in range(24):
            out[j * 24 + r, j * 64 + r] = 1.0
        for r in range(6):
            for k in range(4):
                out[192 + k * 48 + j * 6 + r, j * 64 + 30 + k * 6 + r] = 1.0
            out[384 + j * 6 + r, j * 64 + 24 + r] = 1.0
            out[432 + j * 6 + r, j * 64 + 54 + r] = 1.0
    return out


REGROUP = regroup_matrix()
NT = (((1,), (1,)), ((), ()))
NN = (((1,), (0,)), ((), ()))
TN = (((0,), (0,)), ((), ()))


def dot(left, right, dims=NN):
    return lax.dot_general(left, right, dims, preferred_element_type=F32)


def about(us):
    return pl.CostEstimate(flops=int(us * 1.1e9), bytes_accessed=0, transcendentals=0)


def call(kernel, outs, ins, us, scratch=(), **kwargs):
    return pl.pallas_call(
        kernel,
        out_shape=outs,
        scratch_shapes=list(scratch),
        cost_estimate=about(us),
        compiler_params=pltpu.CompilerParams(vmem_limit_bytes=VMEM_LIMIT),
        **kwargs,
    )(*ins)


def shape(dims, dtype):
    return jax.ShapeDtypeStruct(dims, dtype)


def normalize(values):
    center = jnp.mean(values, axis=-1, keepdims=True)
    shifted = values - center
    spread = jnp.mean(shifted * shifted, axis=-1, keepdims=True)
    scale = lax.rsqrt(spread + EPSILON)
    return shifted * scale, scale


def regroup_kernel(slots_ref, order_ref, rest_ref, qkv_ref):
    rows = dot(order_ref[...], slots_ref[...].reshape(512, 768)).astype(BF)
    rest_ref[...] = rows[0:432]
    for g in range(8):
        qkv_ref[g] = rows[432:480]


def project_kernel(
    core_ref, own_ref, mine_ref, other_ref, order_ref,
    normed_ref, wt_ref, gains_ref, qkv_ref, w_scr, t_scr,
):
    core = core_ref[0]
    mine = pl.ds(pl.multiple_of(core * 384, 384), 384)
    theirs = pl.ds(pl.multiple_of(384 - core * 384, 384), 384)
    w_scr[mine, :] = mine_ref[...].reshape(384, 768)[:, :640]
    w_scr[theirs, :] = other_ref[...].reshape(384, 768)[:, :640]
    t_scr[...] = dot(w_scr[...].T, order_ref[...])
    wt_ref[...] = t_scr[0:576].astype(BF)
    gains = t_scr[576:584]
    gains_ref[...] = gains
    gain, bias = gains[0:1], gains[1:2]
    for j in range(8):
        hat, _ = normalize(own_ref[j].astype(F32))
        normed_ref[j * 128 : (j + 1) * 128, :] = (hat * gain + bias).astype(BF)
    for j in range(4):
        qkv_ref[:, j * 256 : (j + 1) * 256] = dot(
            wt_ref[...], normed_ref[j * 256 : (j + 1) * 256, :], NT
        ).astype(BF)


def tile_mask(first_key, first_query, core, length):
    row = lax.broadcasted_iota(jnp.int32, (256, 256), 0)
    lane = lax.broadcasted_iota(jnp.int32, (256, 256), 1)
    key = first_key + jnp.where(row < 128, row + 128 * core, row - 128 * core)
    query = first_query + 128 * core + jnp.where(lane < 128, lane, lane + 128)
    return (key <= query) & (key < length)


def fill_keys(own_ref, other_ref, k_scr, base):
    for u in range(3):
        for j in range(8):
            rows, lanes = pl.ds(base + u * 64, 64), pl.ds(j * 128, 128)
            k_scr[u, j * 256 : j * 256 + 128, :] = own_ref[rows, lanes].T
            k_scr[u, j * 256 + 128 : j * 256 + 256, :] = other_ref[rows, lanes].T


def fill_lanes(own_ref, other_ref, scr, base):
    for j in range(8):
        scr[:, j * 256 : j * 256 + 128] = own_ref[base : base + 192, j * 128 : j * 128 + 128]
        scr[:, j * 256 + 128 : j * 256 + 256] = other_ref[
            base : base + 192, j * 128 : j * 128 + 128
        ]


def loop_bounds(m, length):
    full = jnp.minimum(2 * m, length // 256)
    every = jnp.minimum(2 * m + 2, (length + 255) // 256)
    return full, every


def forward_kernel(info_ref, q_ref, own_ref, other_ref, o_ref, low_ref, lse_ref, k_scr, v_scr):
    length, core = info_ref[0], info_ref[1]
    fill_keys(own_ref, other_ref, k_scr, 0)
    fill_lanes(own_ref, other_ref, v_scr, 192)
    for m in range(4):
        lanes = slice(m * 256, (m + 1) * 256)
        queries = [q_ref[u * 64 : (u + 1) * 64, lanes] * BF(0.125) for u in range(3)]

        def step(jk, carry, masked, queries=queries, m=m):
            start = pl.multiple_of(jk * 256, 256)
            if masked:
                allowed = tile_mask(start, m * 512, core, length)
            out = []
            for u in range(3):
                top, total, accum = carry[u]
                s = dot(k_scr[u, pl.ds(start, 256), :], queries[u])
                t = s * s + 1.0
                r = lax.rsqrt(t)
                a = t * r
                g = s * r
                if masked:
                    a = jnp.where(allowed, a, -1e30)
                fresh = jnp.maximum(top, jnp.max(a, axis=0, keepdims=True))
                e = jnp.exp(a - fresh)
                rescale = jnp.exp(top - fresh)
                total = total * rescale + jnp.sum(e, axis=0, keepdims=True)
                w = (g * e).astype(BF)
                accum = accum * rescale + dot(
                    v_scr[u * 64 : (u + 1) * 64, pl.ds(start, 256)], w
                )
                out.append((fresh, total, accum))
            return tuple(out)

        zero = (jnp.zeros((1, 256), F32), jnp.zeros((1, 256), F32), jnp.zeros((64, 256), F32))
        full, every = loop_bounds(m, length)
        carry = lax.fori_loop(0, full, functools.partial(step, masked=False), (zero,) * 3)
        carry = lax.fori_loop(full, every, functools.partial(step, masked=True), carry)
        for u in range(3):
            top, total, accum = carry[u]
            o = accum / total
            o_ref[u * 64 : (u + 1) * 64, lanes] = o
            for half in range(2):
                low_ref[2 * m + half, u * 64 : (u + 1) * 64, :] = o[
                    :, half * 128 : half * 128 + 128
                ].astype(BF)
            lse_ref[u : u + 1, lanes] = top + jnp.log(total)


def backward_kernel(
    info_ref, q_ref, own_ref, other_ref, o_ref, lse_ref, da_ref,
    dq_ref, down_ref, dother_ref,
    k_scr, kt_scr, v_scr, dk_scr, dv_scr,
):
    length, core = info_ref[0], info_ref[1]
    fill_keys(own_ref, other_ref, k_scr, 0)
    fill_lanes(own_ref, other_ref, kt_scr, 0)
    fill_keys(own_ref, other_ref, v_scr, 192)
    dk_scr[...] = jnp.zeros_like(dk_scr)
    dv_scr[...] = jnp.zeros_like(dv_scr)
    for m in range(4):
        lanes = slice(m * 256, (m + 1) * 256)
        sets = []
        for u in range(3):
            rows = slice(u * 64, (u + 1) * 64)
            qt = q_ref[rows, lanes] * BF(0.125)
            dat = jnp.concatenate([da_ref[2 * m, rows, :], da_ref[2 * m + 1, rows, :]], axis=1)
            delta = jnp.sum(dat.astype(F32) * o_ref[rows, lanes], axis=0, keepdims=True)
            sets.append((qt, qt.T, dat, dat.T, delta, lse_ref[u : u + 1, lanes]))

        def step(jk, carry, masked, sets=sets, m=m):
            start = pl.multiple_of(jk * 256, 256)
            tile = pl.ds(start, 256)
            if masked:
                allowed = tile_mask(start, m * 512, core, length)
            out = []
            for u in range(3):
                qt, q, dat, da, delta, lse = sets[u]
                s = dot(k_scr[u, tile, :], qt)
                dp = dot(v_scr[u, tile, :], dat)
                t = s * s + 1.0
                r = lax.rsqrt(t)
                g = s * r
                p = jnp.exp(t * r - lse)
                if masked:
                    p = jnp.where(allowed, p, 0.0)
                w = (g * p).astype(BF)
                ds = (p * (dp * (r * r * (r - 1.0) + 1.0) - g * delta)).astype(BF)
                dv_scr[u, tile, :] += dot(w, da)
                dk_scr[u, tile, :] += dot(ds, q)
                out.append(carry[u] + dot(kt_scr[u * 64 : (u + 1) * 64, tile], ds))
            return tuple(out)

        full, every = loop_bounds(m, length)
        carry = (jnp.zeros((64, 256), F32),) * 3
        carry = lax.fori_loop(0, full, functools.partial(step, masked=False), carry)
        carry = lax.fori_loop(full, every, functools.partial(step, masked=True), carry)
        for u in range(3):
            dq_ref[u * 64 : (u + 1) * 64, lanes] = (carry[u] * 0.125).astype(BF)
    for scr, base in ((dk_scr, 0), (dv_scr, 192)):
        for u in range(3):
            for j in range(8):
                rows, lanes = pl.ds(base + u * 64, 64), pl.ds(j * 128, 128)
                down_ref[rows, lanes] = scr[u, j * 256 : j * 256 + 128, :].T
                dother_ref[rows, lanes] = scr[u, j * 256 + 128 : j * 256 + 256, :].T.astype(BF)


GELU_SCALE = math.sqrt(2.0 / math.pi)


def feed_kernel(
    x_ref, dy_ref, att_ref, gains_ref, order_ref, order_t_ref, down_ref, up_ref, out_ref,
    y_ref, dfirst_ref, datt_ref, dgain_ref, grads_ref,
    hat_scr, scale_scr, n2_scr, n2t_scr, acc_scr, dn_scr, attt_scr, gdown, gup, gout, sems,
):
    k = pl.program_id(0)
    gain, bias = gains_ref[2:3], gains_ref[3:4]

    @pl.when(k == 0)
    def _():
        for b in range(2):
            natural = att_ref[b * 4 : b * 4 + 4].reshape(768, 128)
            attt_scr[:, b * 128 : (b + 1) * 128] = dot(order_ref[...], natural).astype(BF)
        first = x_ref[...].astype(F32) + dot(attt_scr[...].T, out_ref[...].reshape(768, 768))
        hat, scale = normalize(first)
        hat_scr[...] = hat
        scale_scr[...] = scale
        n2 = dot((hat * gain + bias).astype(BF), order_ref[...], NT).astype(BF)
        n2_scr[...] = n2
        n2t_scr[...] = n2.T
        acc_scr[...] = first
        dn_scr[...] = jnp.zeros_like(dn_scr)

    up = up_ref[...].reshape(768, 768)
    down = down_ref[...].reshape(768, 768)
    dy = dy_ref[...]
    hidden = dot(n2_scr[...], up)
    d_active = dot(dy, down, NT)
    square = hidden * hidden
    tanh = jnp.tanh(GELU_SCALE * hidden * (1.0 + 0.044715 * square))
    share = 0.5 + 0.5 * tanh
    active = (hidden * share).astype(BF)
    slope = share + 0.5 * hidden * (1.0 - tanh * tanh) * (
        GELU_SCALE * (1.0 + (3 * 0.044715) * square)
    )
    d_hidden = (slope * d_active).astype(BF)
    acc_scr[...] += dot(active, down)
    dn_scr[...] += dot(d_hidden, up, NT)
    gdown[k] = dot(active.T, dy).astype(BF).reshape(16, 48, 768)
    gup[k] = dot(n2t_scr[...], d_hidden).astype(BF).reshape(16, 48, 768)

    def copy(source, block, sem):
        return pltpu.make_async_copy(
            source, grads_ref.at[:, pl.ds(48 * block, 48), :], sems.at[sem]
        )

    for i in range(4):

        @pl.when(k == i)
        def _(i=i):
            copy(gdown.at[i], i, i).start()
            copy(gup.at[i], 4 + i, 4 + i).start()

    @pl.when(k == 3)
    def _():
        y_ref[...] = acc_scr[...].astype(BF)
        dn = dn_scr[...]
        high = dn.astype(BF)
        low = (dn - high.astype(F32)).astype(BF)
        dn = dot(high, order_ref[...]) + dot(low, order_ref[...])
        hat = hat_scr[...]
        dgain_ref[0:1, :] = jnp.sum(dn * hat, axis=0, keepdims=True)
        dgain_ref[1:2, :] = jnp.sum(dn, axis=0, keepdims=True)
        dgain_ref[2:8, :] = jnp.zeros((6, 768), F32)
        t = dn * gain
        part = t - jnp.mean(t, -1, keepdims=True) - hat * jnp.mean(t * hat, -1, keepdims=True)
        d_first = dy.astype(F32) + part * scale_scr[...]
        dfirst_ref[...] = d_first
        low = d_first.astype(BF)
        gout[...] = dot(attt_scr[...], low).astype(BF).reshape(16, 48, 768)
        copy(gout, 8, 8).start()
        d_att = dot(out_ref[...].reshape(768, 768), low, NT).astype(BF)
        d_att = dot(order_t_ref[...], d_att).astype(BF)
        for b in range(2):
            datt_ref[b * 4 : b * 4 + 4] = d_att[:, b * 128 : (b + 1) * 128].reshape(4, 192, 128)
        for i in range(4):
            copy(gdown.at[i], i, i).wait()
            copy(gup.at[i], 4 + i, 4 + i).wait()
        copy(gout, 8, 8).wait()


def whole(*dims):
    return pl.BlockSpec(dims, lambda i: (0,) * len(dims))


def feed(x, dy, att, gains, order, order_t, weights):
    return pl.pallas_call(
        feed_kernel,
        grid=(4,),
        in_specs=[
            whole(256, 768), whole(256, 768), whole(8, 192, 128), whole(8, 768),
            whole(768, 768), whole(768, 768),
            pl.BlockSpec((16, 48, 768), lambda k: (0, k, 0)),
            pl.BlockSpec((16, 48, 768), lambda k: (0, 4 + k, 0)),
            pl.BlockSpec((16, 48, 768), lambda k: (0, 8, 0)),
        ],
        out_specs=[
            whole(256, 768), whole(256, 768), whole(8, 192, 128), whole(8, 768),
            pl.BlockSpec(memory_space=pl.ANY),
        ],
        out_shape=[
            shape((256, 768), BF), shape((256, 768), F32), shape((8, 192, 128), BF),
            shape((8, 768), F32), shape((16, 432, 768), BF),
        ],
        scratch_shapes=[
            pltpu.VMEM((256, 768), F32), pltpu.VMEM((256, 1), F32),
            pltpu.VMEM((256, 768), BF), pltpu.VMEM((768, 256), BF), pltpu.VMEM((256, 768), F32),
            pltpu.VMEM((256, 768), F32), pltpu.VMEM((768, 256), BF),
            pltpu.VMEM((4, 16, 48, 768), BF), pltpu.VMEM((4, 16, 48, 768), BF),
            pltpu.VMEM((16, 48, 768), BF), pltpu.SemaphoreType.DMA((9,)),
        ],
        cost_estimate=about(18),
        compiler_params=pltpu.CompilerParams(vmem_limit_bytes=VMEM_LIMIT),
    )(x, dy, att, gains, order, order_t, weights, weights, weights)


def unproject_kernel(
    core_ref, own_ref, dq_ref, dkv_ref, partner_ref, normed_ref, wt_ref, dgain_ref, order_ref,
    part_ref, mine_ref, theirs_ref, dt_scr, dw_scr, p_scr,
):
    core = core_ref[0]
    dt_scr[0:192, :] = dq_ref[...]
    dt_scr[192:576, :] = (dkv_ref[...] + partner_ref[...].astype(F32)).astype(BF)
    dw_scr[0:576, :] = dot(dt_scr[...], normed_ref[...])
    bias_sum = jnp.zeros((1, 768), F32)
    gain_sum = jnp.zeros((1, 768), F32)
    for j in range(8):
        d_normed = dot(dt_scr[:, j * 128 : (j + 1) * 128].T, wt_ref[...])
        part_ref[j] = d_normed.astype(BF)
        hat, _ = normalize(own_ref[j].astype(F32))
        gain_sum += jnp.sum(d_normed * hat, axis=0, keepdims=True)
        bias_sum += jnp.sum(d_normed, axis=0, keepdims=True)
    dw_scr[576:577, :] = gain_sum
    dw_scr[577:578, :] = bias_sum
    dw_scr[578:580, :] = dgain_ref[0:2, :]
    dw_scr[580:640, :] = jnp.zeros((60, 768), F32)
    p_scr[...] = dot(order_ref[...], dw_scr[...].astype(BF), NT).astype(BF)
    blank = jnp.zeros((8, 48, 128), BF)
    for ref, first in ((mine_ref, core * 384), (theirs_ref, 384 - core * 384)):
        rows = pl.ds(pl.multiple_of(first, 384), 384)
        ref[:, :, 0:640] = p_scr[rows, :].reshape(8, 48, 640)
        ref[:, :, 640:768] = blank


def slots_kernel(rest_ref, qkv_ref, order_ref, out_ref, r_scr):
    r_scr[0:432, :] = rest_ref[...]
    total = jnp.zeros((48, 768), F32)
    for g in range(8):
        total += qkv_ref[g].astype(F32)
    r_scr[432:480, :] = total.astype(BF)
    out_ref[...] = dot(order_ref[...], r_scr[...], TN).astype(BF).reshape(8, 64, 768)


def finish_kernel(x_ref, dfirst_ref, gains_ref, got_ref, dtok_ref):
    gain = gains_ref[0:1]
    for b in range(2):
        rows = slice(b * 128, (b + 1) * 128)
        dn = jnp.zeros((128, 768), F32)
        for e in range(4):
            dn += got_ref[4 * b + e].astype(F32)
        hat, scale = normalize(x_ref[rows, :].astype(F32))
        t = dn * gain
        part = t - jnp.mean(t, -1, keepdims=True) - hat * jnp.mean(t * hat, -1, keepdims=True)
        dtok_ref[rows, :] = (dfirst_ref[rows, :] + part * scale).astype(BF)


def sums_kernel(got_ref, units_ref, sum_ref, up_ref, dw_ref):
    total = jnp.zeros((64, 768), F32)
    for e in range(4):
        both = got_ref[e].astype(F32) + got_ref[4 + e].astype(F32)
        dw_ref[e] = both
        total += both
    sum_ref[...] = total
    up_ref[...] = lax.dot_general(
        total, units_ref[...], NN, precision=lax.Precision.HIGHEST, preferred_element_type=F32
    )


def scalars(count):
    return dict(
        in_specs=[pl.BlockSpec(memory_space=pltpu.SMEM)]
        + [pl.BlockSpec(memory_space=pltpu.VMEM)] * (count - 1)
    )


def body(tokens, lengths, gain_one, bias_one, w_qkv, w_out, gain_two, bias_two, w_up, w_down, d_out):
    place = lax.axis_index("seq")
    core = lax.rem(place, 2)
    length = lengths[place // 8]
    info = jnp.stack([length, core]).astype(jnp.int32)
    core_info = core.reshape(1).astype(jnp.int32)
    order = jnp.asarray(ROW_ORDER, BF)
    order_t = jnp.asarray(ROW_ORDER.T, BF)
    qkv_order = jnp.asarray(QKV_ORDER, BF)
    regroup = jnp.asarray(REGROUP, BF)
    exchange = functools.partial(
        lax.all_to_all, axis_name="seq", split_axis=0, concat_axis=0, tiled=True,
        axis_index_groups=SAME_CORE,
    )

    qkv = w_qkv.reshape(6, 3, 4, 192).transpose(2, 0, 1, 3).reshape(4, 6, 576)
    norms = jnp.stack([gain_one, bias_one, gain_two, bias_two], axis=1)
    qkv = jnp.concatenate(
        [qkv, jnp.broadcast_to(norms[None], (4, 6, 4)), jnp.zeros((4, 6, 188), BF)], axis=2
    )
    up = w_up.reshape(6, 4, 768).transpose(1, 0, 2).reshape(24, 768)
    up = dot(up, jnp.asarray(UNIT_ORDER.T, BF)).astype(BF)
    shared = jnp.concatenate([w_down, w_out, up], axis=0)
    slot = jnp.concatenate(
        [jnp.broadcast_to(shared[None], (4, 54, 768)), qkv, jnp.zeros((4, 4, 768), BF)], axis=1
    )
    slots = exchange(jnp.broadcast_to(slot[None], (2, 4, 64, 768)).reshape(8, 64, 768))
    rest, qkv_rows = call(
        regroup_kernel,
        [shape((432, 768), BF), shape((8, 48, 768), BF)],
        (slots, regroup),
        2,
    )
    weights = lax.all_gather(rest, BOTH, axis=0, axis_index_groups=RINGS)
    qkv_mine = lax.all_to_all(qkv_rows, "batch", 0, 0, tiled=True)
    qkv_other = lax.ppermute(qkv_mine, "seq", SWAP_CORE)
    x = tokens.transpose(1, 0, 2)
    dy = d_out.transpose(1, 0, 2).reshape(256, 768)
    own = exchange(jnp.broadcast_to(x[:, None], (2, 4, 128, 768)).reshape(8, 128, 768))
    x = x.reshape(256, 768)

    normed, wt, gains, qkv_t = call(
        project_kernel,
        [shape((1024, 768), BF), shape((576, 768), BF), shape((8, 768), F32), shape((576, 1024), BF)],
        (core_info, own, qkv_mine, qkv_other, qkv_order),
        5,
        [pltpu.VMEM((768, 640), BF), pltpu.VMEM((640, 768), F32)],
        **scalars(5),
    )
    q_t, kv = qkv_t[:192], qkv_t[192:]
    kv_other = lax.ppermute(kv, "seq", SWAP_CORE)
    o, o_low, lse = call(
        forward_kernel,
        [shape((192, 1024), F32), shape((8, 192, 128), BF), shape((3, 1024), F32)],
        (info, q_t, kv, kv_other),
        13,
        [pltpu.VMEM((3, 2048, 64), BF), pltpu.VMEM((192, 2048), BF)],
        **scalars(4),
    )
    att = exchange(o_low)
    y, d_first, d_att, d_gain, grads = feed(x, dy, att, gains, order, order_t, weights)

    rest_sum = lax.psum_scatter(
        grads.reshape(16 * 432, 768), BOTH, scatter_dimension=0, tiled=True,
        axis_index_groups=RINGS,
    )
    d_att = exchange(d_att)
    dq, dkv, dkv_other = call(
        backward_kernel,
        [shape((192, 1024), BF), shape((384, 1024), F32), shape((384, 1024), BF)],
        (info, q_t, kv, kv_other, o, lse, d_att),
        17,
        [
            pltpu.VMEM((3, 2048, 64), BF),
            pltpu.VMEM((192, 2048), BF),
            pltpu.VMEM((3, 2048, 64), BF),
            pltpu.VMEM((3, 2048, 64), F32),
            pltpu.VMEM((3, 2048, 64), F32),
        ],
        **scalars(7),
    )
    partner = lax.ppermute(dkv_other, "seq", SWAP_CORE)
    part, mine, theirs = call(
        unproject_kernel,
        [shape((8, 128, 768), BF), shape((8, 48, 768), BF), shape((8, 48, 768), BF)],
        (core_info, own, dq, dkv, partner, normed, wt, d_gain, qkv_order),
        7,
        [pltpu.VMEM((576, 1024), BF), pltpu.VMEM((640, 768), F32), pltpu.VMEM((768, 640), BF)],
        **scalars(9),
    )
    theirs = lax.ppermute(theirs, "seq", SWAP_CORE)
    mine = (mine.astype(F32) + theirs.astype(F32)).astype(BF)
    qkv_sums = lax.all_to_all(mine, "batch", 0, 0, tiled=True)
    back = exchange(part)
    d_tokens = call(finish_kernel, shape((256, 768), BF), (x, d_first, gains, back), 3)
    slots = call(
        slots_kernel,
        shape((8, 64, 768), BF),
        (rest_sum, qkv_sums, regroup),
        2,
        [pltpu.VMEM((480, 768), BF)],
    )
    slots = exchange(slots)
    total, d_up, d_qkv = call(
        sums_kernel,
        [shape((64, 768), F32), shape((64, 768), F32), shape((4, 64, 768), F32)],
        (slots, jnp.asarray(UNIT_ORDER, F32)),
        2,
    )
    norms = total[54:60, 576:580]
    d_up = d_up[30:54].reshape(4, 6, 768).transpose(1, 0, 2).reshape(6, 3072)
    d_qkv = d_qkv[:, 54:60, :576].reshape(4, 6, 3, 192).transpose(1, 2, 0, 3).reshape(6, 2304)
    output = y.reshape(2, 128, 768).transpose(1, 0, 2)
    d_tokens = d_tokens.reshape(2, 128, 768).transpose(1, 0, 2)
    return (
        output, d_tokens, norms[:, 0], norms[:, 1], d_qkv, total[24:30], norms[:, 2], norms[:, 3],
        d_up, total[0:24],
    )


def solution(mesh):
    rows = P(("seq", "batch"))
    tokens = P("seq", "batch", None)
    return jax.shard_map(
        body,
        mesh=mesh,
        in_specs=(tokens, P("batch"), rows, rows, rows, rows, rows, rows, rows, rows, tokens),
        out_specs=(tokens, tokens, rows, rows, rows, rows, rows, rows, rows, rows),
        check_vma=False,
    )
```

time: 3430 us -> 262 us (0.08)
  waiting for transfers between devices: 1500 us -> 66.1 us
  local copies, waits for them, and re-layouts: 830 us -> 19.7 us
  blocking collectives: 535 us -> 57.9 us
  starting transfers between devices: 264 us -> 43 us
  matrix products: 166 us -> 1.53 us
  other arithmetic: 81 us -> 1.82 us
  Pallas kernels: 0 us -> 52.6 us
    all_gather x6 -> x1, waiting for transfers between devices: 1240 us -> 0.01 us  [body(): weights = lax.all_gather(rest, BOTH, axis=0, axis_index_groups=RINGS)]
    dynamic_update_slice x32 -> x0, local copies, waits for them, and re-layouts: 599 us -> none  [body(): lax.scan(sender_step, zero_heads, numbers)]
    unnamed x3 -> x0, blocking collectives: 535 us -> none
    unnamed x96 -> x0, starting transfers between devices: 263 us -> none
    reduce_scatter x2 -> x1, waiting for transfers between devices: 238 us -> 0.78 us  [body(): lax.psum_scatter(grads.reshape(16 * 432, 768), BOTH, scatter_dimension=0,...]
    dot_general x68 -> x1, matrix products: 166 us -> 1.53 us  [dot(): return lax.dot_general(left, right, dims, preferred_element_type=F32)]
    unnamed x267 -> x42, local copies, waits for them, and re-layouts: 126 us -> 9.7 us
    all_to_all x0 -> x5, waiting for transfers between devices: none -> 60.7 us  [the longest x1 20.8 us: body(): exchange(jnp.broadcast_to(x[:, None], (2, 4, 128, 768)).reshape(8, 128, 7...]
  transfers between devices with their start and end apart: 104 -> 11, of which waited for: 11 -> 9; matrix products, arithmetic and copies ran while one was open for 17% -> 2% of each run, Pallas kernels for 0% -> 12%
where the time goes in v1:
time: 262 us; the launch traced here: 257 us
  waiting for transfers between devices  66.1 us (25%)
  blocking collectives  57.9 us (22%)
  Pallas kernels  52.6 us (20%)
  starting transfers between devices  43 us (16%)
  local copies, waits for them, and re-layouts  19.7 us (8%)
  between operations  14.3 us (5%)
    pallas_call x8, Pallas kernels, call(): pl.pallas_call(kernel, out_shape=outs, scratch_shapes=list(scratch), cost...  35.6 us
    all_to_all x1, blocking collectives, body(): qkv_sums = lax.all_to_all(mine, 'batch', 0, 0, tiled=True)  28.6 us
    all_to_all x1, waiting for transfers between devices, body(): exchange(jnp.broadcast_to(x[:, None], (2, 4, 128, 768)).reshape(8, 128, 7...  20.8 us
    all_to_all x1, blocking collectives, body(): exchange(jnp.broadcast_to(slot[None], (2, 4, 64, 768)).reshape(8, 64, 768))  18 us
    all_to_all x1, starting transfers between devices, body(): att = exchange(o_low)  18 us
    pallas_call x1, Pallas kernels, feed(): pl.pallas_call(feed_kernel, grid=(4,), in_specs=[whole(256, 768), whole(2...  17 us
    all_to_all x1, waiting for transfers between devices, body(): back = exchange(part)  16.7 us
    all_to_all x1, blocking collectives, body(): d_att = exchange(d_att)  11.2 us
  transfers between devices with their start and end apart: 11, of which 9 were waited for; matrix products, arithmetic and copies ran while one was open for 2% of the time, Pallas kernels for 12%

profile of v1, /device:TPU:64, one launch (start us, length us, event | category | flops | bytes accessed | tf_op | source)
XLA Modules:
  0.0 256.9 jit_solution(1744587399964736355)
XLA Ops:
  7.2 0.7 pad_maximum_fusion.1
  8.0 0.1 copy.49
  8.1 0.1 pad.2.clone
  8.2 0.1 pad.5.clone
  8.2 0.9 reshape.75
  9.1 0.1 reshape.76
  9.2 0.1 maximum_maximum_fusion.1
  9.3 0.8 reshape.74
  10.2 1.5 fusion
  11.8 0.1 maximum_maximum_fusion
  11.9 0.1 broadcast_in_dim.17
  12.0 18.0 %all_to_all.40.slots_ref = bf16[8,64,768]{2,1,0:T(8,128)(2,1)S(1)} all-to-all(bf16[8,64,768]{2,1,0:T(8,128)(2,1)S(1)} %bitcast.45), channel_id=1, replica_groups={{0,16,32,48,64,80,96,112},{8,24,40,56,72,88,104,120},{1,17,33,49,65,81,..., dimensions={0} | all-to-all | bytes 1572864 | tf_op jit(solution)/shard_map/all_to_all | solution.py:476
  30.0 1.6 shard_map.240
  31.6 7.4 %all-to-all-start.2 = ((bf16[8,48,768]{2,1,0:T(8,128)(2,1)}), bf16[8,48,768]{2,1,0:T(8,128)(2,1)S(1)}, u32[]{:S(2)}, u32[]{:S(2)}) async-start(bf16[8,48,768]{2,1,0:T(8,128)(2,1)} %get-tuple-element.33), calls=%async_computation.2 | async-start | bytes 1179648 | tf_op jit(solution)/shard_map/all_to_all | solution.py:484
  39.1 8.3 %all-to-all-done.2.mine_ref = bf16[8,48,768]{2,1,0:T(8,128)(2,1)S(1)} async-done(((bf16[8,48,768]{2,1,0:T(8,128)(2,1)}), bf16[8,48,768]{2,1,0:T(8,128)(2,1)S(1)}, u32[]{:S(2)}, u32[]{:S(2)}) %all-to-all-start.2) | async-done | bytes 589856 | tf_op jit(solution)/shard_map/all_to_all | solution.py:484
  47.4 1.3 broadcast_in_dim.12
  48.7 3.6 %all-to-all-start = ((bf16[8,128,768]{2,1,0:T(8,128)(2,1)}), bf16[8,128,768]{2,1,0:T(8,128)(2,1)S(1)}, u32[]{:S(2)}, u32[]{:S(2)}) async-start(bf16[8,128,768]{2,1,0:T(8,128)(2,1)} %bitcast.5), calls=%async_computation | async-start | bytes 3145728 | tf_op jit(solution)/shard_map/all_to_all | solution.py:488
  52.2 0.1 collective-permute-start
  52.3 20.8 %all-to-all-done.own_ref = bf16[8,128,768]{2,1,0:T(8,128)(2,1)S(1)} async-done(((bf16[8,128,768]{2,1,0:T(8,128)(2,1)}), bf16[8,128,768]{2,1,0:T(8,128)(2,1)S(1)}, u32[]{:S(2)}, u32[]{:S(2)}) %all-to-all-start) | async-done | bytes 1572896 | tf_op jit(solution)/shard_map/all_to_all | solution.py:488
  73.1 1.2 copy-done.15
  74.3 5.1 %shard_map.241 = (bf16[1024,768]{1,0:T(8,128)(2,1)}, bf16[576,768]{1,0:T(8,128)(2,1)S(1)}, f32[8,768]{1,0:T(8,128)S(1)}, bf16[576,1024]{1,0:T(8,128)(2,1)S(1)}) custom-call(s32[1]{0:T(128)} %bitcast.4.core_ref, bf16[8,128,768]{2,1,0:T(8,128)(2,1)} %copy-done.15, bf16[8,48,768]{2,1,0:T(8,128)(2,1)S(1)} %all-to-all-done.2.mine_ref, ...), custom_call_target="tpu_custom_call" | custom-call | flops 5500000256 | tf_op jit(solution)/shard_map/pallas_call | solution.py:74
  79.4 1.0 copy-done.8
  80.4 0.1 slice.36.own_ref
  80.5 0.1 collective-permute-start.1
  80.6 0.5 copy-done.20
  81.1 0.6 dynamic_slice.3
  81.7 0.7 pad_add_fusion.info_ref
  82.4 0.4 collective-permute-done.1.other_ref
  82.8 6.3 %shard_map.242 = (f32[192,1024]{1,0:T(8,128)S(1)}, bf16[8,192,128]{2,1,0:T(8,128)(2,1)}, f32[3,1024]{1,0:T(4,128)S(1)}) custom-call(s32[2]{0:T(128)S(1)} %pad_add_fusion.info_ref, bf16[192,1024]{1,0:T(8,128)(2,1)S(1)} %slice.35.q_ref, bf16[384,1024]{1,0:T(8,128)(2,1)S(1)} %slice.36.own_ref, bf16[384,1024]{1,0:T(8,128)(2,1)S(1)} %collective-permute-done.1.other_ref), custom_call_target="tpu_custom_call" | custom-call | flops 14300000256 | tf_op jit(solution)/shard_map/pallas_call | solution.py:74
  89.2 0.9 copy-done.10
  90.1 0.6 copy-done.13
  90.7 18.0 %all-to-all-start.3 = ((bf16[8,192,128]{2,1,0:T(8,128)(2,1)}), bf16[8,192,128]{2,1,0:T(8,128)(2,1)S(1)}, u32[]{:S(2)}, u32[]{:S(2)}) async-start(bf16[8,192,128]{2,1,0:T(8,128)(2,1)} %get-tuple-element.35), calls=%async_computation.3 | async-start | bytes 786432 | tf_op jit(solution)/shard_map/all_to_all | solution.py:509
  108.6 0.2 reduce-scatter.2.cloned.1.call-start
  108.9 8.2 %all-to-all-done.3.att_ref = bf16[8,192,128]{2,1,0:T(8,128)(2,1)S(1)} async-done(((bf16[8,192,128]{2,1,0:T(8,128)(2,1)}), bf16[8,192,128]{2,1,0:T(8,128)(2,1)S(1)}, u32[]{:S(2)}, u32[]{:S(2)}) %all-to-all-start.3) | async-done | bytes 393248 | tf_op jit(solution)/shard_map/all_to_all | solution.py:509
  117.1 1.3 copy-done.3
  118.4 17.0 %shard_map.243 = (bf16[256,768]{1,0:T(8,128)(2,1)S(1)}, f32[256,768]{1,0:T(8,128)S(1)}, bf16[8,192,128]{2,1,0:T(8,128)(2,1)S(1)}, f32[8,768]{1,0:T(8,128)S(1)}, bf16[16,432,768]{2,1,0:T(8,128)(2,1)}) custom-call(bf16[256,768]{1,0:T(8,128)(2,1)S(1)} %bitcast.39, bf16[256,768]{1,0:T(8,128)(2,1)S(1)} %bitcast.42, ...), custom_call_target="tpu_custom_call" | custom-call | flops 19800000512 | tf_op jit(solution)/shard_map/pallas_call | solution.py:351
  135.4 0.9 copy-done.6
  136.3 11.2 %all_to_all.41.da_ref = bf16[8,192,128]{2,1,0:T(8,128)(2,1)S(1)} all-to-all(bf16[8,192,128]{2,1,0:T(8,128)(2,1)S(1)} %get-tuple-element.42), channel_id=1, replica_groups={{0,16,32,48,64,80,96,112},{8,24,40,56,72,88,104,120},{1,17,33,49,65,81,..., dimensions={0} | all-to-all | bytes 786432 | tf_op jit(solution)/shard_map/all_to_all | solution.py:516
  147.6 10.1 %shard_map.244 = (bf16[192,1024]{1,0:T(8,128)(2,1)S(1)}, f32[384,1024]{1,0:T(8,128)}, bf16[384,1024]{1,0:T(8,128)(2,1)S(1)}) custom-call(s32[2]{0:T(128)S(1)} %pad_add_fusion.info_ref, bf16[192,1024]{1,0:T(8,128)(2,1)S(1)} %slice.35.q_ref, bf16[384,1024]{1,0:T(8,128)(2,1)S(1)} %slice.36.own_ref, bf16[384,1024]{1,0:T(8,128)(2,1)S(1)} %copy-done.1, ...), custom_call_target="tpu_custom_call" | custom-call | flops 18699999232 | tf_op jit(solution)/shard_map/pallas_call | solution.py:74
  157.6 2.3 collective-permute-done.2.partner_ref
  159.9 7.1 %shard_map.245 = (bf16[8,128,768]{2,1,0:T(8,128)(2,1)}, bf16[8,48,768]{2,1,0:T(8,128)(2,1)S(1)}, bf16[8,48,768]{2,1,0:T(8,128)(2,1)S(1)}) custom-call(s32[1]{0:T(128)} %bitcast.4.core_ref, bf16[8,128,768]{2,1,0:T(8,128)(2,1)} %copy-done.15, bf16[192,1024]{1,0:T(8,128)(2,1)S(1)} %get-tuple-element.43.dq_ref, f32[384,1024]{1,0:T(8,128)} %get-tuple-element.44.dkv_ref, ...), custom_call_target="tpu_custom_call" | custom-call | flops 7699999744 | tf_op jit(solution)/shard_map/pallas_call | solution.py:74
  167.0 0.1 collective-permute-start.3
  167.1 1.9 collective-permute-done.3
  169.0 0.1 add_convert_fusion
  169.1 28.6 %all_to_all.42.qkv_ref = bf16[8,48,768]{2,1,0:T(8,128)(2,1)S(1)} all-to-all(bf16[8,48,768]{2,1,0:T(8,128)(2,1)S(1)} %add_convert_fusion), channel_id=1, replica_groups=mesh['seq'=16,'batch'=8] {'batch'}, dimensions={0} | all-to-all | bytes 1179648 | tf_op jit(solution)/shard_map/all_to_all | solution.py:542
  197.7 9.9 %all-to-all-start.5 = ((bf16[8,128,768]{2,1,0:T(8,128)(2,1)}), bf16[8,128,768]{2,1,0:T(8,128)(2,1)S(1)}, u32[]{:S(2)}, u32[]{:S(2)}) async-start(bf16[8,128,768]{2,1,0:T(8,128)(2,1)} %get-tuple-element.49), calls=%async_computation.5 | async-start | bytes 3145728 | tf_op jit(solution)/shard_map/all_to_all | solution.py:543
  207.7 0.8 reduce-scatter.2.cloned.1.call-done.rest_ref
  208.5 1.1 copy-done.2
  209.6 1.0 copy-done.5
  210.6 1.6 shard_map.247
  212.1 16.7 %all-to-all-done.5.got_ref = bf16[8,128,768]{2,1,0:T(8,128)(2,1)S(1)} async-done(((bf16[8,128,768]{2,1,0:T(8,128)(2,1)}), bf16[8,128,768]{2,1,0:T(8,128)(2,1)S(1)}, u32[]{:S(2)}, u32[]{:S(2)}) %all-to-all-start.5) | async-done | bytes 1572896 | tf_op jit(solution)/shard_map/all_to_all | solution.py:543
  228.9 3.5 %all-to-all-start.7 = ((bf16[8,64,768]{2,1,0:T(8,128)(2,1)}), bf16[8,64,768]{2,1,0:T(8,128)(2,1)S(1)}, u32[]{:S(2)}, u32[]{:S(2)}) async-start(bf16[8,64,768]{2,1,0:T(8,128)(2,1)} %shard_map.247), calls=%async_computation.8 | async-start | bytes 1572864 | tf_op jit(solution)/shard_map/all_to_all | solution.py:552
  232.4 1.2 copy.59
  233.6 1.1 copy-done.7
  234.7 0.7 shard_map.246
  235.4 1.2 copy.58
  236.6 6.8 %all-to-all-done.7.got_ref = bf16[8,64,768]{2,1,0:T(8,128)(2,1)S(1)} async-done(((bf16[8,64,768]{2,1,0:T(8,128)(2,1)}), bf16[8,64,768]{2,1,0:T(8,128)(2,1)S(1)}, u32[]{:S(2)}, u32[]{:S(2)}) %all-to-all-start.7) | async-done | bytes 786464 | tf_op jit(solution)/shard_map/all_to_all | solution.py:552
  243.4 3.1 %shard_map.248 = (f32[64,768]{1,0:T(8,128)S(1)}, f32[64,768]{1,0:T(8,128)S(1)}, f32[4,64,768]{2,1,0:T(8,128)S(1)}) custom-call(bf16[8,64,768]{2,1,0:T(8,128)(2,1)S(1)} %all-to-all-done.7.got_ref, f32[768,768]{1,0:T(8,128)} %constant.47.clone.units_ref), custom_call_target="tpu_custom_call" | custom-call | flops 2200000000 | tf_op jit(solution)/shard_map/pallas_call | solution.py:74
  246.5 0.7 slice_reduce_fusion
  247.2 0.6 slice.40
  247.8 0.6 slice.44
  248.5 0.1 reshape.81
  248.7 0.7 reshape.82
  249.4 0.7 reshape.83
  (52 shorter events, 0.4 us)
Async XLA Ops:
  7.2 4.5 %copy-start.18 = (bf16[24,768]{1,0:T(8,128)(2,1)S(1)}, bf16[24,768]{1,0:T(8,128)(2,1)}, u32[]{:S(2)}) copy-start(bf16[24,768]{1,0:T(8,128)(2,1)} %param.26) | copy-start | bytes 110596
  7.2 4.5 %copy-start.19 = (bf16[6,768]{1,0:T(8,128)(2,1)S(1)}, bf16[6,768]{1,0:T(8,128)(2,1)}, u32[]{:S(2)}) copy-start(bf16[6,768]{1,0:T(8,128)(2,1)} %param.22) | copy-start | bytes 27652
  7.2 109.9 %all-gather.3.cloned.1.call-start = ((), (), s32[]{:S(2)}) async-start(), calls=%async_computation.10 | async-start | bytes 11280384 | tf_op jit(solution)/shard_map/all_gather | solution.py:483
  11.9 18.1 %copy-start.4 = (bf16[480,512]{1,0:T(8,128)(2,1)S(1)}, bf16[480,512]{1,0:T(8,128)(2,1)}, u32[]{:S(2)}) copy-start(bf16[480,512]{1,0:T(8,128)(2,1)} %constant.45.clone.order_ref) | copy-start | bytes 1474564
  31.6 7.4 %copy-start.16 = (bf16[128,2,768]{2,1,0:T(2,128)(2,1)S(1)}, bf16[128,2,768]{2,1,0:T(2,128)(2,1)}, u32[]{:S(2)}) copy-start(bf16[128,2,768]{2,1,0:T(2,128)(2,1)} %param.17) | copy-start | bytes 1179652
  31.6 15.7 %all-to-all-start.2 = ((bf16[8,48,768]{2,1,0:T(8,128)(2,1)}), bf16[8,48,768]{2,1,0:T(8,128)(2,1)S(1)}, u32[]{:S(2)}, u32[]{:S(2)}) async-start(bf16[8,48,768]{2,1,0:T(8,128)(2,1)} %get-tuple-element.33), calls=%async_computation.2 | async-start | bytes 1179648 | tf_op jit(solution)/shard_map/all_to_all | solution.py:484
  48.7 24.5 %all-to-all-start = ((bf16[8,128,768]{2,1,0:T(8,128)(2,1)}), bf16[8,128,768]{2,1,0:T(8,128)(2,1)S(1)}, u32[]{:S(2)}, u32[]{:S(2)}) async-start(bf16[8,128,768]{2,1,0:T(8,128)(2,1)} %bitcast.5), calls=%async_computation | async-start | bytes 3145728 | tf_op jit(solution)/shard_map/all_to_all | solution.py:488
  52.2 20.9 %collective-permute-start = (bf16[8,48,768]{2,1,0:T(8,128)(2,1)S(1)}, bf16[8,48,768]{2,1,0:T(8,128)(2,1)S(1)}, u32[]{:S(2)}, u32[]{:S(2)}) collective-permute-start(bf16[8,48,768]{2,1,0:T(8,128)(2,1)S(1)} %all-to-all-done.2.mine_ref), channel_id=1, source_target_pairs={{0,8},{8,0},{16,24},{24,16},{32,40},{40,32},{48,56},{56,48},{64,72... | collective-permute-start | bytes 1769480 | tf_op jit(solution)/shard_map/ppermute | solution.py:485
  73.1 1.2 copy-start.15
  79.4 1.0 copy-start.8
  80.4 1.3 copy-start.11
  80.4 0.7 copy-start.20
  80.5 2.4 collective-permute-start.1
  82.4 26.4 %copy-start.17 = (bf16[128,2,768]{2,1,0:T(2,128)(2,1)S(1)}, bf16[128,2,768]{2,1,0:T(2,128)(2,1)}, u32[]{:S(2)}) copy-start(bf16[128,2,768]{2,1,0:T(2,128)(2,1)} %param.27) | copy-start | bytes 1179652
  82.8 6.3 %copy-start = (bf16[384,1024]{1,0:T(8,128)(2,1)}, bf16[384,1024]{1,0:T(8,128)(2,1)S(1)}, u32[]{:S(2)}) copy-start(bf16[384,1024]{1,0:T(8,128)(2,1)S(1)} %collective-permute-done.1.other_ref) | copy-start | bytes 2359300
  89.2 0.9 copy-start.10
  90.1 0.6 copy-start.13
  90.7 26.4 %copy-start.12 = (f32[8,768]{1,0:T(8,128)S(1)}, f32[8,768]{1,0:T(8,128)}, u32[]{:S(2)}) copy-start(f32[8,768]{1,0:T(8,128)} %copy-done.11) | copy-start | bytes 73732
  90.7 26.4 %all-to-all-start.3 = ((bf16[8,192,128]{2,1,0:T(8,128)(2,1)}), bf16[8,192,128]{2,1,0:T(8,128)(2,1)S(1)}, u32[]{:S(2)}, u32[]{:S(2)}) async-start(bf16[8,192,128]{2,1,0:T(8,128)(2,1)} %get-tuple-element.35), calls=%async_computation.3 | async-start | bytes 786432 | tf_op jit(solution)/shard_map/all_to_all | solution.py:509
  108.6 99.8 %reduce-scatter.2.cloned.1.call-start = ((), (), s32[]{:S(2)}) async-start(), calls=%async_computation.9 | async-start | bytes 11280384 | tf_op jit(solution)/shard_map/reduce_scatter | solution.py:512
  117.1 1.3 copy-start.3
  135.4 0.9 copy-start.6
  136.3 11.3 %copy-start.1 = (bf16[384,1024]{1,0:T(8,128)(2,1)S(1)}, bf16[384,1024]{1,0:T(8,128)(2,1)}, u32[]{:S(2)}) copy-start(bf16[384,1024]{1,0:T(8,128)(2,1)} %copy-done) | copy-start | bytes 2359300
  136.3 11.3 %copy-start.14 = (f32[3,1024]{1,0:T(4,128)S(1)}, f32[3,1024]{1,0:T(4,128)}, u32[]{:S(2)}) copy-start(f32[3,1024]{1,0:T(4,128)} %copy-done.13) | copy-start | bytes 36868
  147.6 12.3 %copy-start.9 = (bf16[576,768]{1,0:T(8,128)(2,1)S(1)}, bf16[576,768]{1,0:T(8,128)(2,1)}, u32[]{:S(2)}) copy-start(bf16[576,768]{1,0:T(8,128)(2,1)} %copy-done.8) | copy-start | bytes 2654212
  157.6 2.3 collective-permute-start.2
  167.0 2.0 collective-permute-start.3
  197.7 31.1 %all-to-all-start.5 = ((bf16[8,128,768]{2,1,0:T(8,128)(2,1)}), bf16[8,128,768]{2,1,0:T(8,128)(2,1)S(1)}, u32[]{:S(2)}, u32[]{:S(2)}) async-start(bf16[8,128,768]{2,1,0:T(8,128)(2,1)} %get-tuple-element.49), calls=%async_computation.5 | async-start | bytes 3145728 | tf_op jit(solution)/shard_map/all_to_all | solution.py:543
  208.5 1.1 copy-start.2
  209.5 1.0 copy-start.5
  228.9 14.5 %all-to-all-start.7 = ((bf16[8,64,768]{2,1,0:T(8,128)(2,1)}), bf16[8,64,768]{2,1,0:T(8,128)(2,1)S(1)}, u32[]{:S(2)}, u32[]{:S(2)}) async-start(bf16[8,64,768]{2,1,0:T(8,128)(2,1)} %shard_map.247), calls=%async_computation.8 | async-start | bytes 1572864 | tf_op jit(solution)/shard_map/all_to_all | solution.py:552
  233.6 1.1 copy-start.7
Sparse Core Ops, SparseCore 0:
  31.8 69.7 all-gather.2
  136.4 71.9 reduce-scatter.1

commit v2 on v1

--- a/solution.py
+++ b/solution.py
@@ -19,12 +19,19 @@
 SAME_CORE = [[2 * k + c for k in range(8)] for c in range(2)]
 SWAP_CORE = [(i, i ^ 1) for i in range(16)]
 TURNS = [(0, 0), (0, 1), (0, 2), (0, 3), (1, 3), (1, 2), (1, 1), (1, 0)]
-RING = [(c ^ (i & 1), z, x) for i, (z, x) in enumerate(TURNS) for c in range(2)]
+RING = [(c, z, x) for z, x in TURNS for c in range(2)]
 RINGS = [
     [((y * 2 + (low ^ z)) * 2 + c) * 8 + z * 4 + x for c, z, x in RING]
     for y in range(4)
     for low in range(2)
 ]
+
+
+SWAP_Z = [(b, b ^ 4) for b in range(8)]
+
+
+def along_x(step):
+    return [(b, b // 4 * 4 + (b + step) % 4) for b in range(8)]
 
 
 def one_hot(rows):
@@ -93,22 +100,43 @@
     return shifted * scale, scale
 
 
+def pack_kernel(down_ref, out_ref, up_ref, qkv_ref, norms_ref, units_ref, slot_ref, scr):
+    up = jnp.concatenate(
+        [up_ref[:, k * 768 : (k + 1) * 768].astype(F32) for k in range(4)], axis=0
+    ).astype(BF)
+    scr[0:24, :] = down_ref[...].astype(F32)
+    scr[24:30, :] = out_ref[...].astype(F32)
+    scr[30:54, :] = dot(up, units_ref[...], NT)
+    scr[60:64, :] = jnp.zeros((4, 768), F32)
+    for e in range(4):
+        parts = [qkv_ref[:, s * 768 + e * 192 : s * 768 + (e + 1) * 192] for s in range(3)]
+        row = jnp.concatenate(parts + [norms_ref[:, 0:64], jnp.zeros((6, 128), BF)], axis=1)
+        scr[54:60, :] = row.astype(F32)
+        slot = scr[...].astype(BF)
+        slot_ref[e] = slot
+        slot_ref[4 + e] = slot
+
+
 def regroup_kernel(slots_ref, order_ref, rest_ref, qkv_ref):
     rows = dot(order_ref[...], slots_ref[...].reshape(512, 768)).astype(BF)
     rest_ref[...] = rows[0:432]
-    for g in range(8):
-        qkv_ref[g] = rows[432:480]
+    qkv_ref[...] = rows[432:480, 0:640]
+
+
+def rows_at(info_ref, dc, dz, dx):
+    c = lax.rem(info_ref[1] + dc, 2)
+    z = lax.rem(info_ref[2] + dz, 2)
+    x = lax.rem(info_ref[3] + dx, 4)
+    return pl.ds(pl.multiple_of((c * 8 + z * 4 + x) * 48, 48), 48)
 
 
 def project_kernel(
-    core_ref, own_ref, mine_ref, other_ref, order_ref,
+    info_ref, own_ref, near_ref, far_ref, near_other_ref, far_other_ref, order_ref,
     normed_ref, wt_ref, gains_ref, qkv_ref, w_scr, t_scr,
 ):
-    core = core_ref[0]
-    mine = pl.ds(pl.multiple_of(core * 384, 384), 384)
-    theirs = pl.ds(pl.multiple_of(384 - core * 384, 384), 384)
-    w_scr[mine, :] = mine_ref[...].reshape(384, 768)[:, :640]
-    w_scr[theirs, :] = other_ref[...].reshape(384, 768)[:, :640]
+    for i, ref in enumerate((near_ref, far_ref, near_other_ref, far_other_ref)):
+        for dx in range(4):
+            w_scr[rows_at(info_ref, i // 2, i % 2, dx), :] = ref[dx]
     t_scr[...] = dot(w_scr[...].T, order_ref[...])
     wt_ref[...] = t_scr[0:576].astype(BF)
     gains = t_scr[576:584]
@@ -379,10 +407,9 @@
 
 
 def unproject_kernel(
-    core_ref, own_ref, dq_ref, dkv_ref, partner_ref, normed_ref, wt_ref, dgain_ref, order_ref,
+    info_ref, own_ref, dq_ref, dkv_ref, partner_ref, normed_ref, wt_ref, dgain_ref, order_ref,
     part_ref, mine_ref, theirs_ref, dt_scr, dw_scr, p_scr,
 ):
-    core = core_ref[0]
     dt_scr[0:192, :] = dq_ref[...]
     dt_scr[192:576, :] = (dkv_ref[...] + partner_ref[...].astype(F32)).astype(BF)
     dw_scr[0:576, :] = dot(dt_scr[...], normed_ref[...])
@@ -399,19 +426,16 @@
     dw_scr[578:580, :] = dgain_ref[0:2, :]
     dw_scr[580:640, :] = jnp.zeros((60, 768), F32)
     p_scr[...] = dot(order_ref[...], dw_scr[...].astype(BF), NT).astype(BF)
-    blank = jnp.zeros((8, 48, 128), BF)
-    for ref, first in ((mine_ref, core * 384), (theirs_ref, 384 - core * 384)):
-        rows = pl.ds(pl.multiple_of(first, 384), 384)
-        ref[:, :, 0:640] = p_scr[rows, :].reshape(8, 48, 640)
-        ref[:, :, 640:768] = blank
+    for dc, ref in enumerate((mine_ref, theirs_ref)):
+        for dx in range(4):
+            for dz in range(2):
+                ref[dx, dz] = p_scr[rows_at(info_ref, dc, dz, dx), :]
 
 
 def slots_kernel(rest_ref, qkv_ref, order_ref, out_ref, r_scr):
     r_scr[0:432, :] = rest_ref[...]
-    total = jnp.zeros((48, 768), F32)
-    for g in range(8):
-        total += qkv_ref[g].astype(F32)
-    r_scr[432:480, :] = total.astype(BF)
+    r_scr[432:480, 0:640] = qkv_ref[...]
+    r_scr[432:480, 640:768] = jnp.zeros((48, 128), BF)
     out_ref[...] = dot(order_ref[...], r_scr[...], TN).astype(BF).reshape(8, 64, 768)
 
 
@@ -428,16 +452,29 @@
         dtok_ref[rows, :] = (dfirst_ref[rows, :] + part * scale).astype(BF)
 
 
-def sums_kernel(got_ref, units_ref, sum_ref, up_ref, dw_ref):
+def sums_kernel(got_ref, units_ref, down_ref, out_ref, up_ref, qkv_ref, g1_ref, b1_ref, g2_ref, b2_ref):
     total = jnp.zeros((64, 768), F32)
+    chunks = []
     for e in range(4):
         both = got_ref[e].astype(F32) + got_ref[4 + e].astype(F32)
-        dw_ref[e] = both
+        chunks.append(both[54:60])
         total += both
-    sum_ref[...] = total
-    up_ref[...] = lax.dot_general(
-        total, units_ref[...], NN, precision=lax.Precision.HIGHEST, preferred_element_type=F32
-    )
+    down_ref[...] = total[0:24]
+    out_ref[...] = total[24:30]
+    left, up = total[30:54], jnp.zeros((24, 768), F32)
+    for _ in range(3):
+        piece = left.astype(BF)
+        left = left - piece.astype(F32)
+        up += dot(piece, units_ref[...])
+    for k in range(4):
+        up_ref[:, k * 768 : (k + 1) * 768] = up[k * 6 : k * 6 + 6]
+    for s in range(3):
+        qkv_ref[:, s * 768 : (s + 1) * 768] = jnp.concatenate(
+            [chunks[e][:, s * 192 : (s + 1) * 192] for e in range(4)], axis=1
+        )
+    norms = total[:, 512:640].T
+    for i, ref in enumerate((g1_ref, b1_ref, g2_ref, b2_ref)):
+        ref[...] = norms[64 + i : 65 + i, 54:60]
 
 
 def scalars(count):
@@ -451,8 +488,8 @@
     place = lax.axis_index("seq")
     core = lax.rem(place, 2)
     length = lengths[place // 8]
-    info = jnp.stack([length, core]).astype(jnp.int32)
-    core_info = core.reshape(1).astype(jnp.int32)
+    row = lax.axis_index("batch")
+    info = jnp.stack([length, core, row // 4, lax.rem(row, 4)]).astype(jnp.int32)
     order = jnp.asarray(ROW_ORDER, BF)
     order_t = jnp.asarray(ROW_ORDER.T, BF)
     qkv_order = jnp.asarray(QKV_ORDER, BF)
@@ -462,27 +499,30 @@
         axis_index_groups=SAME_CORE,
     )
 
-    qkv = w_qkv.reshape(6, 3, 4, 192).transpose(2, 0, 1, 3).reshape(4, 6, 576)
     norms = jnp.stack([gain_one, bias_one, gain_two, bias_two], axis=1)
-    qkv = jnp.concatenate(
-        [qkv, jnp.broadcast_to(norms[None], (4, 6, 4)), jnp.zeros((4, 6, 188), BF)], axis=2
-    )
-    up = w_up.reshape(6, 4, 768).transpose(1, 0, 2).reshape(24, 768)
-    up = dot(up, jnp.asarray(UNIT_ORDER.T, BF)).astype(BF)
-    shared = jnp.concatenate([w_down, w_out, up], axis=0)
-    slot = jnp.concatenate(
-        [jnp.broadcast_to(shared[None], (4, 54, 768)), qkv, jnp.zeros((4, 4, 768), BF)], axis=1
-    )
-    slots = exchange(jnp.broadcast_to(slot[None], (2, 4, 64, 768)).reshape(8, 64, 768))
+    norms = jnp.pad(norms, ((0, 0), (0, 124)))
+    units = jnp.asarray(UNIT_ORDER, BF)
+    slots = call(
+        pack_kernel,
+        shape((8, 64, 768), BF),
+        (w_down, w_out, w_up, w_qkv, norms, units),
+        2,
+        [pltpu.VMEM((64, 768), F32)],
+    )
+    slots = exchange(slots)
     rest, qkv_rows = call(
         regroup_kernel,
-        [shape((432, 768), BF), shape((8, 48, 768), BF)],
+        [shape((432, 768), BF), shape((48, 640), BF)],
         (slots, regroup),
         2,
     )
     weights = lax.all_gather(rest, BOTH, axis=0, axis_index_groups=RINGS)
-    qkv_mine = lax.all_to_all(qkv_rows, "batch", 0, 0, tiled=True)
-    qkv_other = lax.ppermute(qkv_mine, "seq", SWAP_CORE)
+    near = jnp.stack(
+        [qkv_rows] + [lax.ppermute(qkv_rows, "batch", along_x(step)) for step in (-1, 2, 1)]
+    )
+    far = lax.ppermute(near, "batch", SWAP_Z)
+    near_other = lax.ppermute(near, "seq", SWAP_CORE)
+    far_other = lax.ppermute(far, "seq", SWAP_CORE)
     x = tokens.transpose(1, 0, 2)
     dy = d_out.transpose(1, 0, 2).reshape(256, 768)
     own = exchange(jnp.broadcast_to(x[:, None], (2, 4, 128, 768)).reshape(8, 128, 768))
@@ -491,10 +531,10 @@
     normed, wt, gains, qkv_t = call(
         project_kernel,
         [shape((1024, 768), BF), shape((576, 768), BF), shape((8, 768), F32), shape((576, 1024), BF)],
-        (core_info, own, qkv_mine, qkv_other, qkv_order),
+        (info, own, near, far, near_other, far_other, qkv_order),
         5,
         [pltpu.VMEM((768, 640), BF), pltpu.VMEM((640, 768), F32)],
-        **scalars(5),
+        **scalars(7),
     )
     q_t, kv = qkv_t[:192], qkv_t[192:]
     kv_other = lax.ppermute(kv, "seq", SWAP_CORE)
@@ -531,39 +571,44 @@
     partner = lax.ppermute(dkv_other, "seq", SWAP_CORE)
     part, mine, theirs = call(
         unproject_kernel,
-        [shape((8, 128, 768), BF), shape((8, 48, 768), BF), shape((8, 48, 768), BF)],
-        (core_info, own, dq, dkv, partner, normed, wt, d_gain, qkv_order),
+        [shape((8, 128, 768), BF), shape((4, 2, 48, 640), BF), shape((4, 2, 48, 640), BF)],
+        (info, own, dq, dkv, partner, normed, wt, d_gain, qkv_order),
         7,
         [pltpu.VMEM((576, 1024), BF), pltpu.VMEM((640, 768), F32), pltpu.VMEM((768, 640), BF)],
         **scalars(9),
     )
-    theirs = lax.ppermute(theirs, "seq", SWAP_CORE)
-    mine = (mine.astype(F32) + theirs.astype(F32)).astype(BF)
-    qkv_sums = lax.all_to_all(mine, "batch", 0, 0, tiled=True)
+    add = lambda *parts: sum(p.astype(F32) for p in parts).astype(BF)
+    line = add(mine, lax.ppermute(theirs, "seq", SWAP_CORE))
+    line = add(
+        line[0],
+        lax.ppermute(line[1], "batch", along_x(1)),
+        lax.ppermute(line[2], "batch", along_x(2)),
+        lax.ppermute(line[3], "batch", along_x(-1)),
+    )
+    qkv_sum = add(line[0], lax.ppermute(line[1], "batch", SWAP_Z))
     back = exchange(part)
     d_tokens = call(finish_kernel, shape((256, 768), BF), (x, d_first, gains, back), 3)
     slots = call(
         slots_kernel,
         shape((8, 64, 768), BF),
-        (rest_sum, qkv_sums, regroup),
+        (rest_sum, qkv_sum, regroup),
         2,
         [pltpu.VMEM((480, 768), BF)],
     )
     slots = exchange(slots)
-    total, d_up, d_qkv = call(
+    vector = shape((1, 6), F32)
+    d_down, d_out_w, d_up, d_qkv, *norms = call(
         sums_kernel,
-        [shape((64, 768), F32), shape((64, 768), F32), shape((4, 64, 768), F32)],
-        (slots, jnp.asarray(UNIT_ORDER, F32)),
+        [shape((24, 768), F32), shape((6, 768), F32), shape((6, 3072), F32), shape((6, 2304), F32)]
+        + [vector] * 4,
+        (slots, units),
         2,
     )
-    norms = total[54:60, 576:580]
-    d_up = d_up[30:54].reshape(4, 6, 768).transpose(1, 0, 2).reshape(6, 3072)
-    d_qkv = d_qkv[:, 54:60, :576].reshape(4, 6, 3, 192).transpose(1, 2, 0, 3).reshape(6, 2304)
+    norms = [v.reshape(6) for v in norms]
     output = y.reshape(2, 128, 768).transpose(1, 0, 2)
     d_tokens = d_tokens.reshape(2, 128, 768).transpose(1, 0, 2)
     return (
-        output, d_tokens, norms[:, 0], norms[:, 1], d_qkv, total[24:30], norms[:, 2], norms[:, 3],
-        d_up, total[0:24],
+        output, d_tokens, norms[0], norms[1], d_qkv, d_out_w, norms[2], norms[3], d_up, d_down,
     )
 
 

time: 262 us -> 236 us (0.901); the launches traced: 257 us -> 235 us
  Pallas kernels: 52.6 us -> 82.2 us
  blocking collectives: 57.9 us -> 29.4 us
  waiting for transfers between devices: 66.1 us -> 49.3 us
  starting transfers between devices: 43 us -> 37 us
    pallas_call x8 -> x9, Pallas kernels: 35.6 us -> 65.2 us  [call(): pl.pallas_call(kernel, out_shape=outs, scratch_shapes=list(scratch), cost...]
    all_to_all x2 -> x1, blocking collectives: 46.6 us -> 18 us  [body(): slots = exchange(slots)]
    ppermute x2 -> x11, waiting for transfers between devices: 1.88 us -> 27.9 us  [the longest x1 12.3 us: body(): far = lax.ppermute(near, 'batch', SWAP_Z)]
    all_to_all x1, waiting for transfers between devices: 20.8 us -> 0.01 us  [body(): exchange(jnp.broadcast_to(x[:, None], (2, 4, 128, 768)).reshape(8, 128, 7...]
    all_to_all x1, waiting for transfers between devices: 16.7 us -> 0.29 us  [body(): back = exchange(part)]
    ppermute x2 -> x11, starting transfers between devices: 0.21 us -> 15 us  [the longest x3 5.73 us: body(): lax.ppermute(qkv_rows, 'batch', along_x(step))]
    all_to_all x1, starting transfers between devices: 18 us -> 4.71 us  [body(): att = exchange(o_low)]
    all_to_all x1 -> x0, waiting for transfers between devices: 8.27 us -> none  [body(): qkv_mine = lax.all_to_all(qkv_rows, 'batch', 0, 0, tiled=True)]
  transfers between devices with their start and end apart: 11 -> 19, of which waited for: 9 -> 13; matrix products, arithmetic and copies ran while one was open for 2% -> 2% of each run, Pallas kernels for 12% -> 26%
where the time goes in v2:
time: 236 us; the launch traced here: 235 us
  Pallas kernels  82.2 us (35%)
  waiting for transfers between devices  49.3 us (21%)
  starting transfers between devices  37 us (16%)
  blocking collectives  29.4 us (12%)
  local copies, waits for them, and re-layouts  21.4 us (9%)
  between operations  14.3 us (6%)
    pallas_call x9, Pallas kernels, call(): pl.pallas_call(kernel, out_shape=outs, scratch_shapes=list(scratch), cost...  65.2 us
    all_to_all x1, blocking collectives, body(): slots = exchange(slots)  18 us
    pallas_call x1, Pallas kernels, feed(): pl.pallas_call(feed_kernel, grid=(4,), in_specs=[whole(256, 768), whole(2...  17 us
    unnamed x40, local copies, waits for them, and re-layouts  14 us
    ppermute x1, waiting for transfers between devices, body(): far = lax.ppermute(near, 'batch', SWAP_Z)  12.3 us
    all_to_all x1, blocking collectives, body(): d_att = exchange(d_att)  11.4 us
    all_to_all x1, starting transfers between devices, body(): slots = exchange(slots)  8.84 us
    all_to_all x1, waiting for transfers between devices, body(): slots = exchange(slots)  8.45 us
  transfers between devices with their start and end apart: 19, of which 13 were waited for; matrix products, arithmetic and copies ran while one was open for 2% of the time, Pallas kernels for 26%

profile of v2, /device:TPU:64, one launch (start us, length us, event | category | flops | bytes accessed | tf_op | source)
XLA Modules:
  0.0 234.7 jit_solution(4815122753013600631)
XLA Ops:
  7.2 0.8 copy.29
  8.0 0.8 copy.30
  8.7 0.8 copy.31
  9.5 0.8 copy.32
  10.2 0.1 fusion.10.norms_ref
  10.3 0.8 copy-done.3
  11.1 0.8 copy-done.4
  11.9 0.8 copy-done.5
  12.7 0.7 copy-done.6
  13.4 1.3 copy-done.7
  14.6 0.5 shard_map.231
  15.2 18.0 %all_to_all.30.slots_ref = bf16[8,64,768]{2,1,0:T(8,128)(2,1)S(1)} all-to-all(bf16[8,64,768]{2,1,0:T(8,128)(2,1)S(1)} %shard_map.231), channel_id=1, replica_groups={{0,16,32,48,64,80,96,112},{8,24,40,56,72,88,104,120},{1,17,33,49,65,81,..., dimensions={0} | all-to-all | bytes 1572864 | tf_op jit(solution)/shard_map/all_to_all | solution.py:512
  33.2 1.4 shard_map.232
  34.7 1.3 broadcast_in_dim.2
  35.9 4.4 %all-to-all-start = ((bf16[8,128,768]{2,1,0:T(8,128)(2,1)}), bf16[8,128,768]{2,1,0:T(8,128)(2,1)}, u32[]{:S(2)}, u32[]{:S(2)}) async-start(bf16[8,128,768]{2,1,0:T(8,128)(2,1)} %bitcast.7), calls=%async_computation | async-start | bytes 3145728 | tf_op jit(solution)/shard_map/all_to_all | solution.py:528
  40.4 1.6 collective-permute-start.2
  41.9 2.7 %collective-permute-start.1 = (bf16[48,640]{1,0:T(8,128)(2,1)S(1)}, bf16[48,640]{1,0:T(8,128)(2,1)S(1)}, u32[]{:S(2)}, u32[]{:S(2)}) collective-permute-start(bf16[48,640]{1,0:T(8,128)(2,1)S(1)} %get-tuple-element.38), channel_id=1, source_target_pairs={{0,2},{1,3},{2,0},{3,1},{4,6},{5,7},{6,4},{7,5},{8,10},{9,11},{10,... | collective-permute-start | bytes 184328 | tf_op jit(solution)/shard_map/ppermute | solution.py:521
  44.7 1.4 collective-permute-start
  46.1 2.2 collective-permute-done.1
  48.3 1.2 collective-permute-done
  49.6 0.1 collective-permute-start.3
  49.7 0.1 collective-permute-start.4
  49.8 12.3 %collective-permute-done.3.far_ref = bf16[4,48,640]{2,1,0:T(8,128)(2,1)S(1)} collective-permute-done((bf16[4,48,640]{2,1,0:T(8,128)(2,1)S(1)}, bf16[4,48,640]{2,1,0:T(8,128)(2,1)S(1)}, u32[]{:S(2)}, u32[]{:S(2)}) %collective-permute-start.3) | collective-permute-done | bytes 245792 | tf_op jit(solution)/shard_map/ppermute | solution.py:523
  62.1 0.6 dynamic_slice.3
  62.7 0.7 pad_add_fusion.info_ref
  63.4 0.2 collective-permute-done.5.far_other_ref
  63.6 5.1 %shard_map.233 = (bf16[1024,768]{1,0:T(8,128)(2,1)}, bf16[576,768]{1,0:T(8,128)(2,1)S(1)}, f32[8,768]{1,0:T(8,128)S(1)}, bf16[576,1024]{1,0:T(8,128)(2,1)S(1)}) custom-call(s32[4]{0:T(128)S(1)} %pad_add_fusion.info_ref, bf16[8,128,768]{2,1,0:T(8,128)(2,1)} %all-to-all-done.own_ref, bf16[4,48,640]{2,1,0:T(8,128)(2,1)S(1)} %pad_maximum_fusion.near_ref, ...), custom_call_target="tpu_custom_call" | custom-call | flops 5500000256 | tf_op jit(solution)/shard_map/pallas_call | solution.py:81
  68.7 1.0 copy-done.14
  69.7 0.4 collective-permute-start.6
  70.1 1.9 collective-permute-done.6.other_ref
  72.0 21.5 %shard_map.234 = (f32[192,1024]{1,0:T(8,128)S(1)}, bf16[8,192,128]{2,1,0:T(8,128)(2,1)}, f32[3,1024]{1,0:T(4,128)S(1)}) custom-call(s32[4]{0:T(128)S(1)} %pad_add_fusion.info_ref, bf16[192,1024]{1,0:T(8,128)(2,1)S(1)} %slice.24.q_ref, bf16[384,1024]{1,0:T(8,128)(2,1)S(1)} %slice.25.own_ref, bf16[384,1024]{1,0:T(8,128)(2,1)S(1)} %collective-permute-done.6.other_ref), custom_call_target="tpu_custom_call" | custom-call | flops 14300000256 | tf_op jit(solution)/shard_map/pallas_call | solution.py:81
  93.5 0.9 copy-done.16
  94.4 4.7 %all-to-all-start.2 = ((bf16[8,192,128]{2,1,0:T(8,128)(2,1)}), bf16[8,192,128]{2,1,0:T(8,128)(2,1)S(1)}, u32[]{:S(2)}, u32[]{:S(2)}) async-start(bf16[8,192,128]{2,1,0:T(8,128)(2,1)} %get-tuple-element.40), calls=%async_computation.2 | async-start | bytes 786432 | tf_op jit(solution)/shard_map/all_to_all | solution.py:549
  99.2 8.4 %all-to-all-done.2.att_ref = bf16[8,192,128]{2,1,0:T(8,128)(2,1)S(1)} async-done(((bf16[8,192,128]{2,1,0:T(8,128)(2,1)}), bf16[8,192,128]{2,1,0:T(8,128)(2,1)S(1)}, u32[]{:S(2)}, u32[]{:S(2)}) %all-to-all-start.2) | async-done | bytes 393248 | tf_op jit(solution)/shard_map/all_to_all | solution.py:549
  107.7 1.3 copy-done.9
  108.9 17.0 %shard_map.235 = (bf16[256,768]{1,0:T(8,128)(2,1)S(1)}, f32[256,768]{1,0:T(8,128)S(1)}, bf16[8,192,128]{2,1,0:T(8,128)(2,1)S(1)}, f32[8,768]{1,0:T(8,128)S(1)}, bf16[16,432,768]{2,1,0:T(8,128)(2,1)}) custom-call(bf16[256,768]{1,0:T(8,128)(2,1)S(1)} %bitcast.48, bf16[256,768]{1,0:T(8,128)(2,1)S(1)} %bitcast.51, ...), custom_call_target="tpu_custom_call" | custom-call | flops 19800000512 | tf_op jit(solution)/shard_map/pallas_call | solution.py:379
  126.0 0.9 copy-done.12
  126.9 11.4 %all_to_all.31.da_ref = bf16[8,192,128]{2,1,0:T(8,128)(2,1)S(1)} all-to-all(bf16[8,192,128]{2,1,0:T(8,128)(2,1)S(1)} %get-tuple-element.47), channel_id=1, replica_groups={{0,16,32,48,64,80,96,112},{8,24,40,56,72,88,104,120},{1,17,33,49,65,81,..., dimensions={0} | all-to-all | bytes 786432 | tf_op jit(solution)/shard_map/all_to_all | solution.py:556
  138.3 1.1 copy-done.1
  139.4 26.0 %shard_map.236 = (bf16[192,1024]{1,0:T(8,128)(2,1)S(1)}, f32[384,1024]{1,0:T(8,128)}, bf16[384,1024]{1,0:T(8,128)(2,1)S(1)}) custom-call(s32[4]{0:T(128)S(1)} %pad_add_fusion.info_ref, bf16[192,1024]{1,0:T(8,128)(2,1)S(1)} %slice.24.q_ref, bf16[384,1024]{1,0:T(8,128)(2,1)S(1)} %slice.25.own_ref, bf16[384,1024]{1,0:T(8,128)(2,1)S(1)} %copy-done.1, ...), custom_call_target="tpu_custom_call" | custom-call | flops 18699999232 | tf_op jit(solution)/shard_map/pallas_call | solution.py:81
  165.4 2.3 collective-permute-done.7.partner_ref
  167.7 7.2 %shard_map.237 = (bf16[8,128,768]{2,1,0:T(8,128)(2,1)}, bf16[4,2,48,640]{3,2,1,0:T(8,128)(2,1)S(1)}, bf16[4,2,48,640]{3,2,1,0:T(8,128)(2,1)}) custom-call(s32[4]{0:T(128)S(1)} %pad_add_fusion.info_ref, bf16[8,128,768]{2,1,0:T(8,128)(2,1)} %all-to-all-done.own_ref, bf16[192,1024]{1,0:T(8,128)(2,1)S(1)} %get-tuple-element.48.dq_ref, ...), custom_call_target="tpu_custom_call" | custom-call | flops 7699999744 | tf_op jit(solution)/shard_map/pallas_call | solution.py:81
  174.9 0.1 collective-permute-start.8
  175.1 3.6 %all-to-all-start.4 = ((bf16[8,128,768]{2,1,0:T(8,128)(2,1)}), bf16[8,128,768]{2,1,0:T(8,128)(2,1)S(1)}, u32[]{:S(2)}, u32[]{:S(2)}) async-start(bf16[8,128,768]{2,1,0:T(8,128)(2,1)} %get-tuple-element.54), calls=%async_computation.4 | async-start | bytes 3145728 | tf_op jit(solution)/shard_map/all_to_all | solution.py:589
  178.7 0.1 add_convert_fusion
  178.9 3.2 %collective-permute-start.11 = (bf16[2,48,640]{2,1,0:T(8,128)(2,1)S(1)}, bf16[2,48,640]{2,1,0:T(8,128)(2,1)S(1)}, u32[]{:S(2)}, u32[]{:S(2)}) collective-permute-start(bf16[2,48,640]{2,1,0:T(8,128)(2,1)S(1)} %get-tuple-element.67), channel_id=1, source_target_pairs={{0,3},{1,0},{2,1},{3,2},{4,7},{5,4},{6,5},{7,6},{8,11},{9,8},{10,9... | collective-permute-start | bytes 368648 | tf_op jit(solution)/shard_map/ppermute | solution.py:586
  182.2 2.2 collective-permute-start.10
  184.4 1.3 collective-permute-done.9
  185.7 2.1 collective-permute-done.11
  187.8 4.3 %collective-permute-done.10 = bf16[2,48,640]{2,1,0:T(8,128)(2,1)S(1)} collective-permute-done((bf16[2,48,640]{2,1,0:T(8,128)(2,1)S(1)}, bf16[2,48,640]{2,1,0:T(8,128)(2,1)S(1)}, u32[]{:S(2)}, u32[]{:S(2)}) %collective-permute-start.10) | collective-permute-done | bytes 122912 | tf_op jit(solution)/shard_map/ppermute | solution.py:585
  192.2 3.4 %collective-permute-start.12 = (bf16[48,640]{1,0:T(8,128)(2,1)S(1)}, bf16[48,640]{1,0:T(8,128)(2,1)S(1)}, u32[]{:S(2)}, u32[]{:S(2)}) collective-permute-start(bf16[48,640]{1,0:T(8,128)(2,1)S(1)} %slice_bitcast_fusion.4), channel_id=1, source_target_pairs={{0,4},{1,5},{2,6},{3,7},{4,0},{5,1},{6,2},{7,3},{8,12},{9,13},{10,... | collective-permute-start | bytes 184328 | tf_op jit(solution)/shard_map/ppermute | solution.py:588
  195.6 4.2 %collective-permute-done.12 = bf16[48,640]{1,0:T(8,128)(2,1)S(1)} collective-permute-done((bf16[48,640]{1,0:T(8,128)(2,1)S(1)}, bf16[48,640]{1,0:T(8,128)(2,1)S(1)}, u32[]{:S(2)}, u32[]{:S(2)}) %collective-permute-start.12) | collective-permute-done | bytes 61472 | tf_op jit(solution)/shard_map/ppermute | solution.py:588
  199.9 1.1 copy-done.2
  201.0 1.0 copy-done.11
  202.0 1.6 shard_map.239
  203.6 0.3 all-to-all-done.4.got_ref
  203.9 8.8 %all-to-all-start.5 = ((bf16[8,64,768]{2,1,0:T(8,128)(2,1)}), bf16[8,64,768]{2,1,0:T(8,128)(2,1)S(1)}, u32[]{:S(2)}, u32[]{:S(2)}) async-start(bf16[8,64,768]{2,1,0:T(8,128)(2,1)} %shard_map.239), calls=%async_computation.6 | async-start | bytes 1572864 | tf_op jit(solution)/shard_map/all_to_all | solution.py:598
  212.7 1.1 copy.38
  213.9 1.1 copy-done.13
  215.0 0.7 shard_map.238
  215.7 1.2 copy.37
  216.8 8.5 %all-to-all-done.5.got_ref = bf16[8,64,768]{2,1,0:T(8,128)(2,1)S(1)} async-done(((bf16[8,64,768]{2,1,0:T(8,128)(2,1)}), bf16[8,64,768]{2,1,0:T(8,128)(2,1)S(1)}, u32[]{:S(2)}, u32[]{:S(2)}) %all-to-all-start.5) | async-done | bytes 786464 | tf_op jit(solution)/shard_map/all_to_all | solution.py:598
  225.3 1.3 copy-done.8
  226.5 1.3 shard_map.240
  (48 shorter events, 0.6 us)
Async XLA Ops:
  7.2 100.5 %all-gather.3.cloned.1.call-start = ((), (), s32[]{:S(2)}) async-start(), calls=%async_computation.8 | async-start | bytes 11280384 | tf_op jit(solution)/shard_map/all_gather | solution.py:519
  10.3 0.8 copy-start.3
  11.1 0.8 copy-start.4
  11.9 0.8 copy-start.5
  12.7 0.7 copy-start.6
  13.4 1.3 copy-start.7
  15.2 18.0 %copy-start.10 = (bf16[480,512]{1,0:T(8,128)(2,1)S(1)}, bf16[480,512]{1,0:T(8,128)(2,1)}, u32[]{:S(2)}) copy-start(bf16[480,512]{1,0:T(8,128)(2,1)} %constant.54.clone.order_ref) | copy-start | bytes 1474564
  33.2 1.4 copy-start.17
  35.9 26.1 %copy-start.19 = (s32[2]{0:T(128)S(1)}, s32[2]{0:T(128)}, u32[]{:S(2)}) copy-start(s32[2]{0:T(128)} %param.17) | copy-start | bytes 28
  35.9 27.6 %all-to-all-start = ((bf16[8,128,768]{2,1,0:T(8,128)(2,1)}), bf16[8,128,768]{2,1,0:T(8,128)(2,1)}, u32[]{:S(2)}, u32[]{:S(2)}) async-start(bf16[8,128,768]{2,1,0:T(8,128)(2,1)} %bitcast.7), calls=%async_computation | async-start | bytes 3145728 | tf_op jit(solution)/shard_map/all_to_all | solution.py:528
  40.4 5.7 %collective-permute-start.2 = (bf16[48,640]{1,0:T(8,128)(2,1)S(1)}, bf16[48,640]{1,0:T(8,128)(2,1)S(1)}, u32[]{:S(2)}, u32[]{:S(2)}) collective-permute-start(bf16[48,640]{1,0:T(8,128)(2,1)S(1)} %get-tuple-element.38), channel_id=1, source_target_pairs={{0,1},{1,2},{2,3},{3,0},{4,5},{5,6},{6,7},{7,4},{8,9},{9,10},{10,1... | collective-permute-start | bytes 184328 | tf_op jit(solution)/shard_map/ppermute | solution.py:521
  41.9 6.4 %collective-permute-start.1 = (bf16[48,640]{1,0:T(8,128)(2,1)S(1)}, bf16[48,640]{1,0:T(8,128)(2,1)S(1)}, u32[]{:S(2)}, u32[]{:S(2)}) collective-permute-start(bf16[48,640]{1,0:T(8,128)(2,1)S(1)} %get-tuple-element.38), channel_id=1, source_target_pairs={{0,2},{1,3},{2,0},{3,1},{4,6},{5,7},{6,4},{7,5},{8,10},{9,11},{10,... | collective-permute-start | bytes 184328 | tf_op jit(solution)/shard_map/ppermute | solution.py:521
  44.7 4.9 %collective-permute-start = (bf16[48,640]{1,0:T(8,128)(2,1)S(1)}, bf16[48,640]{1,0:T(8,128)(2,1)S(1)}, u32[]{:S(2)}, u32[]{:S(2)}) collective-permute-start(bf16[48,640]{1,0:T(8,128)(2,1)S(1)} %get-tuple-element.38), channel_id=1, source_target_pairs={{0,3},{1,0},{2,1},{3,2},{4,7},{5,4},{6,5},{7,6},{8,11},{9,8},{10,9... | collective-permute-start | bytes 184328 | tf_op jit(solution)/shard_map/ppermute | solution.py:521
  49.6 12.5 %collective-permute-start.3 = (bf16[4,48,640]{2,1,0:T(8,128)(2,1)S(1)}, bf16[4,48,640]{2,1,0:T(8,128)(2,1)S(1)}, u32[]{:S(2)}, u32[]{:S(2)}) collective-permute-start(bf16[4,48,640]{2,1,0:T(8,128)(2,1)S(1)} %pad_maximum_fusion.near_ref), channel_id=1, source_target_pairs={{0,4},{1,5},{2,6},{3,7},{4,0},{5,1},{6,2},{7,3},{8,12},{9,13},{10,... | collective-permute-start | bytes 737288 | tf_op jit(solution)/shard_map/ppermute | solution.py:523
  49.7 13.7 %collective-permute-start.4 = (bf16[4,48,640]{2,1,0:T(8,128)(2,1)S(1)}, bf16[4,48,640]{2,1,0:T(8,128)(2,1)S(1)}, u32[]{:S(2)}, u32[]{:S(2)}) collective-permute-start(bf16[4,48,640]{2,1,0:T(8,128)(2,1)S(1)} %pad_maximum_fusion.near_ref), channel_id=1, source_target_pairs={{0,8},{8,0},{16,24},{24,16},{32,40},{40,32},{48,56},{56,48},{64,72... | collective-permute-start | bytes 737288 | tf_op jit(solution)/shard_map/ppermute | solution.py:524
  62.1 1.5 collective-permute-start.5
  68.7 1.0 copy-start.14
  69.7 2.4 %collective-permute-start.6 = (bf16[384,1024]{1,0:T(8,128)(2,1)S(1)}, bf16[384,1024]{1,0:T(8,128)(2,1)S(1)}, u32[]{:S(2)}, u32[]{:S(2)}) collective-permute-start(bf16[384,1024]{1,0:T(8,128)(2,1)S(1)} %slice.25.own_ref), channel_id=1, source_target_pairs={{0,8},{8,0},{16,24},{24,16},{32,40},{40,32},{48,56},{56,48},{64,72... | collective-permute-start | bytes 2359304 | tf_op jit(solution)/shard_map/ppermute | solution.py:540
  70.1 29.0 %copy-start.18 = (bf16[128,2,768]{2,1,0:T(2,128)(2,1)S(1)}, bf16[128,2,768]{2,1,0:T(2,128)(2,1)}, u32[]{:S(2)}) copy-start(bf16[128,2,768]{2,1,0:T(2,128)(2,1)} %param.26) | copy-start | bytes 1179652
  72.0 21.5 %copy-start = (bf16[384,1024]{1,0:T(8,128)(2,1)}, bf16[384,1024]{1,0:T(8,128)(2,1)S(1)}, u32[]{:S(2)}) copy-start(bf16[384,1024]{1,0:T(8,128)(2,1)S(1)} %collective-permute-done.6.other_ref) | copy-start | bytes 2359300
  93.5 0.9 copy-start.16
  94.4 13.3 %all-to-all-start.2 = ((bf16[8,192,128]{2,1,0:T(8,128)(2,1)}), bf16[8,192,128]{2,1,0:T(8,128)(2,1)S(1)}, u32[]{:S(2)}, u32[]{:S(2)}) async-start(bf16[8,192,128]{2,1,0:T(8,128)(2,1)} %get-tuple-element.40), calls=%async_computation.2 | async-start | bytes 786432 | tf_op jit(solution)/shard_map/all_to_all | solution.py:549
  99.1 100.7 %reduce-scatter.2.cloned.1.call-start = ((), (), s32[]{:S(2)}) async-start(), calls=%async_computation.7 | async-start | bytes 11280384 | tf_op jit(solution)/shard_map/reduce_scatter | solution.py:552
  107.7 1.3 copy-start.9
  126.0 0.9 copy-start.12
  138.3 1.1 copy-start.1
  139.4 28.3 %copy-start.15 = (bf16[576,768]{1,0:T(8,128)(2,1)S(1)}, bf16[576,768]{1,0:T(8,128)(2,1)}, u32[]{:S(2)}) copy-start(bf16[576,768]{1,0:T(8,128)(2,1)} %copy-done.14) | copy-start | bytes 2654212
  165.4 2.3 collective-permute-start.7
  174.9 3.7 %collective-permute-start.8 = (bf16[4,2,48,640]{3,2,1,0:T(8,128)(2,1)}, bf16[4,2,48,640]{3,2,1,0:T(8,128)(2,1)S(1)}, u32[]{:S(2)}, u32[]{:S(2)}) collective-permute-start(bf16[4,2,48,640]{3,2,1,0:T(8,128)(2,1)} %get-tuple-element.57), channel_id=1, source_target_pairs={{0,8},{8,0},{16,24},{24,16},{32,40},{40,32},{48,56},{56,48},{64,72... | collective-permute-start | bytes 1474568 | tf_op jit(solution)/shard_map/ppermute | solution.py:581
  175.1 28.8 %all-to-all-start.4 = ((bf16[8,128,768]{2,1,0:T(8,128)(2,1)}), bf16[8,128,768]{2,1,0:T(8,128)(2,1)S(1)}, u32[]{:S(2)}, u32[]{:S(2)}) async-start(bf16[8,128,768]{2,1,0:T(8,128)(2,1)} %get-tuple-element.54), calls=%async_computation.4 | async-start | bytes 3145728 | tf_op jit(solution)/shard_map/all_to_all | solution.py:589
  178.8 6.9 %collective-permute-start.9 = (bf16[2,48,640]{2,1,0:T(8,128)(2,1)S(1)}, bf16[2,48,640]{2,1,0:T(8,128)(2,1)S(1)}, u32[]{:S(2)}, u32[]{:S(2)}) collective-permute-start(bf16[2,48,640]{2,1,0:T(8,128)(2,1)S(1)} %get-tuple-element.66), channel_id=1, source_target_pairs={{0,1},{1,2},{2,3},{3,0},{4,5},{5,6},{6,7},{7,4},{8,9},{9,10},{10,1... | collective-permute-start | bytes 368648 | tf_op jit(solution)/shard_map/ppermute | solution.py:584
  178.9 8.9 %collective-permute-start.11 = (bf16[2,48,640]{2,1,0:T(8,128)(2,1)S(1)}, bf16[2,48,640]{2,1,0:T(8,128)(2,1)S(1)}, u32[]{:S(2)}, u32[]{:S(2)}) collective-permute-start(bf16[2,48,640]{2,1,0:T(8,128)(2,1)S(1)} %get-tuple-element.67), channel_id=1, source_target_pairs={{0,3},{1,0},{2,1},{3,2},{4,7},{5,4},{6,5},{7,6},{8,11},{9,8},{10,9... | collective-permute-start | bytes 368648 | tf_op jit(solution)/shard_map/ppermute | solution.py:586
  182.2 10.0 %collective-permute-start.10 = (bf16[2,48,640]{2,1,0:T(8,128)(2,1)S(1)}, bf16[2,48,640]{2,1,0:T(8,128)(2,1)S(1)}, u32[]{:S(2)}, u32[]{:S(2)}) collective-permute-start(bf16[2,48,640]{2,1,0:T(8,128)(2,1)S(1)} %get-tuple-element.68), channel_id=1, source_target_pairs={{0,2},{1,3},{2,0},{3,1},{4,6},{5,7},{6,4},{7,5},{8,10},{9,11},{10,... | collective-permute-start | bytes 368648 | tf_op jit(solution)/shard_map/ppermute | solution.py:585
  192.2 7.6 %collective-permute-start.12 = (bf16[48,640]{1,0:T(8,128)(2,1)S(1)}, bf16[48,640]{1,0:T(8,128)(2,1)S(1)}, u32[]{:S(2)}, u32[]{:S(2)}) collective-permute-start(bf16[48,640]{1,0:T(8,128)(2,1)S(1)} %slice_bitcast_fusion.4), channel_id=1, source_target_pairs={{0,4},{1,5},{2,6},{3,7},{4,0},{5,1},{6,2},{7,3},{8,12},{9,13},{10,... | collective-permute-start | bytes 184328 | tf_op jit(solution)/shard_map/ppermute | solution.py:588
  199.9 1.1 copy-start.2
  201.0 1.0 copy-start.11
  203.9 21.4 %all-to-all-start.5 = ((bf16[8,64,768]{2,1,0:T(8,128)(2,1)}), bf16[8,64,768]{2,1,0:T(8,128)(2,1)S(1)}, u32[]{:S(2)}, u32[]{:S(2)}) async-start(bf16[8,64,768]{2,1,0:T(8,128)(2,1)} %shard_map.239), calls=%async_computation.6 | async-start | bytes 1572864 | tf_op jit(solution)/shard_map/all_to_all | solution.py:598
  213.9 1.1 copy-start.13
  225.3 1.3 copy-start.8
Sparse Core Ops, SparseCore 0:
  34.7 67.1 all-gather.2
  127.0 71.4 reduce-scatter.1

commit v3 on v2

v3 whole, which is shorter than its diff:
```python
import functools
import math

import jax
import jax.numpy as jnp
import numpy as np
from jax import lax
from jax.experimental import pallas as pl
from jax.experimental.pallas import tpu as pltpu
from jax.sharding import PartitionSpec as P

H = 12
HD = 64
EPSILON = 1e-05
BF = jnp.bfloat16
F32 = jnp.float32
BOTH = ("seq", "batch")
SAME_CORE = [[2 * k + c for k in range(8)] for c in range(2)]
SWAP_CORE = [(i, i ^ 1) for i in range(16)]
TURNS = [(0, 0), (0, 1), (0, 2), (0, 3), (1, 3), (1, 2), (1, 1), (1, 0)]
RING = [(c, z, x) for z, x in TURNS for c in range(2)]


RINGS = [
    [((y * 2 + (low ^ z)) * 2 + c) * 8 + z * 4 + x for c, z, x in RING]
    for y in range(4)
    for low in range(2)
]
SWAP_Z = [(b, b ^ 4) for b in range(8)]


def along_x(step):
    return [(b, b // 4 * 4 + (b + step) % 4) for b in range(8)]


def in_order(outer, size):
    natural = np.arange(outer * 16 * size, dtype=np.int32).reshape(outer, 2, 8, size)
    return np.stack([natural[:, c, z * 4 + x] for c, z, x in RING]).reshape(1, -1)


QKV_ORDER = (
    np.arange(768, dtype=np.int32).reshape(8, 2, 8, 6).transpose(1, 2, 0, 3).reshape(1, 768)
)
ROW_ORDER = in_order(8, 6)
UNIT_ORDER = in_order(2, 24)


def regroup_order():
    slot = np.arange(512, dtype=np.int32).reshape(8, 64)
    parts = [slot[:, 0:24]] + [slot[:, f : f + 6] for f in (30, 36, 42, 48, 24, 54)]
    return np.concatenate([p.reshape(-1) for p in parts] + [np.full(32, -1, np.int32)])[None]


REGROUP = regroup_order()


def places(order_ref):
    order = order_ref[...]
    size = order.shape[1]
    rows = lax.broadcasted_iota(jnp.int32, (size, size), 0)
    return jnp.where(rows == order, 1.0, 0.0).astype(BF)


NT = (((1,), (1,)), ((), ()))
NN = (((1,), (0,)), ((), ()))
TN = (((0,), (0,)), ((), ()))


def dot(left, right, dims=NN):
    return lax.dot_general(left, right, dims, preferred_element_type=F32)


def about(us):
    return pl.CostEstimate(flops=int(us * 1.1e9), bytes_accessed=0, transcendentals=0)


PARAMS = pltpu.CompilerParams(vmem_limit_bytes=60 * 1024 * 1024)


def call(kernel, outs, ins, us, scratch=(), **kwargs):
    return pl.pallas_call(
        kernel,
        out_shape=outs,
        scratch_shapes=list(scratch),
        cost_estimate=about(us),
        compiler_params=PARAMS,
        **kwargs,
    )(*ins)


def shape(dims, dtype):
    return jax.ShapeDtypeStruct(dims, dtype)


def normalize(values):
    center = jnp.mean(values, axis=-1, keepdims=True)
    shifted = values - center
    spread = jnp.mean(shifted * shifted, axis=-1, keepdims=True)
    scale = lax.rsqrt(spread + EPSILON)
    return shifted * scale, scale


def pack_kernel(
    down_ref, out_ref, up_ref, qkv_ref, g1_ref, b1_ref, g2_ref, b2_ref, units_ref,
    slot_ref, scr, turn_scr,
):
    turn_scr[...] = jnp.zeros_like(turn_scr)
    for i, ref in enumerate((g1_ref, b1_ref, g2_ref, b2_ref)):
        turn_scr[64 + i : 65 + i, 0:6] = ref[...].astype(F32)
    norms = turn_scr[...].T[0:6, 64:128].astype(BF)
    up = jnp.concatenate(
        [up_ref[:, k * 768 : (k + 1) * 768].astype(F32) for k in range(4)], axis=0
    ).astype(BF)
    scr[0:24, :] = down_ref[...].astype(F32)
    scr[24:30, :] = out_ref[...].astype(F32)
    scr[30:54, :] = dot(up, places(units_ref))
    scr[60:64, :] = jnp.zeros((4, 768), F32)
    for e in range(4):
        parts = [qkv_ref[:, s * 768 + e * 192 : s * 768 + (e + 1) * 192] for s in range(3)]
        row = jnp.concatenate(parts + [norms, jnp.zeros((6, 128), BF)], axis=1)
        scr[54:60, :] = row.astype(F32)
        slot = scr[...].astype(BF)
        slot_ref[e] = slot
        slot_ref[4 + e] = slot


def regroup_kernel(slots_ref, order_ref, rest_ref, qkv_ref):
    rows = dot(places(order_ref), slots_ref[...].reshape(512, 768), TN).astype(BF)
    rest_ref[...] = rows[0:432]
    qkv_ref[...] = rows[432:480, 0:640]


def core_of():
    return lax.rem(lax.axis_index("seq"), 2)


def length_of(lengths_ref):
    return jnp.where(lax.axis_index("seq") < 8, lengths_ref[0], lengths_ref[1])


def rows_at(dc, dz, dx):
    row = lax.axis_index("batch")
    c = lax.rem(core_of() + dc, 2)
    z = lax.rem(row // 4 + dz, 2)
    x = lax.rem(row + dx, 4)
    return pl.ds(pl.multiple_of((c * 8 + z * 4 + x) * 48, 48), 48)


def project_kernel(
    own_ref, near_ref, far_ref, near_other_ref, far_other_ref, order_ref,
    normed_ref, wt_ref, gains_ref, q_ref, kv_ref, w_scr, t_scr,
):
    for i, ref in enumerate((near_ref, far_ref, near_other_ref, far_other_ref)):
        for dx in range(4):
            w_scr[rows_at(i // 2, i % 2, dx), :] = ref[dx]
    t_scr[...] = dot(w_scr[...].T, places(order_ref), NT)
    wt_ref[...] = t_scr[0:576].astype(BF)
    gains = t_scr[576:584]
    gains_ref[...] = gains
    gain, bias = gains[0:1], gains[1:2]
    for j in range(8):
        hat, _ = normalize(own_ref[j].astype(F32))
        normed_ref[j * 128 : (j + 1) * 128, :] = (hat * gain + bias).astype(BF)
    for j in range(4):
        lanes = slice(j * 256, (j + 1) * 256)
        qkv = dot(wt_ref[...], normed_ref[lanes, :], NT).astype(BF)
        q_ref[:, lanes] = qkv[0:192]
        kv_ref[:, lanes] = qkv[192:576]


def last_keys(m, core, length):
    lane = lax.broadcasted_iota(jnp.int32, (1, 256), 1)
    query = m * 512 + 128 * core + jnp.where(lane < 128, lane, lane + 128)
    return jnp.minimum(query, length - 1)


def allowed(start, first, last, core):
    offset = start + first + (128 * core if first < 128 else -128 * core)
    return lax.broadcasted_iota(jnp.int32, (64, 256), 0) <= last - offset


def fill_keys(own_ref, other_ref, k_scr, base):
    for u in range(3):
        for j in range(8):
            rows, lanes = pl.ds(base + u * 64, 64), pl.ds(j * 128, 128)
            k_scr[u, j * 256 : j * 256 + 128, :] = own_ref[rows, lanes].T
            k_scr[u, j * 256 + 128 : j * 256 + 256, :] = other_ref[rows, lanes].T


def fill_lanes(own_ref, other_ref, scr, base):
    for j in range(8):
        scr[:, j * 256 : j * 256 + 128] = own_ref[base : base + 192, j * 128 : j * 128 + 128]
        scr[:, j * 256 + 128 : j * 256 + 256] = other_ref[
            base : base + 192, j * 128 : j * 128 + 128
        ]


PAIRS = [(h, u) for h in range(2) for u in range(3)]
CHUNKS = [slice(i * 64, i * 64 + 64) for i in range(4)]


def steps(m, length):
    return jnp.minimum(m + 1, (length + 511) // 512)


def sweep(length, begin, score, step, finish):
    def one(_, place):
        m, jk = place
        more = jk + 1 < steps(m, length)
        next_m = jnp.where(more, m, jnp.minimum(m + 1, 3))
        next_jk = jnp.where(more, jk + 1, 0)

        @pl.when(jk == 0)
        def _():
            begin()

        edge = (jk == m) | (jk * 512 + 512 > length)

        @pl.when(edge)
        def _():
            step(m, jk, next_m, next_jk, True)

        @pl.when(jnp.logical_not(edge))
        def _():
            step(m, jk, next_m, next_jk, False)

        @pl.when(jnp.logical_not(more))
        def _():
            finish(m)

        return jnp.where(more, m, m + 1), next_jk

    for h, u in PAIRS:
        score(h, u, 0, 0)
    total = sum(steps(m, length) for m in range(4))
    lax.fori_loop(0, total, one, (jnp.int32(0), jnp.int32(0)))


def group(m):
    return pl.ds(pl.multiple_of(m * 256, 256), 256)


def key_tile(jk, h):
    return pl.ds(pl.multiple_of(jk * 512, 512) + h * 256, 256)


def forward_plain(q_scr, k_scr, v_scr, scratch, length, core, finish):
    s_scr, w_scr, acc_scr, sum_scr = scratch[0:6], scratch[6:12], scratch[12:15], scratch[15:18]

    def begin():
        for u in range(3):
            acc_scr[u][...] = jnp.zeros((64, 256), F32)
            sum_scr[u][...] = jnp.zeros((8, 256), F32)

    def score(h, u, m, jk):
        queries = q_scr[u * 64 : (u + 1) * 64, group(m)]
        s_scr[h * 3 + u][...] = dot(k_scr[u, key_tile(jk, h), :], queries)

    def step(m, jk, next_m, next_jk, masked):
        last = last_keys(m, core, length)
        for h, u in PAIRS:
            scores, weights = s_scr[h * 3 + u], w_scr[h * 3 + u]
            total = sum_scr[u][...]
            for rows in CHUNKS:
                s = scores[rows, :]
                t = s * s + 1.0
                r = lax.rsqrt(t)
                e = jnp.exp(t * r)
                if masked:
                    e = jnp.where(allowed(jk * 512 + h * 256, rows.start, last, core), e, 0.0)
                total = total + jnp.sum(e.reshape(8, 8, 256), axis=0)
                weights[rows, :] = (s * r * e).astype(BF)
            sum_scr[u][...] = total
            score(h, u, next_m, next_jk)
            acc_scr[u][...] += dot(v_scr[u * 64 : (u + 1) * 64, key_tile(jk, h)], weights[...])

    def close(m):
        for u in range(3):
            total = jnp.sum(sum_scr[u][...], axis=0, keepdims=True)
            finish(m, u, acc_scr[u][...], total, jnp.zeros((1, 256), F32))

    sweep(length, begin, score, step, close)


def forward_any(q_scr, k_scr, v_scr, length, core, finish):
    def one(m, _):
        last = last_keys(m, core, length)

        def step(jk, carry):
            start = pl.multiple_of(jk * 256, 256)
            mask = jnp.concatenate([allowed(start, r.start, last, core) for r in CHUNKS], axis=0)
            out = []
            for u in range(3):
                top, total, accum = carry[u]
                s = dot(k_scr[u, pl.ds(start, 256), :], q_scr[u * 64 : (u + 1) * 64, group(m)])
                t = s * s + 1.0
                r = lax.rsqrt(t)
                a = jnp.where(mask, t * r, -1e30)
                fresh = jnp.maximum(top, jnp.max(a, axis=0, keepdims=True))
                e = jnp.exp(a - fresh)
                rescale = jnp.exp(top - fresh)
                total = total * rescale + jnp.sum(e, axis=0, keepdims=True)
                accum = accum * rescale + dot(
                    v_scr[u * 64 : (u + 1) * 64, pl.ds(start, 256)], (s * r * e).astype(BF)
                )
                out.append((fresh, total, accum))
            return tuple(out)

        zero = (jnp.zeros((1, 256), F32), jnp.zeros((1, 256), F32), jnp.zeros((64, 256), F32))
        carry = lax.fori_loop(0, 2 * steps(m, length), step, (zero,) * 3)
        for u in range(3):
            finish(m, u, carry[u][2], carry[u][1], carry[u][0])
        return 0

    lax.fori_loop(0, 4, one, 0)


def forward_kernel(
    lengths_ref, q_ref, own_ref, other_ref, o_ref, low_ref, lse_ref, q_scr, k_scr, v_scr, *scratch
):
    length, core = length_of(lengths_ref), core_of()
    fill_keys(own_ref, other_ref, k_scr, 0)
    fill_lanes(own_ref, other_ref, v_scr, 192)
    q_scr[...] = q_ref[...] * BF(0.125)

    def finish(m, u, accum, total, top):
        lanes = group(m)
        o = accum / total
        o_ref[u * 64 : (u + 1) * 64, lanes] = o
        for half in range(2):
            low_ref[2 * m + half, u * 64 : (u + 1) * 64, :] = o[
                :, half * 128 : half * 128 + 128
            ].astype(BF)
        lse_ref[u : u + 1, lanes] = top + jnp.log(total)

    def largest(ref):
        values = ref[0:192, :].astype(F32)
        return jnp.max(jnp.sum((values * values).reshape(3, 64, 1024), axis=1))

    bound = largest(q_ref) * jnp.maximum(largest(own_ref), largest(other_ref)) * (1.0 / 64.0)
    small = bound < 3600.0

    @pl.when(small)
    def _():
        forward_plain(q_scr, k_scr, v_scr, scratch, length, core, finish)

    @pl.when(jnp.logical_not(small))
    def _():
        forward_any(q_scr, k_scr, v_scr, length, core, finish)


def backward_kernel(
    lengths_ref, q_ref, own_ref, other_ref, o_ref, lse_ref, da_ref,
    dq_ref, down_ref, dother_ref,
    q_scr, k_scr, kt_scr, v_scr, da_scr, dk_scr, dv_scr, delta_scr, *scratch,
):
    s_scr, dp_scr, w_scr, ds_scr, dq_scr = (scratch[i : i + 6] for i in (0, 6, 12, 18, 24))
    length, core = length_of(lengths_ref), core_of()
    fill_keys(own_ref, other_ref, k_scr, 0)
    fill_lanes(own_ref, other_ref, kt_scr, 0)
    fill_keys(own_ref, other_ref, v_scr, 192)
    q_scr[...] = q_ref[...] * BF(0.125)
    for j in range(8):
        lanes = slice(j * 128, (j + 1) * 128)
        da_scr[:, lanes] = da_ref[j]
        for u in range(3):
            rows = slice(u * 64, (u + 1) * 64)
            delta_scr[u : u + 1, lanes] = jnp.sum(
                da_ref[j, rows, :].astype(F32) * o_ref[rows, lanes], axis=0, keepdims=True
            )
    dk_scr[...] = jnp.zeros_like(dk_scr)
    dv_scr[...] = jnp.zeros_like(dv_scr)

    def begin():
        for u in range(3):
            dq_scr[u][...] = jnp.zeros((64, 256), F32)

    def score(h, u, m, jk):
        rows, tile = slice(u * 64, (u + 1) * 64), key_tile(jk, h)
        s_scr[h * 3 + u][...] = dot(k_scr[u, tile, :], q_scr[rows, group(m)])
        dp_scr[h * 3 + u][...] = dot(v_scr[u, tile, :], da_scr[rows, group(m)])

    def step(m, jk, next_m, next_jk, masked):
        last = last_keys(m, core, length)
        for h, u in PAIRS:
            tile = key_tile(jk, h)
            heads = slice(u * 64, (u + 1) * 64)
            delta, lse = delta_scr[u : u + 1, group(m)], lse_ref[u : u + 1, group(m)]
            place = h * 3 + u
            for rows in CHUNKS:
                s = s_scr[place][rows, :]
                t = s * s + 1.0
                r = lax.rsqrt(t)
                p = jnp.exp(t * r - lse)
                if masked:
                    p = jnp.where(allowed(jk * 512 + h * 256, rows.start, last, core), p, 0.0)
                g = s * r
                w_scr[place][rows, :] = (g * p).astype(BF)
                ds = p * (dp_scr[place][rows, :] * (r * r * (r - 1.0) + 1.0) - g * delta)
                ds_scr[place][rows, :] = ds.astype(BF)
            score(h, u, next_m, next_jk)
            dv_scr[u, :, tile] += dot(da_scr[heads, group(m)], w_scr[place][...], NT)
            dk_scr[u, :, tile] += dot(q_scr[heads, group(m)], ds_scr[place][...], NT)
            dq_scr[u][...] += dot(kt_scr[heads, tile], ds_scr[place][...])

    def close(m):
        for u in range(3):
            dq_ref[u * 64 : (u + 1) * 64, group(m)] = (dq_scr[u][...] * 0.125).astype(BF)

    sweep(length, begin, score, step, close)
    for scr, base in ((dk_scr, 0), (dv_scr, 192)):
        for u in range(3):
            rows = pl.ds(base + u * 64, 64)
            for j in range(8):
                lanes = pl.ds(j * 128, 128)
                down_ref[rows, lanes] = scr[u, :, j * 256 : j * 256 + 128].astype(BF)
                dother_ref[rows, lanes] = scr[u, :, j * 256 + 128 : j * 256 + 256].astype(BF)


GELU_SCALE = math.sqrt(2.0 / math.pi)


def prepare_kernel(att_ref, order_ref, place_ref, attended_ref, attended_t_ref):
    place_ref[...] = places(order_ref)
    natural = [att_ref[b * 4 : b * 4 + 4].reshape(768, 128).T for b in range(2)]
    attended = dot(jnp.concatenate(natural, axis=0), place_ref[...]).astype(BF)
    attended_ref[...] = attended
    attended_t_ref[...] = attended.T


def feed_kernel(
    x_hbm, dy_hbm, att_hbm, att_t_hbm, gains_hbm, place_hbm, weights_hbm,
    y_hbm, dfirst_hbm, datt_hbm, dgain_hbm, grads_hbm,
    x_ref, dy_ref, att_ref, att_t_ref, gains_ref, place_ref, down_ref, up_ref, out_ref,
    y_ref, dfirst_ref, datt_ref, dgain_ref, gdown, gup, gout, acc_scr, dn_scr, loads, stores,
):
    def block(ref, number):
        return ref.at[:, pl.ds(48 * number, 48), :]

    arrivals = [(att_hbm, att_ref), (block(weights_hbm, 8), out_ref), (x_hbm, x_ref)]
    arrivals += [(gains_hbm, gains_ref), (place_hbm, place_ref)]
    for k in range(4):
        arrivals.append((block(weights_hbm, 4 + k), up_ref.at[k]))
        if k == 0:
            arrivals.append((dy_hbm, dy_ref))
        arrivals.append((block(weights_hbm, k), down_ref.at[k]))
    arrivals.append((att_t_hbm, att_t_ref))
    arrivals = [pltpu.make_async_copy(*pair, loads.at[i]) for i, pair in enumerate(arrivals)]
    for copy in arrivals:
        copy.start()
    departures = []

    def send(source, target):
        copy = pltpu.make_async_copy(source, target, stores.at[len(departures)])
        copy.start()
        departures.append(copy)

    for copy in arrivals[0:4]:
        copy.wait()
    gain, bias = gains_ref[2:3], gains_ref[3:4]
    w_out = out_ref[...].reshape(768, 768)
    first = x_ref[...].astype(F32) + dot(att_ref[...], w_out)
    hat, scale = normalize(first)
    acc_scr[...] = first
    arrivals[4].wait()
    n2 = dot((hat * gain + bias).astype(BF), place_ref[...]).astype(BF)
    n2t = n2.T
    waiting = arrivals[5:]
    for k in range(4):
        waiting.pop(0).wait()
        up = up_ref[k].reshape(768, 768)
        hidden = dot(n2, up)
        if k == 0:
            waiting.pop(0).wait()
        waiting.pop(0).wait()
        down = down_ref[k].reshape(768, 768)
        dy = dy_ref[...]
        d_active = dot(dy, down, NT)
        square = hidden * hidden
        tanh = jnp.tanh(GELU_SCALE * hidden * (1.0 + 0.044715 * square))
        share = 0.5 + 0.5 * tanh
        active = (hidden * share).astype(BF)
        slope = share + 0.5 * hidden * (1.0 - tanh * tanh) * (
            GELU_SCALE * (1.0 + (3 * 0.044715) * square)
        )
        d_hidden = (slope * d_active).astype(BF)
        gdown[k] = dot(active.T, dy).astype(BF).reshape(16, 48, 768)
        send(gdown.at[k], block(grads_hbm, k))
        gup[k] = dot(n2t, d_hidden).astype(BF).reshape(16, 48, 768)
        send(gup.at[k], block(grads_hbm, 4 + k))
        acc_scr[...] += dot(active, down)
        if k == 0:
            dn_scr[...] = dot(d_hidden, up, NT)
        else:
            dn_scr[...] += dot(d_hidden, up, NT)
    y_ref[...] = acc_scr[...].astype(BF)
    send(y_ref, y_hbm)
    dn = dot(dn_scr[...].astype(BF), place_ref[...], NT)
    t = dn * gain
    part = t - jnp.mean(t, -1, keepdims=True) - hat * jnp.mean(t * hat, -1, keepdims=True)
    d_first = dy_ref[...].astype(F32) + part * scale
    low = d_first.astype(BF)
    waiting.pop(0).wait()
    gout[...] = dot(att_t_ref[...], low).astype(BF).reshape(16, 48, 768)
    send(gout, block(grads_hbm, 8))
    d_att = dot(w_out, low, NT).astype(BF)
    d_att = dot(place_ref[...], d_att).astype(BF)
    for b in range(2):
        datt_ref[b * 4 : b * 4 + 4] = d_att[:, b * 128 : (b + 1) * 128].reshape(4, 192, 128)
    send(datt_ref, datt_hbm)
    dfirst_ref[...] = d_first
    send(dfirst_ref, dfirst_hbm)
    dgain_ref[0:1, :] = jnp.sum(dn * hat, axis=0, keepdims=True)
    dgain_ref[1:2, :] = jnp.sum(dn, axis=0, keepdims=True)
    dgain_ref[2:8, :] = jnp.zeros((6, 768), F32)
    send(dgain_ref, dgain_hbm)
    for copy in departures:
        copy.wait()


def whole(*dims):
    return pl.BlockSpec(dims, lambda *_: (0,) * len(dims))


def feed(*arrays):
    outs = [
        shape((256, 768), BF), shape((256, 768), F32), shape((8, 192, 128), BF),
        shape((8, 768), F32), shape((16, 432, 768), BF),
    ]
    blocks = pltpu.VMEM((4, 16, 48, 768), BF)
    held = [pltpu.VMEM(a.shape, a.dtype) for a in arrays[:-1]]
    held += [blocks, blocks, pltpu.VMEM((16, 48, 768), BF)]
    held += [pltpu.VMEM(o.shape, o.dtype) for o in outs[:-1]]
    held += [blocks, blocks, pltpu.VMEM((16, 48, 768), BF)]
    held += [pltpu.VMEM((256, 768), F32)] * 2
    held += [pltpu.SemaphoreType.DMA((15,)), pltpu.SemaphoreType.DMA((13,))]
    return call(
        feed_kernel,
        outs,
        arrays,
        17,
        held,
        in_specs=[pl.BlockSpec(memory_space=pl.ANY)] * len(arrays),
        out_specs=[pl.BlockSpec(memory_space=pl.ANY)] * len(outs),
    )


def unproject_kernel(
    own_ref, dq_ref, dkv_ref, partner_ref, normed_ref, wt_ref, dgain_ref, order_ref,
    part_ref, mine_ref, theirs_ref, dt_scr, dw_scr, p_scr,
):
    dt_scr[0:192, :] = dq_ref[...]
    dt_scr[192:576, :] = (dkv_ref[...].astype(F32) + partner_ref[...].astype(F32)).astype(BF)
    bias_sum = jnp.zeros((1, 768), F32)
    gain_sum = jnp.zeros((1, 768), F32)
    for j in range(4):
        d_normed = dot(dt_scr[:, j * 256 : (j + 1) * 256].T, wt_ref[...])
        part_ref[2 * j : 2 * j + 2] = d_normed.astype(BF).reshape(2, 128, 768)
        hat, _ = normalize(own_ref[2 * j : 2 * j + 2].reshape(256, 768).astype(F32))
        gain_sum += jnp.sum(d_normed * hat, axis=0, keepdims=True)
        bias_sum += jnp.sum(d_normed, axis=0, keepdims=True)
    dw_scr[0:576, :] = dot(dt_scr[...], normed_ref[...])
    dw_scr[576:577, :] = gain_sum
    dw_scr[577:578, :] = bias_sum
    dw_scr[578:580, :] = dgain_ref[0:2, :]
    dw_scr[580:640, :] = jnp.zeros((60, 768), F32)
    p_scr[...] = dot(dw_scr[...].astype(BF), places(order_ref)).T.astype(BF)
    for dc, ref in enumerate((mine_ref, theirs_ref)):
        for dx in range(4):
            for dz in range(2):
                ref[dx, dz] = p_scr[rows_at(dc, dz, dx), :]


def slots_kernel(rest_ref, qkv_ref, order_ref, out_ref, r_scr):
    r_scr[0:432, :] = rest_ref[...]
    r_scr[432:480, 0:640] = qkv_ref[...]
    r_scr[432:480, 640:768] = jnp.zeros((48, 128), BF)
    r_scr[480:512, :] = jnp.zeros((32, 768), BF)
    out_ref[...] = dot(places(order_ref), r_scr[...]).astype(BF).reshape(8, 64, 768)


def finish_kernel(x_ref, dfirst_ref, gains_ref, got_ref, dtok_ref):
    gain = gains_ref[0:1]
    for b in range(2):
        rows = slice(b * 128, (b + 1) * 128)
        dn = jnp.zeros((128, 768), F32)
        for e in range(4):
            dn += got_ref[4 * b + e].astype(F32)
        hat, scale = normalize(x_ref[rows, :].astype(F32))
        t = dn * gain
        part = t - jnp.mean(t, -1, keepdims=True) - hat * jnp.mean(t * hat, -1, keepdims=True)
        dtok_ref[rows, :] = (dfirst_ref[rows, :] + part * scale).astype(BF)


def sums_kernel(got_ref, units_ref, down_ref, out_ref, up_ref, qkv_ref, g1_ref, b1_ref, g2_ref, b2_ref):
    total = jnp.zeros((64, 768), F32)
    chunks = []
    for e in range(4):
        both = got_ref[e].astype(F32) + got_ref[4 + e].astype(F32)
        chunks.append(both[54:60])
        total += both
    down_ref[...] = total[0:24]
    out_ref[...] = total[24:30]
    left, up, units = total[30:54], jnp.zeros((24, 768), F32), places(units_ref)
    for _ in range(3):
        piece = left.astype(BF)
        left = left - piece.astype(F32)
        up += dot(piece, units, NT)
    for k in range(4):
        up_ref[:, k * 768 : (k + 1) * 768] = up[k * 6 : k * 6 + 6]
    for s in range(3):
        qkv_ref[:, s * 768 : (s + 1) * 768] = jnp.concatenate(
            [chunks[e][:, s * 192 : (s + 1) * 192] for e in range(4)], axis=1
        )
    norms = total[:, 512:640].T
    for i, ref in enumerate((g1_ref, b1_ref, g2_ref, b2_ref)):
        ref[...] = norms[64 + i : 65 + i, 54:60]


def scalars(count):
    return dict(
        in_specs=[pl.BlockSpec(memory_space=pltpu.SMEM)]
        + [pl.BlockSpec(memory_space=pltpu.VMEM)] * (count - 1)
    )


def body(tokens, lengths, gain_one, bias_one, w_qkv, w_out, gain_two, bias_two, w_up, w_down, d_out):
    order, units, regroup, qkv_order = (
        jnp.asarray(v) for v in (ROW_ORDER, UNIT_ORDER, REGROUP, QKV_ORDER)
    )
    exchange = functools.partial(
        lax.all_to_all, axis_name="seq", split_axis=0, concat_axis=0, tiled=True,
        axis_index_groups=SAME_CORE,
    )

    vectors = [v.reshape(1, 6) for v in (gain_one, bias_one, gain_two, bias_two)]
    slots = pl.pallas_call(
        pack_kernel,
        grid=(1,),
        in_specs=[whole(24, 768), whole(6, 768), whole(6, 3072), whole(6, 2304)]
        + [whole(1, 6)] * 4
        + [whole(1, 768)],
        out_specs=whole(8, 64, 768),
        out_shape=shape((8, 64, 768), BF),
        scratch_shapes=[pltpu.VMEM((64, 768), F32), pltpu.VMEM((128, 128), F32)],
        cost_estimate=about(2),
        compiler_params=PARAMS,
    )(w_down, w_out, w_up, w_qkv, *vectors, units)
    slots = exchange(slots)
    rest, qkv_rows = call(
        regroup_kernel,
        [shape((432, 768), BF), shape((48, 640), BF)],
        (slots, regroup),
        2,
    )
    weights = lax.all_gather(rest, BOTH, axis=0, axis_index_groups=RINGS)
    near = jnp.stack(
        [qkv_rows] + [lax.ppermute(qkv_rows, "batch", along_x(step)) for step in (-1, 2, 1)]
    )
    far = lax.ppermute(near, "batch", SWAP_Z)
    near_other = lax.ppermute(near, "seq", SWAP_CORE)
    far_other = lax.ppermute(far, "seq", SWAP_CORE)
    x = tokens.transpose(1, 0, 2)
    dy = d_out.transpose(1, 0, 2).reshape(256, 768)
    own = exchange(jnp.broadcast_to(x[:, None], (2, 4, 128, 768)).reshape(8, 128, 768))
    x = x.reshape(256, 768)

    normed, wt, gains, q_t, kv = call(
        project_kernel,
        [
            shape((1024, 768), BF), shape((576, 768), BF), shape((8, 768), F32),
            shape((192, 1024), BF), shape((384, 1024), BF),
        ],
        (own, near, far, near_other, far_other, qkv_order),
        5,
        [pltpu.VMEM((768, 640), BF), pltpu.VMEM((640, 768), F32)],
    )
    kv_other = lax.ppermute(kv, "seq", SWAP_CORE)
    o, o_low, lse = call(
        forward_kernel,
        [shape((192, 1024), F32), shape((8, 192, 128), BF), shape((3, 1024), F32)],
        (lengths, q_t, kv, kv_other),
        12,
        [
            pltpu.VMEM((192, 1024), BF), pltpu.VMEM((3, 2048, 64), BF),
            pltpu.VMEM((192, 2048), BF),
        ]
        + [pltpu.VMEM((256, 256), F32)] * 6
        + [pltpu.VMEM((256, 256), BF)] * 6
        + [pltpu.VMEM((64, 256), F32)] * 3
        + [pltpu.VMEM((8, 256), F32)] * 3,
        **scalars(4),
    )
    att = exchange(o_low)
    place, attended, attended_t = call(
        prepare_kernel,
        [shape((768, 768), BF), shape((256, 768), BF), shape((768, 256), BF)],
        (att, order),
        2,
    )
    y, d_first, d_att, d_gain, grads = feed(x, dy, attended, attended_t, gains, place, weights)

    rest_sum = lax.psum_scatter(
        grads.reshape(16 * 432, 768), BOTH, scatter_dimension=0, tiled=True,
        axis_index_groups=RINGS,
    )
    d_att = exchange(d_att)
    dq, dkv, dkv_other = call(
        backward_kernel,
        [shape((192, 1024), BF), shape((384, 1024), BF), shape((384, 1024), BF)],
        (lengths, q_t, kv, kv_other, o, lse, d_att),
        20,
        [
            pltpu.VMEM((192, 1024), BF),
            pltpu.VMEM((3, 2048, 64), BF),
            pltpu.VMEM((192, 2048), BF),
            pltpu.VMEM((3, 2048, 64), BF),
            pltpu.VMEM((192, 1024), BF),
            pltpu.VMEM((3, 64, 2048), F32),
            pltpu.VMEM((3, 64, 2048), F32),
            pltpu.VMEM((3, 1024), F32),
        ]
        + [pltpu.VMEM((256, 256), F32)] * 12
        + [pltpu.VMEM((256, 256), BF)] * 12
        + [pltpu.VMEM((64, 256), F32)] * 3,
        **scalars(7),
    )
    partner = lax.ppermute(dkv_other, "seq", SWAP_CORE)
    part, mine, theirs = call(
        unproject_kernel,
        [shape((8, 128, 768), BF), shape((4, 2, 48, 640), BF), shape((4, 2, 48, 640), BF)],
        (own, dq, dkv, partner, normed, wt, d_gain, qkv_order),
        7,
        [pltpu.VMEM((576, 1024), BF), pltpu.VMEM((640, 768), F32), pltpu.VMEM((768, 640), BF)],
    )
    add = lambda *parts: sum(p.astype(F32) for p in parts).astype(BF)
    line = add(mine, lax.ppermute(theirs, "seq", SWAP_CORE))
    line = add(
        line[0],
        lax.ppermute(line[1], "batch", along_x(1)),
        lax.ppermute(line[2], "batch", along_x(2)),
        lax.ppermute(line[3], "batch", along_x(-1)),
    )
    qkv_sum = add(line[0], lax.ppermute(line[1], "batch", SWAP_Z))
    back = exchange(part)
    d_tokens = call(finish_kernel, shape((256, 768), BF), (x, d_first, gains, back), 3)
    slots = call(
        slots_kernel,
        shape((8, 64, 768), BF),
        (rest_sum, qkv_sum, regroup),
        2,
        [pltpu.VMEM((512, 768), BF)],
    )
    slots = exchange(slots)
    vector = shape((1, 6), F32)
    d_down, d_out_w, d_up, d_qkv, *norms = call(
        sums_kernel,
        [shape((24, 768), F32), shape((6, 768), F32), shape((6, 3072), F32), shape((6, 2304), F32)]
        + [vector] * 4,
        (slots, units),
        2,
    )
    norms = [v.reshape(6) for v in norms]
    output = y.reshape(2, 128, 768).transpose(1, 0, 2)
    d_tokens = d_tokens.reshape(2, 128, 768).transpose(1, 0, 2)
    return (
        output, d_tokens, norms[0], norms[1], d_qkv, d_out_w, norms[2], norms[3], d_up, d_down,
    )


def solution(mesh):
    rows = P(("seq", "batch"))
    tokens = P("seq", "batch", None)
    return jax.shard_map(
        body,
        mesh=mesh,
        in_specs=(tokens, P("batch"), rows, rows, rows, rows, rows, rows, rows, rows, tokens),
        out_specs=(tokens, tokens, rows, rows, rows, rows, rows, rows, rows, rows),
        check_vma=False,
    )
```

time: 236 us -> 224 us (0.949)
  Pallas kernels: 82.2 us -> 64.2 us
  local copies, waits for them, and re-layouts: 21.4 us -> 11.9 us
  starting transfers between devices: 37 us -> 44.3 us
  waiting for transfers between devices: 49.3 us -> 54.8 us
    pallas_call x1, Pallas kernels: 17 us -> 2.14 us  [body(): pl.pallas_call(pack_kernel, grid=(1,), in_specs=[whole(24, 768), whole(6,...]
    unnamed x40 -> x34, local copies, waits for them, and re-layouts: 14 us -> 6.39 us
    all_to_all x1, starting transfers between devices: 3.59 us -> 9.83 us  [body(): back = exchange(part)]
    all_to_all x1, starting transfers between devices: 4.71 us -> 9.45 us  [body(): att = exchange(o_low)]
    ppermute x1, waiting for transfers between devices: 4.21 us -> 7.99 us  [body(): qkv_sum = add(line[0], lax.ppermute(line[1], 'batch', SWAP_Z))]
    pallas_call x9 -> x10, Pallas kernels: 65.2 us -> 62.1 us  [call(): pl.pallas_call(kernel, out_shape=outs, scratch_shapes=list(scratch), cost...]
    another operation x4 -> x0, local copies, waits for them, and re-layouts: 3.02 us -> none  [body(): norms = jnp.stack([gain_one, bias_one, gain_two, bias_two], axis=1)]
    all_to_all x1, starting transfers between devices: 8.84 us -> 6.12 us  [body(): slots = exchange(slots)]
  transfers between devices with their start and end apart: 19 -> 19, of which waited for: 13 -> 13; matrix products, arithmetic and copies ran while one was open for 2% -> 3% of each run, Pallas kernels for 26% -> 18%
where the time goes in v3:
time: 224 us; the launch traced here: 222 us
  Pallas kernels  64.2 us (29%)
  waiting for transfers between devices  54.8 us (24%)
  starting transfers between devices  44.3 us (20%)
  blocking collectives  31.7 us (14%)
  between operations  14.3 us (6%)
  local copies, waits for them, and re-layouts  11.9 us (5%)
    pallas_call x10, Pallas kernels, call(): pl.pallas_call(kernel, out_shape=outs, scratch_shapes=list(scratch), cost...  62.1 us
    all_to_all x1, blocking collectives, body(): slots = exchange(slots)  18.2 us
    all_to_all x1, blocking collectives, body(): d_att = exchange(d_att)  13.5 us
    ppermute x1, waiting for transfers between devices, body(): far = lax.ppermute(near, 'batch', SWAP_Z)  12.3 us
    all_to_all x1, starting transfers between devices, body(): back = exchange(part)  9.83 us
    all_to_all x1, starting transfers between devices, body(): att = exchange(o_low)  9.45 us
    all_to_all x1, waiting for transfers between devices, body(): slots = exchange(slots)  8.31 us
    ppermute x1, waiting for transfers between devices, body(): qkv_sum = add(line[0], lax.ppermute(line[1], 'batch', SWAP_Z))  7.99 us
  transfers between devices with their start and end apart: 19, of which 13 were waited for; matrix products, arithmetic and copies ran while one was open for 3% of the time, Pallas kernels for 18%

profile of v3, /device:TPU:64, one launch (start us, length us, event | category | flops | bytes accessed | tf_op | source)
XLA Modules:
  0.0 222.0 jit_solution(364721785697132922)
XLA Ops:
  7.2 0.0 all-gather.3.cloned.1.call-start
  7.2 2.1 shard_map.222
  9.4 18.2 %all_to_all.30.slots_ref = bf16[8,64,768]{2,1,0:T(8,128)(2,1)} all-to-all(bf16[8,64,768]{2,1,0:T(8,128)(2,1)} %shard_map.222), channel_id=1, replica_groups={{0,16,32,48,64,80,96,112},{8,24,40,56,72,88,104,120},{1,17,33,49,65,81,..., dimensions={0} | all-to-all | bytes 1572864 | tf_op jit(solution)/shard_map/all_to_all | solution.py:649
  27.5 2.7 %shard_map.223 = (bf16[432,768]{1,0:T(8,128)(2,1)}, bf16[48,640]{1,0:T(8,128)(2,1)}) custom-call(bf16[8,64,768]{2,1,0:T(8,128)(2,1)} %all_to_all.30.slots_ref, s32[1,512]{1,0:T(1,128)} %constant.10.clone.order_ref), custom_call_target="tpu_custom_call" | custom-call | flops 2200000000 | tf_op jit(solution)/shard_map/pallas_call | solution.py:81
  30.2 0.0 all-gather.3.cloned.1.call-update
  30.3 0.0 copy-start.2
  30.3 1.3 broadcast_in_dim.2
  31.6 3.7 %all-to-all-start = ((bf16[8,128,768]{2,1,0:T(8,128)(2,1)}), bf16[8,128,768]{2,1,0:T(8,128)(2,1)S(1)}, u32[]{:S(2)}, u32[]{:S(2)}) async-start(bf16[8,128,768]{2,1,0:T(8,128)(2,1)} %bitcast.4), calls=%async_computation | async-start | bytes 3145728 | tf_op jit(solution)/shard_map/all_to_all | solution.py:665
  35.3 1.6 collective-permute-start.2
  36.9 2.7 %collective-permute-start.1 = (bf16[48,640]{1,0:T(8,128)(2,1)S(1)}, bf16[48,640]{1,0:T(8,128)(2,1)S(1)}, u32[]{:S(2)}, u32[]{:S(2)}) collective-permute-start(bf16[48,640]{1,0:T(8,128)(2,1)S(1)} %copy-done.11), channel_id=1, source_target_pairs={{0,2},{1,3},{2,0},{3,1},{4,6},{5,7},{6,4},{7,5},{8,10},{9,11},{10,... | collective-permute-start | bytes 184328 | tf_op jit(solution)/shard_map/ppermute | solution.py:658
  39.6 1.4 collective-permute-start
  41.1 0.0 collective-permute-done.2
  41.1 1.6 collective-permute-done.1
  42.7 1.8 collective-permute-done
  44.5 0.0 copy-start.10
  44.6 0.1 collective-permute-start.3
  44.6 0.1 collective-permute-start.4
  44.7 12.3 %collective-permute-done.3.far_ref = bf16[4,48,640]{2,1,0:T(8,128)(2,1)S(1)} collective-permute-done((bf16[4,48,640]{2,1,0:T(8,128)(2,1)S(1)}, bf16[4,48,640]{2,1,0:T(8,128)(2,1)S(1)}, u32[]{:S(2)}, u32[]{:S(2)}) %collective-permute-start.3) | collective-permute-done | bytes 245792 | tf_op jit(solution)/shard_map/ppermute | solution.py:660
  57.0 1.5 collective-permute-done.5.far_other_ref
  58.5 0.0 all-to-all-done.own_ref
  58.6 0.7 copy-done.16
  59.3 1.2 copy-done
  60.5 5.6 %shard_map.224 = (bf16[1024,768]{1,0:T(8,128)(2,1)}, bf16[576,768]{1,0:T(8,128)(2,1)}, f32[8,768]{1,0:T(8,128)}, bf16[192,1024]{1,0:T(8,128)(2,1)}, bf16[384,1024]{1,0:T(8,128)(2,1)}) custom-call(bf16[8,128,768]{2,1,0:T(8,128)(2,1)} %copy-done, bf16[4,48,640]{2,1,0:T(8,128)(2,1)} %copy-done.10, bf16[4,48,640]{2,1,0:T(8,128)(2,1)} %copy-done.14, ...), custom_call_target="tpu_custom_call" | custom-call | flops 5500000256 | tf_op jit(solution)/shard_map/pallas_call | solution.py:81
  66.1 0.1 collective-permute-start.6
  66.2 2.4 %collective-permute-done.6.other_ref = bf16[384,1024]{1,0:T(8,128)(2,1)S(1)} collective-permute-done((bf16[384,1024]{1,0:T(8,128)(2,1)}, bf16[384,1024]{1,0:T(8,128)(2,1)S(1)}, u32[]{:S(2)}, u32[]{:S(2)}) %collective-permute-start.6) | collective-permute-done | bytes 786464 | tf_op jit(solution)/shard_map/ppermute | solution.py:678
  68.7 0.9 copy-done.12
  69.6 7.3 %shard_map.225 = (f32[192,1024]{1,0:T(8,128)}, bf16[8,192,128]{2,1,0:T(8,128)(2,1)}, f32[3,1024]{1,0:T(4,128)}) custom-call(s32[2]{0:T(128)} %lengths_ref.3, bf16[192,1024]{1,0:T(8,128)(2,1)} %get-tuple-element.43.q_ref, bf16[384,1024]{1,0:T(8,128)(2,1)} %get-tuple-element.44.own_ref, bf16[384,1024]{1,0:T(8,128)(2,1)} %copy-done.12), custom_call_target="tpu_custom_call" | custom-call | flops 13200000000 | tf_op jit(solution)/shard_map/pallas_call | solution.py:81
  76.9 9.5 %all-to-all-start.2 = ((bf16[8,192,128]{2,1,0:T(8,128)(2,1)}), bf16[8,192,128]{2,1,0:T(8,128)(2,1)S(1)}, u32[]{:S(2)}, u32[]{:S(2)}) async-start(bf16[8,192,128]{2,1,0:T(8,128)(2,1)} %get-tuple-element.45), calls=%async_computation.2 | async-start | bytes 786432 | tf_op jit(solution)/shard_map/all_to_all | solution.py:694
  86.3 0.2 reduce-scatter.2.cloned.1.call-start
  86.6 0.8 copy.26
  87.3 7.4 %all-to-all-done.2.att_ref = bf16[8,192,128]{2,1,0:T(8,128)(2,1)S(1)} async-done(((bf16[8,192,128]{2,1,0:T(8,128)(2,1)}), bf16[8,192,128]{2,1,0:T(8,128)(2,1)S(1)}, u32[]{:S(2)}, u32[]{:S(2)}) %all-to-all-start.2) | async-done | bytes 393248 | tf_op jit(solution)/shard_map/all_to_all | solution.py:694
  94.7 0.7 copy-done.9
  95.5 2.8 %shard_map.226 = (bf16[768,768]{1,0:T(8,128)(2,1)}, bf16[256,768]{1,0:T(8,128)(2,1)}, bf16[768,256]{1,0:T(8,128)(2,1)}) custom-call(bf16[8,192,128]{2,1,0:T(8,128)(2,1)} %copy-done.9, s32[1,768]{1,0:T(1,128)} %constant.8.clone.order_ref), custom_call_target="tpu_custom_call" | custom-call | flops 2200000000 | tf_op jit(solution)/shard_map/pallas_call | solution.py:81
  98.2 16.4 %shard_map.227 = (bf16[256,768]{1,0:T(8,128)(2,1)}, f32[256,768]{1,0:T(8,128)}, bf16[8,192,128]{2,1,0:T(8,128)(2,1)}, f32[8,768]{1,0:T(8,128)}, bf16[16,432,768]{2,1,0:T(8,128)(2,1)}) custom-call(bf16[256,768]{1,0:T(8,128)(2,1)} %bitcast.46, bf16[256,768]{1,0:T(8,128)(2,1)} %bitcast.53, bf16[256,768]{1,0:T(8,128)(2,1)} %get-tuple-element.46.att_hbm, ...), custom_call_target="tpu_custom_call" | custom-call | flops 18699999232 | tf_op jit(solution)/shard_map/pallas_call | solution.py:81
  114.6 0.0 reduce-scatter.2.cloned.1.call-update
  114.7 1.0 copy-done.8
  115.6 13.5 %all_to_all.31.da_ref = bf16[8,192,128]{2,1,0:T(8,128)(2,1)} all-to-all(bf16[8,192,128]{2,1,0:T(8,128)(2,1)S(1)} %copy-done.8), channel_id=1, replica_groups={{0,16,32,48,64,80,96,112},{8,24,40,56,72,88,104,120},{1,17,33,49,65,81,..., dimensions={0} | all-to-all | bytes 786432 | tf_op jit(solution)/shard_map/all_to_all | solution.py:707
  129.2 10.9 %shard_map.228 = (bf16[192,1024]{1,0:T(8,128)(2,1)}, bf16[384,1024]{1,0:T(8,128)(2,1)}, bf16[384,1024]{1,0:T(8,128)(2,1)}) custom-call(s32[2]{0:T(128)} %lengths_ref.3, bf16[192,1024]{1,0:T(8,128)(2,1)} %get-tuple-element.43.q_ref, bf16[384,1024]{1,0:T(8,128)(2,1)} %get-tuple-element.44.own_ref, bf16[384,1024]{1,0:T(8,128)(2,1)} %copy-done.12, ...), custom_call_target="tpu_custom_call" | custom-call | flops 22000001024 | tf_op jit(solution)/shard_map/pallas_call | solution.py:81
  140.1 1.5 collective-permute-start.7
  141.6 2.4 %collective-permute-done.7.partner_ref = bf16[384,1024]{1,0:T(8,128)(2,1)S(1)} collective-permute-done((bf16[384,1024]{1,0:T(8,128)(2,1)}, bf16[384,1024]{1,0:T(8,128)(2,1)S(1)}, u32[]{:S(2)}, u32[]{:S(2)}) %collective-permute-start.7) | collective-permute-done | bytes 786464 | tf_op jit(solution)/shard_map/ppermute | solution.py:728
  143.9 1.0 copy-done.13
  144.9 7.6 %shard_map.229 = (bf16[8,128,768]{2,1,0:T(8,128)(2,1)}, bf16[4,2,48,640]{3,2,1,0:T(8,128)(2,1)}, bf16[4,2,48,640]{3,2,1,0:T(8,128)(2,1)}) custom-call(bf16[8,128,768]{2,1,0:T(8,128)(2,1)} %copy-done, bf16[192,1024]{1,0:T(8,128)(2,1)} %get-tuple-element.56.dq_ref, bf16[384,1024]{1,0:T(8,128)(2,1)} %get-tuple-element.57.dkv_ref, bf16[384,1024]{1,0:T(8,128)(2,1)} %copy-done.13, ...), custom_call_target="tpu_custom_call" | custom-call | flops 7699999744 | tf_op jit(solution)/shard_map/pallas_call | solution.py:81
  152.5 0.4 collective-permute-start.8
  152.9 9.8 %all-to-all-start.4 = ((bf16[8,128,768]{2,1,0:T(8,128)(2,1)}), bf16[8,128,768]{2,1,0:T(8,128)(2,1)S(1)}, u32[]{:S(2)}, u32[]{:S(2)}) async-start(bf16[8,128,768]{2,1,0:T(8,128)(2,1)} %get-tuple-element.62), calls=%async_computation.4 | async-start | bytes 3145728 | tf_op jit(solution)/shard_map/all_to_all | solution.py:745
  162.7 0.1 add_convert_fusion
  162.9 2.0 collective-permute-start.9
  164.9 1.4 collective-permute-start.11
  166.3 2.2 collective-permute-start.10
  168.5 1.6 collective-permute-done.9
  170.0 2.4 %collective-permute-done.11 = bf16[2,48,640]{2,1,0:T(8,128)(2,1)S(1)} collective-permute-done((bf16[2,48,640]{2,1,0:T(8,128)(2,1)S(1)}, bf16[2,48,640]{2,1,0:T(8,128)(2,1)S(1)}, u32[]{:S(2)}, u32[]{:S(2)}) %collective-permute-start.11) | collective-permute-done | bytes 122912 | tf_op jit(solution)/shard_map/ppermute | solution.py:742
  172.4 4.4 %collective-permute-done.10 = bf16[2,48,640]{2,1,0:T(8,128)(2,1)S(1)} collective-permute-done((bf16[2,48,640]{2,1,0:T(8,128)(2,1)S(1)}, bf16[2,48,640]{2,1,0:T(8,128)(2,1)S(1)}, u32[]{:S(2)}, u32[]{:S(2)}) %collective-permute-start.10) | collective-permute-done | bytes 122912 | tf_op jit(solution)/shard_map/ppermute | solution.py:741
  176.8 0.1 fusion.2
  176.9 1.5 collective-permute-start.12
  178.4 8.0 %collective-permute-done.12 = bf16[48,640]{1,0:T(8,128)(2,1)S(1)} collective-permute-done((bf16[48,640]{1,0:T(8,128)(2,1)S(1)}, bf16[48,640]{1,0:T(8,128)(2,1)S(1)}, u32[]{:S(2)}, u32[]{:S(2)}) %collective-permute-start.12) | collective-permute-done | bytes 61472 | tf_op jit(solution)/shard_map/ppermute | solution.py:744
  186.4 0.6 fusion.3.qkv_ref
  187.0 0.7 reduce-scatter.2.cloned.1.call-done.rest_ref
  187.8 2.6 %shard_map.231 = bf16[8,64,768]{2,1,0:T(8,128)(2,1)} custom-call(bf16[432,768]{1,0:T(8,128)(2,1)} %reduce-scatter.2.cloned.1.call-done.rest_ref, bf16[48,640]{1,0:T(8,128)(2,1)} %fusion.3.qkv_ref, s32[1,512]{1,0:T(1,128)} %constant.10.clone.order_ref), custom_call_target="tpu_custom_call" | custom-call | flops 2200000000 | tf_op jit(solution)/shard_map/pallas_call | solution.py:81
  190.4 6.1 %all-to-all-start.5 = ((bf16[8,64,768]{2,1,0:T(8,128)(2,1)}), bf16[8,64,768]{2,1,0:T(8,128)(2,1)S(1)}, u32[]{:S(2)}, u32[]{:S(2)}) async-start(bf16[8,64,768]{2,1,0:T(8,128)(2,1)} %shard_map.231), calls=%async_computation.6 | async-start | bytes 1572864 | tf_op jit(solution)/shard_map/all_to_all | solution.py:754
  196.5 1.2 copy.33
  197.7 3.2 %shard_map.230 = bf16[256,768]{1,0:T(8,128)(2,1)} custom-call(bf16[256,768]{1,0:T(8,128)(2,1)} %bitcast.47, f32[256,768]{1,0:T(8,128)} %get-tuple-element.52.dfirst_ref, f32[8,768]{1,0:T(8,128)} %get-tuple-element.48.gains_hbm.gains_ref, bf16[8,128,768]{2,1,0:T(8,128)(2,1)} %copy-done.1), custom_call_target="tpu_custom_call" | custom-call | flops 3300000000 | tf_op jit(solution)/shard_map/pallas_call | solution.py:81
  200.8 2.1 copy.32
  203.0 8.3 %all-to-all-done.5.got_ref = bf16[8,64,768]{2,1,0:T(8,128)(2,1)S(1)} async-done(((bf16[8,64,768]{2,1,0:T(8,128)(2,1)}), bf16[8,64,768]{2,1,0:T(8,128)(2,1)S(1)}, u32[]{:S(2)}, u32[]{:S(2)}) %all-to-all-start.5) | async-done | bytes 786464 | tf_op jit(solution)/shard_map/all_to_all | solution.py:754
  211.3 0.9 copy-done.3
  212.2 3.0 %shard_map.232 = (f32[24,768]{1,0:T(8,128)}, f32[6,768]{1,0:T(8,128)}, f32[6,3072]{1,0:T(8,128)}, f32[6,2304]{1,0:T(8,128)}, f32[1,6]{1,0:T(1,128)}, /*index=5*/...) custom-call(bf16[8,64,768]{2,1,0:T(8,128)(2,1)} %copy-done.3, s32[1,768]{1,0:T(1,128)} %constant.9.clone.units_ref), custom_call_target="tpu_custom_call" | custom-call | flops 2200000000 | tf_op jit(solution)/shard_map/pallas_call | solution.py:81
  (34 shorter events, 0.2 us)
Async XLA Ops:
  7.2 91.1 %all-gather.3.cloned.1.call-start = ((), (), s32[]{:S(2)}) async-start(), calls=%async_computation.8 | async-start | bytes 11280384 | tf_op jit(solution)/shard_map/all_gather | solution.py:656
  27.5 2.7 %copy-start.5 = (bf16[128,2,768]{2,1,0:T(2,128)(2,1)S(1)}, bf16[128,2,768]{2,1,0:T(2,128)(2,1)}, u32[]{:S(2)}) copy-start(bf16[128,2,768]{2,1,0:T(2,128)(2,1)} %param.15) | copy-start | bytes 1179652
  30.3 1.3 copy-start.2
  31.6 3.7 %copy-start.11 = (bf16[48,640]{1,0:T(8,128)(2,1)S(1)}, bf16[48,640]{1,0:T(8,128)(2,1)}, u32[]{:S(2)}) copy-start(bf16[48,640]{1,0:T(8,128)(2,1)} %get-tuple-element.42) | copy-start | bytes 184324
  31.6 26.9 %all-to-all-start = ((bf16[8,128,768]{2,1,0:T(8,128)(2,1)}), bf16[8,128,768]{2,1,0:T(8,128)(2,1)S(1)}, u32[]{:S(2)}, u32[]{:S(2)}) async-start(bf16[8,128,768]{2,1,0:T(8,128)(2,1)} %bitcast.4), calls=%async_computation | async-start | bytes 3145728 | tf_op jit(solution)/shard_map/all_to_all | solution.py:665
  35.3 5.7 %collective-permute-start.2 = (bf16[48,640]{1,0:T(8,128)(2,1)S(1)}, bf16[48,640]{1,0:T(8,128)(2,1)S(1)}, u32[]{:S(2)}, u32[]{:S(2)}) collective-permute-start(bf16[48,640]{1,0:T(8,128)(2,1)S(1)} %copy-done.11), channel_id=1, source_target_pairs={{0,1},{1,2},{2,3},{3,0},{4,5},{5,6},{6,7},{7,4},{8,9},{9,10},{10,1... | collective-permute-start | bytes 184328 | tf_op jit(solution)/shard_map/ppermute | solution.py:658
  36.9 5.8 %collective-permute-start.1 = (bf16[48,640]{1,0:T(8,128)(2,1)S(1)}, bf16[48,640]{1,0:T(8,128)(2,1)S(1)}, u32[]{:S(2)}, u32[]{:S(2)}) collective-permute-start(bf16[48,640]{1,0:T(8,128)(2,1)S(1)} %copy-done.11), channel_id=1, source_target_pairs={{0,2},{1,3},{2,0},{3,1},{4,6},{5,7},{6,4},{7,5},{8,10},{9,11},{10,... | collective-permute-start | bytes 184328 | tf_op jit(solution)/shard_map/ppermute | solution.py:658
  39.6 4.9 %collective-permute-start = (bf16[48,640]{1,0:T(8,128)(2,1)S(1)}, bf16[48,640]{1,0:T(8,128)(2,1)S(1)}, u32[]{:S(2)}, u32[]{:S(2)}) collective-permute-start(bf16[48,640]{1,0:T(8,128)(2,1)S(1)} %copy-done.11), channel_id=1, source_target_pairs={{0,3},{1,0},{2,1},{3,2},{4,7},{5,4},{6,5},{7,6},{8,11},{9,8},{10,9... | collective-permute-start | bytes 184328 | tf_op jit(solution)/shard_map/ppermute | solution.py:658
  44.5 14.0 %copy-start.10 = (bf16[4,48,640]{2,1,0:T(8,128)(2,1)}, bf16[4,48,640]{2,1,0:T(8,128)(2,1)S(1)}, u32[]{:S(2)}) copy-start(bf16[4,48,640]{2,1,0:T(8,128)(2,1)S(1)} %pad_maximum_fusion.near_ref) | copy-start | bytes 737284
  44.6 12.5 %collective-permute-start.3 = (bf16[4,48,640]{2,1,0:T(8,128)(2,1)S(1)}, bf16[4,48,640]{2,1,0:T(8,128)(2,1)S(1)}, u32[]{:S(2)}, u32[]{:S(2)}) collective-permute-start(bf16[4,48,640]{2,1,0:T(8,128)(2,1)S(1)} %pad_maximum_fusion.near_ref), channel_id=1, source_target_pairs={{0,4},{1,5},{2,6},{3,7},{4,0},{5,1},{6,2},{7,3},{8,12},{9,13},{10,... | collective-permute-start | bytes 737288 | tf_op jit(solution)/shard_map/ppermute | solution.py:660
  44.6 12.4 %collective-permute-start.4 = (bf16[4,48,640]{2,1,0:T(8,128)(2,1)S(1)}, bf16[4,48,640]{2,1,0:T(8,128)(2,1)S(1)}, u32[]{:S(2)}, u32[]{:S(2)}) collective-permute-start(bf16[4,48,640]{2,1,0:T(8,128)(2,1)S(1)} %pad_maximum_fusion.near_ref), channel_id=1, source_target_pairs={{0,8},{8,0},{16,24},{24,16},{32,40},{40,32},{48,56},{56,48},{64,72... | collective-permute-start | bytes 737288 | tf_op jit(solution)/shard_map/ppermute | solution.py:661
  57.0 1.5 copy-start.14
  57.0 1.5 collective-permute-start.5
  57.0 1.5 copy-start.15
  58.5 0.7 copy-start.16
  59.3 1.2 copy-start
  66.1 2.6 %collective-permute-start.6 = (bf16[384,1024]{1,0:T(8,128)(2,1)}, bf16[384,1024]{1,0:T(8,128)(2,1)S(1)}, u32[]{:S(2)}, u32[]{:S(2)}) collective-permute-start(bf16[384,1024]{1,0:T(8,128)(2,1)} %get-tuple-element.44.own_ref), channel_id=1, source_target_pairs={{0,8},{8,0},{16,24},{24,16},{32,40},{40,32},{48,56},{56,48},{64,72... | collective-permute-start | bytes 2359304 | tf_op jit(solution)/shard_map/ppermute | solution.py:678
  68.7 0.9 copy-start.12
  69.6 17.0 %copy-start.6 = (bf16[128,2,768]{2,1,0:T(2,128)(2,1)S(1)}, bf16[128,2,768]{2,1,0:T(2,128)(2,1)}, u32[]{:S(2)}) copy-start(bf16[128,2,768]{2,1,0:T(2,128)(2,1)} %param.25) | copy-start | bytes 1179652
  76.9 17.9 %all-to-all-start.2 = ((bf16[8,192,128]{2,1,0:T(8,128)(2,1)}), bf16[8,192,128]{2,1,0:T(8,128)(2,1)S(1)}, u32[]{:S(2)}, u32[]{:S(2)}) async-start(bf16[8,192,128]{2,1,0:T(8,128)(2,1)} %get-tuple-element.45), calls=%async_computation.2 | async-start | bytes 786432 | tf_op jit(solution)/shard_map/all_to_all | solution.py:694
  86.3 101.4 %reduce-scatter.2.cloned.1.call-start = ((), (), s32[]{:S(2)}) async-start(), calls=%async_computation.7 | async-start | bytes 11280384 | tf_op jit(solution)/shard_map/reduce_scatter | solution.py:703
  94.7 0.7 copy-start.9
  114.6 1.0 copy-start.8
  140.1 3.8 %collective-permute-start.7 = (bf16[384,1024]{1,0:T(8,128)(2,1)}, bf16[384,1024]{1,0:T(8,128)(2,1)S(1)}, u32[]{:S(2)}, u32[]{:S(2)}) collective-permute-start(bf16[384,1024]{1,0:T(8,128)(2,1)} %get-tuple-element.58), channel_id=1, source_target_pairs={{0,8},{8,0},{16,24},{24,16},{32,40},{40,32},{48,56},{56,48},{64,72... | collective-permute-start | bytes 2359304 | tf_op jit(solution)/shard_map/ppermute | solution.py:728
  143.9 1.0 copy-start.13
  152.5 10.2 %collective-permute-start.8 = (bf16[4,2,48,640]{3,2,1,0:T(8,128)(2,1)}, bf16[4,2,48,640]{3,2,1,0:T(8,128)(2,1)S(1)}, u32[]{:S(2)}, u32[]{:S(2)}) collective-permute-start(bf16[4,2,48,640]{3,2,1,0:T(8,128)(2,1)} %get-tuple-element.65), channel_id=1, source_target_pairs={{0,8},{8,0},{16,24},{24,16},{32,40},{40,32},{48,56},{56,48},{64,72... | collective-permute-start | bytes 1474568 | tf_op jit(solution)/shard_map/ppermute | solution.py:737
  152.9 9.8 %copy-start.4 = (bf16[4,2,48,640]{3,2,1,0:T(8,128)(2,1)S(1)}, bf16[4,2,48,640]{3,2,1,0:T(8,128)(2,1)}, u32[]{:S(2)}) copy-start(bf16[4,2,48,640]{3,2,1,0:T(8,128)(2,1)} %get-tuple-element.64) | copy-start | bytes 1474564
  152.9 37.5 %all-to-all-start.4 = ((bf16[8,128,768]{2,1,0:T(8,128)(2,1)}), bf16[8,128,768]{2,1,0:T(8,128)(2,1)S(1)}, u32[]{:S(2)}, u32[]{:S(2)}) async-start(bf16[8,128,768]{2,1,0:T(8,128)(2,1)} %get-tuple-element.62), calls=%async_computation.4 | async-start | bytes 3145728 | tf_op jit(solution)/shard_map/all_to_all | solution.py:745
  162.9 7.1 %collective-permute-start.9 = (bf16[2,48,640]{2,1,0:T(8,128)(2,1)S(1)}, bf16[2,48,640]{2,1,0:T(8,128)(2,1)S(1)}, u32[]{:S(2)}, u32[]{:S(2)}) collective-permute-start(bf16[2,48,640]{2,1,0:T(8,128)(2,1)S(1)} %get-tuple-element.74), channel_id=1, source_target_pairs={{0,1},{1,2},{2,3},{3,0},{4,5},{5,6},{6,7},{7,4},{8,9},{9,10},{10,1... | collective-permute-start | bytes 368648 | tf_op jit(solution)/shard_map/ppermute | solution.py:740
  164.9 7.5 %collective-permute-start.11 = (bf16[2,48,640]{2,1,0:T(8,128)(2,1)S(1)}, bf16[2,48,640]{2,1,0:T(8,128)(2,1)S(1)}, u32[]{:S(2)}, u32[]{:S(2)}) collective-permute-start(bf16[2,48,640]{2,1,0:T(8,128)(2,1)S(1)} %get-tuple-element.75), channel_id=1, source_target_pairs={{0,3},{1,0},{2,1},{3,2},{4,7},{5,4},{6,5},{7,6},{8,11},{9,8},{10,9... | collective-permute-start | bytes 368648 | tf_op jit(solution)/shard_map/ppermute | solution.py:742
  166.3 10.6 %collective-permute-start.10 = (bf16[2,48,640]{2,1,0:T(8,128)(2,1)S(1)}, bf16[2,48,640]{2,1,0:T(8,128)(2,1)S(1)}, u32[]{:S(2)}, u32[]{:S(2)}) collective-permute-start(bf16[2,48,640]{2,1,0:T(8,128)(2,1)S(1)} %get-tuple-element.76), channel_id=1, source_target_pairs={{0,2},{1,3},{2,0},{3,1},{4,6},{5,7},{6,4},{7,5},{8,10},{9,11},{10,... | collective-permute-start | bytes 368648 | tf_op jit(solution)/shard_map/ppermute | solution.py:741
  176.9 9.5 %collective-permute-start.12 = (bf16[48,640]{1,0:T(8,128)(2,1)S(1)}, bf16[48,640]{1,0:T(8,128)(2,1)S(1)}, u32[]{:S(2)}, u32[]{:S(2)}) collective-permute-start(bf16[48,640]{1,0:T(8,128)(2,1)S(1)} %slice_bitcast_fusion.4), channel_id=1, source_target_pairs={{0,4},{1,5},{2,6},{3,7},{4,0},{5,1},{6,2},{7,3},{8,12},{9,13},{10,... | collective-permute-start | bytes 184328 | tf_op jit(solution)/shard_map/ppermute | solution.py:744
  190.4 6.1 %copy-start.7 = (bf16[256,768]{1,0:T(8,128)(2,1)S(1)}, bf16[256,768]{1,0:T(8,128)(2,1)}, u32[]{:S(2)}) copy-start(bf16[256,768]{1,0:T(8,128)(2,1)} %get-tuple-element.51) | copy-start | bytes 1179652
  190.4 7.3 %copy-start.1 = (bf16[8,128,768]{2,1,0:T(8,128)(2,1)}, bf16[8,128,768]{2,1,0:T(8,128)(2,1)S(1)}, u32[]{:S(2)}) copy-start(bf16[8,128,768]{2,1,0:T(8,128)(2,1)S(1)} %all-to-all-done.4.got_ref) | copy-start | bytes 4718596
  190.4 20.9 %all-to-all-start.5 = ((bf16[8,64,768]{2,1,0:T(8,128)(2,1)}), bf16[8,64,768]{2,1,0:T(8,128)(2,1)S(1)}, u32[]{:S(2)}, u32[]{:S(2)}) async-start(bf16[8,64,768]{2,1,0:T(8,128)(2,1)} %shard_map.231), calls=%async_computation.6 | async-start | bytes 1572864 | tf_op jit(solution)/shard_map/all_to_all | solution.py:754
  211.3 0.9 copy-start.3
Sparse Core Ops, SparseCore 0:
  30.3 67.0 all-gather.2
  114.8 72.9 reduce-scatter.1

commit v4 on v3

--- a/solution.py
+++ b/solution.py
@@ -74,16 +74,13 @@
     return pl.CostEstimate(flops=int(us * 1.1e9), bytes_accessed=0, transcendentals=0)
 
 
-PARAMS = pltpu.CompilerParams(vmem_limit_bytes=60 * 1024 * 1024)
-
-
-def call(kernel, outs, ins, us, scratch=(), **kwargs):
+def call(kernel, outs, ins, us, scratch=(), mib=60, **kwargs):
     return pl.pallas_call(
         kernel,
         out_shape=outs,
         scratch_shapes=list(scratch),
         cost_estimate=about(us),
-        compiler_params=PARAMS,
+        compiler_params=pltpu.CompilerParams(vmem_limit_bytes=mib * 1024 * 1024),
         **kwargs,
     )(*ins)
 
@@ -644,7 +641,7 @@
         out_shape=shape((8, 64, 768), BF),
         scratch_shapes=[pltpu.VMEM((64, 768), F32), pltpu.VMEM((128, 128), F32)],
         cost_estimate=about(2),
-        compiler_params=PARAMS,
+        compiler_params=pltpu.CompilerParams(vmem_limit_bytes=60 * 1024 * 1024),
     )(w_down, w_out, w_up, w_qkv, *vectors, units)
     slots = exchange(slots)
     rest, qkv_rows = call(
@@ -652,6 +649,7 @@
         [shape((432, 768), BF), shape((48, 640), BF)],
         (slots, regroup),
         2,
+        mib=12,
     )
     weights = lax.all_gather(rest, BOTH, axis=0, axis_index_groups=RINGS)
     near = jnp.stack(
@@ -674,6 +672,7 @@
         (own, near, far, near_other, far_other, qkv_order),
         5,
         [pltpu.VMEM((768, 640), BF), pltpu.VMEM((640, 768), F32)],
+        mib=30,
     )
     kv_other = lax.ppermute(kv, "seq", SWAP_CORE)
     o, o_low, lse = call(
@@ -689,6 +688,7 @@
         + [pltpu.VMEM((256, 256), BF)] * 6
         + [pltpu.VMEM((64, 256), F32)] * 3
         + [pltpu.VMEM((8, 256), F32)] * 3,
+        mib=30,
         **scalars(4),
     )
     att = exchange(o_low)
@@ -697,6 +697,7 @@
         [shape((768, 768), BF), shape((256, 768), BF), shape((768, 256), BF)],
         (att, order),
         2,
+        mib=16,
     )
     y, d_first, d_att, d_gain, grads = feed(x, dy, attended, attended_t, gains, place, weights)
 
@@ -723,6 +724,7 @@
         + [pltpu.VMEM((256, 256), F32)] * 12
         + [pltpu.VMEM((256, 256), BF)] * 12
         + [pltpu.VMEM((64, 256), F32)] * 3,
+        mib=36,
         **scalars(7),
     )
     partner = lax.ppermute(dkv_other, "seq", SWAP_CORE)
@@ -732,6 +734,7 @@
         (own, dq, dkv, partner, normed, wt, d_gain, qkv_order),
         7,
         [pltpu.VMEM((576, 1024), BF), pltpu.VMEM((640, 768), F32), pltpu.VMEM((768, 640), BF)],
+        mib=30,
     )
     add = lambda *parts: sum(p.astype(F32) for p in parts).astype(BF)
     line = add(mine, lax.ppermute(theirs, "seq", SWAP_CORE))
@@ -743,13 +746,14 @@
     )
     qkv_sum = add(line[0], lax.ppermute(line[1], "batch", SWAP_Z))
     back = exchange(part)
-    d_tokens = call(finish_kernel, shape((256, 768), BF), (x, d_first, gains, back), 3)
+    d_tokens = call(finish_kernel, shape((256, 768), BF), (x, d_first, gains, back), 3, mib=16)
     slots = call(
         slots_kernel,
         shape((8, 64, 768), BF),
         (rest_sum, qkv_sum, regroup),
         2,
         [pltpu.VMEM((512, 768), BF)],
+        mib=12,
     )
     slots = exchange(slots)
     vector = shape((1, 6), F32)
@@ -759,6 +763,7 @@
         + [vector] * 4,
         (slots, units),
         2,
+        mib=12,
     )
     norms = [v.reshape(6) for v in norms]
     output = y.reshape(2, 128, 768).transpose(1, 0, 2)

time: 224 us -> 220 us (0.982)
  Pallas kernels: 64.2 us -> 53.1 us
  waiting for transfers between devices: 54.8 us -> 65 us
  starting transfers between devices: 44.3 us -> 34.1 us
  local copies, waits for them, and re-layouts: 11.9 us -> 17.1 us
    pallas_call x10, Pallas kernels: 62.1 us -> 50.9 us  [call(): pl.pallas_call(kernel, out_shape=outs, scratch_shapes=list(scratch), cost...]
    reduce_scatter x1, waiting for transfers between devices: 0.72 us -> 7.39 us  [body(): lax.psum_scatter(grads.reshape(16 * 432, 768), BOTH, scatter_dimension=0,...]
    all_to_all x1, starting transfers between devices: 9.83 us -> 3.59 us  [body(): back = exchange(part)]
    all_gather x1, waiting for transfers between devices: 0.01 us -> 4.8 us  [body(): weights = lax.all_gather(rest, BOTH, axis=0, axis_index_groups=RINGS)]
    all_to_all x1, starting transfers between devices: 9.45 us -> 4.66 us  [body(): att = exchange(o_low)]
    ppermute x1, starting transfers between devices: 1.4 us -> 5.89 us  [body(): lax.ppermute(line[3], 'batch', along_x(-1))]
    unnamed x34 -> x52, local copies, waits for them, and re-layouts: 6.39 us -> 10.6 us
    ppermute x1, waiting for transfers between devices: 4.44 us -> 6.9 us  [body(): lax.ppermute(line[2], 'batch', along_x(2))]
  transfers between devices with their start and end apart: 19 -> 19, of which waited for: 13 -> 13; matrix products, arithmetic and copies ran while one was open for 3% -> 3% of each run, Pallas kernels for 18% -> 14%
where the time goes in v4:
time: 220 us; the launch traced here: 217 us
  waiting for transfers between devices  65 us (30%)
  Pallas kernels  53.1 us (24%)
  starting transfers between devices  34.1 us (16%)
  blocking collectives  33 us (15%)
  local copies, waits for them, and re-layouts  17.1 us (8%)
  between operations  14.3 us (6%)
    pallas_call x10, Pallas kernels, call(): pl.pallas_call(kernel, out_shape=outs, scratch_shapes=list(scratch), cost...  50.9 us
    all_to_all x1, blocking collectives, body(): slots = exchange(slots)  18.2 us
    all_to_all x1, blocking collectives, body(): d_att = exchange(d_att)  14.8 us
    ppermute x1, waiting for transfers between devices, body(): far = lax.ppermute(near, 'batch', SWAP_Z)  12.3 us
    unnamed x52, local copies, waits for them, and re-layouts  10.6 us
    all_to_all x1, waiting for transfers between devices, body(): slots = exchange(slots)  8.74 us
    reduce_scatter x1, waiting for transfers between devices, body(): lax.psum_scatter(grads.reshape(16 * 432, 768), BOTH, scatter_dimension=0,...  7.39 us
    ppermute x1, waiting for transfers between devices, body(): qkv_sum = add(line[0], lax.ppermute(line[1], 'batch', SWAP_Z))  7.31 us
  transfers between devices with their start and end apart: 19, of which 13 were waited for; matrix products, arithmetic and copies ran while one was open for 3% of the time, Pallas kernels for 14%

profile of v4, /device:TPU:64, one launch (start us, length us, event | category | flops | bytes accessed | tf_op | source)
XLA Modules:
  0.0 216.8 jit_solution(6622939058335765009)
XLA Ops:
  7.2 0.0 all-gather.3.cloned.1.call-start
  7.2 2.2 shard_map.222
  9.4 18.2 %all_to_all.30.slots_ref = bf16[8,64,768]{2,1,0:T(8,128)(2,1)S(1)} all-to-all(bf16[8,64,768]{2,1,0:T(8,128)(2,1)} %shard_map.222), channel_id=1, replica_groups={{0,16,32,48,64,80,96,112},{8,24,40,56,72,88,104,120},{1,17,33,49,65,81,..., dimensions={0} | all-to-all | bytes 1572864 | tf_op jit(solution)/shard_map/all_to_all | solution.py:646
  27.6 1.5 shard_map.223
  29.1 0.0 all-gather.3.cloned.1.call-update
  29.2 1.3 broadcast_in_dim.2
  30.5 3.7 %all-to-all-start = ((bf16[8,128,768]{2,1,0:T(8,128)(2,1)}), bf16[8,128,768]{2,1,0:T(8,128)(2,1)S(1)}, u32[]{:S(2)}, u32[]{:S(2)}) async-start(bf16[8,128,768]{2,1,0:T(8,128)(2,1)} %bitcast.50), calls=%async_computation | async-start | bytes 3145728 | tf_op jit(solution)/shard_map/all_to_all | solution.py:663
  34.2 1.6 collective-permute-start.2
  35.8 2.7 %collective-permute-start.1 = (bf16[48,640]{1,0:T(8,128)(2,1)S(1)}, bf16[48,640]{1,0:T(8,128)(2,1)S(1)}, u32[]{:S(2)}, u32[]{:S(2)}) collective-permute-start(bf16[48,640]{1,0:T(8,128)(2,1)S(1)} %get-tuple-element.42), channel_id=1, source_target_pairs={{0,2},{1,3},{2,0},{3,1},{4,6},{5,7},{6,4},{7,5},{8,10},{9,11},{10,... | collective-permute-start | bytes 184328 | tf_op jit(solution)/shard_map/ppermute | solution.py:656
  38.5 1.4 collective-permute-start
  39.9 1.6 collective-permute-done.1
  41.6 1.8 collective-permute-done
  43.4 0.1 collective-permute-start.3
  43.5 0.1 collective-permute-start.4
  43.6 12.3 %collective-permute-done.3.far_ref = bf16[4,48,640]{2,1,0:T(8,128)(2,1)S(1)} collective-permute-done((bf16[4,48,640]{2,1,0:T(8,128)(2,1)S(1)}, bf16[4,48,640]{2,1,0:T(8,128)(2,1)S(1)}, u32[]{:S(2)}, u32[]{:S(2)}) %collective-permute-start.3) | collective-permute-done | bytes 245792 | tf_op jit(solution)/shard_map/ppermute | solution.py:658
  55.9 1.5 collective-permute-done.5.far_other_ref
  57.4 3.0 %shard_map.224 = (bf16[1024,768]{1,0:T(8,128)(2,1)S(1)}, bf16[576,768]{1,0:T(8,128)(2,1)S(1)}, f32[8,768]{1,0:T(8,128)S(1)}, bf16[192,1024]{1,0:T(8,128)(2,1)S(1)}, bf16[384,1024]{1,0:T(8,128)(2,1)S(1)}) custom-call(bf16[8,128,768]{2,1,0:T(8,128)(2,1)S(1)} %all-to-all-done.own_ref, bf16[4,48,640]{2,1,0:T(8,128)(2,1)S(1)} %pad_maximum_fusion.near_ref, ...), custom_call_target="tpu_custom_call" | custom-call | flops 5500000256 | tf_op jit(solution)/shard_map/pallas_call | solution.py:78
  60.4 1.2 copy-done.12
  61.6 1.0 copy-done.14
  62.6 0.6 copy-done.20
  63.2 0.1 collective-permute-start.6
  63.4 2.2 %collective-permute-done.6.other_ref = bf16[384,1024]{1,0:T(8,128)(2,1)S(1)} collective-permute-done((bf16[384,1024]{1,0:T(8,128)(2,1)S(1)}, bf16[384,1024]{1,0:T(8,128)(2,1)S(1)}, u32[]{:S(2)}, u32[]{:S(2)}) %collective-permute-start.6) | collective-permute-done | bytes 786464 | tf_op jit(solution)/shard_map/ppermute | solution.py:677
  65.6 8.1 %shard_map.225 = (f32[192,1024]{1,0:T(8,128)S(1)}, bf16[8,192,128]{2,1,0:T(8,128)(2,1)}, f32[3,1024]{1,0:T(4,128)S(1)}) custom-call(s32[2]{0:T(128)S(1)} %copy-done.3, bf16[192,1024]{1,0:T(8,128)(2,1)S(1)} %get-tuple-element.43.q_ref, bf16[384,1024]{1,0:T(8,128)(2,1)S(1)} %get-tuple-element.44.own_ref, bf16[384,1024]{1,0:T(8,128)(2,1)S(1)} %collective-permute-done.6.other_ref), custom_call_target="tpu_custom_call" | custom-call | flops 13200000000 | tf_op jit(solution)/shard_map/pallas_call | solution.py:78
  73.7 0.9 copy-done.18
  74.6 0.6 copy-done.23
  75.2 4.7 %all-to-all-start.2 = ((bf16[8,192,128]{2,1,0:T(8,128)(2,1)}), bf16[8,192,128]{2,1,0:T(8,128)(2,1)S(1)}, u32[]{:S(2)}, u32[]{:S(2)}) async-start(bf16[8,192,128]{2,1,0:T(8,128)(2,1)} %get-tuple-element.45), calls=%async_computation.2 | async-start | bytes 786432 | tf_op jit(solution)/shard_map/all_to_all | solution.py:694
  79.8 0.2 reduce-scatter.2.cloned.1.call-start
  80.1 1.8 copy.26
  81.9 6.4 %all-to-all-done.2.att_ref = bf16[8,192,128]{2,1,0:T(8,128)(2,1)S(1)} async-done(((bf16[8,192,128]{2,1,0:T(8,128)(2,1)}), bf16[8,192,128]{2,1,0:T(8,128)(2,1)S(1)}, u32[]{:S(2)}, u32[]{:S(2)}) %all-to-all-start.2) | async-done | bytes 393248 | tf_op jit(solution)/shard_map/all_to_all | solution.py:694
  88.3 0.7 shard_map.226
  89.0 1.0 copy-done.8
  90.0 0.7 copy-done.10
  90.8 0.8 copy-done.11
  91.5 4.8 %all-gather.3.cloned.1.call-done = bf16[6912,768]{1,0:T(8,128)(2,1)} async-done(((bf16[432,768]{1,0:T(8,128)(2,1)}), bf16[6912,768]{1,0:T(8,128)(2,1)}) %all-gather.3.cloned.1.call-update) | async-done | bytes 10616848 | tf_op jit(solution)/shard_map/all_gather | solution.py:654
  96.3 16.4 %shard_map.227 = (bf16[256,768]{1,0:T(8,128)(2,1)}, f32[256,768]{1,0:T(8,128)}, bf16[8,192,128]{2,1,0:T(8,128)(2,1)}, f32[8,768]{1,0:T(8,128)}, bf16[16,432,768]{2,1,0:T(8,128)(2,1)}) custom-call(bf16[256,768]{1,0:T(8,128)(2,1)} %bitcast.45, bf16[256,768]{1,0:T(8,128)(2,1)} %bitcast.56, bf16[256,768]{1,0:T(8,128)(2,1)} %copy-done.10, ...), custom_call_target="tpu_custom_call" | custom-call | flops 18699999232 | tf_op jit(solution)/shard_map/pallas_call | solution.py:78
  112.8 0.0 reduce-scatter.2.cloned.1.call-update
  112.8 14.8 %all_to_all.31.da_ref = bf16[8,192,128]{2,1,0:T(8,128)(2,1)S(1)} all-to-all(bf16[8,192,128]{2,1,0:T(8,128)(2,1)} %get-tuple-element.55), channel_id=1, replica_groups={{0,16,32,48,64,80,96,112},{8,24,40,56,72,88,104,120},{1,17,33,49,65,81,..., dimensions={0} | all-to-all | bytes 786432 | tf_op jit(solution)/shard_map/all_to_all | solution.py:708
  127.5 1.1 copy-done.19
  128.7 0.7 copy-done.24
  129.4 12.7 %shard_map.228 = (bf16[192,1024]{1,0:T(8,128)(2,1)S(1)}, bf16[384,1024]{1,0:T(8,128)(2,1)S(1)}, bf16[384,1024]{1,0:T(8,128)(2,1)S(1)}) custom-call(s32[2]{0:T(128)S(1)} %copy-done.3, bf16[192,1024]{1,0:T(8,128)(2,1)S(1)} %copy-done.17, bf16[384,1024]{1,0:T(8,128)(2,1)S(1)} %get-tuple-element.44.own_ref, ...), custom_call_target="tpu_custom_call" | custom-call | flops 22000001024 | tf_op jit(solution)/shard_map/pallas_call | solution.py:78
  142.1 1.5 collective-permute-start.7
  143.6 1.9 collective-permute-done.7.partner_ref
  145.5 4.5 %shard_map.229 = (bf16[8,128,768]{2,1,0:T(8,128)(2,1)}, bf16[4,2,48,640]{3,2,1,0:T(8,128)(2,1)S(1)}, bf16[4,2,48,640]{3,2,1,0:T(8,128)(2,1)S(1)}) custom-call(bf16[8,128,768]{2,1,0:T(8,128)(2,1)S(1)} %all-to-all-done.own_ref, bf16[192,1024]{1,0:T(8,128)(2,1)S(1)} %get-tuple-element.56.dq_ref, bf16[384,1024]{1,0:T(8,128)(2,1)S(1)} %get-tuple-element.57.dkv_ref, ...), custom_call_target="tpu_custom_call" | custom-call | flops 7699999744 | tf_op jit(solution)/shard_map/pallas_call | solution.py:78
  150.0 0.4 collective-permute-start.8
  150.3 3.6 %all-to-all-start.4 = ((bf16[8,128,768]{2,1,0:T(8,128)(2,1)}), bf16[8,128,768]{2,1,0:T(8,128)(2,1)S(1)}, u32[]{:S(2)}, u32[]{:S(2)}) async-start(bf16[8,128,768]{2,1,0:T(8,128)(2,1)} %get-tuple-element.62), calls=%async_computation.4 | async-start | bytes 3145728 | tf_op jit(solution)/shard_map/all_to_all | solution.py:748
  153.9 0.1 add_convert_fusion
  154.1 0.1 collective-permute-start.9
  154.2 5.9 %collective-permute-start.11 = (bf16[2,48,640]{2,1,0:T(8,128)(2,1)S(1)}, bf16[2,48,640]{2,1,0:T(8,128)(2,1)S(1)}, u32[]{:S(2)}, u32[]{:S(2)}) collective-permute-start(bf16[2,48,640]{2,1,0:T(8,128)(2,1)S(1)} %get-tuple-element.75), channel_id=1, source_target_pairs={{0,3},{1,0},{2,1},{3,2},{4,7},{5,4},{6,5},{7,6},{8,11},{9,8},{10,9... | collective-permute-start | bytes 368648 | tf_op jit(solution)/shard_map/ppermute | solution.py:745
  160.1 1.4 collective-permute-start.10
  161.5 2.1 collective-permute-done.9
  163.6 6.9 %collective-permute-done.10 = bf16[2,48,640]{2,1,0:T(8,128)(2,1)S(1)} collective-permute-done((bf16[2,48,640]{2,1,0:T(8,128)(2,1)S(1)}, bf16[2,48,640]{2,1,0:T(8,128)(2,1)S(1)}, u32[]{:S(2)}, u32[]{:S(2)}) %collective-permute-start.10) | collective-permute-done | bytes 122912 | tf_op jit(solution)/shard_map/ppermute | solution.py:744
  170.5 0.1 fusion.2
  170.6 1.5 collective-permute-start.12
  172.1 7.3 %collective-permute-done.12 = bf16[48,640]{1,0:T(8,128)(2,1)S(1)} collective-permute-done((bf16[48,640]{1,0:T(8,128)(2,1)S(1)}, bf16[48,640]{1,0:T(8,128)(2,1)S(1)}, u32[]{:S(2)}, u32[]{:S(2)}) %collective-permute-start.12) | collective-permute-done | bytes 61472 | tf_op jit(solution)/shard_map/ppermute | solution.py:747
  179.4 7.4 %reduce-scatter.2.cloned.1.call-done.rest_ref = bf16[432,768]{1,0:T(8,128)(2,1)} async-done(((bf16[6912,768]{1,0:T(8,128)(2,1)}), bf16[432,768]{1,0:T(8,128)(2,1)}) %reduce-scatter.2.cloned.1.call-update) | async-done | bytes 663568 | tf_op jit(solution)/shard_map/reduce_scatter | solution.py:704
  186.8 1.1 copy-done.2
  187.9 1.5 shard_map.231
  189.4 5.2 %all-to-all-start.5 = ((bf16[8,64,768]{2,1,0:T(8,128)(2,1)}), bf16[8,64,768]{2,1,0:T(8,128)(2,1)S(1)}, u32[]{:S(2)}, u32[]{:S(2)}) async-start(bf16[8,64,768]{2,1,0:T(8,128)(2,1)} %shard_map.231), calls=%async_computation.6 | async-start | bytes 1572864 | tf_op jit(solution)/shard_map/all_to_all | solution.py:758
  194.5 2.1 copy.33
  196.7 0.7 copy-done.21
  197.4 0.7 shard_map.230
  198.1 1.2 copy.32
  199.3 8.7 %all-to-all-done.5.got_ref = bf16[8,64,768]{2,1,0:T(8,128)(2,1)S(1)} async-done(((bf16[8,64,768]{2,1,0:T(8,128)(2,1)}), bf16[8,64,768]{2,1,0:T(8,128)(2,1)S(1)}, u32[]{:S(2)}, u32[]{:S(2)}) %all-to-all-start.5) | async-done | bytes 786464 | tf_op jit(solution)/shard_map/all_to_all | solution.py:758
  208.0 1.9 shard_map.232
  (52 shorter events, 0.2 us)
Async XLA Ops:
  7.2 89.2 %all-gather.3.cloned.1.call-start = ((), (), s32[]{:S(2)}) async-start(), calls=%async_computation.8 | async-start | bytes 11280384 | tf_op jit(solution)/shard_map/all_gather | solution.py:654
  9.4 18.2 %copy-start.7 = (s32[1,512]{1,0:T(1,128)S(1)}, s32[1,512]{1,0:T(1,128)}, u32[]{:S(2)}) copy-start(s32[1,512]{1,0:T(1,128)} %constant.10.clone.order_ref) | copy-start | bytes 6148
  27.6 1.5 copy-start.25
  29.2 1.3 copy-start
  30.5 26.9 %copy-start.5 = (s32[1,768]{1,0:T(1,128)S(1)}, s32[1,768]{1,0:T(1,128)}, u32[]{:S(2)}) copy-start(s32[1,768]{1,0:T(1,128)} %constant.11.clone.order_ref) | copy-start | bytes 9220
  30.5 26.9 %all-to-all-start = ((bf16[8,128,768]{2,1,0:T(8,128)(2,1)}), bf16[8,128,768]{2,1,0:T(8,128)(2,1)S(1)}, u32[]{:S(2)}, u32[]{:S(2)}) async-start(bf16[8,128,768]{2,1,0:T(8,128)(2,1)} %bitcast.50), calls=%async_computation | async-start | bytes 3145728 | tf_op jit(solution)/shard_map/all_to_all | solution.py:663
  34.2 5.7 %collective-permute-start.2 = (bf16[48,640]{1,0:T(8,128)(2,1)S(1)}, bf16[48,640]{1,0:T(8,128)(2,1)S(1)}, u32[]{:S(2)}, u32[]{:S(2)}) collective-permute-start(bf16[48,640]{1,0:T(8,128)(2,1)S(1)} %get-tuple-element.42), channel_id=1, source_target_pairs={{0,1},{1,2},{2,3},{3,0},{4,5},{5,6},{6,7},{7,4},{8,9},{9,10},{10,1... | collective-permute-start | bytes 184328 | tf_op jit(solution)/shard_map/ppermute | solution.py:656
  35.8 5.8 %collective-permute-start.1 = (bf16[48,640]{1,0:T(8,128)(2,1)S(1)}, bf16[48,640]{1,0:T(8,128)(2,1)S(1)}, u32[]{:S(2)}, u32[]{:S(2)}) collective-permute-start(bf16[48,640]{1,0:T(8,128)(2,1)S(1)} %get-tuple-element.42), channel_id=1, source_target_pairs={{0,2},{1,3},{2,0},{3,1},{4,6},{5,7},{6,4},{7,5},{8,10},{9,11},{10,... | collective-permute-start | bytes 184328 | tf_op jit(solution)/shard_map/ppermute | solution.py:656
  38.5 4.9 %collective-permute-start = (bf16[48,640]{1,0:T(8,128)(2,1)S(1)}, bf16[48,640]{1,0:T(8,128)(2,1)S(1)}, u32[]{:S(2)}, u32[]{:S(2)}) collective-permute-start(bf16[48,640]{1,0:T(8,128)(2,1)S(1)} %get-tuple-element.42), channel_id=1, source_target_pairs={{0,3},{1,0},{2,1},{3,2},{4,7},{5,4},{6,5},{7,6},{8,11},{9,8},{10,9... | collective-permute-start | bytes 184328 | tf_op jit(solution)/shard_map/ppermute | solution.py:656
  43.4 22.1 %copy-start.3 = (s32[2]{0:T(128)S(1)}, s32[2]{0:T(128)}, u32[]{:S(2)}) copy-start(s32[2]{0:T(128)} %lengths_ref.3) | copy-start | bytes 28
  43.4 12.5 %collective-permute-start.3 = (bf16[4,48,640]{2,1,0:T(8,128)(2,1)S(1)}, bf16[4,48,640]{2,1,0:T(8,128)(2,1)S(1)}, u32[]{:S(2)}, u32[]{:S(2)}) collective-permute-start(bf16[4,48,640]{2,1,0:T(8,128)(2,1)S(1)} %pad_maximum_fusion.near_ref), channel_id=1, source_target_pairs={{0,4},{1,5},{2,6},{3,7},{4,0},{5,1},{6,2},{7,3},{8,12},{9,13},{10,... | collective-permute-start | bytes 737288 | tf_op jit(solution)/shard_map/ppermute | solution.py:658
  43.5 12.4 %collective-permute-start.4 = (bf16[4,48,640]{2,1,0:T(8,128)(2,1)S(1)}, bf16[4,48,640]{2,1,0:T(8,128)(2,1)S(1)}, u32[]{:S(2)}, u32[]{:S(2)}) collective-permute-start(bf16[4,48,640]{2,1,0:T(8,128)(2,1)S(1)} %pad_maximum_fusion.near_ref), channel_id=1, source_target_pairs={{0,8},{8,0},{16,24},{24,16},{32,40},{40,32},{48,56},{56,48},{64,72... | collective-permute-start | bytes 737288 | tf_op jit(solution)/shard_map/ppermute | solution.py:659
  55.9 1.5 collective-permute-start.5
  60.4 1.2 copy-start.12
  61.6 1.0 copy-start.14
  62.6 0.6 copy-start.20
  63.2 10.4 %copy-start.16 = (bf16[192,1024]{1,0:T(8,128)(2,1)}, bf16[192,1024]{1,0:T(8,128)(2,1)S(1)}, u32[]{:S(2)}) copy-start(bf16[192,1024]{1,0:T(8,128)(2,1)S(1)} %get-tuple-element.43.q_ref) | copy-start | bytes 1179652
  63.2 2.3 %collective-permute-start.6 = (bf16[384,1024]{1,0:T(8,128)(2,1)S(1)}, bf16[384,1024]{1,0:T(8,128)(2,1)S(1)}, u32[]{:S(2)}, u32[]{:S(2)}) collective-permute-start(bf16[384,1024]{1,0:T(8,128)(2,1)S(1)} %get-tuple-element.44.own_ref), channel_id=1, source_target_pairs={{0,8},{8,0},{16,24},{24,16},{32,40},{40,32},{48,56},{56,48},{64,72... | collective-permute-start | bytes 2359304 | tf_op jit(solution)/shard_map/ppermute | solution.py:677
  73.7 0.9 copy-start.18
  74.6 0.6 copy-start.23
  75.2 13.1 %copy-start.6 = (s32[1,768]{1,0:T(1,128)S(1)}, s32[1,768]{1,0:T(1,128)}, u32[]{:S(2)}) copy-start(s32[1,768]{1,0:T(1,128)} %constant.8.clone.order_ref) | copy-start | bytes 9220
  75.2 13.1 %all-to-all-start.2 = ((bf16[8,192,128]{2,1,0:T(8,128)(2,1)}), bf16[8,192,128]{2,1,0:T(8,128)(2,1)S(1)}, u32[]{:S(2)}, u32[]{:S(2)}) async-start(bf16[8,192,128]{2,1,0:T(8,128)(2,1)} %get-tuple-element.45), calls=%async_computation.2 | async-start | bytes 786432 | tf_op jit(solution)/shard_map/all_to_all | solution.py:694
  79.8 107.0 %reduce-scatter.2.cloned.1.call-start = ((), (), s32[]{:S(2)}) async-start(), calls=%async_computation.7 | async-start | bytes 11280384 | tf_op jit(solution)/shard_map/reduce_scatter | solution.py:704
  89.0 1.0 copy-start.8
  90.0 0.7 copy-start.10
  90.8 0.8 copy-start.11
  112.8 14.8 %copy-start.17 = (bf16[192,1024]{1,0:T(8,128)(2,1)S(1)}, bf16[192,1024]{1,0:T(8,128)(2,1)}, u32[]{:S(2)}) copy-start(bf16[192,1024]{1,0:T(8,128)(2,1)} %copy-done.16) | copy-start | bytes 1179652
  127.5 1.1 copy-start.19
  128.7 0.7 copy-start.24
  129.4 16.1 %copy-start.13 = (bf16[1024,768]{1,0:T(8,128)(2,1)S(1)}, bf16[1024,768]{1,0:T(8,128)(2,1)}, u32[]{:S(2)}) copy-start(bf16[1024,768]{1,0:T(8,128)(2,1)} %copy-done.12) | copy-start | bytes 4718596
  129.4 16.1 %copy-start.15 = (bf16[576,768]{1,0:T(8,128)(2,1)S(1)}, bf16[576,768]{1,0:T(8,128)(2,1)}, u32[]{:S(2)}) copy-start(bf16[576,768]{1,0:T(8,128)(2,1)} %copy-done.14) | copy-start | bytes 2654212
  129.4 16.1 %copy-start.22 = (f32[8,768]{1,0:T(8,128)S(1)}, f32[8,768]{1,0:T(8,128)}, u32[]{:S(2)}) copy-start(f32[8,768]{1,0:T(8,128)} %get-tuple-element.61.dgain_ref) | copy-start | bytes 73732
  142.1 3.4 %collective-permute-start.7 = (bf16[384,1024]{1,0:T(8,128)(2,1)S(1)}, bf16[384,1024]{1,0:T(8,128)(2,1)S(1)}, u32[]{:S(2)}, u32[]{:S(2)}) collective-permute-start(bf16[384,1024]{1,0:T(8,128)(2,1)S(1)} %get-tuple-element.58), channel_id=1, source_target_pairs={{0,8},{8,0},{16,24},{24,16},{32,40},{40,32},{48,56},{56,48},{64,72... | collective-permute-start | bytes 2359304 | tf_op jit(solution)/shard_map/ppermute | solution.py:730
  150.0 4.0 %collective-permute-start.8 = (bf16[4,2,48,640]{3,2,1,0:T(8,128)(2,1)S(1)}, bf16[4,2,48,640]{3,2,1,0:T(8,128)(2,1)S(1)}, u32[]{:S(2)}, u32[]{:S(2)}) collective-permute-start(bf16[4,2,48,640]{3,2,1,0:T(8,128)(2,1)S(1)} %get-tuple-element.65), channel_id=1, source_target_pairs={{0,8},{8,0},{16,24},{24,16},{32,40},{40,32},{48,56},{56,48},{64,72... | collective-permute-start | bytes 1474568 | tf_op jit(solution)/shard_map/ppermute | solution.py:740
  150.3 39.0 %all-to-all-start.4 = ((bf16[8,128,768]{2,1,0:T(8,128)(2,1)}), bf16[8,128,768]{2,1,0:T(8,128)(2,1)S(1)}, u32[]{:S(2)}, u32[]{:S(2)}) async-start(bf16[8,128,768]{2,1,0:T(8,128)(2,1)} %get-tuple-element.62), calls=%async_computation.4 | async-start | bytes 3145728 | tf_op jit(solution)/shard_map/all_to_all | solution.py:748
  154.1 9.5 %collective-permute-start.9 = (bf16[2,48,640]{2,1,0:T(8,128)(2,1)S(1)}, bf16[2,48,640]{2,1,0:T(8,128)(2,1)S(1)}, u32[]{:S(2)}, u32[]{:S(2)}) collective-permute-start(bf16[2,48,640]{2,1,0:T(8,128)(2,1)S(1)} %get-tuple-element.74), channel_id=1, source_target_pairs={{0,1},{1,2},{2,3},{3,0},{4,5},{5,6},{6,7},{7,4},{8,9},{9,10},{10,1... | collective-permute-start | bytes 368648 | tf_op jit(solution)/shard_map/ppermute | solution.py:743
  154.2 9.4 %collective-permute-start.11 = (bf16[2,48,640]{2,1,0:T(8,128)(2,1)S(1)}, bf16[2,48,640]{2,1,0:T(8,128)(2,1)S(1)}, u32[]{:S(2)}, u32[]{:S(2)}) collective-permute-start(bf16[2,48,640]{2,1,0:T(8,128)(2,1)S(1)} %get-tuple-element.75), channel_id=1, source_target_pairs={{0,3},{1,0},{2,1},{3,2},{4,7},{5,4},{6,5},{7,6},{8,11},{9,8},{10,9... | collective-permute-start | bytes 368648 | tf_op jit(solution)/shard_map/ppermute | solution.py:745
  160.1 10.4 %collective-permute-start.10 = (bf16[2,48,640]{2,1,0:T(8,128)(2,1)S(1)}, bf16[2,48,640]{2,1,0:T(8,128)(2,1)S(1)}, u32[]{:S(2)}, u32[]{:S(2)}) collective-permute-start(bf16[2,48,640]{2,1,0:T(8,128)(2,1)S(1)} %get-tuple-element.76), channel_id=1, source_target_pairs={{0,2},{1,3},{2,0},{3,1},{4,6},{5,7},{6,4},{7,5},{8,10},{9,11},{10,... | collective-permute-start | bytes 368648 | tf_op jit(solution)/shard_map/ppermute | solution.py:744
  170.6 8.8 %collective-permute-start.12 = (bf16[48,640]{1,0:T(8,128)(2,1)S(1)}, bf16[48,640]{1,0:T(8,128)(2,1)S(1)}, u32[]{:S(2)}, u32[]{:S(2)}) collective-permute-start(bf16[48,640]{1,0:T(8,128)(2,1)S(1)} %slice_bitcast_fusion.4), channel_id=1, source_target_pairs={{0,4},{1,5},{2,6},{3,7},{4,0},{5,1},{6,2},{7,3},{8,12},{9,13},{10,... | collective-permute-start | bytes 184328 | tf_op jit(solution)/shard_map/ppermute | solution.py:747
  186.8 1.1 copy-start.2
  189.4 7.3 %copy-start.1 = (bf16[2,128,768]{2,1,0:T(8,128)(2,1)S(1)}, bf16[2,128,768]{2,1,0:T(8,128)(2,1)}, u32[]{:S(2)}) copy-start(bf16[2,128,768]{2,1,0:T(8,128)(2,1)} %copy-done) | copy-start | bytes 1179652
  189.4 7.3 %copy-start.9 = (f32[256,768]{1,0:T(8,128)S(1)}, f32[256,768]{1,0:T(8,128)}, u32[]{:S(2)}) copy-start(f32[256,768]{1,0:T(8,128)} %get-tuple-element.52.dfirst_ref) | copy-start | bytes 2359300
  189.4 18.7 %all-to-all-start.5 = ((bf16[8,64,768]{2,1,0:T(8,128)(2,1)}), bf16[8,64,768]{2,1,0:T(8,128)(2,1)S(1)}, u32[]{:S(2)}, u32[]{:S(2)}) async-start(bf16[8,64,768]{2,1,0:T(8,128)(2,1)} %shard_map.231), calls=%async_computation.6 | async-start | bytes 1572864 | tf_op jit(solution)/shard_map/all_to_all | solution.py:758
  196.7 0.7 copy-start.21
  197.4 10.6 %copy-start.4 = (s32[1,768]{1,0:T(1,128)S(1)}, s32[1,768]{1,0:T(1,128)}, u32[]{:S(2)}) copy-start(s32[1,768]{1,0:T(1,128)} %constant.9.clone.units_ref) | copy-start | bytes 9220
Sparse Core Ops, SparseCore 0:
  29.2 67.0 all-gather.2
  112.9 73.8 reduce-scatter.1

commit v5 on v4

--- a/solution.py
+++ b/solution.py
@@ -26,7 +26,7 @@
     for y in range(4)
     for low in range(2)
 ]
-SWAP_Z = [(b, b ^ 4) for b in range(8)]
+SWAP_HALF = [(s * 8 + b, (s ^ 2) * 8 + (b ^ 4)) for s in range(16) for b in range(8)]
 
 
 def along_x(step):
@@ -52,6 +52,9 @@
 
 
 REGROUP = regroup_order()
+SPREAD = np.concatenate(
+    [np.arange(96, dtype=np.int32).reshape(16, 6), np.full((16, 2), -1, np.int32)], axis=1
+).reshape(128, 1)
 
 
 def places(order_ref):
@@ -117,8 +120,8 @@
         row = jnp.concatenate(parts + [norms, jnp.zeros((6, 128), BF)], axis=1)
         scr[54:60, :] = row.astype(F32)
         slot = scr[...].astype(BF)
-        slot_ref[e] = slot
-        slot_ref[4 + e] = slot
+        slot_ref[2 * e] = slot
+        slot_ref[2 * e + 1] = slot
 
 
 def regroup_kernel(slots_ref, order_ref, rest_ref, qkv_ref):
@@ -132,15 +135,15 @@
 
 
 def length_of(lengths_ref):
-    return jnp.where(lax.axis_index("seq") < 8, lengths_ref[0], lengths_ref[1])
-
-
-def rows_at(dc, dz, dx):
+    return jnp.where(lax.rem(lax.axis_index("seq") // 2, 2) == 0, lengths_ref[0], lengths_ref[1])
+
+
+def rows_at(dc, dz, dx, size=48):
     row = lax.axis_index("batch")
     c = lax.rem(core_of() + dc, 2)
     z = lax.rem(row // 4 + dz, 2)
     x = lax.rem(row + dx, 4)
-    return pl.ds(pl.multiple_of((c * 8 + z * 4 + x) * 48, 48), 48)
+    return pl.ds(pl.multiple_of((c * 8 + z * 4 + x) * size, size), size)
 
 
 def project_kernel(
@@ -419,17 +422,17 @@
 
 def prepare_kernel(att_ref, order_ref, place_ref, attended_ref, attended_t_ref):
     place_ref[...] = places(order_ref)
-    natural = [att_ref[b * 4 : b * 4 + 4].reshape(768, 128).T for b in range(2)]
-    attended = dot(jnp.concatenate(natural, axis=0), place_ref[...]).astype(BF)
-    attended_ref[...] = attended
-    attended_t_ref[...] = attended.T
+    for b in range(2):
+        for e in range(4):
+            attended_t_ref[e * 192 : (e + 1) * 192, b * 128 : (b + 1) * 128] = att_ref[2 * e + b]
+    attended_ref[...] = dot(attended_t_ref[...].T, place_ref[...]).astype(BF)
 
 
 def feed_kernel(
-    x_hbm, dy_hbm, att_hbm, att_t_hbm, gains_hbm, place_hbm, weights_hbm,
-    y_hbm, dfirst_hbm, datt_hbm, dgain_hbm, grads_hbm,
-    x_ref, dy_ref, att_ref, att_t_ref, gains_ref, place_ref, down_ref, up_ref, out_ref,
-    y_ref, dfirst_ref, datt_ref, dgain_ref, gdown, gup, gout, acc_scr, dn_scr, loads, stores,
+    x_hbm, dy_hbm, att_hbm, gains_hbm, place_hbm, weights_hbm,
+    y_hbm, dfirst_hbm, low_hbm, datt_hbm, dgain_hbm, grads_hbm,
+    x_ref, dy_ref, att_ref, gains_ref, place_ref, down_ref, up_ref, out_ref,
+    y_ref, dfirst_ref, low_ref, datt_ref, dgain_ref, gdown, gup, acc_scr, dn_scr, loads, stores,
 ):
     def block(ref, number):
         return ref.at[:, pl.ds(48 * number, 48), :]
@@ -441,7 +444,6 @@
         if k == 0:
             arrivals.append((dy_hbm, dy_ref))
         arrivals.append((block(weights_hbm, k), down_ref.at[k]))
-    arrivals.append((att_t_hbm, att_t_ref))
     arrivals = [pltpu.make_async_copy(*pair, loads.at[i]) for i, pair in enumerate(arrivals)]
     for copy in arrivals:
         copy.start()
@@ -486,10 +488,8 @@
         gup[k] = dot(n2t, d_hidden).astype(BF).reshape(16, 48, 768)
         send(gup.at[k], block(grads_hbm, 4 + k))
         acc_scr[...] += dot(active, down)
-        if k == 0:
-            dn_scr[...] = dot(d_hidden, up, NT)
-        else:
-            dn_scr[...] += dot(d_hidden, up, NT)
+        d_n2 = dot(d_hidden, up, NT)
+        dn_scr[...] = d_n2 if k == 0 else dn_scr[...] + d_n2
     y_ref[...] = acc_scr[...].astype(BF)
     send(y_ref, y_hbm)
     dn = dot(dn_scr[...].astype(BF), place_ref[...], NT)
@@ -497,16 +497,16 @@
     part = t - jnp.mean(t, -1, keepdims=True) - hat * jnp.mean(t * hat, -1, keepdims=True)
     d_first = dy_ref[...].astype(F32) + part * scale
     low = d_first.astype(BF)
-    waiting.pop(0).wait()
-    gout[...] = dot(att_t_ref[...], low).astype(BF).reshape(16, 48, 768)
-    send(gout, block(grads_hbm, 8))
+    low_ref[...] = low
+    send(low_ref, low_hbm)
+    dfirst_ref[...] = d_first
+    send(dfirst_ref, dfirst_hbm)
     d_att = dot(w_out, low, NT).astype(BF)
     d_att = dot(place_ref[...], d_att).astype(BF)
     for b in range(2):
-        datt_ref[b * 4 : b * 4 + 4] = d_att[:, b * 128 : (b + 1) * 128].reshape(4, 192, 128)
+        for e in range(4):
+            datt_ref[2 * e + b] = d_att[e * 192 : (e + 1) * 192, b * 128 : (b + 1) * 128]
     send(datt_ref, datt_hbm)
-    dfirst_ref[...] = d_first
-    send(dfirst_ref, dfirst_hbm)
     dgain_ref[0:1, :] = jnp.sum(dn * hat, axis=0, keepdims=True)
     dgain_ref[1:2, :] = jnp.sum(dn, axis=0, keepdims=True)
     dgain_ref[2:8, :] = jnp.zeros((6, 768), F32)
@@ -515,27 +515,36 @@
         copy.wait()
 
 
+def out_kernel(attended_t_ref, low_ref, grad_ref):
+    grad = dot(attended_t_ref[...], low_ref[...]).reshape(8, 2, 2, 24, 768)
+    half = lax.axis_index("batch") // 4
+    for j in range(8):
+        rows = [
+            jnp.where(half == z, grad[j, c, z], grad[j ^ 1, c, z]) for c in range(2) for z in range(2)
+        ]
+        grad_ref[j] = jnp.concatenate(rows, axis=0).astype(BF)
+
+
 def whole(*dims):
     return pl.BlockSpec(dims, lambda *_: (0,) * len(dims))
 
 
 def feed(*arrays):
     outs = [
-        shape((256, 768), BF), shape((256, 768), F32), shape((8, 192, 128), BF),
-        shape((8, 768), F32), shape((16, 432, 768), BF),
+        shape((256, 768), BF), shape((256, 768), F32), shape((256, 768), BF),
+        shape((8, 192, 128), BF), shape((8, 768), F32), shape((16, 384, 768), BF),
     ]
     blocks = pltpu.VMEM((4, 16, 48, 768), BF)
     held = [pltpu.VMEM(a.shape, a.dtype) for a in arrays[:-1]]
     held += [blocks, blocks, pltpu.VMEM((16, 48, 768), BF)]
     held += [pltpu.VMEM(o.shape, o.dtype) for o in outs[:-1]]
-    held += [blocks, blocks, pltpu.VMEM((16, 48, 768), BF)]
-    held += [pltpu.VMEM((256, 768), F32)] * 2
-    held += [pltpu.SemaphoreType.DMA((15,)), pltpu.SemaphoreType.DMA((13,))]
+    held += [blocks, blocks] + [pltpu.VMEM((256, 768), F32)] * 2
+    held += [pltpu.SemaphoreType.DMA((14,)), pltpu.SemaphoreType.DMA((13,))]
     return call(
         feed_kernel,
         outs,
         arrays,
-        17,
+        15,
         held,
         in_specs=[pl.BlockSpec(memory_space=pl.ANY)] * len(arrays),
         out_specs=[pl.BlockSpec(memory_space=pl.ANY)] * len(outs),
@@ -544,7 +553,8 @@
 
 def unproject_kernel(
     own_ref, dq_ref, dkv_ref, partner_ref, normed_ref, wt_ref, dgain_ref, order_ref,
-    part_ref, mine_ref, theirs_ref, dt_scr, dw_scr, p_scr,
+    out_ref, spread_ref,
+    part_ref, mine_ref, theirs_ref, dt_scr, dw_scr, p_scr, o_scr,
 ):
     dt_scr[0:192, :] = dq_ref[...]
     dt_scr[192:576, :] = (dkv_ref[...].astype(F32) + partner_ref[...].astype(F32)).astype(BF)
@@ -562,42 +572,54 @@
     dw_scr[578:580, :] = dgain_ref[0:2, :]
     dw_scr[580:640, :] = jnp.zeros((60, 768), F32)
     p_scr[...] = dot(dw_scr[...].astype(BF), places(order_ref)).T.astype(BF)
+    out = jnp.zeros((96, 768), F32)
+    for j in range(8):
+        out += out_ref[j].astype(F32)
+    lanes = lax.broadcasted_iota(jnp.int32, (128, 96), 1)
+    spread = jnp.where(lanes == spread_ref[...], 1.0, 0.0).astype(BF)
+    o_scr[...] = dot(spread, out.astype(BF))
     for dc, ref in enumerate((mine_ref, theirs_ref)):
         for dx in range(4):
             for dz in range(2):
-                ref[dx, dz] = p_scr[rows_at(dc, dz, dx), :]
+                ref[dx, dz, :, 0:640] = p_scr[rows_at(dc, dz, dx), :]
+                few = o_scr[rows_at(dc, dz, dx, 8), :]
+                ref[dx, dz, :, 640:768] = jnp.concatenate(
+                    [few[:, q * 128 : (q + 1) * 128] for q in range(6)], axis=0
+                ).astype(BF)
 
 
 def slots_kernel(rest_ref, qkv_ref, order_ref, out_ref, r_scr):
-    r_scr[0:432, :] = rest_ref[...]
-    r_scr[432:480, 0:640] = qkv_ref[...]
+    r_scr[0:384, :] = rest_ref[...]
+    r_scr[384:432, :] = jnp.zeros((48, 768), BF)
+    r_scr[432:480, 0:640] = qkv_ref[:, 0:640]
     r_scr[432:480, 640:768] = jnp.zeros((48, 128), BF)
     r_scr[480:512, :] = jnp.zeros((32, 768), BF)
     out_ref[...] = dot(places(order_ref), r_scr[...]).astype(BF).reshape(8, 64, 768)
 
 
-def finish_kernel(x_ref, dfirst_ref, gains_ref, got_ref, dtok_ref):
+def finish_kernel(x_ref, dfirst_ref, gains_ref, got_ref, qkv_ref, dtok_ref, out_ref):
+    for q in range(6):
+        out_ref[:, q * 128 : (q + 1) * 128] = qkv_ref[q * 8 : q * 8 + 8, 640:768].astype(F32)[0:6]
     gain = gains_ref[0:1]
     for b in range(2):
         rows = slice(b * 128, (b + 1) * 128)
         dn = jnp.zeros((128, 768), F32)
         for e in range(4):
-            dn += got_ref[4 * b + e].astype(F32)
+            dn += got_ref[2 * e + b].astype(F32)
         hat, scale = normalize(x_ref[rows, :].astype(F32))
         t = dn * gain
         part = t - jnp.mean(t, -1, keepdims=True) - hat * jnp.mean(t * hat, -1, keepdims=True)
         dtok_ref[rows, :] = (dfirst_ref[rows, :] + part * scale).astype(BF)
 
 
-def sums_kernel(got_ref, units_ref, down_ref, out_ref, up_ref, qkv_ref, g1_ref, b1_ref, g2_ref, b2_ref):
+def sums_kernel(got_ref, units_ref, down_ref, up_ref, qkv_ref, g1_ref, b1_ref, g2_ref, b2_ref):
     total = jnp.zeros((64, 768), F32)
     chunks = []
     for e in range(4):
-        both = got_ref[e].astype(F32) + got_ref[4 + e].astype(F32)
+        both = got_ref[2 * e].astype(F32) + got_ref[2 * e + 1].astype(F32)
         chunks.append(both[54:60])
         total += both
     down_ref[...] = total[0:24]
-    out_ref[...] = total[24:30]
     left, up, units = total[30:54], jnp.zeros((24, 768), F32), places(units_ref)
     for _ in range(3):
         piece = left.astype(BF)
@@ -655,12 +677,12 @@
     near = jnp.stack(
         [qkv_rows] + [lax.ppermute(qkv_rows, "batch", along_x(step)) for step in (-1, 2, 1)]
     )
-    far = lax.ppermute(near, "batch", SWAP_Z)
+    far = lax.ppermute(near, BOTH, SWAP_HALF)
     near_other = lax.ppermute(near, "seq", SWAP_CORE)
     far_other = lax.ppermute(far, "seq", SWAP_CORE)
     x = tokens.transpose(1, 0, 2)
     dy = d_out.transpose(1, 0, 2).reshape(256, 768)
-    own = exchange(jnp.broadcast_to(x[:, None], (2, 4, 128, 768)).reshape(8, 128, 768))
+    own = exchange(jnp.broadcast_to(x[None], (4, 2, 128, 768)).reshape(8, 128, 768))
     x = x.reshape(256, 768)
 
     normed, wt, gains, q_t, kv = call(
@@ -699,13 +721,13 @@
         2,
         mib=16,
     )
-    y, d_first, d_att, d_gain, grads = feed(x, dy, attended, attended_t, gains, place, weights)
-
+    y, d_first, low, d_att, d_gain, grads = feed(x, dy, attended, gains, place, weights)
     rest_sum = lax.psum_scatter(
-        grads.reshape(16 * 432, 768), BOTH, scatter_dimension=0, tiled=True,
+        grads.reshape(16 * 384, 768), BOTH, scatter_dimension=0, tiled=True,
         axis_index_groups=RINGS,
     )
     d_att = exchange(d_att)
+    out_grad = exchange(call(out_kernel, shape((8, 96, 768), BF), (attended_t, low), 2))
     dq, dkv, dkv_other = call(
         backward_kernel,
         [shape((192, 1024), BF), shape((384, 1024), BF), shape((384, 1024), BF)],
@@ -724,17 +746,20 @@
         + [pltpu.VMEM((256, 256), F32)] * 12
         + [pltpu.VMEM((256, 256), BF)] * 12
         + [pltpu.VMEM((64, 256), F32)] * 3,
-        mib=36,
+        mib=60,
         **scalars(7),
     )
     partner = lax.ppermute(dkv_other, "seq", SWAP_CORE)
     part, mine, theirs = call(
         unproject_kernel,
-        [shape((8, 128, 768), BF), shape((4, 2, 48, 640), BF), shape((4, 2, 48, 640), BF)],
-        (own, dq, dkv, partner, normed, wt, d_gain, qkv_order),
+        [shape((8, 128, 768), BF), shape((4, 2, 48, 768), BF), shape((4, 2, 48, 768), BF)],
+        (own, dq, dkv, partner, normed, wt, d_gain, qkv_order, out_grad, jnp.asarray(SPREAD)),
         7,
-        [pltpu.VMEM((576, 1024), BF), pltpu.VMEM((640, 768), F32), pltpu.VMEM((768, 640), BF)],
-        mib=30,
+        [
+            pltpu.VMEM((576, 1024), BF), pltpu.VMEM((640, 768), F32),
+            pltpu.VMEM((768, 640), BF), pltpu.VMEM((128, 768), F32),
+        ],
+        mib=60,
     )
     add = lambda *parts: sum(p.astype(F32) for p in parts).astype(BF)
     line = add(mine, lax.ppermute(theirs, "seq", SWAP_CORE))
@@ -744,9 +769,15 @@
         lax.ppermute(line[2], "batch", along_x(2)),
         lax.ppermute(line[3], "batch", along_x(-1)),
     )
-    qkv_sum = add(line[0], lax.ppermute(line[1], "batch", SWAP_Z))
+    qkv_sum = add(line[0], lax.ppermute(line[1], BOTH, SWAP_HALF))
     back = exchange(part)
-    d_tokens = call(finish_kernel, shape((256, 768), BF), (x, d_first, gains, back), 3, mib=16)
+    d_tokens, d_out_w = call(
+        finish_kernel,
+        [shape((256, 768), BF), shape((6, 768), F32)],
+        (x, d_first, gains, back, qkv_sum),
+        3,
+        mib=16,
+    )
     slots = call(
         slots_kernel,
         shape((8, 64, 768), BF),
@@ -757,9 +788,9 @@
     )
     slots = exchange(slots)
     vector = shape((1, 6), F32)
-    d_down, d_out_w, d_up, d_qkv, *norms = call(
+    d_down, d_up, d_qkv, *norms = call(
         sums_kernel,
-        [shape((24, 768), F32), shape((6, 768), F32), shape((6, 3072), F32), shape((6, 2304), F32)]
+        [shape((24, 768), F32), shape((6, 3072), F32), shape((6, 2304), F32)]
         + [vector] * 4,
         (slots, units),
         2,

time: 220 us -> 218 us (level)
  blocking collectives: 33 us -> 18.1 us
  Pallas kernels: 53.1 us -> 66.9 us
  starting transfers between devices: 34.1 us -> 41.2 us
  waiting for transfers between devices: 65 us -> 60.8 us
  local copies, waits for them, and re-layouts: 17.1 us -> 13.9 us
    all_to_all x1 -> x0, blocking collectives: 14.8 us -> none  [body(): d_att = exchange(d_att)]
    pallas_call x10 -> x11, Pallas kernels: 50.9 us -> 64.7 us  [call(): pl.pallas_call(kernel, out_shape=outs, scratch_shapes=list(scratch), cost...]
    all_to_all x1 -> x3, starting transfers between devices: 3.71 us -> 13.6 us  [the longest x1 6.11 us: body(): d_att = exchange(d_att)]
    all_to_all x1 -> x3, waiting for transfers between devices: 0.01 us -> 8.75 us  [the longest x1 6.12 us: body(): d_att = exchange(d_att)]
    reduce_scatter x1, waiting for transfers between devices: 7.39 us -> 0.02 us  [body(): lax.psum_scatter(grads.reshape(16 * 384, 768), BOTH, scatter_dimension=0,...]
    ppermute x2, waiting for transfers between devices: 19.6 us -> 13.3 us  [the longest x1 8.99 us: body(): far = lax.ppermute(near, BOTH, SWAP_HALF)]
    all_to_all x1, waiting for transfers between devices: 8.74 us -> 5.45 us  [body(): slots = exchange(slots)]
    ppermute x1, starting transfers between devices: 5.89 us -> 3.25 us  [body(): lax.ppermute(line[3], 'batch', along_x(-1))]
  transfers between devices with their start and end apart: 19 -> 21, of which waited for: 13 -> 17; matrix products, arithmetic and copies ran while one was open for 3% -> 2% of each run, Pallas kernels for 14% -> 21%
where the time goes in v5:
time: 218 us; the launch traced here: 215 us
  Pallas kernels  66.9 us (31%)
  waiting for transfers between devices  60.8 us (28%)
  starting transfers between devices  41.2 us (19%)
  blocking collectives  18.1 us (8%)
  between operations  14.3 us (7%)
  local copies, waits for them, and re-layouts  13.9 us (6%)
    pallas_call x11, Pallas kernels, call(): pl.pallas_call(kernel, out_shape=outs, scratch_shapes=list(scratch), cost...  64.7 us
    all_to_all x1, blocking collectives, body(): slots = exchange(slots)  18.1 us
    unnamed x58, local copies, waits for them, and re-layouts  9.39 us
    ppermute x1, waiting for transfers between devices, body(): far = lax.ppermute(near, BOTH, SWAP_HALF)  8.99 us
    all_to_all x1, waiting for transfers between devices, body(): att = exchange(o_low)  7.64 us
    all_gather x1, waiting for transfers between devices, body(): weights = lax.all_gather(rest, BOTH, axis=0, axis_index_groups=RINGS)  6.32 us
    all_to_all x1, starting transfers between devices, body(): slots = exchange(slots)  6.15 us
    all_to_all x1, waiting for transfers between devices, body(): d_att = exchange(d_att)  6.12 us
  transfers between devices with their start and end apart: 21, of which 17 were waited for; matrix products, arithmetic and copies ran while one was open for 2% of the time, Pallas kernels for 21%

profile of v5, /device:TPU:64, one launch (start us, length us, event | category | flops | bytes accessed | tf_op | source)
XLA Modules:
  0.0 215.4 jit_solution(15918902365552416749)
XLA Ops:
  7.2 2.2 %shard_map.231 = bf16[8,64,768]{2,1,0:T(8,128)(2,1)} custom-call(bf16[24,768]{1,0:T(8,128)(2,1)} %down_ref.1, bf16[6,768]{1,0:T(8,128)(2,1)} %out_ref.1, bf16[6,3072]{1,0:T(8,128)(2,1)} %up_ref.1, bf16[6,2304]{1,0:T(8,128)(2,1)} %qkv_ref.1, bf16[1,6]{1,0:T(2,128)(2,1)} %bitcast.61, bf16[1,6]{1,0:T(2,128)(2,1)} %bitcast.62, bf16[1,6]{1,0:T(2,128)(2,1)} %bitcast.63, ...), custom_call_target="tpu_custom_call" | custom-call | flops 2200000000 | tf_op jit(solution)/shard_map/pallas_call | solution.py:656
  9.4 18.1 %all_to_all.35.slots_ref = bf16[8,64,768]{2,1,0:T(8,128)(2,1)S(1)} all-to-all(bf16[8,64,768]{2,1,0:T(8,128)(2,1)} %shard_map.231), channel_id=1, replica_groups={{0,16,32,48,64,80,96,112},{8,24,40,56,72,88,104,120},{1,17,33,49,65,81,..., dimensions={0} | all-to-all | bytes 1572864 | tf_op jit(solution)/shard_map/all_to_all | solution.py:668
  27.5 1.5 shard_map.232
  29.0 1.3 broadcast_in_dim.2
  30.4 3.7 %all-to-all-start = ((bf16[8,128,768]{2,1,0:T(8,128)(2,1)}), bf16[8,128,768]{2,1,0:T(8,128)(2,1)S(1)}, u32[]{:S(2)}, u32[]{:S(2)}) async-start(bf16[8,128,768]{2,1,0:T(8,128)(2,1)} %bitcast.50), calls=%async_computation | async-start | bytes 3145728 | tf_op jit(solution)/shard_map/all_to_all | solution.py:685
  34.1 1.6 collective-permute-start.2
  35.6 2.7 %collective-permute-start.1 = (bf16[48,640]{1,0:T(8,128)(2,1)S(1)}, bf16[48,640]{1,0:T(8,128)(2,1)S(1)}, u32[]{:S(2)}, u32[]{:S(2)}) collective-permute-start(bf16[48,640]{1,0:T(8,128)(2,1)S(1)} %get-tuple-element.44), channel_id=1, source_target_pairs={{0,2},{1,3},{2,0},{3,1},{4,6},{5,7},{6,4},{7,5},{8,10},{9,11},{10,... | collective-permute-start | bytes 184328 | tf_op jit(solution)/shard_map/ppermute | solution.py:678
  38.4 1.4 collective-permute-start
  39.8 1.6 collective-permute-done.1
  41.5 1.8 collective-permute-done
  43.3 0.4 collective-permute-start.3
  43.7 9.0 %collective-permute-done.3.far_ref = bf16[4,48,640]{2,1,0:T(8,128)(2,1)S(1)} collective-permute-done((bf16[4,48,640]{2,1,0:T(8,128)(2,1)S(1)}, bf16[4,48,640]{2,1,0:T(8,128)(2,1)S(1)}, u32[]{:S(2)}, u32[]{:S(2)}) %collective-permute-start.3) | collective-permute-done | bytes 245792 | tf_op jit(solution)/shard_map/ppermute | solution.py:680
  52.7 1.5 collective-permute-done.5.far_other_ref
  54.2 1.5 all-to-all-done.own_ref
  55.7 3.0 %shard_map.233 = (bf16[1024,768]{1,0:T(8,128)(2,1)S(1)}, bf16[576,768]{1,0:T(8,128)(2,1)S(1)}, f32[8,768]{1,0:T(8,128)S(1)}, bf16[192,1024]{1,0:T(8,128)(2,1)S(1)}, bf16[384,1024]{1,0:T(8,128)(2,1)S(1)}) custom-call(bf16[8,128,768]{2,1,0:T(8,128)(2,1)S(1)} %all-to-all-done.own_ref, bf16[4,48,640]{2,1,0:T(8,128)(2,1)S(1)} %pad_maximum_fusion.near_ref, ...), custom_call_target="tpu_custom_call" | custom-call | flops 5500000256 | tf_op jit(solution)/shard_map/pallas_call | solution.py:81
  58.8 1.1 copy-done.15
  59.9 1.0 copy-done.16
  60.9 2.3 %collective-permute-done.6.other_ref = bf16[384,1024]{1,0:T(8,128)(2,1)S(1)} collective-permute-done((bf16[384,1024]{1,0:T(8,128)(2,1)S(1)}, bf16[384,1024]{1,0:T(8,128)(2,1)S(1)}, u32[]{:S(2)}, u32[]{:S(2)}) %collective-permute-start.6) | collective-permute-done | bytes 786464 | tf_op jit(solution)/shard_map/ppermute | solution.py:699
  63.2 9.5 %shard_map.234 = (f32[192,1024]{1,0:T(8,128)S(1)}, bf16[8,192,128]{2,1,0:T(8,128)(2,1)}, f32[3,1024]{1,0:T(4,128)S(1)}) custom-call(s32[2]{0:T(128)S(1)} %copy-done.6, bf16[192,1024]{1,0:T(8,128)(2,1)S(1)} %get-tuple-element.45.q_ref, bf16[384,1024]{1,0:T(8,128)(2,1)S(1)} %get-tuple-element.46.own_ref, bf16[384,1024]{1,0:T(8,128)(2,1)S(1)} %collective-permute-done.6.other_ref), custom_call_target="tpu_custom_call" | custom-call | flops 13200000000 | tf_op jit(solution)/shard_map/pallas_call | solution.py:81
  72.8 0.9 copy-done.18
  73.7 0.6 copy-done.21
  74.3 3.6 %all-to-all-start.2 = ((bf16[8,192,128]{2,1,0:T(8,128)(2,1)}), bf16[8,192,128]{2,1,0:T(8,128)(2,1)S(1)}, u32[]{:S(2)}, u32[]{:S(2)}) async-start(bf16[8,192,128]{2,1,0:T(8,128)(2,1)} %get-tuple-element.47), calls=%async_computation.2 | async-start | bytes 786432 | tf_op jit(solution)/shard_map/all_to_all | solution.py:716
  77.9 0.2 reduce-scatter.2.cloned.1.call-start
  78.1 0.8 copy.27
  78.9 7.6 %all-to-all-done.2.att_ref = bf16[8,192,128]{2,1,0:T(8,128)(2,1)S(1)} async-done(((bf16[8,192,128]{2,1,0:T(8,128)(2,1)}), bf16[8,192,128]{2,1,0:T(8,128)(2,1)S(1)}, u32[]{:S(2)}, u32[]{:S(2)}) %all-to-all-start.2) | async-done | bytes 393248 | tf_op jit(solution)/shard_map/all_to_all | solution.py:716
  86.5 0.7 shard_map.235
  87.3 1.1 copy-done.11
  88.4 0.8 copy-done.12
  89.1 0.8 copy-done.14
  89.9 6.3 %all-gather.3.cloned.1.call-done = bf16[6912,768]{1,0:T(8,128)(2,1)} async-done(((bf16[432,768]{1,0:T(8,128)(2,1)}), bf16[6912,768]{1,0:T(8,128)(2,1)}) %all-gather.3.cloned.1.call-update) | async-done | bytes 10616848 | tf_op jit(solution)/shard_map/all_gather | solution.py:676
  96.2 15.8 %shard_map.236 = (bf16[256,768]{1,0:T(8,128)(2,1)}, f32[256,768]{1,0:T(8,128)}, bf16[256,768]{1,0:T(8,128)(2,1)}, bf16[8,192,128]{2,1,0:T(8,128)(2,1)}, f32[8,768]{1,0:T(8,128)}, /*index=5*/bf16[16,384,768]{2,1,0:T(8,128)(2,1)}) custom-call(bf16[256,768]{1,0:T(8,128)(2,1)} %bitcast.45, bf16[256,768]{1,0:T(8,128)(2,1)} %bitcast.56, ...), custom_call_target="tpu_custom_call" | custom-call | flops 16499999744 | tf_op jit(solution)/shard_map/pallas_call | solution.py:81
  112.0 6.1 %all-to-all-start.3 = ((bf16[8,192,128]{2,1,0:T(8,128)(2,1)}), bf16[8,192,128]{2,1,0:T(8,128)(2,1)S(1)}, u32[]{:S(2)}, u32[]{:S(2)}) async-start(bf16[8,192,128]{2,1,0:T(8,128)(2,1)} %get-tuple-element.56), calls=%async_computation.3 | async-start | bytes 786432 | tf_op jit(solution)/shard_map/all_to_all | solution.py:729
  118.2 2.6 %shard_map.238 = bf16[8,96,768]{2,1,0:T(8,128)(2,1)} custom-call(bf16[768,256]{1,0:T(8,128)(2,1)} %copy-done.12, bf16[256,768]{1,0:T(8,128)(2,1)} %get-tuple-element.64.low_ref), custom_call_target="tpu_custom_call" | custom-call | flops 2200000000 | tf_op jit(solution)/shard_map/pallas_call | solution.py:81
  120.8 6.1 %all-to-all-done.3.da_ref = bf16[8,192,128]{2,1,0:T(8,128)(2,1)S(1)} async-done(((bf16[8,192,128]{2,1,0:T(8,128)(2,1)}), bf16[8,192,128]{2,1,0:T(8,128)(2,1)S(1)}, u32[]{:S(2)}, u32[]{:S(2)}) %all-to-all-start.3) | async-done | bytes 393248 | tf_op jit(solution)/shard_map/all_to_all | solution.py:729
  126.9 3.8 %all-to-all-start.4 = ((bf16[8,96,768]{2,1,0:T(8,128)(2,1)}), bf16[8,96,768]{2,1,0:T(8,128)(2,1)S(1)}, u32[]{:S(2)}, u32[]{:S(2)}) async-start(bf16[8,96,768]{2,1,0:T(8,128)(2,1)} %shard_map.238), calls=%async_computation.4 | async-start | bytes 2359296 | tf_op jit(solution)/shard_map/all_to_all | solution.py:730
  130.7 18.1 %shard_map.237 = (bf16[192,1024]{1,0:T(8,128)(2,1)}, bf16[384,1024]{1,0:T(8,128)(2,1)}, bf16[384,1024]{1,0:T(8,128)(2,1)}) custom-call(s32[2]{0:T(128)} %lengths_ref.3, bf16[192,1024]{1,0:T(8,128)(2,1)} %copy-done.17, bf16[384,1024]{1,0:T(8,128)(2,1)} %copy-done.3, bf16[384,1024]{1,0:T(8,128)(2,1)} %copy-done.4, f32[192,1024]{1,0:T(8,128)} %copy-done.18, ...), custom_call_target="tpu_custom_call" | custom-call | flops 22000001024 | tf_op jit(solution)/shard_map/pallas_call | solution.py:81
  148.8 0.6 collective-permute-start.7
  149.5 1.2 all-to-all-done.4.out_ref
  150.6 1.0 collective-permute-done.7.partner_ref
  151.6 0.1 copy-done.22
  151.7 0.8 copy-done.28
  152.5 8.7 %shard_map.239 = (bf16[8,128,768]{2,1,0:T(8,128)(2,1)}, bf16[4,2,48,768]{3,2,1,0:T(8,128)(2,1)}, bf16[4,2,48,768]{3,2,1,0:T(8,128)(2,1)}) custom-call(bf16[8,128,768]{2,1,0:T(8,128)(2,1)} %copy-done, bf16[192,1024]{1,0:T(8,128)(2,1)} %get-tuple-element.57.dq_ref, bf16[384,1024]{1,0:T(8,128)(2,1)} %get-tuple-element.58.dkv_ref, bf16[384,1024]{1,0:T(8,128)(2,1)} %copy-done.28, ...), custom_call_target="tpu_custom_call" | custom-call | flops 7699999744 | tf_op jit(solution)/shard_map/pallas_call | solution.py:81
  161.2 0.4 collective-permute-start.8
  161.6 4.4 %all-to-all-start.5 = ((bf16[8,128,768]{2,1,0:T(8,128)(2,1)}), bf16[8,128,768]{2,1,0:T(8,128)(2,1)S(1)}, u32[]{:S(2)}, u32[]{:S(2)}) async-start(bf16[8,128,768]{2,1,0:T(8,128)(2,1)} %get-tuple-element.65), calls=%async_computation.5 | async-start | bytes 3145728 | tf_op jit(solution)/shard_map/all_to_all | solution.py:773
  166.0 0.1 add_convert_fusion
  166.1 1.1 collective-permute-start.9
  167.2 3.2 %collective-permute-start.11 = (bf16[2,48,768]{2,1,0:T(8,128)(2,1)S(1)}, bf16[2,48,768]{2,1,0:T(8,128)(2,1)S(1)}, u32[]{:S(2)}, u32[]{:S(2)}) collective-permute-start(bf16[2,48,768]{2,1,0:T(8,128)(2,1)S(1)} %get-tuple-element.79), channel_id=1, source_target_pairs={{0,3},{1,0},{2,1},{3,2},{4,7},{5,4},{6,5},{7,6},{8,11},{9,8},{10,9... | collective-permute-start | bytes 442376 | tf_op jit(solution)/shard_map/ppermute | solution.py:770
  170.5 1.6 collective-permute-start.10
  172.1 2.4 %collective-permute-done.9 = bf16[2,48,768]{2,1,0:T(8,128)(2,1)S(1)} collective-permute-done((bf16[2,48,768]{2,1,0:T(8,128)(2,1)S(1)}, bf16[2,48,768]{2,1,0:T(8,128)(2,1)S(1)}, u32[]{:S(2)}, u32[]{:S(2)}) %collective-permute-start.9) | collective-permute-done | bytes 147488 | tf_op jit(solution)/shard_map/ppermute | solution.py:768
  174.5 1.8 collective-permute-done.11
  176.3 6.1 %collective-permute-done.10 = bf16[2,48,768]{2,1,0:T(8,128)(2,1)S(1)} collective-permute-done((bf16[2,48,768]{2,1,0:T(8,128)(2,1)S(1)}, bf16[2,48,768]{2,1,0:T(8,128)(2,1)S(1)}, u32[]{:S(2)}, u32[]{:S(2)}) %collective-permute-start.10) | collective-permute-done | bytes 147488 | tf_op jit(solution)/shard_map/ppermute | solution.py:769
  182.4 0.1 fusion.2
  182.5 0.1 collective-permute-start.12
  182.6 4.3 %collective-permute-done.12 = bf16[48,768]{1,0:T(8,128)(2,1)S(1)} collective-permute-done((bf16[48,768]{1,0:T(8,128)(2,1)S(1)}, bf16[48,768]{1,0:T(8,128)(2,1)S(1)}, u32[]{:S(2)}, u32[]{:S(2)}) %collective-permute-start.12) | collective-permute-done | bytes 73760 | tf_op jit(solution)/shard_map/ppermute | solution.py:772
  187.0 1.1 copy-done.5
  188.0 1.5 shard_map.241
  189.5 0.8 all-to-all-done.5.got_ref
  190.3 6.1 %all-to-all-start.6 = ((bf16[8,64,768]{2,1,0:T(8,128)(2,1)}), bf16[8,64,768]{2,1,0:T(8,128)(2,1)S(1)}, u32[]{:S(2)}, u32[]{:S(2)}) async-start(bf16[8,64,768]{2,1,0:T(8,128)(2,1)} %shard_map.241), calls=%async_computation.7 | async-start | bytes 1572864 | tf_op jit(solution)/shard_map/all_to_all | solution.py:789
  196.4 1.2 copy.34
  197.6 1.1 copy-done.13
  198.7 1.3 shard_map.240
  200.0 1.1 copy.33
  201.2 5.5 %all-to-all-done.6.got_ref = bf16[8,64,768]{2,1,0:T(8,128)(2,1)S(1)} async-done(((bf16[8,64,768]{2,1,0:T(8,128)(2,1)}), bf16[8,64,768]{2,1,0:T(8,128)(2,1)S(1)}, u32[]{:S(2)}, u32[]{:S(2)}) %all-to-all-start.6) | async-done | bytes 786464 | tf_op jit(solution)/shard_map/all_to_all | solution.py:789
  206.6 1.9 shard_map.242
  (62 shorter events, 0.3 us)
Async XLA Ops:
  7.2 89.0 %all-gather.3.cloned.1.call-start = ((), (), s32[]{:S(2)}) async-start(), calls=%async_computation.9 | async-start | bytes 11280384 | tf_op jit(solution)/shard_map/all_gather | solution.py:676
  7.2 20.2 %copy-start.10 = (s32[1,512]{1,0:T(1,128)S(1)}, s32[1,512]{1,0:T(1,128)}, u32[]{:S(2)}) copy-start(s32[1,512]{1,0:T(1,128)} %constant.12.clone.order_ref) | copy-start | bytes 6148
  27.5 1.5 copy-start.24
  29.0 1.4 copy-start.1
  30.4 25.3 %copy-start.8 = (s32[1,768]{1,0:T(1,128)S(1)}, s32[1,768]{1,0:T(1,128)}, u32[]{:S(2)}) copy-start(s32[1,768]{1,0:T(1,128)} %constant.13.clone.order_ref) | copy-start | bytes 9220
  30.4 25.3 %all-to-all-start = ((bf16[8,128,768]{2,1,0:T(8,128)(2,1)}), bf16[8,128,768]{2,1,0:T(8,128)(2,1)S(1)}, u32[]{:S(2)}, u32[]{:S(2)}) async-start(bf16[8,128,768]{2,1,0:T(8,128)(2,1)} %bitcast.50), calls=%async_computation | async-start | bytes 3145728 | tf_op jit(solution)/shard_map/all_to_all | solution.py:685
  34.1 5.7 %collective-permute-start.2 = (bf16[48,640]{1,0:T(8,128)(2,1)S(1)}, bf16[48,640]{1,0:T(8,128)(2,1)S(1)}, u32[]{:S(2)}, u32[]{:S(2)}) collective-permute-start(bf16[48,640]{1,0:T(8,128)(2,1)S(1)} %get-tuple-element.44), channel_id=1, source_target_pairs={{0,1},{1,2},{2,3},{3,0},{4,5},{5,6},{6,7},{7,4},{8,9},{9,10},{10,1... | collective-permute-start | bytes 184328 | tf_op jit(solution)/shard_map/ppermute | solution.py:678
  35.6 5.8 %collective-permute-start.1 = (bf16[48,640]{1,0:T(8,128)(2,1)S(1)}, bf16[48,640]{1,0:T(8,128)(2,1)S(1)}, u32[]{:S(2)}, u32[]{:S(2)}) collective-permute-start(bf16[48,640]{1,0:T(8,128)(2,1)S(1)} %get-tuple-element.44), channel_id=1, source_target_pairs={{0,2},{1,3},{2,0},{3,1},{4,6},{5,7},{6,4},{7,5},{8,10},{9,11},{10,... | collective-permute-start | bytes 184328 | tf_op jit(solution)/shard_map/ppermute | solution.py:678
  38.4 4.9 %collective-permute-start = (bf16[48,640]{1,0:T(8,128)(2,1)S(1)}, bf16[48,640]{1,0:T(8,128)(2,1)S(1)}, u32[]{:S(2)}, u32[]{:S(2)}) collective-permute-start(bf16[48,640]{1,0:T(8,128)(2,1)S(1)} %get-tuple-element.44), channel_id=1, source_target_pairs={{0,3},{1,0},{2,1},{3,2},{4,7},{5,4},{6,5},{7,6},{8,11},{9,8},{10,9... | collective-permute-start | bytes 184328 | tf_op jit(solution)/shard_map/ppermute | solution.py:678
  43.3 19.9 %copy-start.6 = (s32[2]{0:T(128)S(1)}, s32[2]{0:T(128)}, u32[]{:S(2)}) copy-start(s32[2]{0:T(128)} %lengths_ref.3) | copy-start | bytes 28
  43.3 9.4 %collective-permute-start.3 = (bf16[4,48,640]{2,1,0:T(8,128)(2,1)S(1)}, bf16[4,48,640]{2,1,0:T(8,128)(2,1)S(1)}, u32[]{:S(2)}, u32[]{:S(2)}) collective-permute-start(bf16[4,48,640]{2,1,0:T(8,128)(2,1)S(1)} %pad_maximum_fusion.near_ref), channel_id=1, source_target_pairs={{0,20},{1,21},{2,22},{3,23},{4,16},{5,17},{6,18},{7,19},{8,28},{9,... | collective-permute-start | bytes 737288 | tf_op jit(solution)/shard_map/ppermute | solution.py:680
  43.7 9.0 %collective-permute-start.4 = (bf16[4,48,640]{2,1,0:T(8,128)(2,1)S(1)}, bf16[4,48,640]{2,1,0:T(8,128)(2,1)S(1)}, u32[]{:S(2)}, u32[]{:S(2)}) collective-permute-start(bf16[4,48,640]{2,1,0:T(8,128)(2,1)S(1)} %pad_maximum_fusion.near_ref), channel_id=1, source_target_pairs={{0,8},{8,0},{16,24},{24,16},{32,40},{40,32},{48,56},{56,48},{64,72... | collective-permute-start | bytes 737288 | tf_op jit(solution)/shard_map/ppermute | solution.py:681
  52.7 1.5 collective-permute-start.5
  55.7 3.0 %copy-start = (bf16[8,128,768]{2,1,0:T(8,128)(2,1)}, bf16[8,128,768]{2,1,0:T(8,128)(2,1)S(1)}, u32[]{:S(2)}) copy-start(bf16[8,128,768]{2,1,0:T(8,128)(2,1)S(1)} %all-to-all-done.own_ref) | copy-start | bytes 4718596
  58.7 1.2 copy-start.15
  59.9 1.0 copy-start.16
  60.9 11.8 %copy-start.3 = (bf16[384,1024]{1,0:T(8,128)(2,1)}, bf16[384,1024]{1,0:T(8,128)(2,1)S(1)}, u32[]{:S(2)}) copy-start(bf16[384,1024]{1,0:T(8,128)(2,1)S(1)} %get-tuple-element.46.own_ref) | copy-start | bytes 2359300
  60.9 11.8 %copy-start.17 = (bf16[192,1024]{1,0:T(8,128)(2,1)}, bf16[192,1024]{1,0:T(8,128)(2,1)S(1)}, u32[]{:S(2)}) copy-start(bf16[192,1024]{1,0:T(8,128)(2,1)S(1)} %get-tuple-element.45.q_ref) | copy-start | bytes 1179652
  60.9 11.8 %copy-start.19 = (f32[8,768]{1,0:T(8,128)}, f32[8,768]{1,0:T(8,128)S(1)}, u32[]{:S(2)}) copy-start(f32[8,768]{1,0:T(8,128)S(1)} %get-tuple-element.49.gains_hbm.gains_ref) | copy-start | bytes 73732
  60.9 2.3 %collective-permute-start.6 = (bf16[384,1024]{1,0:T(8,128)(2,1)S(1)}, bf16[384,1024]{1,0:T(8,128)(2,1)S(1)}, u32[]{:S(2)}, u32[]{:S(2)}) collective-permute-start(bf16[384,1024]{1,0:T(8,128)(2,1)S(1)} %get-tuple-element.46.own_ref), channel_id=1, source_target_pairs={{0,8},{8,0},{16,24},{24,16},{32,40},{40,32},{48,56},{56,48},{64,72... | collective-permute-start | bytes 2359304 | tf_op jit(solution)/shard_map/ppermute | solution.py:699
  63.2 9.6 %copy-start.4 = (bf16[384,1024]{1,0:T(8,128)(2,1)}, bf16[384,1024]{1,0:T(8,128)(2,1)S(1)}, u32[]{:S(2)}) copy-start(bf16[384,1024]{1,0:T(8,128)(2,1)S(1)} %collective-permute-done.6.other_ref) | copy-start | bytes 2359300
  63.2 14.9 %copy-start.25 = (bf16[128,2,768]{2,1,0:T(2,128)(2,1)S(1)}, bf16[128,2,768]{2,1,0:T(2,128)(2,1)}, u32[]{:S(2)}) copy-start(bf16[128,2,768]{2,1,0:T(2,128)(2,1)} %param.26) | copy-start | bytes 1179652
  72.8 0.9 copy-start.18
  73.7 0.6 copy-start.21
  74.3 12.3 %copy-start.9 = (s32[1,768]{1,0:T(1,128)S(1)}, s32[1,768]{1,0:T(1,128)}, u32[]{:S(2)}) copy-start(s32[1,768]{1,0:T(1,128)} %constant.10.clone.order_ref) | copy-start | bytes 9220
  74.3 12.3 %all-to-all-start.2 = ((bf16[8,192,128]{2,1,0:T(8,128)(2,1)}), bf16[8,192,128]{2,1,0:T(8,128)(2,1)S(1)}, u32[]{:S(2)}, u32[]{:S(2)}) async-start(bf16[8,192,128]{2,1,0:T(8,128)(2,1)} %get-tuple-element.47), calls=%async_computation.2 | async-start | bytes 786432 | tf_op jit(solution)/shard_map/all_to_all | solution.py:716
  77.9 109.1 %reduce-scatter.2.cloned.1.call-start = ((), (), s32[]{:S(2)}) async-start(), calls=%async_computation.8 | async-start | bytes 10027008 | tf_op jit(solution)/shard_map/reduce_scatter | solution.py:725
  87.3 1.1 copy-start.11
  88.4 0.8 copy-start.12
  89.1 0.8 copy-start.14
  112.0 14.9 %all-to-all-start.3 = ((bf16[8,192,128]{2,1,0:T(8,128)(2,1)}), bf16[8,192,128]{2,1,0:T(8,128)(2,1)S(1)}, u32[]{:S(2)}, u32[]{:S(2)}) async-start(bf16[8,192,128]{2,1,0:T(8,128)(2,1)} %get-tuple-element.56), calls=%async_computation.3 | async-start | bytes 786432 | tf_op jit(solution)/shard_map/all_to_all | solution.py:729
  126.9 3.8 %copy-start.27 = (bf16[8,192,128]{2,1,0:T(8,128)(2,1)}, bf16[8,192,128]{2,1,0:T(8,128)(2,1)S(1)}, u32[]{:S(2)}) copy-start(bf16[8,192,128]{2,1,0:T(8,128)(2,1)S(1)} %all-to-all-done.3.da_ref) | copy-start | bytes 1179652
  126.9 23.7 %all-to-all-start.4 = ((bf16[8,96,768]{2,1,0:T(8,128)(2,1)}), bf16[8,96,768]{2,1,0:T(8,128)(2,1)S(1)}, u32[]{:S(2)}, u32[]{:S(2)}) async-start(bf16[8,96,768]{2,1,0:T(8,128)(2,1)} %shard_map.238), calls=%async_computation.4 | async-start | bytes 2359296 | tf_op jit(solution)/shard_map/all_to_all | solution.py:730
  148.8 2.7 %collective-permute-start.7 = (bf16[384,1024]{1,0:T(8,128)(2,1)}, bf16[384,1024]{1,0:T(8,128)(2,1)S(1)}, u32[]{:S(2)}, u32[]{:S(2)}) collective-permute-start(bf16[384,1024]{1,0:T(8,128)(2,1)} %get-tuple-element.59), channel_id=1, source_target_pairs={{0,8},{8,0},{16,24},{24,16},{32,40},{40,32},{48,56},{56,48},{64,72... | collective-permute-start | bytes 2359304 | tf_op jit(solution)/shard_map/ppermute | solution.py:752
  150.6 1.0 copy-start.22
  151.6 0.9 copy-start.28
  161.2 4.8 %collective-permute-start.8 = (bf16[4,2,48,768]{3,2,1,0:T(8,128)(2,1)}, bf16[4,2,48,768]{3,2,1,0:T(8,128)(2,1)S(1)}, u32[]{:S(2)}, u32[]{:S(2)}) collective-permute-start(bf16[4,2,48,768]{3,2,1,0:T(8,128)(2,1)} %get-tuple-element.67), channel_id=1, source_target_pairs={{0,8},{8,0},{16,24},{24,16},{32,40},{40,32},{48,56},{56,48},{64,72... | collective-permute-start | bytes 1769480 | tf_op jit(solution)/shard_map/ppermute | solution.py:765
  161.6 4.4 %copy-start.23 = (bf16[4,2,48,768]{3,2,1,0:T(8,128)(2,1)S(1)}, bf16[4,2,48,768]{3,2,1,0:T(8,128)(2,1)}, u32[]{:S(2)}) copy-start(bf16[4,2,48,768]{3,2,1,0:T(8,128)(2,1)} %get-tuple-element.66) | copy-start | bytes 1769476
  161.6 28.7 %all-to-all-start.5 = ((bf16[8,128,768]{2,1,0:T(8,128)(2,1)}), bf16[8,128,768]{2,1,0:T(8,128)(2,1)S(1)}, u32[]{:S(2)}, u32[]{:S(2)}) async-start(bf16[8,128,768]{2,1,0:T(8,128)(2,1)} %get-tuple-element.65), calls=%async_computation.5 | async-start | bytes 3145728 | tf_op jit(solution)/shard_map/all_to_all | solution.py:773
  166.1 8.3 %collective-permute-start.9 = (bf16[2,48,768]{2,1,0:T(8,128)(2,1)S(1)}, bf16[2,48,768]{2,1,0:T(8,128)(2,1)S(1)}, u32[]{:S(2)}, u32[]{:S(2)}) collective-permute-start(bf16[2,48,768]{2,1,0:T(8,128)(2,1)S(1)} %get-tuple-element.78), channel_id=1, source_target_pairs={{0,1},{1,2},{2,3},{3,0},{4,5},{5,6},{6,7},{7,4},{8,9},{9,10},{10,1... | collective-permute-start | bytes 442376 | tf_op jit(solution)/shard_map/ppermute | solution.py:768
  167.2 9.0 %collective-permute-start.11 = (bf16[2,48,768]{2,1,0:T(8,128)(2,1)S(1)}, bf16[2,48,768]{2,1,0:T(8,128)(2,1)S(1)}, u32[]{:S(2)}, u32[]{:S(2)}) collective-permute-start(bf16[2,48,768]{2,1,0:T(8,128)(2,1)S(1)} %get-tuple-element.79), channel_id=1, source_target_pairs={{0,3},{1,0},{2,1},{3,2},{4,7},{5,4},{6,5},{7,6},{8,11},{9,8},{10,9... | collective-permute-start | bytes 442376 | tf_op jit(solution)/shard_map/ppermute | solution.py:770
  170.5 11.9 %collective-permute-start.10 = (bf16[2,48,768]{2,1,0:T(8,128)(2,1)S(1)}, bf16[2,48,768]{2,1,0:T(8,128)(2,1)S(1)}, u32[]{:S(2)}, u32[]{:S(2)}) collective-permute-start(bf16[2,48,768]{2,1,0:T(8,128)(2,1)S(1)} %get-tuple-element.80), channel_id=1, source_target_pairs={{0,2},{1,3},{2,0},{3,1},{4,6},{5,7},{6,4},{7,5},{8,10},{9,11},{10,... | collective-permute-start | bytes 442376 | tf_op jit(solution)/shard_map/ppermute | solution.py:769
  182.5 4.4 %collective-permute-start.12 = (bf16[48,768]{1,0:T(8,128)(2,1)S(1)}, bf16[48,768]{1,0:T(8,128)(2,1)S(1)}, u32[]{:S(2)}, u32[]{:S(2)}) collective-permute-start(bf16[48,768]{1,0:T(8,128)(2,1)S(1)} %slice_bitcast_fusion.4), channel_id=1, source_target_pairs={{0,20},{1,21},{2,22},{3,23},{4,16},{5,17},{6,18},{7,19},{8,28},{9,... | collective-permute-start | bytes 221192 | tf_op jit(solution)/shard_map/ppermute | solution.py:772
  187.0 1.1 copy-start.5
  189.5 6.9 %copy-start.26 = (bf16[256,768]{1,0:T(8,128)(2,1)S(1)}, bf16[256,768]{1,0:T(8,128)(2,1)}, u32[]{:S(2)}) copy-start(bf16[256,768]{1,0:T(8,128)(2,1)} %get-tuple-element.52) | copy-start | bytes 1179652
  189.5 8.1 %copy-start.2 = (bf16[2,128,768]{2,1,0:T(8,128)(2,1)S(1)}, bf16[2,128,768]{2,1,0:T(8,128)(2,1)}, u32[]{:S(2)}) copy-start(bf16[2,128,768]{2,1,0:T(8,128)(2,1)} %copy-done.1) | copy-start | bytes 1179652
  189.5 8.1 %copy-start.20 = (f32[8,768]{1,0:T(8,128)S(1)}, f32[8,768]{1,0:T(8,128)}, u32[]{:S(2)}) copy-start(f32[8,768]{1,0:T(8,128)} %copy-done.19) | copy-start | bytes 73732
  190.3 16.4 %all-to-all-start.6 = ((bf16[8,64,768]{2,1,0:T(8,128)(2,1)}), bf16[8,64,768]{2,1,0:T(8,128)(2,1)S(1)}, u32[]{:S(2)}, u32[]{:S(2)}) async-start(bf16[8,64,768]{2,1,0:T(8,128)(2,1)} %shard_map.241), calls=%async_computation.7 | async-start | bytes 1572864 | tf_op jit(solution)/shard_map/all_to_all | solution.py:789
  197.6 1.1 copy-start.13
  198.7 7.9 %copy-start.7 = (s32[1,768]{1,0:T(1,128)S(1)}, s32[1,768]{1,0:T(1,128)}, u32[]{:S(2)}) copy-start(s32[1,768]{1,0:T(1,128)} %constant.11.clone.units_ref) | copy-start | bytes 9220
Sparse Core Ops, SparseCore 0:
  29.1 67.0 all-gather.2
  112.2 71.7 reduce-scatter.1

commit v6 on v5

--- a/solution.py
+++ b/solution.py
@@ -52,13 +52,20 @@
 
 
 REGROUP = regroup_order()
+
+
+def arrival_places():
+    s, j, dz, dx, r = np.indices((2, 8, 2, 4, 6), dtype=np.int32).reshape(5, 768)
+    return np.stack([j ^ dz, s, dz, dx, r] + [np.zeros_like(r)] * 3)
+
+
+ARRIVAL = arrival_places()
 SPREAD = np.concatenate(
     [np.arange(96, dtype=np.int32).reshape(16, 6), np.full((16, 2), -1, np.int32)], axis=1
 ).reshape(128, 1)
 
 
-def places(order_ref):
-    order = order_ref[...]
+def places(order):
     size = order.shape[1]
     rows = lax.broadcasted_iota(jnp.int32, (size, size), 0)
     return jnp.where(rows == order, 1.0, 0.0).astype(BF)
@@ -102,7 +109,7 @@
 
 def pack_kernel(
     down_ref, out_ref, up_ref, qkv_ref, g1_ref, b1_ref, g2_ref, b2_ref, units_ref,
-    slot_ref, scr, turn_scr,
+    slot_ref, raw_ref, scr, turn_scr, raw_scr,
 ):
     turn_scr[...] = jnp.zeros_like(turn_scr)
     for i, ref in enumerate((g1_ref, b1_ref, g2_ref, b2_ref)):
@@ -113,21 +120,33 @@
     ).astype(BF)
     scr[0:24, :] = down_ref[...].astype(F32)
     scr[24:30, :] = out_ref[...].astype(F32)
-    scr[30:54, :] = dot(up, places(units_ref))
-    scr[60:64, :] = jnp.zeros((4, 768), F32)
+    scr[30:54, :] = dot(up, places(units_ref[...]))
+    scr[54:64, :] = jnp.zeros((10, 768), F32)
+    slot = scr[...].astype(BF)
+    for j in range(8):
+        slot_ref[j] = slot
     for e in range(4):
         parts = [qkv_ref[:, s * 768 + e * 192 : s * 768 + (e + 1) * 192] for s in range(3)]
-        row = jnp.concatenate(parts + [norms, jnp.zeros((6, 128), BF)], axis=1)
-        scr[54:60, :] = row.astype(F32)
-        slot = scr[...].astype(BF)
-        slot_ref[2 * e] = slot
-        slot_ref[2 * e + 1] = slot
-
-
-def regroup_kernel(slots_ref, order_ref, rest_ref, qkv_ref):
-    rows = dot(places(order_ref), slots_ref[...].reshape(512, 768), TN).astype(BF)
+        row = jnp.concatenate(parts + [norms], axis=1)
+        raw_scr[e * 6 : e * 6 + 6, :] = row.astype(F32)
+    raw_ref[...] = raw_scr[...].astype(BF)
+
+
+def regroup_kernel(slots_ref, order_ref, far_ref, rest_ref):
+    rows = dot(places(order_ref[...]), slots_ref[...].reshape(512, 768), TN).astype(BF)
     rest_ref[...] = rows[0:432]
-    qkv_ref[...] = rows[432:480, 0:640]
+
+
+def address_kernel(x_ref, near_ref, far_ref, out_ref, scr):
+    for e in range(4):
+        for dz, ref in enumerate((near_ref, far_ref)):
+            for dx in range(4):
+                first = (dz * 4 + dx) * 6
+                scr[e, first : first + 6, :] = ref[dx].astype(F32)[e * 6 : e * 6 + 6]
+        for b in range(2):
+            out_ref[2 * e + b, 0:128, :] = x_ref[b]
+            out_ref[2 * e + b, 128:176, 0:640] = scr[e].astype(BF)
+            out_ref[2 * e + b, 128:176, 640:768] = jnp.zeros((48, 128), BF)
 
 
 def core_of():
@@ -147,19 +166,26 @@
 
 
 def project_kernel(
-    own_ref, near_ref, far_ref, near_other_ref, far_other_ref, order_ref,
+    own_ref, other_ref, arrival_ref,
     normed_ref, wt_ref, gains_ref, q_ref, kv_ref, w_scr, t_scr,
 ):
-    for i, ref in enumerate((near_ref, far_ref, near_other_ref, far_other_ref)):
-        for dx in range(4):
-            w_scr[rows_at(i // 2, i % 2, dx), :] = ref[dx]
-    t_scr[...] = dot(w_scr[...].T, places(order_ref), NT)
+    for j in range(8):
+        w_scr[j * 48 : j * 48 + 48, :] = own_ref[j, 128:176, 0:640]
+        w_scr[384 + j * 48 : 432 + j * 48, :] = other_ref[j]
+    core, row = core_of(), lax.axis_index("batch")
+    half, column = row // 4, lax.rem(row, 4)
+    table = [arrival_ref[i : i + 1, :] for i in range(5)]
+    c = jnp.where(table[1] == 0, core, 1 - core)
+    z = jnp.where(table[2] == 0, half, 1 - half)
+    x = jnp.bitwise_and(table[3] + column, 3)
+    order = ((table[0] * 2 + c) * 8 + z * 4 + x) * 6 + table[4]
+    t_scr[...] = dot(w_scr[...].T, places(order), NT)
     wt_ref[...] = t_scr[0:576].astype(BF)
     gains = t_scr[576:584]
     gains_ref[...] = gains
     gain, bias = gains[0:1], gains[1:2]
     for j in range(8):
-        hat, _ = normalize(own_ref[j].astype(F32))
+        hat, _ = normalize(own_ref[j, 0:128, :].astype(F32))
         normed_ref[j * 128 : (j + 1) * 128, :] = (hat * gain + bias).astype(BF)
     for j in range(4):
         lanes = slice(j * 256, (j + 1) * 256)
@@ -421,7 +447,7 @@
 
 
 def prepare_kernel(att_ref, order_ref, place_ref, attended_ref, attended_t_ref):
-    place_ref[...] = places(order_ref)
+    place_ref[...] = places(order_ref[...])
     for b in range(2):
         for e in range(4):
             attended_t_ref[e * 192 : (e + 1) * 192, b * 128 : (b + 1) * 128] = att_ref[2 * e + b]
@@ -563,7 +589,8 @@
     for j in range(4):
         d_normed = dot(dt_scr[:, j * 256 : (j + 1) * 256].T, wt_ref[...])
         part_ref[2 * j : 2 * j + 2] = d_normed.astype(BF).reshape(2, 128, 768)
-        hat, _ = normalize(own_ref[2 * j : 2 * j + 2].reshape(256, 768).astype(F32))
+        pair = jnp.concatenate([own_ref[2 * j, 0:128, :], own_ref[2 * j + 1, 0:128, :]], axis=0)
+        hat, _ = normalize(pair.astype(F32))
         gain_sum += jnp.sum(d_normed * hat, axis=0, keepdims=True)
         bias_sum += jnp.sum(d_normed, axis=0, keepdims=True)
     dw_scr[0:576, :] = dot(dt_scr[...], normed_ref[...])
@@ -571,7 +598,7 @@
     dw_scr[577:578, :] = bias_sum
     dw_scr[578:580, :] = dgain_ref[0:2, :]
     dw_scr[580:640, :] = jnp.zeros((60, 768), F32)
-    p_scr[...] = dot(dw_scr[...].astype(BF), places(order_ref)).T.astype(BF)
+    p_scr[...] = dot(dw_scr[...].astype(BF), places(order_ref[...])).T.astype(BF)
     out = jnp.zeros((96, 768), F32)
     for j in range(8):
         out += out_ref[j].astype(F32)
@@ -594,7 +621,7 @@
     r_scr[432:480, 0:640] = qkv_ref[:, 0:640]
     r_scr[432:480, 640:768] = jnp.zeros((48, 128), BF)
     r_scr[480:512, :] = jnp.zeros((32, 768), BF)
-    out_ref[...] = dot(places(order_ref), r_scr[...]).astype(BF).reshape(8, 64, 768)
+    out_ref[...] = dot(places(order_ref[...]), r_scr[...]).astype(BF).reshape(8, 64, 768)
 
 
 def finish_kernel(x_ref, dfirst_ref, gains_ref, got_ref, qkv_ref, dtok_ref, out_ref):
@@ -620,7 +647,7 @@
         chunks.append(both[54:60])
         total += both
     down_ref[...] = total[0:24]
-    left, up, units = total[30:54], jnp.zeros((24, 768), F32), places(units_ref)
+    left, up, units = total[30:54], jnp.zeros((24, 768), F32), places(units_ref[...])
     for _ in range(3):
         piece = left.astype(BF)
         left = left - piece.astype(F32)
@@ -653,36 +680,45 @@
     )
 
     vectors = [v.reshape(1, 6) for v in (gain_one, bias_one, gain_two, bias_two)]
-    slots = pl.pallas_call(
+    slots, raw = pl.pallas_call(
         pack_kernel,
         grid=(1,),
         in_specs=[whole(24, 768), whole(6, 768), whole(6, 3072), whole(6, 2304)]
         + [whole(1, 6)] * 4
         + [whole(1, 768)],
-        out_specs=whole(8, 64, 768),
-        out_shape=shape((8, 64, 768), BF),
-        scratch_shapes=[pltpu.VMEM((64, 768), F32), pltpu.VMEM((128, 128), F32)],
+        out_specs=[whole(8, 64, 768), whole(24, 640)],
+        out_shape=[shape((8, 64, 768), BF), shape((24, 640), BF)],
+        scratch_shapes=[
+            pltpu.VMEM((64, 768), F32), pltpu.VMEM((128, 128), F32), pltpu.VMEM((24, 640), F32),
+        ],
         cost_estimate=about(2),
         compiler_params=pltpu.CompilerParams(vmem_limit_bytes=60 * 1024 * 1024),
     )(w_down, w_out, w_up, w_qkv, *vectors, units)
     slots = exchange(slots)
-    rest, qkv_rows = call(
+    near = jnp.stack([raw] + [lax.ppermute(raw, "batch", along_x(step)) for step in (-1, 2, 1)])
+    far = lax.ppermute(near, BOTH, SWAP_HALF)
+    rest = call(
         regroup_kernel,
-        [shape((432, 768), BF), shape((48, 640), BF)],
-        (slots, regroup),
+        shape((432, 768), BF),
+        (slots, regroup, far),
         2,
         mib=12,
+        in_specs=[pl.BlockSpec(memory_space=pltpu.VMEM)] * 2
+        + [pl.BlockSpec(memory_space=pl.ANY)],
     )
     weights = lax.all_gather(rest, BOTH, axis=0, axis_index_groups=RINGS)
-    near = jnp.stack(
-        [qkv_rows] + [lax.ppermute(qkv_rows, "batch", along_x(step)) for step in (-1, 2, 1)]
-    )
-    far = lax.ppermute(near, BOTH, SWAP_HALF)
-    near_other = lax.ppermute(near, "seq", SWAP_CORE)
-    far_other = lax.ppermute(far, "seq", SWAP_CORE)
     x = tokens.transpose(1, 0, 2)
     dy = d_out.transpose(1, 0, 2).reshape(256, 768)
-    own = exchange(jnp.broadcast_to(x[None], (4, 2, 128, 768)).reshape(8, 128, 768))
+    sent = call(
+        address_kernel,
+        shape((8, 176, 768), BF),
+        (x, near, far),
+        2,
+        [pltpu.VMEM((4, 48, 640), F32)],
+        mib=16,
+    )
+    own = exchange(sent)
+    other = lax.ppermute(own[:, 128:176, 0:640], "seq", SWAP_CORE)
     x = x.reshape(256, 768)
 
     normed, wt, gains, q_t, kv = call(
@@ -691,7 +727,7 @@
             shape((1024, 768), BF), shape((576, 768), BF), shape((8, 768), F32),
             shape((192, 1024), BF), shape((384, 1024), BF),
         ],
-        (own, near, far, near_other, far_other, qkv_order),
+        (own, other, jnp.asarray(ARRIVAL)),
         5,
         [pltpu.VMEM((768, 640), BF), pltpu.VMEM((640, 768), F32)],
         mib=30,

time: 218 us -> 219 us (level)
  blocking collectives: 18.1 us -> 31.7 us
  Pallas kernels: 66.9 us -> 56.6 us
  waiting for transfers between devices: 60.8 us -> 54.8 us
    all_to_all x1, blocking collectives: 18.1 us -> 31.7 us  [body(): own = exchange(sent)]
    pallas_call x11 -> x12, Pallas kernels: 64.7 us -> 54.5 us  [call(): pl.pallas_call(kernel, out_shape=outs, scratch_shapes=list(scratch), cost...]
    all_to_all x1, waiting for transfers between devices: 1.15 us -> 7.65 us  [body(): exchange(call(out_kernel, shape((8, 96, 768), BF), (attended_t, low), 2))]
    all_to_all x1 -> x2, starting transfers between devices: 6.15 us -> 11.7 us  [body(): slots = exchange(slots)]
    ppermute x1, waiting for transfers between devices: 8.99 us -> 4.42 us  [body(): far = lax.ppermute(near, BOTH, SWAP_HALF)]
    all_gather x1, waiting for transfers between devices: 6.32 us -> 2.4 us  [body(): weights = lax.all_gather(rest, BOTH, axis=0, axis_index_groups=RINGS)]
    all_to_all x1 -> x0, starting transfers between devices: 3.71 us -> none  [body(): exchange(jnp.broadcast_to(x[None], (4, 2, 128, 768)).reshape(8, 128, 768))]
    unnamed x58 -> x61, local copies, waits for them, and re-layouts: 9.39 us -> 10.2 us
  transfers between devices with their start and end apart: 21 -> 20, of which waited for: 17 -> 15; matrix products, arithmetic and copies ran while one was open for 2% -> 2% of each run, Pallas kernels for 21% -> 16%
where the time goes in v6:
time: 219 us; the launch traced here: 214 us
  Pallas kernels  56.6 us (26%)
  waiting for transfers between devices  54.8 us (25%)
  starting transfers between devices  43.2 us (20%)
  blocking collectives  31.7 us (14%)
  between operations  14.3 us (7%)
  local copies, waits for them, and re-layouts  13.4 us (6%)
    pallas_call x12, Pallas kernels, call(): pl.pallas_call(kernel, out_shape=outs, scratch_shapes=list(scratch), cost...  54.5 us
    all_to_all x1, blocking collectives, body(): own = exchange(sent)  31.7 us
    all_to_all x2, starting transfers between devices, body(): slots = exchange(slots)  11.7 us
    unnamed x61, local copies, waits for them, and re-layouts  10.2 us
    all_to_all x1, waiting for transfers between devices, body(): exchange(call(out_kernel, shape((8, 96, 768), BF), (attended_t, low), 2))  7.65 us
    all_to_all x1, waiting for transfers between devices, body(): att = exchange(o_low)  7.64 us
    all_to_all x1, waiting for transfers between devices, body(): d_att = exchange(d_att)  6.82 us
    ppermute x1, waiting for transfers between devices, body(): lax.ppermute(line[2], 'batch', along_x(2))  5.73 us
  transfers between devices with their start and end apart: 20, of which 15 were waited for; matrix products, arithmetic and copies ran while one was open for 2% of the time, Pallas kernels for 16%

profile of v6, /device:TPU:64, one launch (start us, length us, event | category | flops | bytes accessed | tf_op | source)
XLA Modules:
  0.0 214.3 jit_solution(12223720203640685098)
XLA Ops:
  7.2 2.1 shard_map.240
  9.3 5.7 %all-to-all-start.2 = ((bf16[8,64,768]{2,1,0:T(8,128)(2,1)}), bf16[8,64,768]{2,1,0:T(8,128)(2,1)S(1)}, u32[]{:S(2)}, u32[]{:S(2)}) async-start(bf16[8,64,768]{2,1,0:T(8,128)(2,1)} %get-tuple-element.51), calls=%async_computation.2 | async-start | bytes 1572864 | tf_op jit(solution)/shard_map/all_to_all | solution.py:697
  15.0 1.6 collective-permute-start.2
  16.6 2.7 %collective-permute-start.1 = (bf16[24,640]{1,0:T(8,128)(2,1)S(1)}, bf16[24,640]{1,0:T(8,128)(2,1)S(1)}, u32[]{:S(2)}, u32[]{:S(2)}) collective-permute-start(bf16[24,640]{1,0:T(8,128)(2,1)S(1)} %copy-done.28), channel_id=1, source_target_pairs={{0,2},{1,3},{2,0},{3,1},{4,6},{5,7},{6,4},{7,5},{8,10},{9,11},{10,... | collective-permute-start | bytes 92168 | tf_op jit(solution)/shard_map/ppermute | solution.py:698
  19.3 1.4 collective-permute-start
  20.8 1.2 collective-permute-done.1
  22.0 1.2 collective-permute-done
  23.3 0.5 collective-permute-start.3
  23.8 4.4 %collective-permute-done.3.far_ref = bf16[4,24,640]{2,1,0:T(8,128)(2,1)S(1)} collective-permute-done((bf16[4,24,640]{2,1,0:T(8,128)(2,1)S(1)}, bf16[4,24,640]{2,1,0:T(8,128)(2,1)S(1)}, u32[]{:S(2)}, u32[]{:S(2)}) %collective-permute-start.3) | collective-permute-done | bytes 122912 | tf_op jit(solution)/shard_map/ppermute | solution.py:699
  28.2 1.5 shard_map.245
  29.8 0.2 shard_map.241
  30.1 0.5 copy-done.1
  30.6 31.7 %all_to_all.35.own_ref = bf16[8,176,768]{2,1,0:T(8,128)(2,1)S(1)} all-to-all(bf16[8,176,768]{2,1,0:T(8,128)(2,1)S(1)} %shard_map.241), channel_id=1, replica_groups={{0,16,32,48,64,80,96,112},{8,24,40,56,72,88,104,120},{1,17,33,49,65,81,..., dimensions={0} | all-to-all | bytes 4325376 | tf_op jit(solution)/shard_map/all_to_all | solution.py:720
  62.3 0.1 collective-permute-start.4
  62.4 1.9 collective-permute-done.4.other_ref
  64.3 3.0 %shard_map.242 = (bf16[1024,768]{1,0:T(8,128)(2,1)S(1)}, bf16[576,768]{1,0:T(8,128)(2,1)S(1)}, f32[8,768]{1,0:T(8,128)S(1)}, bf16[192,1024]{1,0:T(8,128)(2,1)S(1)}, bf16[384,1024]{1,0:T(8,128)(2,1)S(1)}) custom-call(bf16[8,176,768]{2,1,0:T(8,128)(2,1)S(1)} %all_to_all.35.own_ref, bf16[8,48,640]{2,1,0:T(8,128)(2,1)S(1)} %collective-permute-done.4.other_ref, ...), custom_call_target="tpu_custom_call" | custom-call | flops 5500000256 | tf_op jit(solution)/shard_map/pallas_call | solution.py:88
  67.3 1.1 copy-done.15
  68.4 0.9 copy-done.16
  69.3 0.6 copy-done.19
  70.0 0.1 collective-permute-start.5
  70.1 2.1 %collective-permute-done.5.other_ref = bf16[384,1024]{1,0:T(8,128)(2,1)S(1)} collective-permute-done((bf16[384,1024]{1,0:T(8,128)(2,1)S(1)}, bf16[384,1024]{1,0:T(8,128)(2,1)S(1)}, u32[]{:S(2)}, u32[]{:S(2)}) %collective-permute-start.5) | collective-permute-done | bytes 786464 | tf_op jit(solution)/shard_map/ppermute | solution.py:735
  72.2 6.0 %shard_map.243 = (f32[192,1024]{1,0:T(8,128)S(1)}, bf16[8,192,128]{2,1,0:T(8,128)(2,1)}, f32[3,1024]{1,0:T(4,128)S(1)}) custom-call(s32[2]{0:T(128)S(1)} %copy-done.6, bf16[192,1024]{1,0:T(8,128)(2,1)S(1)} %get-tuple-element.45.q_ref, bf16[384,1024]{1,0:T(8,128)(2,1)S(1)} %get-tuple-element.46.own_ref, bf16[384,1024]{1,0:T(8,128)(2,1)S(1)} %collective-permute-done.5.other_ref), custom_call_target="tpu_custom_call" | custom-call | flops 13200000000 | tf_op jit(solution)/shard_map/pallas_call | solution.py:88
  78.2 0.9 copy-done.18
  79.1 3.6 %all-to-all-start.1 = ((bf16[8,192,128]{2,1,0:T(8,128)(2,1)}), bf16[8,192,128]{2,1,0:T(8,128)(2,1)S(1)}, u32[]{:S(2)}, u32[]{:S(2)}) async-start(bf16[8,192,128]{2,1,0:T(8,128)(2,1)} %get-tuple-element.47), calls=%async_computation.1 | async-start | bytes 786432 | tf_op jit(solution)/shard_map/all_to_all | solution.py:752
  82.7 0.2 reduce-scatter.2.cloned.1.call-start
  83.0 0.8 copy.28
  83.8 7.6 %all-to-all-done.1.att_ref = bf16[8,192,128]{2,1,0:T(8,128)(2,1)S(1)} async-done(((bf16[8,192,128]{2,1,0:T(8,128)(2,1)}), bf16[8,192,128]{2,1,0:T(8,128)(2,1)S(1)}, u32[]{:S(2)}, u32[]{:S(2)}) %all-to-all-start.1) | async-done | bytes 393248 | tf_op jit(solution)/shard_map/all_to_all | solution.py:752
  91.4 0.7 shard_map.244
  92.2 1.1 copy-done.11
  93.2 0.8 copy-done.12
  94.0 0.8 copy-done.14
  94.8 2.4 %all-gather.3.cloned.1.call-done = bf16[6912,768]{1,0:T(8,128)(2,1)} async-done(((bf16[432,768]{1,0:T(8,128)(2,1)}), bf16[6912,768]{1,0:T(8,128)(2,1)}) %all-gather.3.cloned.1.call-update) | async-done | bytes 10616848 | tf_op jit(solution)/shard_map/all_gather | solution.py:709
  97.2 15.8 %shard_map.246 = (bf16[256,768]{1,0:T(8,128)(2,1)}, f32[256,768]{1,0:T(8,128)}, bf16[256,768]{1,0:T(8,128)(2,1)}, bf16[8,192,128]{2,1,0:T(8,128)(2,1)}, f32[8,768]{1,0:T(8,128)}, /*index=5*/bf16[16,384,768]{2,1,0:T(8,128)(2,1)}) custom-call(bf16[256,768]{1,0:T(8,128)(2,1)} %bitcast.48, bf16[256,768]{1,0:T(8,128)(2,1)} %bitcast.56, ...), custom_call_target="tpu_custom_call" | custom-call | flops 16499999744 | tf_op jit(solution)/shard_map/pallas_call | solution.py:88
  113.0 5.0 %all-to-all-start.3 = ((bf16[8,192,128]{2,1,0:T(8,128)(2,1)}), bf16[8,192,128]{2,1,0:T(8,128)(2,1)S(1)}, u32[]{:S(2)}, u32[]{:S(2)}) async-start(bf16[8,192,128]{2,1,0:T(8,128)(2,1)} %get-tuple-element.56), calls=%async_computation.3 | async-start | bytes 786432 | tf_op jit(solution)/shard_map/all_to_all | solution.py:765
  118.0 2.6 %shard_map.248 = bf16[8,96,768]{2,1,0:T(8,128)(2,1)} custom-call(bf16[768,256]{1,0:T(8,128)(2,1)} %copy-done.12, bf16[256,768]{1,0:T(8,128)(2,1)} %get-tuple-element.64.low_ref), custom_call_target="tpu_custom_call" | custom-call | flops 2200000000 | tf_op jit(solution)/shard_map/pallas_call | solution.py:88
  120.6 6.8 %all-to-all-done.3.da_ref = bf16[8,192,128]{2,1,0:T(8,128)(2,1)S(1)} async-done(((bf16[8,192,128]{2,1,0:T(8,128)(2,1)}), bf16[8,192,128]{2,1,0:T(8,128)(2,1)S(1)}, u32[]{:S(2)}, u32[]{:S(2)}) %all-to-all-start.3) | async-done | bytes 393248 | tf_op jit(solution)/shard_map/all_to_all | solution.py:765
  127.5 3.8 %all-to-all-start.4 = ((bf16[8,96,768]{2,1,0:T(8,128)(2,1)}), bf16[8,96,768]{2,1,0:T(8,128)(2,1)S(1)}, u32[]{:S(2)}, u32[]{:S(2)}) async-start(bf16[8,96,768]{2,1,0:T(8,128)(2,1)} %shard_map.248), calls=%async_computation.4 | async-start | bytes 2359296 | tf_op jit(solution)/shard_map/all_to_all | solution.py:766
  131.3 11.1 %shard_map.247 = (bf16[192,1024]{1,0:T(8,128)(2,1)}, bf16[384,1024]{1,0:T(8,128)(2,1)}, bf16[384,1024]{1,0:T(8,128)(2,1)}) custom-call(s32[2]{0:T(128)} %lengths_ref.3, bf16[192,1024]{1,0:T(8,128)(2,1)} %copy-done.17, bf16[384,1024]{1,0:T(8,128)(2,1)} %copy-done.3, bf16[384,1024]{1,0:T(8,128)(2,1)} %copy-done.4, f32[192,1024]{1,0:T(8,128)} %copy-done.18, ...), custom_call_target="tpu_custom_call" | custom-call | flops 22000001024 | tf_op jit(solution)/shard_map/pallas_call | solution.py:88
  142.3 0.1 collective-permute-start.6
  142.4 7.7 %all-to-all-done.4.out_ref = bf16[8,96,768]{2,1,0:T(8,128)(2,1)S(1)} async-done(((bf16[8,96,768]{2,1,0:T(8,128)(2,1)}), bf16[8,96,768]{2,1,0:T(8,128)(2,1)S(1)}, u32[]{:S(2)}, u32[]{:S(2)}) %all-to-all-start.4) | async-done | bytes 1179680 | tf_op jit(solution)/shard_map/all_to_all | solution.py:766
  150.1 1.0 copy-done.22
  151.1 0.2 copy-done.29
  151.3 8.9 %shard_map.249 = (bf16[8,128,768]{2,1,0:T(8,128)(2,1)}, bf16[4,2,48,768]{3,2,1,0:T(8,128)(2,1)}, bf16[4,2,48,768]{3,2,1,0:T(8,128)(2,1)}) custom-call(bf16[8,176,768]{2,1,0:T(8,128)(2,1)} %copy-done, bf16[192,1024]{1,0:T(8,128)(2,1)} %get-tuple-element.57.dq_ref, bf16[384,1024]{1,0:T(8,128)(2,1)} %get-tuple-element.58.dkv_ref, bf16[384,1024]{1,0:T(8,128)(2,1)} %copy-done.29, ...), custom_call_target="tpu_custom_call" | custom-call | flops 7699999744 | tf_op jit(solution)/shard_map/pallas_call | solution.py:88
  160.2 3.7 %all-to-all-start.5 = ((bf16[8,128,768]{2,1,0:T(8,128)(2,1)}), bf16[8,128,768]{2,1,0:T(8,128)(2,1)S(1)}, u32[]{:S(2)}, u32[]{:S(2)}) async-start(bf16[8,128,768]{2,1,0:T(8,128)(2,1)} %get-tuple-element.65), calls=%async_computation.5 | async-start | bytes 3145728 | tf_op jit(solution)/shard_map/all_to_all | solution.py:809
  164.0 0.1 add_convert_fusion
  164.2 2.7 %collective-permute-start.8 = (bf16[2,48,768]{2,1,0:T(8,128)(2,1)S(1)}, bf16[2,48,768]{2,1,0:T(8,128)(2,1)S(1)}, u32[]{:S(2)}, u32[]{:S(2)}) collective-permute-start(bf16[2,48,768]{2,1,0:T(8,128)(2,1)S(1)} %get-tuple-element.78), channel_id=1, source_target_pairs={{0,1},{1,2},{2,3},{3,0},{4,5},{5,6},{6,7},{7,4},{8,9},{9,10},{10,1... | collective-permute-start | bytes 442376 | tf_op jit(solution)/shard_map/ppermute | solution.py:804
  166.9 2.4 %collective-permute-start.10 = (bf16[2,48,768]{2,1,0:T(8,128)(2,1)S(1)}, bf16[2,48,768]{2,1,0:T(8,128)(2,1)S(1)}, u32[]{:S(2)}, u32[]{:S(2)}) collective-permute-start(bf16[2,48,768]{2,1,0:T(8,128)(2,1)S(1)} %get-tuple-element.79), channel_id=1, source_target_pairs={{0,3},{1,0},{2,1},{3,2},{4,7},{5,4},{6,5},{7,6},{8,11},{9,8},{10,9... | collective-permute-start | bytes 442376 | tf_op jit(solution)/shard_map/ppermute | solution.py:806
  169.2 2.0 collective-permute-start.9
  171.3 2.0 collective-permute-done.8
  173.2 2.2 %collective-permute-done.10 = bf16[2,48,768]{2,1,0:T(8,128)(2,1)S(1)} collective-permute-done((bf16[2,48,768]{2,1,0:T(8,128)(2,1)S(1)}, bf16[2,48,768]{2,1,0:T(8,128)(2,1)S(1)}, u32[]{:S(2)}, u32[]{:S(2)}) %collective-permute-start.10) | collective-permute-done | bytes 147488 | tf_op jit(solution)/shard_map/ppermute | solution.py:806
  175.5 5.7 %collective-permute-done.9 = bf16[2,48,768]{2,1,0:T(8,128)(2,1)S(1)} collective-permute-done((bf16[2,48,768]{2,1,0:T(8,128)(2,1)S(1)}, bf16[2,48,768]{2,1,0:T(8,128)(2,1)S(1)}, u32[]{:S(2)}, u32[]{:S(2)}) %collective-permute-start.9) | collective-permute-done | bytes 147488 | tf_op jit(solution)/shard_map/ppermute | solution.py:805
  181.2 0.1 fusion.2
  181.3 1.5 collective-permute-start.11
  182.8 2.9 %collective-permute-done.11 = bf16[48,768]{1,0:T(8,128)(2,1)S(1)} collective-permute-done((bf16[48,768]{1,0:T(8,128)(2,1)S(1)}, bf16[48,768]{1,0:T(8,128)(2,1)S(1)}, u32[]{:S(2)}, u32[]{:S(2)}) %collective-permute-start.11) | collective-permute-done | bytes 73760 | tf_op jit(solution)/shard_map/ppermute | solution.py:808
  185.8 1.1 copy-done.5
  186.8 1.5 shard_map.251
  188.3 0.9 all-to-all-done.5.got_ref
  189.2 6.0 %all-to-all-start.6 = ((bf16[8,64,768]{2,1,0:T(8,128)(2,1)}), bf16[8,64,768]{2,1,0:T(8,128)(2,1)S(1)}, u32[]{:S(2)}, u32[]{:S(2)}) async-start(bf16[8,64,768]{2,1,0:T(8,128)(2,1)} %shard_map.251), calls=%async_computation.7 | async-start | bytes 1572864 | tf_op jit(solution)/shard_map/all_to_all | solution.py:825
  195.2 1.2 copy.36
  196.4 1.1 copy-done.13
  197.5 1.3 shard_map.250
  198.8 1.1 copy.35
  200.0 5.6 %all-to-all-done.6.got_ref = bf16[8,64,768]{2,1,0:T(8,128)(2,1)S(1)} async-done(((bf16[8,64,768]{2,1,0:T(8,128)(2,1)}), bf16[8,64,768]{2,1,0:T(8,128)(2,1)S(1)}, u32[]{:S(2)}, u32[]{:S(2)}) %all-to-all-start.6) | async-done | bytes 786464 | tf_op jit(solution)/shard_map/all_to_all | solution.py:825
  205.6 1.9 shard_map.252
  (63 shorter events, 0.4 us)
Async XLA Ops:
  9.3 5.7 %copy-start.28 = (bf16[24,640]{1,0:T(8,128)(2,1)S(1)}, bf16[24,640]{1,0:T(8,128)(2,1)}, u32[]{:S(2)}) copy-start(bf16[24,640]{1,0:T(8,128)(2,1)} %get-tuple-element.44) | copy-start | bytes 92164
  9.3 18.9 %copy-start.10 = (s32[1,512]{1,0:T(1,128)S(1)}, s32[1,512]{1,0:T(1,128)}, u32[]{:S(2)}) copy-start(s32[1,512]{1,0:T(1,128)} %constant.14.clone.order_ref) | copy-start | bytes 6148
  9.3 18.9 %all-to-all-start.2 = ((bf16[8,64,768]{2,1,0:T(8,128)(2,1)}), bf16[8,64,768]{2,1,0:T(8,128)(2,1)S(1)}, u32[]{:S(2)}, u32[]{:S(2)}) async-start(bf16[8,64,768]{2,1,0:T(8,128)(2,1)} %get-tuple-element.51), calls=%async_computation.2 | async-start | bytes 1572864 | tf_op jit(solution)/shard_map/all_to_all | solution.py:697
  15.0 82.2 %all-gather.3.cloned.1.call-start = ((), (), s32[]{:S(2)}) async-start(), calls=%async_computation.9 | async-start | bytes 11280384 | tf_op jit(solution)/shard_map/all_gather | solution.py:709
  15.0 5.7 %collective-permute-start.2 = (bf16[24,640]{1,0:T(8,128)(2,1)S(1)}, bf16[24,640]{1,0:T(8,128)(2,1)S(1)}, u32[]{:S(2)}, u32[]{:S(2)}) collective-permute-start(bf16[24,640]{1,0:T(8,128)(2,1)S(1)} %copy-done.28), channel_id=1, source_target_pairs={{0,1},{1,2},{2,3},{3,0},{4,5},{5,6},{6,7},{7,4},{8,9},{9,10},{10,1... | collective-permute-start | bytes 92168 | tf_op jit(solution)/shard_map/ppermute | solution.py:698
  16.6 5.4 %collective-permute-start.1 = (bf16[24,640]{1,0:T(8,128)(2,1)S(1)}, bf16[24,640]{1,0:T(8,128)(2,1)S(1)}, u32[]{:S(2)}, u32[]{:S(2)}) collective-permute-start(bf16[24,640]{1,0:T(8,128)(2,1)S(1)} %copy-done.28), channel_id=1, source_target_pairs={{0,2},{1,3},{2,0},{3,1},{4,6},{5,7},{6,4},{7,5},{8,10},{9,11},{10,... | collective-permute-start | bytes 92168 | tf_op jit(solution)/shard_map/ppermute | solution.py:698
  19.3 3.9 %collective-permute-start = (bf16[24,640]{1,0:T(8,128)(2,1)S(1)}, bf16[24,640]{1,0:T(8,128)(2,1)S(1)}, u32[]{:S(2)}, u32[]{:S(2)}) collective-permute-start(bf16[24,640]{1,0:T(8,128)(2,1)S(1)} %copy-done.28), channel_id=1, source_target_pairs={{0,3},{1,0},{2,1},{3,2},{4,7},{5,4},{6,5},{7,6},{8,11},{9,8},{10,9... | collective-permute-start | bytes 92168 | tf_op jit(solution)/shard_map/ppermute | solution.py:698
  23.3 6.5 %copy-start.24 = (bf16[128,2,768]{2,1,0:T(2,128)(2,1)S(1)}, bf16[128,2,768]{2,1,0:T(2,128)(2,1)}, u32[]{:S(2)}) copy-start(bf16[128,2,768]{2,1,0:T(2,128)(2,1)} %param.17) | copy-start | bytes 1179652
  23.3 5.0 %collective-permute-start.3 = (bf16[4,24,640]{2,1,0:T(8,128)(2,1)S(1)}, bf16[4,24,640]{2,1,0:T(8,128)(2,1)S(1)}, u32[]{:S(2)}, u32[]{:S(2)}) collective-permute-start(bf16[4,24,640]{2,1,0:T(8,128)(2,1)S(1)} %pad_maximum_fusion.near_ref), channel_id=1, source_target_pairs={{0,20},{1,21},{2,22},{3,23},{4,16},{5,17},{6,18},{7,19},{8,28},{9,... | collective-permute-start | bytes 368648 | tf_op jit(solution)/shard_map/ppermute | solution.py:699
  29.8 0.7 copy-start.1
  30.6 33.7 %copy-start.7 = (s32[8,768]{1,0:T(8,128)S(1)}, s32[8,768]{1,0:T(8,128)}, u32[]{:S(2)}) copy-start(s32[8,768]{1,0:T(8,128)} %constant.16.clone.arrival_ref) | copy-start | bytes 73732
  62.3 5.0 %copy-start = (bf16[8,176,768]{2,1,0:T(8,128)(2,1)}, bf16[8,176,768]{2,1,0:T(8,128)(2,1)S(1)}, u32[]{:S(2)}) copy-start(bf16[8,176,768]{2,1,0:T(8,128)(2,1)S(1)} %all_to_all.35.own_ref) | copy-start | bytes 6488068
  62.3 9.9 %copy-start.6 = (s32[2]{0:T(128)S(1)}, s32[2]{0:T(128)}, u32[]{:S(2)}) copy-start(s32[2]{0:T(128)} %lengths_ref.3) | copy-start | bytes 28
  62.3 1.9 collective-permute-start.4
  67.3 1.2 copy-start.15
  68.4 0.9 copy-start.16
  69.3 0.6 copy-start.19
  70.0 8.3 %copy-start.3 = (bf16[384,1024]{1,0:T(8,128)(2,1)}, bf16[384,1024]{1,0:T(8,128)(2,1)S(1)}, u32[]{:S(2)}) copy-start(bf16[384,1024]{1,0:T(8,128)(2,1)S(1)} %get-tuple-element.46.own_ref) | copy-start | bytes 2359300
  70.0 8.3 %copy-start.17 = (bf16[192,1024]{1,0:T(8,128)(2,1)}, bf16[192,1024]{1,0:T(8,128)(2,1)S(1)}, u32[]{:S(2)}) copy-start(bf16[192,1024]{1,0:T(8,128)(2,1)S(1)} %get-tuple-element.45.q_ref) | copy-start | bytes 1179652
  70.0 2.3 %collective-permute-start.5 = (bf16[384,1024]{1,0:T(8,128)(2,1)S(1)}, bf16[384,1024]{1,0:T(8,128)(2,1)S(1)}, u32[]{:S(2)}, u32[]{:S(2)}) collective-permute-start(bf16[384,1024]{1,0:T(8,128)(2,1)S(1)} %get-tuple-element.46.own_ref), channel_id=1, source_target_pairs={{0,8},{8,0},{16,24},{24,16},{32,40},{40,32},{48,56},{56,48},{64,72... | collective-permute-start | bytes 2359304 | tf_op jit(solution)/shard_map/ppermute | solution.py:735
  72.2 6.0 %copy-start.4 = (bf16[384,1024]{1,0:T(8,128)(2,1)}, bf16[384,1024]{1,0:T(8,128)(2,1)S(1)}, u32[]{:S(2)}) copy-start(bf16[384,1024]{1,0:T(8,128)(2,1)S(1)} %collective-permute-done.5.other_ref) | copy-start | bytes 2359300
  72.2 10.7 %copy-start.25 = (bf16[128,2,768]{2,1,0:T(2,128)(2,1)S(1)}, bf16[128,2,768]{2,1,0:T(2,128)(2,1)}, u32[]{:S(2)}) copy-start(bf16[128,2,768]{2,1,0:T(2,128)(2,1)} %param.27) | copy-start | bytes 1179652
  78.2 0.9 copy-start.18
  79.1 13.0 %copy-start.21 = (f32[3,1024]{1,0:T(4,128)}, f32[3,1024]{1,0:T(4,128)S(1)}, u32[]{:S(2)}) copy-start(f32[3,1024]{1,0:T(4,128)S(1)} %get-tuple-element.55.lse_ref) | copy-start | bytes 36868
  79.1 12.3 %copy-start.9 = (s32[1,768]{1,0:T(1,128)S(1)}, s32[1,768]{1,0:T(1,128)}, u32[]{:S(2)}) copy-start(s32[1,768]{1,0:T(1,128)} %constant.12.clone.order_ref) | copy-start | bytes 9220
  79.1 12.3 %all-to-all-start.1 = ((bf16[8,192,128]{2,1,0:T(8,128)(2,1)}), bf16[8,192,128]{2,1,0:T(8,128)(2,1)S(1)}, u32[]{:S(2)}, u32[]{:S(2)}) async-start(bf16[8,192,128]{2,1,0:T(8,128)(2,1)} %get-tuple-element.47), calls=%async_computation.1 | async-start | bytes 786432 | tf_op jit(solution)/shard_map/all_to_all | solution.py:752
  82.7 103.0 %reduce-scatter.2.cloned.1.call-start = ((), (), s32[]{:S(2)}) async-start(), calls=%async_computation.8 | async-start | bytes 10027008 | tf_op jit(solution)/shard_map/reduce_scatter | solution.py:761
  92.2 1.1 copy-start.11
  93.2 0.8 copy-start.12
  94.0 0.8 copy-start.14
  113.0 14.4 %all-to-all-start.3 = ((bf16[8,192,128]{2,1,0:T(8,128)(2,1)}), bf16[8,192,128]{2,1,0:T(8,128)(2,1)S(1)}, u32[]{:S(2)}, u32[]{:S(2)}) async-start(bf16[8,192,128]{2,1,0:T(8,128)(2,1)} %get-tuple-element.56), calls=%async_computation.3 | async-start | bytes 786432 | tf_op jit(solution)/shard_map/all_to_all | solution.py:765
  127.5 3.8 %copy-start.27 = (bf16[8,192,128]{2,1,0:T(8,128)(2,1)}, bf16[8,192,128]{2,1,0:T(8,128)(2,1)S(1)}, u32[]{:S(2)}) copy-start(bf16[8,192,128]{2,1,0:T(8,128)(2,1)S(1)} %all-to-all-done.3.da_ref) | copy-start | bytes 1179652
  127.5 22.6 %all-to-all-start.4 = ((bf16[8,96,768]{2,1,0:T(8,128)(2,1)}), bf16[8,96,768]{2,1,0:T(8,128)(2,1)S(1)}, u32[]{:S(2)}, u32[]{:S(2)}) async-start(bf16[8,96,768]{2,1,0:T(8,128)(2,1)} %shard_map.248), calls=%async_computation.4 | async-start | bytes 2359296 | tf_op jit(solution)/shard_map/all_to_all | solution.py:766
  142.3 7.8 %collective-permute-start.6 = (bf16[384,1024]{1,0:T(8,128)(2,1)}, bf16[384,1024]{1,0:T(8,128)(2,1)S(1)}, u32[]{:S(2)}, u32[]{:S(2)}) collective-permute-start(bf16[384,1024]{1,0:T(8,128)(2,1)} %get-tuple-element.59), channel_id=1, source_target_pairs={{0,8},{8,0},{16,24},{24,16},{32,40},{40,32},{48,56},{56,48},{64,72... | collective-permute-start | bytes 2359304 | tf_op jit(solution)/shard_map/ppermute | solution.py:788
  150.1 1.0 copy-start.22
  150.1 1.3 copy-start.29
  160.2 3.7 %collective-permute-start.7 = (bf16[4,2,48,768]{3,2,1,0:T(8,128)(2,1)}, bf16[4,2,48,768]{3,2,1,0:T(8,128)(2,1)S(1)}, u32[]{:S(2)}, u32[]{:S(2)}) collective-permute-start(bf16[4,2,48,768]{3,2,1,0:T(8,128)(2,1)} %get-tuple-element.67), channel_id=1, source_target_pairs={{0,8},{8,0},{16,24},{24,16},{32,40},{40,32},{48,56},{56,48},{64,72... | collective-permute-start | bytes 1769480 | tf_op jit(solution)/shard_map/ppermute | solution.py:801
  160.2 3.8 %copy-start.23 = (bf16[4,2,48,768]{3,2,1,0:T(8,128)(2,1)S(1)}, bf16[4,2,48,768]{3,2,1,0:T(8,128)(2,1)}, u32[]{:S(2)}) copy-start(bf16[4,2,48,768]{3,2,1,0:T(8,128)(2,1)} %get-tuple-element.66) | copy-start | bytes 1769476
  160.2 29.0 %all-to-all-start.5 = ((bf16[8,128,768]{2,1,0:T(8,128)(2,1)}), bf16[8,128,768]{2,1,0:T(8,128)(2,1)S(1)}, u32[]{:S(2)}, u32[]{:S(2)}) async-start(bf16[8,128,768]{2,1,0:T(8,128)(2,1)} %get-tuple-element.65), calls=%async_computation.5 | async-start | bytes 3145728 | tf_op jit(solution)/shard_map/all_to_all | solution.py:809
  164.2 9.1 %collective-permute-start.8 = (bf16[2,48,768]{2,1,0:T(8,128)(2,1)S(1)}, bf16[2,48,768]{2,1,0:T(8,128)(2,1)S(1)}, u32[]{:S(2)}, u32[]{:S(2)}) collective-permute-start(bf16[2,48,768]{2,1,0:T(8,128)(2,1)S(1)} %get-tuple-element.78), channel_id=1, source_target_pairs={{0,1},{1,2},{2,3},{3,0},{4,5},{5,6},{6,7},{7,4},{8,9},{9,10},{10,1... | collective-permute-start | bytes 442376 | tf_op jit(solution)/shard_map/ppermute | solution.py:804
  166.9 8.6 %collective-permute-start.10 = (bf16[2,48,768]{2,1,0:T(8,128)(2,1)S(1)}, bf16[2,48,768]{2,1,0:T(8,128)(2,1)S(1)}, u32[]{:S(2)}, u32[]{:S(2)}) collective-permute-start(bf16[2,48,768]{2,1,0:T(8,128)(2,1)S(1)} %get-tuple-element.79), channel_id=1, source_target_pairs={{0,3},{1,0},{2,1},{3,2},{4,7},{5,4},{6,5},{7,6},{8,11},{9,8},{10,9... | collective-permute-start | bytes 442376 | tf_op jit(solution)/shard_map/ppermute | solution.py:806
  169.2 11.9 %collective-permute-start.9 = (bf16[2,48,768]{2,1,0:T(8,128)(2,1)S(1)}, bf16[2,48,768]{2,1,0:T(8,128)(2,1)S(1)}, u32[]{:S(2)}, u32[]{:S(2)}) collective-permute-start(bf16[2,48,768]{2,1,0:T(8,128)(2,1)S(1)} %get-tuple-element.80), channel_id=1, source_target_pairs={{0,2},{1,3},{2,0},{3,1},{4,6},{5,7},{6,4},{7,5},{8,10},{9,11},{10,... | collective-permute-start | bytes 442376 | tf_op jit(solution)/shard_map/ppermute | solution.py:805
  181.3 4.4 %collective-permute-start.11 = (bf16[48,768]{1,0:T(8,128)(2,1)S(1)}, bf16[48,768]{1,0:T(8,128)(2,1)S(1)}, u32[]{:S(2)}, u32[]{:S(2)}) collective-permute-start(bf16[48,768]{1,0:T(8,128)(2,1)S(1)} %slice_bitcast_fusion.4), channel_id=1, source_target_pairs={{0,20},{1,21},{2,22},{3,23},{4,16},{5,17},{6,18},{7,19},{8,28},{9,... | collective-permute-start | bytes 221192 | tf_op jit(solution)/shard_map/ppermute | solution.py:808
  185.8 1.1 copy-start.5
  188.3 6.9 %copy-start.26 = (bf16[256,768]{1,0:T(8,128)(2,1)S(1)}, bf16[256,768]{1,0:T(8,128)(2,1)}, u32[]{:S(2)}) copy-start(bf16[256,768]{1,0:T(8,128)(2,1)} %get-tuple-element.52) | copy-start | bytes 1179652
  188.3 8.1 %copy-start.2 = (bf16[128,2,768]{2,0,1:T(8,128)(2,1)S(1)}, bf16[128,2,768]{2,0,1:T(8,128)(2,1)}, u32[]{:S(2)}) copy-start(bf16[128,2,768]{2,0,1:T(8,128)(2,1)} %copy-done.1) | copy-start | bytes 1179652
  188.3 8.1 %copy-start.20 = (f32[8,768]{1,0:T(8,128)S(1)}, f32[8,768]{1,0:T(8,128)}, u32[]{:S(2)}) copy-start(f32[8,768]{1,0:T(8,128)} %copy-done.19) | copy-start | bytes 73732
  189.2 16.4 %all-to-all-start.6 = ((bf16[8,64,768]{2,1,0:T(8,128)(2,1)}), bf16[8,64,768]{2,1,0:T(8,128)(2,1)S(1)}, u32[]{:S(2)}, u32[]{:S(2)}) async-start(bf16[8,64,768]{2,1,0:T(8,128)(2,1)} %shard_map.251), calls=%async_computation.7 | async-start | bytes 1572864 | tf_op jit(solution)/shard_map/all_to_all | solution.py:825
  196.4 1.1 copy-start.13
  197.5 8.1 %copy-start.8 = (s32[1,768]{1,0:T(1,128)S(1)}, s32[1,768]{1,0:T(1,128)}, u32[]{:S(2)}) copy-start(s32[1,768]{1,0:T(1,128)} %constant.13.clone.units_ref) | copy-start | bytes 9220
Sparse Core Ops, SparseCore 0:
  29.9 67.2 all-gather.2
  113.1 69.1 reduce-scatter.1

commit v7 on v6

--- a/solution.py
+++ b/solution.py
@@ -46,9 +46,9 @@
 
 
 def regroup_order():
-    slot = np.arange(512, dtype=np.int32).reshape(8, 64)
-    parts = [slot[:, 0:24]] + [slot[:, f : f + 6] for f in (30, 36, 42, 48, 24, 54)]
-    return np.concatenate([p.reshape(-1) for p in parts] + [np.full(32, -1, np.int32)])[None]
+    slot = np.arange(448, dtype=np.int32).reshape(8, 56)
+    parts = [slot[:, 0:24]] + [slot[:, f : f + 6] for f in (24, 30, 36, 42, 48)]
+    return np.concatenate([p.reshape(-1) for p in parts] + [np.full(80, -1, np.int32)])[None]
 
 
 REGROUP = regroup_order()
@@ -65,9 +65,9 @@
 ).reshape(128, 1)
 
 
-def places(order):
+def places(order, count=None):
     size = order.shape[1]
-    rows = lax.broadcasted_iota(jnp.int32, (size, size), 0)
+    rows = lax.broadcasted_iota(jnp.int32, (count or size, size), 0)
     return jnp.where(rows == order, 1.0, 0.0).astype(BF)
 
 
@@ -119,9 +119,9 @@
         [up_ref[:, k * 768 : (k + 1) * 768].astype(F32) for k in range(4)], axis=0
     ).astype(BF)
     scr[0:24, :] = down_ref[...].astype(F32)
-    scr[24:30, :] = out_ref[...].astype(F32)
-    scr[30:54, :] = dot(up, places(units_ref[...]))
-    scr[54:64, :] = jnp.zeros((10, 768), F32)
+    scr[24:48, :] = dot(up, places(units_ref[...]))
+    scr[48:54, :] = out_ref[...].astype(F32)
+    scr[54:56, :] = jnp.zeros((2, 768), F32)
     slot = scr[...].astype(BF)
     for j in range(8):
         slot_ref[j] = slot
@@ -132,8 +132,10 @@
     raw_ref[...] = raw_scr[...].astype(BF)
 
 
-def regroup_kernel(slots_ref, order_ref, far_ref, rest_ref):
-    rows = dot(places(order_ref[...]), slots_ref[...].reshape(512, 768), TN).astype(BF)
+def regroup_kernel(slots_ref, order_ref, far_ref, rest_ref, scr):
+    for j in range(8):
+        scr[j * 56 : j * 56 + 56, :] = slots_ref[j].astype(F32)
+    rows = dot(places(order_ref[...], 448), scr[...].astype(BF), TN).astype(BF)
     rest_ref[...] = rows[0:432]
 
 
@@ -617,11 +619,12 @@
 
 def slots_kernel(rest_ref, qkv_ref, order_ref, out_ref, r_scr):
     r_scr[0:384, :] = rest_ref[...]
-    r_scr[384:432, :] = jnp.zeros((48, 768), BF)
-    r_scr[432:480, 0:640] = qkv_ref[:, 0:640]
-    r_scr[432:480, 640:768] = jnp.zeros((48, 128), BF)
-    r_scr[480:512, :] = jnp.zeros((32, 768), BF)
-    out_ref[...] = dot(places(order_ref[...]), r_scr[...]).astype(BF).reshape(8, 64, 768)
+    r_scr[384:432, 0:640] = qkv_ref[:, 0:640]
+    r_scr[384:432, 640:768] = jnp.zeros((48, 128), BF)
+    r_scr[432:512, :] = jnp.zeros((80, 768), BF)
+    rows = dot(places(order_ref[...], 448), r_scr[...])
+    for j in range(8):
+        out_ref[j] = rows[j * 56 : j * 56 + 56].astype(BF)
 
 
 def finish_kernel(x_ref, dfirst_ref, gains_ref, got_ref, qkv_ref, dtok_ref, out_ref):
@@ -640,14 +643,14 @@
 
 
 def sums_kernel(got_ref, units_ref, down_ref, up_ref, qkv_ref, g1_ref, b1_ref, g2_ref, b2_ref):
-    total = jnp.zeros((64, 768), F32)
+    total = jnp.zeros((56, 768), F32)
     chunks = []
     for e in range(4):
         both = got_ref[2 * e].astype(F32) + got_ref[2 * e + 1].astype(F32)
-        chunks.append(both[54:60])
+        chunks.append(both[48:54])
         total += both
     down_ref[...] = total[0:24]
-    left, up, units = total[30:54], jnp.zeros((24, 768), F32), places(units_ref[...])
+    left, up, units = total[24:48], jnp.zeros((24, 768), F32), places(units_ref[...])
     for _ in range(3):
         piece = left.astype(BF)
         left = left - piece.astype(F32)
@@ -660,7 +663,7 @@
         )
     norms = total[:, 512:640].T
     for i, ref in enumerate((g1_ref, b1_ref, g2_ref, b2_ref)):
-        ref[...] = norms[64 + i : 65 + i, 54:60]
+        ref[...] = norms[64 + i : 65 + i, 48:54]
 
 
 def scalars(count):
@@ -686,10 +689,10 @@
         in_specs=[whole(24, 768), whole(6, 768), whole(6, 3072), whole(6, 2304)]
         + [whole(1, 6)] * 4
         + [whole(1, 768)],
-        out_specs=[whole(8, 64, 768), whole(24, 640)],
-        out_shape=[shape((8, 64, 768), BF), shape((24, 640), BF)],
+        out_specs=[whole(8, 56, 768), whole(24, 640)],
+        out_shape=[shape((8, 56, 768), BF), shape((24, 640), BF)],
         scratch_shapes=[
-            pltpu.VMEM((64, 768), F32), pltpu.VMEM((128, 128), F32), pltpu.VMEM((24, 640), F32),
+            pltpu.VMEM((56, 768), F32), pltpu.VMEM((128, 128), F32), pltpu.VMEM((24, 640), F32),
         ],
         cost_estimate=about(2),
         compiler_params=pltpu.CompilerParams(vmem_limit_bytes=60 * 1024 * 1024),
@@ -702,6 +705,7 @@
         shape((432, 768), BF),
         (slots, regroup, far),
         2,
+        [pltpu.VMEM((448, 768), F32)],
         mib=12,
         in_specs=[pl.BlockSpec(memory_space=pltpu.VMEM)] * 2
         + [pl.BlockSpec(memory_space=pl.ANY)],
@@ -816,7 +820,7 @@
     )
     slots = call(
         slots_kernel,
-        shape((8, 64, 768), BF),
+        shape((8, 56, 768), BF),
         (rest_sum, qkv_sum, regroup),
         2,
         [pltpu.VMEM((512, 768), BF)],

time: 219 us -> 219 us (level)
  Pallas kernels: 56.6 us -> 62.9 us
  waiting for transfers between devices: 54.8 us -> 49.6 us
    pallas_call x12, Pallas kernels: 54.5 us -> 60.8 us  [call(): pl.pallas_call(kernel, out_shape=outs, scratch_shapes=list(scratch), cost...]
    all_to_all x1, waiting for transfers between devices: 7.65 us -> 3.17 us  [body(): exchange(call(out_kernel, shape((8, 96, 768), BF), (attended_t, low), 2))]
    all_to_all x1, starting transfers between devices: 3.73 us -> 7.42 us  [body(): back = exchange(part)]
    all_gather x1, waiting for transfers between devices: 2.4 us -> 0.01 us  [body(): weights = lax.all_gather(rest, BOTH, axis=0, axis_index_groups=RINGS)]
    unnamed x61 -> x57, local copies, waits for them, and re-layouts: 10.2 us -> 9.1 us
  transfers between devices with their start and end apart: 20 -> 20, of which waited for: 15 -> 14; matrix products, arithmetic and copies ran while one was open for 2% -> 2% of each run, Pallas kernels for 16% -> 19%
where the time goes in v7:
time: 219 us; the launch traced here: 216 us
  Pallas kernels  62.9 us (29%)
  waiting for transfers between devices  49.6 us (23%)
  starting transfers between devices  43 us (20%)
  blocking collectives  31.7 us (14%)
  between operations  14.3 us (7%)
  local copies, waits for them, and re-layouts  13.3 us (6%)
    pallas_call x12, Pallas kernels, call(): pl.pallas_call(kernel, out_shape=outs, scratch_shapes=list(scratch), cost...  60.8 us
    all_to_all x1, blocking collectives, body(): own = exchange(sent)  31.7 us
    all_to_all x2, starting transfers between devices, body(): slots = exchange(slots)  10.4 us
    unnamed x57, local copies, waits for them, and re-layouts  9.1 us
    all_to_all x1, waiting for transfers between devices, body(): att = exchange(o_low)  7.6 us
    all_to_all x1, starting transfers between devices, body(): back = exchange(part)  7.42 us
    all_to_all x1, waiting for transfers between devices, body(): d_att = exchange(d_att)  6.66 us
    ppermute x1, waiting for transfers between devices, body(): lax.ppermute(line[2], 'batch', along_x(2))  5.79 us
  transfers between devices with their start and end apart: 20, of which 14 were waited for; matrix products, arithmetic and copies ran while one was open for 2% of the time, Pallas kernels for 19%

profile of v7, /device:TPU:64, one launch (start us, length us, event | category | flops | bytes accessed | tf_op | source)
XLA Modules:
  0.0 215.8 jit_solution(5271006914026766439)
XLA Ops:
  7.2 2.1 shard_map.240
  9.3 5.7 %all-to-all-start.2 = ((bf16[8,56,768]{2,1,0:T(8,128)(2,1)}), bf16[8,56,768]{2,1,0:T(8,128)(2,1)S(1)}, u32[]{:S(2)}, u32[]{:S(2)}) async-start(bf16[8,56,768]{2,1,0:T(8,128)(2,1)} %get-tuple-element.51), calls=%async_computation.2 | async-start | bytes 1376256 | tf_op jit(solution)/shard_map/all_to_all | solution.py:700
  15.0 0.0 all-gather.3.cloned.1.call-start
  15.0 1.6 collective-permute-start.2
  16.6 2.7 %collective-permute-start.1 = (bf16[24,640]{1,0:T(8,128)(2,1)}, bf16[24,640]{1,0:T(8,128)(2,1)S(1)}, u32[]{:S(2)}, u32[]{:S(2)}) collective-permute-start(bf16[24,640]{1,0:T(8,128)(2,1)} %get-tuple-element.44), channel_id=1, source_target_pairs={{0,2},{1,3},{2,0},{3,1},{4,6},{5,7},{6,4},{7,5},{8,10},{9,11},{10,... | collective-permute-start | bytes 92168 | tf_op jit(solution)/shard_map/ppermute | solution.py:701
  19.3 1.4 collective-permute-start
  20.7 1.4 collective-permute-done.1
  22.2 1.2 collective-permute-done
  23.4 0.8 pad_maximum_fusion.near_ref
  24.2 0.5 collective-permute-start.3
  24.7 4.5 %collective-permute-done.3.far_ref = bf16[4,24,640]{2,1,0:T(8,128)(2,1)S(1)} collective-permute-done((bf16[4,24,640]{2,1,0:T(8,128)(2,1)S(1)}, bf16[4,24,640]{2,1,0:T(8,128)(2,1)S(1)}, u32[]{:S(2)}, u32[]{:S(2)}) %collective-permute-start.3) | collective-permute-done | bytes 122912 | tf_op jit(solution)/shard_map/ppermute | solution.py:702
  29.1 1.5 shard_map.245
  30.7 0.2 shard_map.241
  30.9 0.5 copy-done.1
  31.4 31.7 %all_to_all.35.own_ref = bf16[8,176,768]{2,1,0:T(8,128)(2,1)S(1)} all-to-all(bf16[8,176,768]{2,1,0:T(8,128)(2,1)S(1)} %shard_map.241), channel_id=1, replica_groups={{0,16,32,48,64,80,96,112},{8,24,40,56,72,88,104,120},{1,17,33,49,65,81,..., dimensions={0} | all-to-all | bytes 4325376 | tf_op jit(solution)/shard_map/all_to_all | solution.py:724
  63.2 0.1 collective-permute-start.4
  63.3 1.9 collective-permute-done.4.other_ref
  65.1 3.0 %shard_map.242 = (bf16[1024,768]{1,0:T(8,128)(2,1)S(1)}, bf16[576,768]{1,0:T(8,128)(2,1)S(1)}, f32[8,768]{1,0:T(8,128)S(1)}, bf16[192,1024]{1,0:T(8,128)(2,1)S(1)}, bf16[384,1024]{1,0:T(8,128)(2,1)S(1)}) custom-call(bf16[8,176,768]{2,1,0:T(8,128)(2,1)S(1)} %all_to_all.35.own_ref, bf16[8,48,640]{2,1,0:T(8,128)(2,1)S(1)} %collective-permute-done.4.other_ref, ...), custom_call_target="tpu_custom_call" | custom-call | flops 5500000256 | tf_op jit(solution)/shard_map/pallas_call | solution.py:88
  68.1 1.1 copy-done.15
  69.3 0.9 copy-done.16
  70.2 0.6 copy-done.19
  70.8 0.1 collective-permute-start.5
  70.9 2.1 collective-permute-done.5.other_ref
  73.1 8.1 %shard_map.243 = (f32[192,1024]{1,0:T(8,128)S(1)}, bf16[8,192,128]{2,1,0:T(8,128)(2,1)}, f32[3,1024]{1,0:T(4,128)S(1)}) custom-call(s32[2]{0:T(128)S(1)} %copy-done.6, bf16[192,1024]{1,0:T(8,128)(2,1)S(1)} %get-tuple-element.45.q_ref, bf16[384,1024]{1,0:T(8,128)(2,1)S(1)} %get-tuple-element.46.own_ref, bf16[384,1024]{1,0:T(8,128)(2,1)S(1)} %collective-permute-done.5.other_ref), custom_call_target="tpu_custom_call" | custom-call | flops 13200000000 | tf_op jit(solution)/shard_map/pallas_call | solution.py:88
  81.2 0.9 copy-done.18
  82.1 4.3 %all-to-all-start.1 = ((bf16[8,192,128]{2,1,0:T(8,128)(2,1)}), bf16[8,192,128]{2,1,0:T(8,128)(2,1)S(1)}, u32[]{:S(2)}, u32[]{:S(2)}) async-start(bf16[8,192,128]{2,1,0:T(8,128)(2,1)} %get-tuple-element.47), calls=%async_computation.1 | async-start | bytes 786432 | tf_op jit(solution)/shard_map/all_to_all | solution.py:756
  86.4 0.2 reduce-scatter.2.cloned.1.call-start
  86.7 0.8 copy.28
  87.4 7.6 %all-to-all-done.1.att_ref = bf16[8,192,128]{2,1,0:T(8,128)(2,1)S(1)} async-done(((bf16[8,192,128]{2,1,0:T(8,128)(2,1)}), bf16[8,192,128]{2,1,0:T(8,128)(2,1)S(1)}, u32[]{:S(2)}, u32[]{:S(2)}) %all-to-all-start.1) | async-done | bytes 393248 | tf_op jit(solution)/shard_map/all_to_all | solution.py:756
  95.0 0.7 shard_map.244
  95.8 1.1 copy-done.11
  96.9 0.8 copy-done.12
  97.6 0.8 copy-done.14
  98.4 15.8 %shard_map.246 = (bf16[256,768]{1,0:T(8,128)(2,1)}, f32[256,768]{1,0:T(8,128)}, bf16[256,768]{1,0:T(8,128)(2,1)}, bf16[8,192,128]{2,1,0:T(8,128)(2,1)}, f32[8,768]{1,0:T(8,128)}, /*index=5*/bf16[16,384,768]{2,1,0:T(8,128)(2,1)}) custom-call(bf16[256,768]{1,0:T(8,128)(2,1)} %bitcast.48, bf16[256,768]{1,0:T(8,128)(2,1)} %bitcast.56, ...), custom_call_target="tpu_custom_call" | custom-call | flops 16499999744 | tf_op jit(solution)/shard_map/pallas_call | solution.py:88
  114.2 4.6 %all-to-all-start.3 = ((bf16[8,192,128]{2,1,0:T(8,128)(2,1)}), bf16[8,192,128]{2,1,0:T(8,128)(2,1)S(1)}, u32[]{:S(2)}, u32[]{:S(2)}) async-start(bf16[8,192,128]{2,1,0:T(8,128)(2,1)} %get-tuple-element.56), calls=%async_computation.3 | async-start | bytes 786432 | tf_op jit(solution)/shard_map/all_to_all | solution.py:769
  118.8 2.7 %shard_map.248 = bf16[8,96,768]{2,1,0:T(8,128)(2,1)} custom-call(bf16[768,256]{1,0:T(8,128)(2,1)} %copy-done.12, bf16[256,768]{1,0:T(8,128)(2,1)} %get-tuple-element.64.low_ref), custom_call_target="tpu_custom_call" | custom-call | flops 2200000000 | tf_op jit(solution)/shard_map/pallas_call | solution.py:88
  121.5 6.7 %all-to-all-done.3.da_ref = bf16[8,192,128]{2,1,0:T(8,128)(2,1)S(1)} async-done(((bf16[8,192,128]{2,1,0:T(8,128)(2,1)}), bf16[8,192,128]{2,1,0:T(8,128)(2,1)S(1)}, u32[]{:S(2)}, u32[]{:S(2)}) %all-to-all-start.3) | async-done | bytes 393248 | tf_op jit(solution)/shard_map/all_to_all | solution.py:769
  128.1 3.8 %all-to-all-start.4 = ((bf16[8,96,768]{2,1,0:T(8,128)(2,1)}), bf16[8,96,768]{2,1,0:T(8,128)(2,1)S(1)}, u32[]{:S(2)}, u32[]{:S(2)}) async-start(bf16[8,96,768]{2,1,0:T(8,128)(2,1)} %shard_map.248), calls=%async_computation.4 | async-start | bytes 2359296 | tf_op jit(solution)/shard_map/all_to_all | solution.py:770
  131.9 15.3 %shard_map.247 = (bf16[192,1024]{1,0:T(8,128)(2,1)}, bf16[384,1024]{1,0:T(8,128)(2,1)}, bf16[384,1024]{1,0:T(8,128)(2,1)}) custom-call(s32[2]{0:T(128)} %lengths_ref.3, bf16[192,1024]{1,0:T(8,128)(2,1)} %copy-done.17, bf16[384,1024]{1,0:T(8,128)(2,1)} %copy-done.3, bf16[384,1024]{1,0:T(8,128)(2,1)} %copy-done.4, f32[192,1024]{1,0:T(8,128)} %copy-done.18, ...), custom_call_target="tpu_custom_call" | custom-call | flops 22000001024 | tf_op jit(solution)/shard_map/pallas_call | solution.py:88
  147.3 3.2 %all-to-all-done.4.out_ref = bf16[8,96,768]{2,1,0:T(8,128)(2,1)S(1)} async-done(((bf16[8,96,768]{2,1,0:T(8,128)(2,1)}), bf16[8,96,768]{2,1,0:T(8,128)(2,1)S(1)}, u32[]{:S(2)}, u32[]{:S(2)}) %all-to-all-start.4) | async-done | bytes 1179680 | tf_op jit(solution)/shard_map/all_to_all | solution.py:770
  150.5 1.0 copy-done.22
  151.5 0.2 copy-done.27
  151.7 8.9 %shard_map.249 = (bf16[8,128,768]{2,1,0:T(8,128)(2,1)}, bf16[4,2,48,768]{3,2,1,0:T(8,128)(2,1)}, bf16[4,2,48,768]{3,2,1,0:T(8,128)(2,1)}) custom-call(bf16[8,176,768]{2,1,0:T(8,128)(2,1)} %copy-done, bf16[192,1024]{1,0:T(8,128)(2,1)} %get-tuple-element.57.dq_ref, bf16[384,1024]{1,0:T(8,128)(2,1)} %get-tuple-element.58.dkv_ref, bf16[384,1024]{1,0:T(8,128)(2,1)} %copy-done.27, ...), custom_call_target="tpu_custom_call" | custom-call | flops 7699999744 | tf_op jit(solution)/shard_map/pallas_call | solution.py:88
  160.6 7.4 %all-to-all-start.5 = ((bf16[8,128,768]{2,1,0:T(8,128)(2,1)}), bf16[8,128,768]{2,1,0:T(8,128)(2,1)S(1)}, u32[]{:S(2)}, u32[]{:S(2)}) async-start(bf16[8,128,768]{2,1,0:T(8,128)(2,1)} %get-tuple-element.65), calls=%async_computation.5 | async-start | bytes 3145728 | tf_op jit(solution)/shard_map/all_to_all | solution.py:813
  168.1 0.1 add_convert_fusion
  168.2 0.9 collective-permute-start.8
  169.1 2.4 %collective-permute-start.10 = (bf16[2,48,768]{2,1,0:T(8,128)(2,1)S(1)}, bf16[2,48,768]{2,1,0:T(8,128)(2,1)S(1)}, u32[]{:S(2)}, u32[]{:S(2)}) collective-permute-start(bf16[2,48,768]{2,1,0:T(8,128)(2,1)S(1)} %get-tuple-element.79), channel_id=1, source_target_pairs={{0,3},{1,0},{2,1},{3,2},{4,7},{5,4},{6,5},{7,6},{8,11},{9,8},{10,9... | collective-permute-start | bytes 442376 | tf_op jit(solution)/shard_map/ppermute | solution.py:810
  171.6 1.2 collective-permute-start.9
  172.8 2.7 %collective-permute-done.8 = bf16[2,48,768]{2,1,0:T(8,128)(2,1)S(1)} collective-permute-done((bf16[2,48,768]{2,1,0:T(8,128)(2,1)S(1)}, bf16[2,48,768]{2,1,0:T(8,128)(2,1)S(1)}, u32[]{:S(2)}, u32[]{:S(2)}) %collective-permute-start.8) | collective-permute-done | bytes 147488 | tf_op jit(solution)/shard_map/ppermute | solution.py:808
  175.5 2.0 collective-permute-done.10
  177.5 5.8 %collective-permute-done.9 = bf16[2,48,768]{2,1,0:T(8,128)(2,1)S(1)} collective-permute-done((bf16[2,48,768]{2,1,0:T(8,128)(2,1)S(1)}, bf16[2,48,768]{2,1,0:T(8,128)(2,1)S(1)}, u32[]{:S(2)}, u32[]{:S(2)}) %collective-permute-start.9) | collective-permute-done | bytes 147488 | tf_op jit(solution)/shard_map/ppermute | solution.py:809
  183.3 0.1 fusion.2
  183.4 1.4 collective-permute-start.11
  184.7 3.1 %collective-permute-done.11 = bf16[48,768]{1,0:T(8,128)(2,1)S(1)} collective-permute-done((bf16[48,768]{1,0:T(8,128)(2,1)S(1)}, bf16[48,768]{1,0:T(8,128)(2,1)S(1)}, u32[]{:S(2)}, u32[]{:S(2)}) %collective-permute-start.11) | collective-permute-done | bytes 73760 | tf_op jit(solution)/shard_map/ppermute | solution.py:812
  187.8 0.0 reduce-scatter.2.cloned.1.call-done.rest_ref
  187.9 1.1 copy-done.5
  188.9 1.4 shard_map.251
  190.3 2.3 %all-to-all-done.5.got_ref = bf16[8,128,768]{2,1,0:T(8,128)(2,1)S(1)} async-done(((bf16[8,128,768]{2,1,0:T(8,128)(2,1)}), bf16[8,128,768]{2,1,0:T(8,128)(2,1)S(1)}, u32[]{:S(2)}, u32[]{:S(2)}) %all-to-all-start.5) | async-done | bytes 1572896 | tf_op jit(solution)/shard_map/all_to_all | solution.py:813
  192.6 4.7 %all-to-all-start.6 = ((bf16[8,56,768]{2,1,0:T(8,128)(2,1)}), bf16[8,56,768]{2,1,0:T(8,128)(2,1)S(1)}, u32[]{:S(2)}, u32[]{:S(2)}) async-start(bf16[8,56,768]{2,1,0:T(8,128)(2,1)} %shard_map.251), calls=%async_computation.7 | async-start | bytes 1376256 | tf_op jit(solution)/shard_map/all_to_all | solution.py:829
  197.3 2.1 copy.36
  199.5 1.3 shard_map.250
  200.8 1.1 copy.35
  202.0 5.1 %all-to-all-done.6.got_ref = bf16[8,56,768]{2,1,0:T(8,128)(2,1)S(1)} async-done(((bf16[8,56,768]{2,1,0:T(8,128)(2,1)}), bf16[8,56,768]{2,1,0:T(8,128)(2,1)S(1)}, u32[]{:S(2)}, u32[]{:S(2)}) %all-to-all-start.6) | async-done | bytes 688160 | tf_op jit(solution)/shard_map/all_to_all | solution.py:829
  207.1 1.9 shard_map.252
  (59 shorter events, 0.3 us)
Async XLA Ops:
  9.3 19.9 %copy-start.10 = (s32[1,512]{1,0:T(1,128)S(1)}, s32[1,512]{1,0:T(1,128)}, u32[]{:S(2)}) copy-start(s32[1,512]{1,0:T(1,128)} %constant.14.clone.order_ref) | copy-start | bytes 6148
  9.3 19.9 %all-to-all-start.2 = ((bf16[8,56,768]{2,1,0:T(8,128)(2,1)}), bf16[8,56,768]{2,1,0:T(8,128)(2,1)S(1)}, u32[]{:S(2)}, u32[]{:S(2)}) async-start(bf16[8,56,768]{2,1,0:T(8,128)(2,1)} %get-tuple-element.51), calls=%async_computation.2 | async-start | bytes 1376256 | tf_op jit(solution)/shard_map/all_to_all | solution.py:700
  15.0 83.4 %all-gather.3.cloned.1.call-start = ((), (), s32[]{:S(2)}) async-start(), calls=%async_computation.9 | async-start | bytes 11280384 | tf_op jit(solution)/shard_map/all_gather | solution.py:713
  15.0 5.7 %collective-permute-start.2 = (bf16[24,640]{1,0:T(8,128)(2,1)}, bf16[24,640]{1,0:T(8,128)(2,1)S(1)}, u32[]{:S(2)}, u32[]{:S(2)}) collective-permute-start(bf16[24,640]{1,0:T(8,128)(2,1)} %get-tuple-element.44), channel_id=1, source_target_pairs={{0,1},{1,2},{2,3},{3,0},{4,5},{5,6},{6,7},{7,4},{8,9},{9,10},{10,1... | collective-permute-start | bytes 92168 | tf_op jit(solution)/shard_map/ppermute | solution.py:701
  16.6 5.6 %collective-permute-start.1 = (bf16[24,640]{1,0:T(8,128)(2,1)}, bf16[24,640]{1,0:T(8,128)(2,1)S(1)}, u32[]{:S(2)}, u32[]{:S(2)}) collective-permute-start(bf16[24,640]{1,0:T(8,128)(2,1)} %get-tuple-element.44), channel_id=1, source_target_pairs={{0,2},{1,3},{2,0},{3,1},{4,6},{5,7},{6,4},{7,5},{8,10},{9,11},{10,... | collective-permute-start | bytes 92168 | tf_op jit(solution)/shard_map/ppermute | solution.py:701
  19.3 4.1 %collective-permute-start = (bf16[24,640]{1,0:T(8,128)(2,1)}, bf16[24,640]{1,0:T(8,128)(2,1)S(1)}, u32[]{:S(2)}, u32[]{:S(2)}) collective-permute-start(bf16[24,640]{1,0:T(8,128)(2,1)} %get-tuple-element.44), channel_id=1, source_target_pairs={{0,3},{1,0},{2,1},{3,2},{4,7},{5,4},{6,5},{7,6},{8,11},{9,8},{10,9... | collective-permute-start | bytes 92168 | tf_op jit(solution)/shard_map/ppermute | solution.py:701
  24.2 6.5 %copy-start.24 = (bf16[128,2,768]{2,1,0:T(2,128)(2,1)S(1)}, bf16[128,2,768]{2,1,0:T(2,128)(2,1)}, u32[]{:S(2)}) copy-start(bf16[128,2,768]{2,1,0:T(2,128)(2,1)} %param.17) | copy-start | bytes 1179652
  24.2 5.0 %collective-permute-start.3 = (bf16[4,24,640]{2,1,0:T(8,128)(2,1)S(1)}, bf16[4,24,640]{2,1,0:T(8,128)(2,1)S(1)}, u32[]{:S(2)}, u32[]{:S(2)}) collective-permute-start(bf16[4,24,640]{2,1,0:T(8,128)(2,1)S(1)} %pad_maximum_fusion.near_ref), channel_id=1, source_target_pairs={{0,20},{1,21},{2,22},{3,23},{4,16},{5,17},{6,18},{7,19},{8,28},{9,... | collective-permute-start | bytes 368648 | tf_op jit(solution)/shard_map/ppermute | solution.py:702
  30.7 0.7 copy-start.1
  31.4 33.7 %copy-start.7 = (s32[8,768]{1,0:T(8,128)S(1)}, s32[8,768]{1,0:T(8,128)}, u32[]{:S(2)}) copy-start(s32[8,768]{1,0:T(8,128)} %constant.16.clone.arrival_ref) | copy-start | bytes 73732
  63.1 5.0 %copy-start = (bf16[8,176,768]{2,1,0:T(8,128)(2,1)}, bf16[8,176,768]{2,1,0:T(8,128)(2,1)S(1)}, u32[]{:S(2)}) copy-start(bf16[8,176,768]{2,1,0:T(8,128)(2,1)S(1)} %all_to_all.35.own_ref) | copy-start | bytes 6488068
  63.2 9.9 %copy-start.6 = (s32[2]{0:T(128)S(1)}, s32[2]{0:T(128)}, u32[]{:S(2)}) copy-start(s32[2]{0:T(128)} %lengths_ref.3) | copy-start | bytes 28
  63.2 1.9 collective-permute-start.4
  68.1 1.1 copy-start.15
  69.3 0.9 copy-start.16
  70.2 0.6 copy-start.19
  70.8 10.4 %copy-start.3 = (bf16[384,1024]{1,0:T(8,128)(2,1)}, bf16[384,1024]{1,0:T(8,128)(2,1)S(1)}, u32[]{:S(2)}) copy-start(bf16[384,1024]{1,0:T(8,128)(2,1)S(1)} %get-tuple-element.46.own_ref) | copy-start | bytes 2359300
  70.8 10.4 %copy-start.17 = (bf16[192,1024]{1,0:T(8,128)(2,1)}, bf16[192,1024]{1,0:T(8,128)(2,1)S(1)}, u32[]{:S(2)}) copy-start(bf16[192,1024]{1,0:T(8,128)(2,1)S(1)} %get-tuple-element.45.q_ref) | copy-start | bytes 1179652
  70.8 2.3 %collective-permute-start.5 = (bf16[384,1024]{1,0:T(8,128)(2,1)S(1)}, bf16[384,1024]{1,0:T(8,128)(2,1)S(1)}, u32[]{:S(2)}, u32[]{:S(2)}) collective-permute-start(bf16[384,1024]{1,0:T(8,128)(2,1)S(1)} %get-tuple-element.46.own_ref), channel_id=1, source_target_pairs={{0,8},{8,0},{16,24},{24,16},{32,40},{40,32},{48,56},{56,48},{64,72... | collective-permute-start | bytes 2359304 | tf_op jit(solution)/shard_map/ppermute | solution.py:739
  73.1 8.1 %copy-start.4 = (bf16[384,1024]{1,0:T(8,128)(2,1)}, bf16[384,1024]{1,0:T(8,128)(2,1)S(1)}, u32[]{:S(2)}) copy-start(bf16[384,1024]{1,0:T(8,128)(2,1)S(1)} %collective-permute-done.5.other_ref) | copy-start | bytes 2359300
  73.1 13.6 %copy-start.25 = (bf16[128,2,768]{2,1,0:T(2,128)(2,1)S(1)}, bf16[128,2,768]{2,1,0:T(2,128)(2,1)}, u32[]{:S(2)}) copy-start(bf16[128,2,768]{2,1,0:T(2,128)(2,1)} %param.27) | copy-start | bytes 1179652
  81.2 0.9 copy-start.18
  82.1 13.7 %copy-start.21 = (f32[3,1024]{1,0:T(4,128)}, f32[3,1024]{1,0:T(4,128)S(1)}, u32[]{:S(2)}) copy-start(f32[3,1024]{1,0:T(4,128)S(1)} %get-tuple-element.55.lse_ref) | copy-start | bytes 36868
  82.1 12.9 %copy-start.9 = (s32[1,768]{1,0:T(1,128)S(1)}, s32[1,768]{1,0:T(1,128)}, u32[]{:S(2)}) copy-start(s32[1,768]{1,0:T(1,128)} %constant.12.clone.order_ref) | copy-start | bytes 9220
  82.1 12.9 %all-to-all-start.1 = ((bf16[8,192,128]{2,1,0:T(8,128)(2,1)}), bf16[8,192,128]{2,1,0:T(8,128)(2,1)S(1)}, u32[]{:S(2)}, u32[]{:S(2)}) async-start(bf16[8,192,128]{2,1,0:T(8,128)(2,1)} %get-tuple-element.47), calls=%async_computation.1 | async-start | bytes 786432 | tf_op jit(solution)/shard_map/all_to_all | solution.py:756
  86.4 101.4 %reduce-scatter.2.cloned.1.call-start = ((), (), s32[]{:S(2)}) async-start(), calls=%async_computation.8 | async-start | bytes 10027008 | tf_op jit(solution)/shard_map/reduce_scatter | solution.py:765
  95.8 1.1 copy-start.11
  96.9 0.8 copy-start.12
  97.6 0.8 copy-start.14
  114.2 13.9 %all-to-all-start.3 = ((bf16[8,192,128]{2,1,0:T(8,128)(2,1)}), bf16[8,192,128]{2,1,0:T(8,128)(2,1)S(1)}, u32[]{:S(2)}, u32[]{:S(2)}) async-start(bf16[8,192,128]{2,1,0:T(8,128)(2,1)} %get-tuple-element.56), calls=%async_computation.3 | async-start | bytes 786432 | tf_op jit(solution)/shard_map/all_to_all | solution.py:769
  128.1 3.8 %copy-start.26 = (bf16[8,192,128]{2,1,0:T(8,128)(2,1)}, bf16[8,192,128]{2,1,0:T(8,128)(2,1)S(1)}, u32[]{:S(2)}) copy-start(bf16[8,192,128]{2,1,0:T(8,128)(2,1)S(1)} %all-to-all-done.3.da_ref) | copy-start | bytes 1179652
  128.1 22.3 %all-to-all-start.4 = ((bf16[8,96,768]{2,1,0:T(8,128)(2,1)}), bf16[8,96,768]{2,1,0:T(8,128)(2,1)S(1)}, u32[]{:S(2)}, u32[]{:S(2)}) async-start(bf16[8,96,768]{2,1,0:T(8,128)(2,1)} %shard_map.248), calls=%async_computation.4 | async-start | bytes 2359296 | tf_op jit(solution)/shard_map/all_to_all | solution.py:770
  147.3 3.2 %collective-permute-start.6 = (bf16[384,1024]{1,0:T(8,128)(2,1)}, bf16[384,1024]{1,0:T(8,128)(2,1)S(1)}, u32[]{:S(2)}, u32[]{:S(2)}) collective-permute-start(bf16[384,1024]{1,0:T(8,128)(2,1)} %get-tuple-element.59), channel_id=1, source_target_pairs={{0,8},{8,0},{16,24},{24,16},{32,40},{40,32},{48,56},{56,48},{64,72... | collective-permute-start | bytes 2359304 | tf_op jit(solution)/shard_map/ppermute | solution.py:792
  150.5 1.0 copy-start.22
  150.5 1.3 copy-start.27
  160.6 7.4 %collective-permute-start.7 = (bf16[4,2,48,768]{3,2,1,0:T(8,128)(2,1)}, bf16[4,2,48,768]{3,2,1,0:T(8,128)(2,1)S(1)}, u32[]{:S(2)}, u32[]{:S(2)}) collective-permute-start(bf16[4,2,48,768]{3,2,1,0:T(8,128)(2,1)} %get-tuple-element.67), channel_id=1, source_target_pairs={{0,8},{8,0},{16,24},{24,16},{32,40},{40,32},{48,56},{56,48},{64,72... | collective-permute-start | bytes 1769480 | tf_op jit(solution)/shard_map/ppermute | solution.py:805
  160.6 7.4 %copy-start.23 = (bf16[4,2,48,768]{3,2,1,0:T(8,128)(2,1)S(1)}, bf16[4,2,48,768]{3,2,1,0:T(8,128)(2,1)}, u32[]{:S(2)}) copy-start(bf16[4,2,48,768]{3,2,1,0:T(8,128)(2,1)} %get-tuple-element.66) | copy-start | bytes 1769476
  160.6 32.0 %all-to-all-start.5 = ((bf16[8,128,768]{2,1,0:T(8,128)(2,1)}), bf16[8,128,768]{2,1,0:T(8,128)(2,1)S(1)}, u32[]{:S(2)}, u32[]{:S(2)}) async-start(bf16[8,128,768]{2,1,0:T(8,128)(2,1)} %get-tuple-element.65), calls=%async_computation.5 | async-start | bytes 3145728 | tf_op jit(solution)/shard_map/all_to_all | solution.py:813
  168.2 7.2 %collective-permute-start.8 = (bf16[2,48,768]{2,1,0:T(8,128)(2,1)S(1)}, bf16[2,48,768]{2,1,0:T(8,128)(2,1)S(1)}, u32[]{:S(2)}, u32[]{:S(2)}) collective-permute-start(bf16[2,48,768]{2,1,0:T(8,128)(2,1)S(1)} %get-tuple-element.78), channel_id=1, source_target_pairs={{0,1},{1,2},{2,3},{3,0},{4,5},{5,6},{6,7},{7,4},{8,9},{9,10},{10,1... | collective-permute-start | bytes 442376 | tf_op jit(solution)/shard_map/ppermute | solution.py:808
  169.1 8.3 %collective-permute-start.10 = (bf16[2,48,768]{2,1,0:T(8,128)(2,1)S(1)}, bf16[2,48,768]{2,1,0:T(8,128)(2,1)S(1)}, u32[]{:S(2)}, u32[]{:S(2)}) collective-permute-start(bf16[2,48,768]{2,1,0:T(8,128)(2,1)S(1)} %get-tuple-element.79), channel_id=1, source_target_pairs={{0,3},{1,0},{2,1},{3,2},{4,7},{5,4},{6,5},{7,6},{8,11},{9,8},{10,9... | collective-permute-start | bytes 442376 | tf_op jit(solution)/shard_map/ppermute | solution.py:810
  171.6 11.7 %collective-permute-start.9 = (bf16[2,48,768]{2,1,0:T(8,128)(2,1)S(1)}, bf16[2,48,768]{2,1,0:T(8,128)(2,1)S(1)}, u32[]{:S(2)}, u32[]{:S(2)}) collective-permute-start(bf16[2,48,768]{2,1,0:T(8,128)(2,1)S(1)} %get-tuple-element.80), channel_id=1, source_target_pairs={{0,2},{1,3},{2,0},{3,1},{4,6},{5,7},{6,4},{7,5},{8,10},{9,11},{10,... | collective-permute-start | bytes 442376 | tf_op jit(solution)/shard_map/ppermute | solution.py:809
  183.4 4.4 %collective-permute-start.11 = (bf16[48,768]{1,0:T(8,128)(2,1)S(1)}, bf16[48,768]{1,0:T(8,128)(2,1)S(1)}, u32[]{:S(2)}, u32[]{:S(2)}) collective-permute-start(bf16[48,768]{1,0:T(8,128)(2,1)S(1)} %slice_bitcast_fusion.4), channel_id=1, source_target_pairs={{0,20},{1,21},{2,22},{3,23},{4,16},{5,17},{6,18},{7,19},{8,28},{9,... | collective-permute-start | bytes 221192 | tf_op jit(solution)/shard_map/ppermute | solution.py:812
  187.8 1.1 copy-start.5
  190.3 9.2 %copy-start.2 = (bf16[128,2,768]{2,0,1:T(8,128)(2,1)S(1)}, bf16[128,2,768]{2,0,1:T(8,128)(2,1)}, u32[]{:S(2)}) copy-start(bf16[128,2,768]{2,0,1:T(8,128)(2,1)} %copy-done.1) | copy-start | bytes 1179652
  190.3 9.2 %copy-start.13 = (f32[256,768]{1,0:T(8,128)S(1)}, f32[256,768]{1,0:T(8,128)}, u32[]{:S(2)}) copy-start(f32[256,768]{1,0:T(8,128)} %get-tuple-element.53.dfirst_ref) | copy-start | bytes 2359300
  190.3 9.2 %copy-start.20 = (f32[8,768]{1,0:T(8,128)S(1)}, f32[8,768]{1,0:T(8,128)}, u32[]{:S(2)}) copy-start(f32[8,768]{1,0:T(8,128)} %copy-done.19) | copy-start | bytes 73732
  192.6 14.5 %all-to-all-start.6 = ((bf16[8,56,768]{2,1,0:T(8,128)(2,1)}), bf16[8,56,768]{2,1,0:T(8,128)(2,1)S(1)}, u32[]{:S(2)}, u32[]{:S(2)}) async-start(bf16[8,56,768]{2,1,0:T(8,128)(2,1)} %shard_map.251), calls=%async_computation.7 | async-start | bytes 1376256 | tf_op jit(solution)/shard_map/all_to_all | solution.py:829
  199.5 7.6 %copy-start.8 = (s32[1,768]{1,0:T(1,128)S(1)}, s32[1,768]{1,0:T(1,128)}, u32[]{:S(2)}) copy-start(s32[1,768]{1,0:T(1,128)} %constant.13.clone.units_ref) | copy-start | bytes 9220
Sparse Core Ops, SparseCore 0:
  30.7 67.1 all-gather.2
  114.4 68.9 reduce-scatter.1

commit v8 on v7

--- a/solution.py
+++ b/solution.py
@@ -132,7 +132,7 @@
     raw_ref[...] = raw_scr[...].astype(BF)
 
 
-def regroup_kernel(slots_ref, order_ref, far_ref, rest_ref, scr):
+def regroup_kernel(slots_ref, order_ref, near_ref, rest_ref, scr):
     for j in range(8):
         scr[j * 56 : j * 56 + 56, :] = slots_ref[j].astype(F32)
     rows = dot(places(order_ref[...], 448), scr[...].astype(BF), TN).astype(BF)
@@ -703,7 +703,7 @@
     rest = call(
         regroup_kernel,
         shape((432, 768), BF),
-        (slots, regroup, far),
+        (slots, regroup, near),
         2,
         [pltpu.VMEM((448, 768), F32)],
         mib=12,

time: 219 us -> 217 us (level); the launches traced: 216 us -> 216 us
  starting transfers between devices: 43 us -> 35.4 us
  Pallas kernels: 62.9 us -> 69.2 us
  waiting for transfers between devices: 49.6 us -> 53.6 us
    pallas_call x12, Pallas kernels: 60.8 us -> 67.1 us  [call(): pl.pallas_call(kernel, out_shape=outs, scratch_shapes=list(scratch), cost...]
    all_to_all x1, waiting for transfers between devices: 3.17 us -> 0.01 us  [body(): exchange(call(out_kernel, shape((8, 96, 768), BF), (attended_t, low), 2))]
    all_to_all x2, waiting for transfers between devices: 5.11 us -> 8.18 us  [body(): slots = exchange(slots)]
    ppermute x1, waiting for transfers between devices: 5.79 us -> 2.99 us  [body(): lax.ppermute(line[2], 'batch', along_x(2))]
    all_to_all x1, waiting for transfers between devices: 2.3 us -> 4.82 us  [body(): back = exchange(part)]
    ppermute x1, waiting for transfers between devices: 0.01 us -> 2.48 us  [body(): partner = lax.ppermute(dkv_other, 'seq', SWAP_CORE)]
  transfers between devices with their start and end apart: 20 -> 20, of which waited for: 14 -> 15; matrix products, arithmetic and copies ran while one was open for 2% -> 2% of each run, Pallas kernels for 19% -> 22%
where the time goes in v8:
time: 217 us; the launch traced here: 216 us
  Pallas kernels  69.2 us (32%)
  waiting for transfers between devices  53.6 us (25%)
  starting transfers between devices  35.4 us (16%)
  blocking collectives  30.4 us (14%)
  between operations  14.4 us (7%)
  local copies, waits for them, and re-layouts  12.4 us (6%)
    pallas_call x12, Pallas kernels, call(): pl.pallas_call(kernel, out_shape=outs, scratch_shapes=list(scratch), cost...  67.1 us
    all_to_all x1, blocking collectives, body(): own = exchange(sent)  30.4 us
    all_to_all x2, starting transfers between devices, body(): slots = exchange(slots)  9.21 us
    unnamed x57, local copies, waits for them, and re-layouts  8.22 us
    all_to_all x2, waiting for transfers between devices, body(): slots = exchange(slots)  8.18 us
    all_to_all x1, waiting for transfers between devices, body(): att = exchange(o_low)  7.65 us
    ppermute x3, starting transfers between devices, body(): lax.ppermute(raw, 'batch', along_x(step))  5.72 us
    all_to_all x1, starting transfers between devices, body(): back = exchange(part)  5.54 us
  transfers between devices with their start and end apart: 20, of which 15 were waited for; matrix products, arithmetic and copies ran while one was open for 2% of the time, Pallas kernels for 22%

profile of v8, /device:TPU:64, one launch (start us, length us, event | category | flops | bytes accessed | tf_op | source)
XLA Modules:
  0.0 216.5 jit_solution(5088234554033960080)
XLA Ops:
  7.2 2.1 shard_map.240
  9.3 5.7 %all-to-all-start.2 = ((bf16[8,56,768]{2,1,0:T(8,128)(2,1)}), bf16[8,56,768]{2,1,0:T(8,128)(2,1)S(1)}, u32[]{:S(2)}, u32[]{:S(2)}) async-start(bf16[8,56,768]{2,1,0:T(8,128)(2,1)} %get-tuple-element.51), calls=%async_computation.2 | async-start | bytes 1376256 | tf_op jit(solution)/shard_map/all_to_all | solution.py:700
  15.0 0.0 all-gather.3.cloned.1.call-start
  15.0 1.6 collective-permute-start.2
  16.6 2.7 %collective-permute-start.1 = (bf16[24,640]{1,0:T(8,128)(2,1)}, bf16[24,640]{1,0:T(8,128)(2,1)S(1)}, u32[]{:S(2)}, u32[]{:S(2)}) collective-permute-start(bf16[24,640]{1,0:T(8,128)(2,1)} %get-tuple-element.44), channel_id=1, source_target_pairs={{0,2},{1,3},{2,0},{3,1},{4,6},{5,7},{6,4},{7,5},{8,10},{9,11},{10,... | collective-permute-start | bytes 92168 | tf_op jit(solution)/shard_map/ppermute | solution.py:701
  19.3 1.4 collective-permute-start
  20.7 1.4 collective-permute-done.1
  22.2 1.2 collective-permute-done
  23.4 0.8 pad_maximum_fusion.near_ref
  24.2 2.0 all-to-all-done.2.slots_ref
  26.2 1.5 shard_map.245
  27.7 0.1 collective-permute-start.3
  27.8 4.8 %collective-permute-done.3.far_ref = bf16[4,24,640]{2,1,0:T(8,128)(2,1)S(1)} collective-permute-done((bf16[4,24,640]{2,1,0:T(8,128)(2,1)S(1)}, bf16[4,24,640]{2,1,0:T(8,128)(2,1)S(1)}, u32[]{:S(2)}, u32[]{:S(2)}) %collective-permute-start.3) | collective-permute-done | bytes 122912 | tf_op jit(solution)/shard_map/ppermute | solution.py:702
  32.6 0.2 shard_map.241
  32.9 30.4 %all_to_all.35.own_ref = bf16[8,176,768]{2,1,0:T(8,128)(2,1)S(1)} all-to-all(bf16[8,176,768]{2,1,0:T(8,128)(2,1)S(1)} %shard_map.241), channel_id=1, replica_groups={{0,16,32,48,64,80,96,112},{8,24,40,56,72,88,104,120},{1,17,33,49,65,81,..., dimensions={0} | all-to-all | bytes 4325376 | tf_op jit(solution)/shard_map/all_to_all | solution.py:724
  63.4 0.1 collective-permute-start.4
  63.5 2.0 collective-permute-done.4.other_ref
  65.5 3.0 %shard_map.242 = (bf16[1024,768]{1,0:T(8,128)(2,1)S(1)}, bf16[576,768]{1,0:T(8,128)(2,1)S(1)}, f32[8,768]{1,0:T(8,128)S(1)}, bf16[192,1024]{1,0:T(8,128)(2,1)S(1)}, bf16[384,1024]{1,0:T(8,128)(2,1)S(1)}) custom-call(bf16[8,176,768]{2,1,0:T(8,128)(2,1)S(1)} %all_to_all.35.own_ref, bf16[8,48,640]{2,1,0:T(8,128)(2,1)S(1)} %collective-permute-done.4.other_ref, ...), custom_call_target="tpu_custom_call" | custom-call | flops 5500000256 | tf_op jit(solution)/shard_map/pallas_call | solution.py:88
  68.5 1.1 copy-done.15
  69.6 0.9 copy-done.16
  70.5 0.6 copy-done.19
  71.1 0.1 collective-permute-start.5
  71.3 2.1 collective-permute-done.5.other_ref
  73.4 10.2 %shard_map.243 = (f32[192,1024]{1,0:T(8,128)S(1)}, bf16[8,192,128]{2,1,0:T(8,128)(2,1)}, f32[3,1024]{1,0:T(4,128)S(1)}) custom-call(s32[2]{0:T(128)S(1)} %copy-done.6, bf16[192,1024]{1,0:T(8,128)(2,1)S(1)} %get-tuple-element.45.q_ref, bf16[384,1024]{1,0:T(8,128)(2,1)S(1)} %get-tuple-element.46.own_ref, bf16[384,1024]{1,0:T(8,128)(2,1)S(1)} %collective-permute-done.5.other_ref), custom_call_target="tpu_custom_call" | custom-call | flops 13200000000 | tf_op jit(solution)/shard_map/pallas_call | solution.py:88
  83.7 0.9 copy-done.18
  84.6 3.6 %all-to-all-start.1 = ((bf16[8,192,128]{2,1,0:T(8,128)(2,1)}), bf16[8,192,128]{2,1,0:T(8,128)(2,1)S(1)}, u32[]{:S(2)}, u32[]{:S(2)}) async-start(bf16[8,192,128]{2,1,0:T(8,128)(2,1)} %get-tuple-element.47), calls=%async_computation.1 | async-start | bytes 786432 | tf_op jit(solution)/shard_map/all_to_all | solution.py:756
  88.2 0.2 reduce-scatter.2.cloned.1.call-start
  88.4 0.8 copy.28
  89.2 7.7 %all-to-all-done.1.att_ref = bf16[8,192,128]{2,1,0:T(8,128)(2,1)S(1)} async-done(((bf16[8,192,128]{2,1,0:T(8,128)(2,1)}), bf16[8,192,128]{2,1,0:T(8,128)(2,1)S(1)}, u32[]{:S(2)}, u32[]{:S(2)}) %all-to-all-start.1) | async-done | bytes 393248 | tf_op jit(solution)/shard_map/all_to_all | solution.py:756
  96.9 0.7 shard_map.244
  97.6 1.1 copy-done.11
  98.7 0.8 copy-done.12
  99.5 0.8 copy-done.14
  100.2 15.8 %shard_map.246 = (bf16[256,768]{1,0:T(8,128)(2,1)}, f32[256,768]{1,0:T(8,128)}, bf16[256,768]{1,0:T(8,128)(2,1)}, bf16[8,192,128]{2,1,0:T(8,128)(2,1)}, f32[8,768]{1,0:T(8,128)}, /*index=5*/bf16[16,384,768]{2,1,0:T(8,128)(2,1)}) custom-call(bf16[256,768]{1,0:T(8,128)(2,1)} %bitcast.48, bf16[256,768]{1,0:T(8,128)(2,1)} %bitcast.56, ...), custom_call_target="tpu_custom_call" | custom-call | flops 16499999744 | tf_op jit(solution)/shard_map/pallas_call | solution.py:88
  116.1 0.0 reduce-scatter.2.cloned.1.call-update
  116.1 3.5 %all-to-all-start.3 = ((bf16[8,192,128]{2,1,0:T(8,128)(2,1)}), bf16[8,192,128]{2,1,0:T(8,128)(2,1)S(1)}, u32[]{:S(2)}, u32[]{:S(2)}) async-start(bf16[8,192,128]{2,1,0:T(8,128)(2,1)} %get-tuple-element.56), calls=%async_computation.3 | async-start | bytes 786432 | tf_op jit(solution)/shard_map/all_to_all | solution.py:769
  119.6 2.7 %shard_map.248 = bf16[8,96,768]{2,1,0:T(8,128)(2,1)} custom-call(bf16[768,256]{1,0:T(8,128)(2,1)} %copy-done.12, bf16[256,768]{1,0:T(8,128)(2,1)} %get-tuple-element.64.low_ref), custom_call_target="tpu_custom_call" | custom-call | flops 2200000000 | tf_op jit(solution)/shard_map/pallas_call | solution.py:88
  122.2 5.3 %all-to-all-done.3.da_ref = bf16[8,192,128]{2,1,0:T(8,128)(2,1)S(1)} async-done(((bf16[8,192,128]{2,1,0:T(8,128)(2,1)}), bf16[8,192,128]{2,1,0:T(8,128)(2,1)S(1)}, u32[]{:S(2)}, u32[]{:S(2)}) %all-to-all-start.3) | async-done | bytes 393248 | tf_op jit(solution)/shard_map/all_to_all | solution.py:769
  127.5 3.8 %all-to-all-start.4 = ((bf16[8,96,768]{2,1,0:T(8,128)(2,1)}), bf16[8,96,768]{2,1,0:T(8,128)(2,1)S(1)}, u32[]{:S(2)}, u32[]{:S(2)}) async-start(bf16[8,96,768]{2,1,0:T(8,128)(2,1)} %shard_map.248), calls=%async_computation.4 | async-start | bytes 2359296 | tf_op jit(solution)/shard_map/all_to_all | solution.py:770
  131.3 19.6 %shard_map.247 = (bf16[192,1024]{1,0:T(8,128)(2,1)}, bf16[384,1024]{1,0:T(8,128)(2,1)}, bf16[384,1024]{1,0:T(8,128)(2,1)}) custom-call(s32[2]{0:T(128)} %lengths_ref.3, bf16[192,1024]{1,0:T(8,128)(2,1)} %copy-done.17, bf16[384,1024]{1,0:T(8,128)(2,1)} %copy-done.3, bf16[384,1024]{1,0:T(8,128)(2,1)} %copy-done.4, f32[192,1024]{1,0:T(8,128)} %copy-done.18, ...), custom_call_target="tpu_custom_call" | custom-call | flops 22000001024 | tf_op jit(solution)/shard_map/pallas_call | solution.py:88
  150.9 2.5 %collective-permute-done.6.partner_ref = bf16[384,1024]{1,0:T(8,128)(2,1)S(1)} collective-permute-done((bf16[384,1024]{1,0:T(8,128)(2,1)}, bf16[384,1024]{1,0:T(8,128)(2,1)S(1)}, u32[]{:S(2)}, u32[]{:S(2)}) %collective-permute-start.6) | collective-permute-done | bytes 786464 | tf_op jit(solution)/shard_map/ppermute | solution.py:792
  153.4 0.9 copy-done.27
  154.3 8.9 %shard_map.249 = (bf16[8,128,768]{2,1,0:T(8,128)(2,1)}, bf16[4,2,48,768]{3,2,1,0:T(8,128)(2,1)}, bf16[4,2,48,768]{3,2,1,0:T(8,128)(2,1)}) custom-call(bf16[8,176,768]{2,1,0:T(8,128)(2,1)} %copy-done, bf16[192,1024]{1,0:T(8,128)(2,1)} %get-tuple-element.57.dq_ref, bf16[384,1024]{1,0:T(8,128)(2,1)} %get-tuple-element.58.dkv_ref, bf16[384,1024]{1,0:T(8,128)(2,1)} %copy-done.27, ...), custom_call_target="tpu_custom_call" | custom-call | flops 7699999744 | tf_op jit(solution)/shard_map/pallas_call | solution.py:88
  163.2 0.2 collective-permute-start.7
  163.3 5.5 %all-to-all-start.5 = ((bf16[8,128,768]{2,1,0:T(8,128)(2,1)}), bf16[8,128,768]{2,1,0:T(8,128)(2,1)S(1)}, u32[]{:S(2)}, u32[]{:S(2)}) async-start(bf16[8,128,768]{2,1,0:T(8,128)(2,1)} %get-tuple-element.65), calls=%async_computation.5 | async-start | bytes 3145728 | tf_op jit(solution)/shard_map/all_to_all | solution.py:813
  168.9 0.1 add_convert_fusion
  169.1 1.1 collective-permute-start.8
  170.2 2.2 %collective-permute-start.10 = (bf16[2,48,768]{2,1,0:T(8,128)(2,1)S(1)}, bf16[2,48,768]{2,1,0:T(8,128)(2,1)S(1)}, u32[]{:S(2)}, u32[]{:S(2)}) collective-permute-start(bf16[2,48,768]{2,1,0:T(8,128)(2,1)S(1)} %get-tuple-element.79), channel_id=1, source_target_pairs={{0,3},{1,0},{2,1},{3,2},{4,7},{5,4},{6,5},{7,6},{8,11},{9,8},{10,9... | collective-permute-start | bytes 442376 | tf_op jit(solution)/shard_map/ppermute | solution.py:810
  172.4 3.9 %collective-permute-done.8 = bf16[2,48,768]{2,1,0:T(8,128)(2,1)S(1)} collective-permute-done((bf16[2,48,768]{2,1,0:T(8,128)(2,1)S(1)}, bf16[2,48,768]{2,1,0:T(8,128)(2,1)S(1)}, u32[]{:S(2)}, u32[]{:S(2)}) %collective-permute-start.8) | collective-permute-done | bytes 147488 | tf_op jit(solution)/shard_map/ppermute | solution.py:808
  176.3 2.3 %collective-permute-done.10 = bf16[2,48,768]{2,1,0:T(8,128)(2,1)S(1)} collective-permute-done((bf16[2,48,768]{2,1,0:T(8,128)(2,1)S(1)}, bf16[2,48,768]{2,1,0:T(8,128)(2,1)S(1)}, u32[]{:S(2)}, u32[]{:S(2)}) %collective-permute-start.10) | collective-permute-done | bytes 147488 | tf_op jit(solution)/shard_map/ppermute | solution.py:810
  178.6 3.0 %collective-permute-done.9 = bf16[2,48,768]{2,1,0:T(8,128)(2,1)S(1)} collective-permute-done((bf16[2,48,768]{2,1,0:T(8,128)(2,1)S(1)}, bf16[2,48,768]{2,1,0:T(8,128)(2,1)S(1)}, u32[]{:S(2)}, u32[]{:S(2)}) %collective-permute-start.9) | collective-permute-done | bytes 147488 | tf_op jit(solution)/shard_map/ppermute | solution.py:809
  181.6 0.1 fusion.2
  181.7 0.1 collective-permute-start.11
  181.8 4.3 %collective-permute-done.11 = bf16[48,768]{1,0:T(8,128)(2,1)S(1)} collective-permute-done((bf16[48,768]{1,0:T(8,128)(2,1)S(1)}, bf16[48,768]{1,0:T(8,128)(2,1)S(1)}, u32[]{:S(2)}, u32[]{:S(2)}) %collective-permute-start.11) | collective-permute-done | bytes 73760 | tf_op jit(solution)/shard_map/ppermute | solution.py:812
  186.1 0.0 reduce-scatter.2.cloned.1.call-done.rest_ref
  186.2 1.1 copy-done.5
  187.2 1.4 shard_map.251
  188.6 4.8 %all-to-all-done.5.got_ref = bf16[8,128,768]{2,1,0:T(8,128)(2,1)S(1)} async-done(((bf16[8,128,768]{2,1,0:T(8,128)(2,1)}), bf16[8,128,768]{2,1,0:T(8,128)(2,1)S(1)}, u32[]{:S(2)}, u32[]{:S(2)}) %all-to-all-start.5) | async-done | bytes 1572896 | tf_op jit(solution)/shard_map/all_to_all | solution.py:813
  193.4 3.5 %all-to-all-start.6 = ((bf16[8,56,768]{2,1,0:T(8,128)(2,1)}), bf16[8,56,768]{2,1,0:T(8,128)(2,1)S(1)}, u32[]{:S(2)}, u32[]{:S(2)}) async-start(bf16[8,56,768]{2,1,0:T(8,128)(2,1)} %shard_map.251), calls=%async_computation.7 | async-start | bytes 1376256 | tf_op jit(solution)/shard_map/all_to_all | solution.py:829
  197.0 2.1 copy.36
  199.1 1.3 shard_map.250
  200.5 1.1 copy.35
  201.6 6.2 %all-to-all-done.6.got_ref = bf16[8,56,768]{2,1,0:T(8,128)(2,1)S(1)} async-done(((bf16[8,56,768]{2,1,0:T(8,128)(2,1)}), bf16[8,56,768]{2,1,0:T(8,128)(2,1)S(1)}, u32[]{:S(2)}, u32[]{:S(2)}) %all-to-all-start.6) | async-done | bytes 688160 | tf_op jit(solution)/shard_map/all_to_all | solution.py:829
  207.8 1.9 shard_map.252
  (59 shorter events, 0.3 us)
Async XLA Ops:
  9.3 16.9 %copy-start.10 = (s32[1,512]{1,0:T(1,128)S(1)}, s32[1,512]{1,0:T(1,128)}, u32[]{:S(2)}) copy-start(s32[1,512]{1,0:T(1,128)} %constant.14.clone.order_ref) | copy-start | bytes 6148
  9.3 16.9 %all-to-all-start.2 = ((bf16[8,56,768]{2,1,0:T(8,128)(2,1)}), bf16[8,56,768]{2,1,0:T(8,128)(2,1)S(1)}, u32[]{:S(2)}, u32[]{:S(2)}) async-start(bf16[8,56,768]{2,1,0:T(8,128)(2,1)} %get-tuple-element.51), calls=%async_computation.2 | async-start | bytes 1376256 | tf_op jit(solution)/shard_map/all_to_all | solution.py:700
  15.0 85.3 %all-gather.3.cloned.1.call-start = ((), (), s32[]{:S(2)}) async-start(), calls=%async_computation.9 | async-start | bytes 11280384 | tf_op jit(solution)/shard_map/all_gather | solution.py:713
  15.0 5.7 %collective-permute-start.2 = (bf16[24,640]{1,0:T(8,128)(2,1)}, bf16[24,640]{1,0:T(8,128)(2,1)S(1)}, u32[]{:S(2)}, u32[]{:S(2)}) collective-permute-start(bf16[24,640]{1,0:T(8,128)(2,1)} %get-tuple-element.44), channel_id=1, source_target_pairs={{0,1},{1,2},{2,3},{3,0},{4,5},{5,6},{6,7},{7,4},{8,9},{9,10},{10,1... | collective-permute-start | bytes 92168 | tf_op jit(solution)/shard_map/ppermute | solution.py:701
  16.6 5.6 %collective-permute-start.1 = (bf16[24,640]{1,0:T(8,128)(2,1)}, bf16[24,640]{1,0:T(8,128)(2,1)S(1)}, u32[]{:S(2)}, u32[]{:S(2)}) collective-permute-start(bf16[24,640]{1,0:T(8,128)(2,1)} %get-tuple-element.44), channel_id=1, source_target_pairs={{0,2},{1,3},{2,0},{3,1},{4,6},{5,7},{6,4},{7,5},{8,10},{9,11},{10,... | collective-permute-start | bytes 92168 | tf_op jit(solution)/shard_map/ppermute | solution.py:701
  19.3 4.1 %collective-permute-start = (bf16[24,640]{1,0:T(8,128)(2,1)}, bf16[24,640]{1,0:T(8,128)(2,1)S(1)}, u32[]{:S(2)}, u32[]{:S(2)}) collective-permute-start(bf16[24,640]{1,0:T(8,128)(2,1)} %get-tuple-element.44), channel_id=1, source_target_pairs={{0,3},{1,0},{2,1},{3,2},{4,7},{5,4},{6,5},{7,6},{8,11},{9,8},{10,9... | collective-permute-start | bytes 92168 | tf_op jit(solution)/shard_map/ppermute | solution.py:701
  24.2 3.6 %copy-start.24 = (bf16[128,2,768]{2,1,0:T(2,128)(2,1)S(1)}, bf16[128,2,768]{2,1,0:T(2,128)(2,1)}, u32[]{:S(2)}) copy-start(bf16[128,2,768]{2,1,0:T(2,128)(2,1)} %param.17) | copy-start | bytes 1179652
  27.7 5.0 %collective-permute-start.3 = (bf16[4,24,640]{2,1,0:T(8,128)(2,1)S(1)}, bf16[4,24,640]{2,1,0:T(8,128)(2,1)S(1)}, u32[]{:S(2)}, u32[]{:S(2)}) collective-permute-start(bf16[4,24,640]{2,1,0:T(8,128)(2,1)S(1)} %pad_maximum_fusion.near_ref), channel_id=1, source_target_pairs={{0,20},{1,21},{2,22},{3,23},{4,16},{5,17},{6,18},{7,19},{8,28},{9,... | collective-permute-start | bytes 368648 | tf_op jit(solution)/shard_map/ppermute | solution.py:702
  27.8 5.0 %copy-start.1 = (bf16[128,2,768]{2,0,1:T(8,128)(2,1)}, bf16[128,2,768]{2,0,1:T(8,128)(2,1)S(1)}, u32[]{:S(2)}) copy-start(bf16[128,2,768]{2,0,1:T(8,128)(2,1)S(1)} %copy.37) | copy-start | bytes 1179652
  32.9 32.6 %copy-start.7 = (s32[8,768]{1,0:T(8,128)S(1)}, s32[8,768]{1,0:T(8,128)}, u32[]{:S(2)}) copy-start(s32[8,768]{1,0:T(8,128)} %constant.16.clone.arrival_ref) | copy-start | bytes 73732
  63.3 5.1 %copy-start = (bf16[8,176,768]{2,1,0:T(8,128)(2,1)}, bf16[8,176,768]{2,1,0:T(8,128)(2,1)S(1)}, u32[]{:S(2)}) copy-start(bf16[8,176,768]{2,1,0:T(8,128)(2,1)S(1)} %all_to_all.35.own_ref) | copy-start | bytes 6488068
  63.4 10.1 %copy-start.6 = (s32[2]{0:T(128)S(1)}, s32[2]{0:T(128)}, u32[]{:S(2)}) copy-start(s32[2]{0:T(128)} %lengths_ref.3) | copy-start | bytes 28
  63.4 2.1 collective-permute-start.4
  68.5 1.1 copy-start.15
  69.6 0.9 copy-start.16
  70.5 0.6 copy-start.19
  71.1 12.5 %copy-start.3 = (bf16[384,1024]{1,0:T(8,128)(2,1)}, bf16[384,1024]{1,0:T(8,128)(2,1)S(1)}, u32[]{:S(2)}) copy-start(bf16[384,1024]{1,0:T(8,128)(2,1)S(1)} %get-tuple-element.46.own_ref) | copy-start | bytes 2359300
  71.1 12.5 %copy-start.17 = (bf16[192,1024]{1,0:T(8,128)(2,1)}, bf16[192,1024]{1,0:T(8,128)(2,1)S(1)}, u32[]{:S(2)}) copy-start(bf16[192,1024]{1,0:T(8,128)(2,1)S(1)} %get-tuple-element.45.q_ref) | copy-start | bytes 1179652
  71.1 2.3 %collective-permute-start.5 = (bf16[384,1024]{1,0:T(8,128)(2,1)S(1)}, bf16[384,1024]{1,0:T(8,128)(2,1)S(1)}, u32[]{:S(2)}, u32[]{:S(2)}) collective-permute-start(bf16[384,1024]{1,0:T(8,128)(2,1)S(1)} %get-tuple-element.46.own_ref), channel_id=1, source_target_pairs={{0,8},{8,0},{16,24},{24,16},{32,40},{40,32},{48,56},{56,48},{64,72... | collective-permute-start | bytes 2359304 | tf_op jit(solution)/shard_map/ppermute | solution.py:739
  73.4 10.3 %copy-start.4 = (bf16[384,1024]{1,0:T(8,128)(2,1)}, bf16[384,1024]{1,0:T(8,128)(2,1)S(1)}, u32[]{:S(2)}) copy-start(bf16[384,1024]{1,0:T(8,128)(2,1)S(1)} %collective-permute-done.5.other_ref) | copy-start | bytes 2359300
  73.4 15.0 %copy-start.25 = (bf16[128,2,768]{2,1,0:T(2,128)(2,1)S(1)}, bf16[128,2,768]{2,1,0:T(2,128)(2,1)}, u32[]{:S(2)}) copy-start(bf16[128,2,768]{2,1,0:T(2,128)(2,1)} %param.27) | copy-start | bytes 1179652
  83.7 0.9 copy-start.18
  84.6 13.0 %copy-start.21 = (f32[3,1024]{1,0:T(4,128)}, f32[3,1024]{1,0:T(4,128)S(1)}, u32[]{:S(2)}) copy-start(f32[3,1024]{1,0:T(4,128)S(1)} %get-tuple-element.55.lse_ref) | copy-start | bytes 36868
  84.6 12.3 %copy-start.9 = (s32[1,768]{1,0:T(1,128)S(1)}, s32[1,768]{1,0:T(1,128)}, u32[]{:S(2)}) copy-start(s32[1,768]{1,0:T(1,128)} %constant.12.clone.order_ref) | copy-start | bytes 9220
  84.6 12.3 %all-to-all-start.1 = ((bf16[8,192,128]{2,1,0:T(8,128)(2,1)}), bf16[8,192,128]{2,1,0:T(8,128)(2,1)S(1)}, u32[]{:S(2)}, u32[]{:S(2)}) async-start(bf16[8,192,128]{2,1,0:T(8,128)(2,1)} %get-tuple-element.47), calls=%async_computation.1 | async-start | bytes 786432 | tf_op jit(solution)/shard_map/all_to_all | solution.py:756
  88.2 97.9 %reduce-scatter.2.cloned.1.call-start = ((), (), s32[]{:S(2)}) async-start(), calls=%async_computation.8 | async-start | bytes 10027008 | tf_op jit(solution)/shard_map/reduce_scatter | solution.py:765
  97.6 1.1 copy-start.11
  98.7 0.8 copy-start.12
  99.5 0.8 copy-start.14
  116.1 11.4 %all-to-all-start.3 = ((bf16[8,192,128]{2,1,0:T(8,128)(2,1)}), bf16[8,192,128]{2,1,0:T(8,128)(2,1)S(1)}, u32[]{:S(2)}, u32[]{:S(2)}) async-start(bf16[8,192,128]{2,1,0:T(8,128)(2,1)} %get-tuple-element.56), calls=%async_computation.3 | async-start | bytes 786432 | tf_op jit(solution)/shard_map/all_to_all | solution.py:769
  127.5 3.8 %copy-start.26 = (bf16[8,192,128]{2,1,0:T(8,128)(2,1)}, bf16[8,192,128]{2,1,0:T(8,128)(2,1)S(1)}, u32[]{:S(2)}) copy-start(bf16[8,192,128]{2,1,0:T(8,128)(2,1)S(1)} %all-to-all-done.3.da_ref) | copy-start | bytes 1179652
  127.5 23.4 %all-to-all-start.4 = ((bf16[8,96,768]{2,1,0:T(8,128)(2,1)}), bf16[8,96,768]{2,1,0:T(8,128)(2,1)S(1)}, u32[]{:S(2)}, u32[]{:S(2)}) async-start(bf16[8,96,768]{2,1,0:T(8,128)(2,1)} %shard_map.248), calls=%async_computation.4 | async-start | bytes 2359296 | tf_op jit(solution)/shard_map/all_to_all | solution.py:770
  150.9 2.5 %collective-permute-start.6 = (bf16[384,1024]{1,0:T(8,128)(2,1)}, bf16[384,1024]{1,0:T(8,128)(2,1)S(1)}, u32[]{:S(2)}, u32[]{:S(2)}) collective-permute-start(bf16[384,1024]{1,0:T(8,128)(2,1)} %get-tuple-element.59), channel_id=1, source_target_pairs={{0,8},{8,0},{16,24},{24,16},{32,40},{40,32},{48,56},{56,48},{64,72... | collective-permute-start | bytes 2359304 | tf_op jit(solution)/shard_map/ppermute | solution.py:792
  150.9 2.5 %copy-start.22 = (bf16[8,96,768]{2,1,0:T(8,128)(2,1)}, bf16[8,96,768]{2,1,0:T(8,128)(2,1)S(1)}, u32[]{:S(2)}) copy-start(bf16[8,96,768]{2,1,0:T(8,128)(2,1)S(1)} %all-to-all-done.4.out_ref) | copy-start | bytes 3538948
  153.4 0.9 copy-start.27
  163.2 5.7 %collective-permute-start.7 = (bf16[4,2,48,768]{3,2,1,0:T(8,128)(2,1)}, bf16[4,2,48,768]{3,2,1,0:T(8,128)(2,1)S(1)}, u32[]{:S(2)}, u32[]{:S(2)}) collective-permute-start(bf16[4,2,48,768]{3,2,1,0:T(8,128)(2,1)} %get-tuple-element.67), channel_id=1, source_target_pairs={{0,8},{8,0},{16,24},{24,16},{32,40},{40,32},{48,56},{56,48},{64,72... | collective-permute-start | bytes 1769480 | tf_op jit(solution)/shard_map/ppermute | solution.py:805
  163.3 5.6 %copy-start.23 = (bf16[4,2,48,768]{3,2,1,0:T(8,128)(2,1)S(1)}, bf16[4,2,48,768]{3,2,1,0:T(8,128)(2,1)}, u32[]{:S(2)}) copy-start(bf16[4,2,48,768]{3,2,1,0:T(8,128)(2,1)} %get-tuple-element.66) | copy-start | bytes 1769476
  163.3 30.1 %all-to-all-start.5 = ((bf16[8,128,768]{2,1,0:T(8,128)(2,1)}), bf16[8,128,768]{2,1,0:T(8,128)(2,1)S(1)}, u32[]{:S(2)}, u32[]{:S(2)}) async-start(bf16[8,128,768]{2,1,0:T(8,128)(2,1)} %get-tuple-element.65), calls=%async_computation.5 | async-start | bytes 3145728 | tf_op jit(solution)/shard_map/all_to_all | solution.py:813
  169.1 7.2 %collective-permute-start.8 = (bf16[2,48,768]{2,1,0:T(8,128)(2,1)S(1)}, bf16[2,48,768]{2,1,0:T(8,128)(2,1)S(1)}, u32[]{:S(2)}, u32[]{:S(2)}) collective-permute-start(bf16[2,48,768]{2,1,0:T(8,128)(2,1)S(1)} %get-tuple-element.78), channel_id=1, source_target_pairs={{0,1},{1,2},{2,3},{3,0},{4,5},{5,6},{6,7},{7,4},{8,9},{9,10},{10,1... | collective-permute-start | bytes 442376 | tf_op jit(solution)/shard_map/ppermute | solution.py:808
  170.2 8.4 %collective-permute-start.10 = (bf16[2,48,768]{2,1,0:T(8,128)(2,1)S(1)}, bf16[2,48,768]{2,1,0:T(8,128)(2,1)S(1)}, u32[]{:S(2)}, u32[]{:S(2)}) collective-permute-start(bf16[2,48,768]{2,1,0:T(8,128)(2,1)S(1)} %get-tuple-element.79), channel_id=1, source_target_pairs={{0,3},{1,0},{2,1},{3,2},{4,7},{5,4},{6,5},{7,6},{8,11},{9,8},{10,9... | collective-permute-start | bytes 442376 | tf_op jit(solution)/shard_map/ppermute | solution.py:810
  172.4 9.2 %collective-permute-start.9 = (bf16[2,48,768]{2,1,0:T(8,128)(2,1)S(1)}, bf16[2,48,768]{2,1,0:T(8,128)(2,1)S(1)}, u32[]{:S(2)}, u32[]{:S(2)}) collective-permute-start(bf16[2,48,768]{2,1,0:T(8,128)(2,1)S(1)} %get-tuple-element.80), channel_id=1, source_target_pairs={{0,2},{1,3},{2,0},{3,1},{4,6},{5,7},{6,4},{7,5},{8,10},{9,11},{10,... | collective-permute-start | bytes 442376 | tf_op jit(solution)/shard_map/ppermute | solution.py:809
  181.7 4.4 %collective-permute-start.11 = (bf16[48,768]{1,0:T(8,128)(2,1)S(1)}, bf16[48,768]{1,0:T(8,128)(2,1)S(1)}, u32[]{:S(2)}, u32[]{:S(2)}) collective-permute-start(bf16[48,768]{1,0:T(8,128)(2,1)S(1)} %slice_bitcast_fusion.4), channel_id=1, source_target_pairs={{0,20},{1,21},{2,22},{3,23},{4,16},{5,17},{6,18},{7,19},{8,28},{9,... | collective-permute-start | bytes 221192 | tf_op jit(solution)/shard_map/ppermute | solution.py:812
  186.1 1.1 copy-start.5
  188.6 10.5 %copy-start.2 = (bf16[128,2,768]{2,0,1:T(8,128)(2,1)S(1)}, bf16[128,2,768]{2,0,1:T(8,128)(2,1)}, u32[]{:S(2)}) copy-start(bf16[128,2,768]{2,0,1:T(8,128)(2,1)} %copy-done.1) | copy-start | bytes 1179652
  188.6 10.5 %copy-start.13 = (f32[256,768]{1,0:T(8,128)S(1)}, f32[256,768]{1,0:T(8,128)}, u32[]{:S(2)}) copy-start(f32[256,768]{1,0:T(8,128)} %get-tuple-element.53.dfirst_ref) | copy-start | bytes 2359300
  188.6 10.5 %copy-start.20 = (f32[8,768]{1,0:T(8,128)S(1)}, f32[8,768]{1,0:T(8,128)}, u32[]{:S(2)}) copy-start(f32[8,768]{1,0:T(8,128)} %copy-done.19) | copy-start | bytes 73732
  193.4 14.4 %all-to-all-start.6 = ((bf16[8,56,768]{2,1,0:T(8,128)(2,1)}), bf16[8,56,768]{2,1,0:T(8,128)(2,1)S(1)}, u32[]{:S(2)}, u32[]{:S(2)}) async-start(bf16[8,56,768]{2,1,0:T(8,128)(2,1)} %shard_map.251), calls=%async_computation.7 | async-start | bytes 1376256 | tf_op jit(solution)/shard_map/all_to_all | solution.py:829
  199.1 8.7 %copy-start.8 = (s32[1,768]{1,0:T(1,128)S(1)}, s32[1,768]{1,0:T(1,128)}, u32[]{:S(2)}) copy-start(s32[1,768]{1,0:T(1,128)} %constant.13.clone.units_ref) | copy-start | bytes 9220
Sparse Core Ops, SparseCore 0:
  27.8 64.3 all-gather.2
  116.2 67.8 reduce-scatter.1

commit v9 on v8

--- a/solution.py
+++ b/solution.py
@@ -448,25 +448,18 @@
 GELU_SCALE = math.sqrt(2.0 / math.pi)
 
 
-def prepare_kernel(att_ref, order_ref, place_ref, attended_ref, attended_t_ref):
-    place_ref[...] = places(order_ref[...])
-    for b in range(2):
-        for e in range(4):
-            attended_t_ref[e * 192 : (e + 1) * 192, b * 128 : (b + 1) * 128] = att_ref[2 * e + b]
-    attended_ref[...] = dot(attended_t_ref[...].T, place_ref[...]).astype(BF)
-
-
 def feed_kernel(
-    x_hbm, dy_hbm, att_hbm, gains_hbm, place_hbm, weights_hbm,
+    att_hbm, order_hbm, x_hbm, gains_hbm, dy_hbm, weights_hbm,
     y_hbm, dfirst_hbm, low_hbm, datt_hbm, dgain_hbm, grads_hbm,
-    x_ref, dy_ref, att_ref, gains_ref, place_ref, down_ref, up_ref, out_ref,
-    y_ref, dfirst_ref, low_ref, datt_ref, dgain_ref, gdown, gup, acc_scr, dn_scr, loads, stores,
+    att_ref, order_ref, x_ref, gains_ref, dy_ref, down_ref, up_ref, out_ref,
+    y_ref, dfirst_ref, low_ref, datt_ref, dgain_ref, gdown, gup, acc_scr, dn_scr,
+    place_ref, loads, stores,
 ):
     def block(ref, number):
         return ref.at[:, pl.ds(48 * number, 48), :]
 
-    arrivals = [(att_hbm, att_ref), (block(weights_hbm, 8), out_ref), (x_hbm, x_ref)]
-    arrivals += [(gains_hbm, gains_ref), (place_hbm, place_ref)]
+    arrivals = [(att_hbm, att_ref), (order_hbm, order_ref), (x_hbm, x_ref)]
+    arrivals += [(gains_hbm, gains_ref), (block(weights_hbm, 8), out_ref)]
     for k in range(4):
         arrivals.append((block(weights_hbm, 4 + k), up_ref.at[k]))
         if k == 0:
@@ -485,11 +478,16 @@
     for copy in arrivals[0:4]:
         copy.wait()
     gain, bias = gains_ref[2:3], gains_ref[3:4]
+    place_ref[...] = places(order_ref[...])
+    natural = [
+        jnp.concatenate([att_ref[2 * e + b] for e in range(4)], axis=0).T for b in range(2)
+    ]
+    attended = dot(jnp.concatenate(natural, axis=0), place_ref[...]).astype(BF)
+    arrivals[4].wait()
     w_out = out_ref[...].reshape(768, 768)
-    first = x_ref[...].astype(F32) + dot(att_ref[...], w_out)
+    first = x_ref[...].astype(F32) + dot(attended, w_out)
     hat, scale = normalize(first)
     acc_scr[...] = first
-    arrivals[4].wait()
     n2 = dot((hat * gain + bias).astype(BF), place_ref[...]).astype(BF)
     n2t = n2.T
     waiting = arrivals[5:]
@@ -543,8 +541,11 @@
         copy.wait()
 
 
-def out_kernel(attended_t_ref, low_ref, grad_ref):
-    grad = dot(attended_t_ref[...], low_ref[...]).reshape(8, 2, 2, 24, 768)
+def out_kernel(att_ref, low_ref, grad_ref):
+    attended_t = [
+        jnp.concatenate([att_ref[2 * e + b] for e in range(4)], axis=0) for b in range(2)
+    ]
+    grad = dot(jnp.concatenate(attended_t, axis=1), low_ref[...]).reshape(8, 2, 2, 24, 768)
     half = lax.axis_index("batch") // 4
     for j in range(8):
         rows = [
@@ -567,6 +568,7 @@
     held += [blocks, blocks, pltpu.VMEM((16, 48, 768), BF)]
     held += [pltpu.VMEM(o.shape, o.dtype) for o in outs[:-1]]
     held += [blocks, blocks] + [pltpu.VMEM((256, 768), F32)] * 2
+    held += [pltpu.VMEM((768, 768), BF)]
     held += [pltpu.SemaphoreType.DMA((14,)), pltpu.SemaphoreType.DMA((13,))]
     return call(
         feed_kernel,
@@ -754,20 +756,13 @@
         **scalars(4),
     )
     att = exchange(o_low)
-    place, attended, attended_t = call(
-        prepare_kernel,
-        [shape((768, 768), BF), shape((256, 768), BF), shape((768, 256), BF)],
-        (att, order),
-        2,
-        mib=16,
-    )
-    y, d_first, low, d_att, d_gain, grads = feed(x, dy, attended, gains, place, weights)
+    y, d_first, low, d_att, d_gain, grads = feed(att, order, x, gains, dy, weights)
     rest_sum = lax.psum_scatter(
         grads.reshape(16 * 384, 768), BOTH, scatter_dimension=0, tiled=True,
         axis_index_groups=RINGS,
     )
     d_att = exchange(d_att)
-    out_grad = exchange(call(out_kernel, shape((8, 96, 768), BF), (attended_t, low), 2))
+    out_grad = exchange(call(out_kernel, shape((8, 96, 768), BF), (att, low), 2))
     dq, dkv, dkv_other = call(
         backward_kernel,
         [shape((192, 1024), BF), shape((384, 1024), BF), shape((384, 1024), BF)],

time: 217 us -> 214 us (0.986); the launches traced: 216 us -> 211 us
  starting transfers between devices: 35.4 us -> 45.1 us
  Pallas kernels: 69.2 us -> 62.3 us
  waiting for transfers between devices: 53.6 us -> 48.3 us
  local copies, waits for them, and re-layouts: 12.4 us -> 9.74 us
    pallas_call x12 -> x11, Pallas kernels: 67.1 us -> 60.2 us  [call(): pl.pallas_call(kernel, out_shape=outs, scratch_shapes=list(scratch), cost...]
    ppermute x1, starting transfers between devices: 0.01 us -> 4.31 us  [body(): lax.ppermute(line[2], 'batch', along_x(2))]
    ppermute x1, waiting for transfers between devices: 3.87 us -> 0.01 us  [body(): lax.ppermute(line[1], 'batch', along_x(1))]
    all_to_all x1, waiting for transfers between devices: 4.82 us -> 1.38 us  [body(): back = exchange(part)]
    unnamed x57 -> x51, local copies, waits for them, and re-layouts: 8.22 us -> 5.58 us
    all_to_all x1, starting transfers between devices: 5.54 us -> 8.18 us  [body(): back = exchange(part)]
  transfers between devices with their start and end apart: 20 -> 20, of which waited for: 15 -> 15; matrix products, arithmetic and copies ran while one was open for 2% -> 2% of each run, Pallas kernels for 22% -> 19%
where the time goes in v9:
time: 214 us; the launch traced here: 211 us
  Pallas kernels  62.3 us (29%)
  waiting for transfers between devices  48.3 us (23%)
  starting transfers between devices  45.1 us (21%)
  blocking collectives  30.4 us (14%)
  between operations  14.3 us (7%)
  local copies, waits for them, and re-layouts  9.74 us (5%)
    pallas_call x11, Pallas kernels, call(): pl.pallas_call(kernel, out_shape=outs, scratch_shapes=list(scratch), cost...  60.2 us
    all_to_all x1, blocking collectives, body(): own = exchange(sent)  30.4 us
    all_to_all x2, starting transfers between devices, body(): slots = exchange(slots)  11.2 us
    all_to_all x1, starting transfers between devices, body(): back = exchange(part)  8.18 us
    all_to_all x1, waiting for transfers between devices, body(): att = exchange(o_low)  7.43 us
    all_to_all x2, waiting for transfers between devices, body(): slots = exchange(slots)  7.02 us
    ppermute x3, starting transfers between devices, body(): lax.ppermute(raw, 'batch', along_x(step))  5.72 us
    all_to_all x1, waiting for transfers between devices, body(): d_att = exchange(d_att)  5.62 us
  transfers between devices with their start and end apart: 20, of which 15 were waited for; matrix products, arithmetic and copies ran while one was open for 2% of the time, Pallas kernels for 19%

profile of v9, /device:TPU:64, one launch (start us, length us, event | category | flops | bytes accessed | tf_op | source)
XLA Modules:
  0.0 211.2 jit_solution(4840011790948603319)
XLA Ops:
  7.2 2.1 shard_map.240
  9.3 5.7 %all-to-all-start.2 = ((bf16[8,56,768]{2,1,0:T(8,128)(2,1)}), bf16[8,56,768]{2,1,0:T(8,128)(2,1)S(1)}, u32[]{:S(2)}, u32[]{:S(2)}) async-start(bf16[8,56,768]{2,1,0:T(8,128)(2,1)} %get-tuple-element.46), calls=%async_computation.2 | async-start | bytes 1376256 | tf_op jit(solution)/shard_map/all_to_all | solution.py:702
  14.9 0.0 all-gather.3.cloned.1.call-start
  15.0 1.6 collective-permute-start.2
  16.5 2.7 %collective-permute-start.1 = (bf16[24,640]{1,0:T(8,128)(2,1)}, bf16[24,640]{1,0:T(8,128)(2,1)S(1)}, u32[]{:S(2)}, u32[]{:S(2)}) collective-permute-start(bf16[24,640]{1,0:T(8,128)(2,1)} %get-tuple-element.41), channel_id=1, source_target_pairs={{0,2},{1,3},{2,0},{3,1},{4,6},{5,7},{6,4},{7,5},{8,10},{9,11},{10,... | collective-permute-start | bytes 92168 | tf_op jit(solution)/shard_map/ppermute | solution.py:703
  19.3 1.4 collective-permute-start
  20.7 1.4 collective-permute-done.1
  22.2 1.2 collective-permute-done
  23.4 0.8 pad_maximum_fusion.near_ref
  24.2 2.0 all-to-all-done.2.slots_ref
  26.2 1.5 shard_map.244
  27.7 0.0 all-gather.3.cloned.1.call-update
  27.7 0.1 collective-permute-start.3
  27.9 4.8 %collective-permute-done.3.far_ref = bf16[4,24,640]{2,1,0:T(8,128)(2,1)S(1)} collective-permute-done((bf16[4,24,640]{2,1,0:T(8,128)(2,1)S(1)}, bf16[4,24,640]{2,1,0:T(8,128)(2,1)S(1)}, u32[]{:S(2)}, u32[]{:S(2)}) %collective-permute-start.3) | collective-permute-done | bytes 122912 | tf_op jit(solution)/shard_map/ppermute | solution.py:704
  32.7 0.2 shard_map.241
  32.9 0.0 copy-start.7
  32.9 30.4 %all_to_all.35.own_ref = bf16[8,176,768]{2,1,0:T(8,128)(2,1)S(1)} all-to-all(bf16[8,176,768]{2,1,0:T(8,128)(2,1)S(1)} %shard_map.241), channel_id=1, replica_groups={{0,16,32,48,64,80,96,112},{8,24,40,56,72,88,104,120},{1,17,33,49,65,81,..., dimensions={0} | all-to-all | bytes 4325376 | tf_op jit(solution)/shard_map/all_to_all | solution.py:726
  63.4 0.1 collective-permute-start.4
  63.5 2.0 collective-permute-done.4.other_ref
  65.5 3.0 %shard_map.242 = (bf16[1024,768]{1,0:T(8,128)(2,1)S(1)}, bf16[576,768]{1,0:T(8,128)(2,1)S(1)}, f32[8,768]{1,0:T(8,128)S(1)}, bf16[192,1024]{1,0:T(8,128)(2,1)S(1)}, bf16[384,1024]{1,0:T(8,128)(2,1)S(1)}) custom-call(bf16[8,176,768]{2,1,0:T(8,128)(2,1)S(1)} %all_to_all.35.own_ref, bf16[8,48,640]{2,1,0:T(8,128)(2,1)S(1)} %collective-permute-done.4.other_ref, ...), custom_call_target="tpu_custom_call" | custom-call | flops 5500000256 | tf_op jit(solution)/shard_map/pallas_call | solution.py:88
  68.5 1.1 copy-done.11
  69.6 1.0 copy-done.12
  70.7 0.6 copy-done.15
  71.3 0.1 collective-permute-start.5
  71.4 2.1 %collective-permute-done.5.other_ref = bf16[384,1024]{1,0:T(8,128)(2,1)S(1)} collective-permute-done((bf16[384,1024]{1,0:T(8,128)(2,1)S(1)}, bf16[384,1024]{1,0:T(8,128)(2,1)S(1)}, u32[]{:S(2)}, u32[]{:S(2)}) %collective-permute-start.5) | collective-permute-done | bytes 786464 | tf_op jit(solution)/shard_map/ppermute | solution.py:741
  73.6 8.1 %shard_map.243 = (f32[192,1024]{1,0:T(8,128)S(1)}, bf16[8,192,128]{2,1,0:T(8,128)(2,1)}, f32[3,1024]{1,0:T(4,128)S(1)}) custom-call(s32[2]{0:T(128)S(1)} %copy-done.6, bf16[192,1024]{1,0:T(8,128)(2,1)S(1)} %get-tuple-element.42.q_ref, bf16[384,1024]{1,0:T(8,128)(2,1)S(1)} %get-tuple-element.43.own_ref, bf16[384,1024]{1,0:T(8,128)(2,1)S(1)} %collective-permute-done.5.other_ref), custom_call_target="tpu_custom_call" | custom-call | flops 13200000000 | tf_op jit(solution)/shard_map/pallas_call | solution.py:88
  81.7 4.0 %all-to-all-start.1 = ((bf16[8,192,128]{2,1,0:T(8,128)(2,1)}), bf16[8,192,128]{2,1,0:T(8,128)(2,1)S(1)}, u32[]{:S(2)}, u32[]{:S(2)}) async-start(bf16[8,192,128]{2,1,0:T(8,128)(2,1)} %get-tuple-element.44), calls=%async_computation.1 | async-start | bytes 786432 | tf_op jit(solution)/shard_map/all_to_all | solution.py:758
  85.7 0.2 reduce-scatter.2.cloned.1.call-start
  85.9 0.8 copy.28
  86.7 7.4 %all-to-all-done.1.att_hbm.att_ref = bf16[8,192,128]{2,1,0:T(8,128)(2,1)S(1)} async-done(((bf16[8,192,128]{2,1,0:T(8,128)(2,1)}), bf16[8,192,128]{2,1,0:T(8,128)(2,1)S(1)}, u32[]{:S(2)}, u32[]{:S(2)}) %all-to-all-start.1) | async-done | bytes 393248 | tf_op jit(solution)/shard_map/all_to_all | solution.py:758
  94.2 0.7 copy-done.22
  94.9 16.0 %shard_map.245 = (bf16[256,768]{1,0:T(8,128)(2,1)}, f32[256,768]{1,0:T(8,128)}, bf16[256,768]{1,0:T(8,128)(2,1)}, bf16[8,192,128]{2,1,0:T(8,128)(2,1)}, f32[8,768]{1,0:T(8,128)}, /*index=5*/bf16[16,384,768]{2,1,0:T(8,128)(2,1)}) custom-call(bf16[8,192,128]{2,1,0:T(8,128)(2,1)} %copy-done.22, s32[1,768]{1,0:T(1,128)} %constant.12.clone.order_hbm, ...), custom_call_target="tpu_custom_call" | custom-call | flops 16499999744 | tf_op jit(solution)/shard_map/pallas_call | solution.py:88
  110.9 0.0 reduce-scatter.2.cloned.1.call-update
  110.9 3.5 %all-to-all-start.3 = ((bf16[8,192,128]{2,1,0:T(8,128)(2,1)}), bf16[8,192,128]{2,1,0:T(8,128)(2,1)S(1)}, u32[]{:S(2)}, u32[]{:S(2)}) async-start(bf16[8,192,128]{2,1,0:T(8,128)(2,1)} %get-tuple-element.51), calls=%async_computation.3 | async-start | bytes 786432 | tf_op jit(solution)/shard_map/all_to_all | solution.py:764
  114.4 2.7 %shard_map.247 = bf16[8,96,768]{2,1,0:T(8,128)(2,1)} custom-call(bf16[8,192,128]{2,1,0:T(8,128)(2,1)} %copy-done.22, bf16[256,768]{1,0:T(8,128)(2,1)} %get-tuple-element.58.low_ref), custom_call_target="tpu_custom_call" | custom-call | flops 2200000000 | tf_op jit(solution)/shard_map/pallas_call | solution.py:88
  117.1 5.6 %all-to-all-done.3.da_ref = bf16[8,192,128]{2,1,0:T(8,128)(2,1)S(1)} async-done(((bf16[8,192,128]{2,1,0:T(8,128)(2,1)}), bf16[8,192,128]{2,1,0:T(8,128)(2,1)S(1)}, u32[]{:S(2)}, u32[]{:S(2)}) %all-to-all-start.3) | async-done | bytes 393248 | tf_op jit(solution)/shard_map/all_to_all | solution.py:764
  122.7 3.8 %all-to-all-start.4 = ((bf16[8,96,768]{2,1,0:T(8,128)(2,1)}), bf16[8,96,768]{2,1,0:T(8,128)(2,1)S(1)}, u32[]{:S(2)}, u32[]{:S(2)}) async-start(bf16[8,96,768]{2,1,0:T(8,128)(2,1)} %shard_map.247), calls=%async_computation.4 | async-start | bytes 2359296 | tf_op jit(solution)/shard_map/all_to_all | solution.py:765
  126.5 15.3 %shard_map.246 = (bf16[192,1024]{1,0:T(8,128)(2,1)}, bf16[384,1024]{1,0:T(8,128)(2,1)}, bf16[384,1024]{1,0:T(8,128)(2,1)}) custom-call(s32[2]{0:T(128)} %lengths_ref.3, bf16[192,1024]{1,0:T(8,128)(2,1)} %copy-done.13, bf16[384,1024]{1,0:T(8,128)(2,1)} %copy-done.3, bf16[384,1024]{1,0:T(8,128)(2,1)} %copy-done.4, f32[192,1024]{1,0:T(8,128)} %copy-done.14, ...), custom_call_target="tpu_custom_call" | custom-call | flops 22000001024 | tf_op jit(solution)/shard_map/pallas_call | solution.py:88
  141.8 1.3 all-to-all-done.4.out_ref
  143.1 1.3 collective-permute-done.6.partner_ref
  144.4 0.9 copy-done.24
  145.2 8.9 %shard_map.248 = (bf16[8,128,768]{2,1,0:T(8,128)(2,1)}, bf16[4,2,48,768]{3,2,1,0:T(8,128)(2,1)}, bf16[4,2,48,768]{3,2,1,0:T(8,128)(2,1)}) custom-call(bf16[8,176,768]{2,1,0:T(8,128)(2,1)} %copy-done, bf16[192,1024]{1,0:T(8,128)(2,1)} %get-tuple-element.52.dq_ref, bf16[384,1024]{1,0:T(8,128)(2,1)} %get-tuple-element.53.dkv_ref, bf16[384,1024]{1,0:T(8,128)(2,1)} %copy-done.24, ...), custom_call_target="tpu_custom_call" | custom-call | flops 7699999744 | tf_op jit(solution)/shard_map/pallas_call | solution.py:88
  154.2 0.1 collective-permute-start.7
  154.3 8.2 %all-to-all-start.5 = ((bf16[8,128,768]{2,1,0:T(8,128)(2,1)}), bf16[8,128,768]{2,1,0:T(8,128)(2,1)S(1)}, u32[]{:S(2)}, u32[]{:S(2)}) async-start(bf16[8,128,768]{2,1,0:T(8,128)(2,1)} %get-tuple-element.59), calls=%async_computation.5 | async-start | bytes 3145728 | tf_op jit(solution)/shard_map/all_to_all | solution.py:808
  162.5 0.1 add_convert_fusion
  162.7 0.1 collective-permute-start.8
  162.8 3.2 %collective-permute-start.10 = (bf16[2,48,768]{2,1,0:T(8,128)(2,1)S(1)}, bf16[2,48,768]{2,1,0:T(8,128)(2,1)S(1)}, u32[]{:S(2)}, u32[]{:S(2)}) collective-permute-start(bf16[2,48,768]{2,1,0:T(8,128)(2,1)S(1)} %get-tuple-element.73), channel_id=1, source_target_pairs={{0,3},{1,0},{2,1},{3,2},{4,7},{5,4},{6,5},{7,6},{8,11},{9,8},{10,9... | collective-permute-start | bytes 442376 | tf_op jit(solution)/shard_map/ppermute | solution.py:805
  166.0 4.3 %collective-permute-start.9 = (bf16[2,48,768]{2,1,0:T(8,128)(2,1)S(1)}, bf16[2,48,768]{2,1,0:T(8,128)(2,1)S(1)}, u32[]{:S(2)}, u32[]{:S(2)}) collective-permute-start(bf16[2,48,768]{2,1,0:T(8,128)(2,1)S(1)} %get-tuple-element.74), channel_id=1, source_target_pairs={{0,2},{1,3},{2,0},{3,1},{4,6},{5,7},{6,4},{7,5},{8,10},{9,11},{10,... | collective-permute-start | bytes 442376 | tf_op jit(solution)/shard_map/ppermute | solution.py:804
  170.3 3.9 %collective-permute-done.10 = bf16[2,48,768]{2,1,0:T(8,128)(2,1)S(1)} collective-permute-done((bf16[2,48,768]{2,1,0:T(8,128)(2,1)S(1)}, bf16[2,48,768]{2,1,0:T(8,128)(2,1)S(1)}, u32[]{:S(2)}, u32[]{:S(2)}) %collective-permute-start.10) | collective-permute-done | bytes 147488 | tf_op jit(solution)/shard_map/ppermute | solution.py:805
  174.2 4.7 %collective-permute-done.9 = bf16[2,48,768]{2,1,0:T(8,128)(2,1)S(1)} collective-permute-done((bf16[2,48,768]{2,1,0:T(8,128)(2,1)S(1)}, bf16[2,48,768]{2,1,0:T(8,128)(2,1)S(1)}, u32[]{:S(2)}, u32[]{:S(2)}) %collective-permute-start.9) | collective-permute-done | bytes 147488 | tf_op jit(solution)/shard_map/ppermute | solution.py:804
  178.9 0.1 fusion.2
  179.0 0.3 collective-permute-start.11
  179.3 4.1 %collective-permute-done.11 = bf16[48,768]{1,0:T(8,128)(2,1)S(1)} collective-permute-done((bf16[48,768]{1,0:T(8,128)(2,1)S(1)}, bf16[48,768]{1,0:T(8,128)(2,1)S(1)}, u32[]{:S(2)}, u32[]{:S(2)}) %collective-permute-start.11) | collective-permute-done | bytes 73760 | tf_op jit(solution)/shard_map/ppermute | solution.py:807
  183.4 0.0 reduce-scatter.2.cloned.1.call-done.rest_ref
  183.5 1.1 copy-done.5
  184.5 1.4 shard_map.250
  185.9 1.4 all-to-all-done.5.got_ref
  187.3 5.6 %all-to-all-start.6 = ((bf16[8,56,768]{2,1,0:T(8,128)(2,1)}), bf16[8,56,768]{2,1,0:T(8,128)(2,1)S(1)}, u32[]{:S(2)}, u32[]{:S(2)}) async-start(bf16[8,56,768]{2,1,0:T(8,128)(2,1)} %shard_map.250), calls=%async_computation.7 | async-start | bytes 1376256 | tf_op jit(solution)/shard_map/all_to_all | solution.py:824
  192.9 2.1 %copy.36 = bf16[2,128,768]{2,0,1:T(2,128)(2,1)} copy(bf16[2,128,768]{2,1,0:T(8,128)(2,1)} %bitcast.52) | data formatting | bytes 786432 | tf_op jit(solution)/shard_map/reshape | solution.py:835
  195.1 0.0 copy-start.8
  195.1 1.3 shard_map.249
  196.4 1.1 copy.35
  197.5 5.0 %all-to-all-done.6.got_ref = bf16[8,56,768]{2,1,0:T(8,128)(2,1)S(1)} async-done(((bf16[8,56,768]{2,1,0:T(8,128)(2,1)}), bf16[8,56,768]{2,1,0:T(8,128)(2,1)S(1)}, u32[]{:S(2)}, u32[]{:S(2)}) %all-to-all-start.6) | async-done | bytes 688160 | tf_op jit(solution)/shard_map/all_to_all | solution.py:824
  202.5 1.9 shard_map.251
  (52 shorter events, 0.2 us)
Async XLA Ops:
  9.3 16.9 %copy-start.9 = (s32[1,512]{1,0:T(1,128)S(1)}, s32[1,512]{1,0:T(1,128)}, u32[]{:S(2)}) copy-start(s32[1,512]{1,0:T(1,128)} %constant.14.clone.order_ref) | copy-start | bytes 6148
  9.3 16.9 %all-to-all-start.2 = ((bf16[8,56,768]{2,1,0:T(8,128)(2,1)}), bf16[8,56,768]{2,1,0:T(8,128)(2,1)S(1)}, u32[]{:S(2)}, u32[]{:S(2)}) async-start(bf16[8,56,768]{2,1,0:T(8,128)(2,1)} %get-tuple-element.46), calls=%async_computation.2 | async-start | bytes 1376256 | tf_op jit(solution)/shard_map/all_to_all | solution.py:702
  14.9 79.2 %all-gather.3.cloned.1.call-start = ((), (), s32[]{:S(2)}) async-start(), calls=%async_computation.9 | async-start | bytes 11280384 | tf_op jit(solution)/shard_map/all_gather | solution.py:715
  15.0 5.7 %collective-permute-start.2 = (bf16[24,640]{1,0:T(8,128)(2,1)}, bf16[24,640]{1,0:T(8,128)(2,1)S(1)}, u32[]{:S(2)}, u32[]{:S(2)}) collective-permute-start(bf16[24,640]{1,0:T(8,128)(2,1)} %get-tuple-element.41), channel_id=1, source_target_pairs={{0,1},{1,2},{2,3},{3,0},{4,5},{5,6},{6,7},{7,4},{8,9},{9,10},{10,1... | collective-permute-start | bytes 92168 | tf_op jit(solution)/shard_map/ppermute | solution.py:703
  16.5 5.6 %collective-permute-start.1 = (bf16[24,640]{1,0:T(8,128)(2,1)}, bf16[24,640]{1,0:T(8,128)(2,1)S(1)}, u32[]{:S(2)}, u32[]{:S(2)}) collective-permute-start(bf16[24,640]{1,0:T(8,128)(2,1)} %get-tuple-element.41), channel_id=1, source_target_pairs={{0,2},{1,3},{2,0},{3,1},{4,6},{5,7},{6,4},{7,5},{8,10},{9,11},{10,... | collective-permute-start | bytes 92168 | tf_op jit(solution)/shard_map/ppermute | solution.py:703
  19.3 4.1 %collective-permute-start = (bf16[24,640]{1,0:T(8,128)(2,1)}, bf16[24,640]{1,0:T(8,128)(2,1)S(1)}, u32[]{:S(2)}, u32[]{:S(2)}) collective-permute-start(bf16[24,640]{1,0:T(8,128)(2,1)} %get-tuple-element.41), channel_id=1, source_target_pairs={{0,3},{1,0},{2,1},{3,2},{4,7},{5,4},{6,5},{7,6},{8,11},{9,8},{10,9... | collective-permute-start | bytes 92168 | tf_op jit(solution)/shard_map/ppermute | solution.py:703
  24.2 3.7 %copy-start.20 = (bf16[128,2,768]{2,1,0:T(2,128)(2,1)S(1)}, bf16[128,2,768]{2,1,0:T(2,128)(2,1)}, u32[]{:S(2)}) copy-start(bf16[128,2,768]{2,1,0:T(2,128)(2,1)} %param.17) | copy-start | bytes 1179652
  27.7 5.0 %collective-permute-start.3 = (bf16[4,24,640]{2,1,0:T(8,128)(2,1)S(1)}, bf16[4,24,640]{2,1,0:T(8,128)(2,1)S(1)}, u32[]{:S(2)}, u32[]{:S(2)}) collective-permute-start(bf16[4,24,640]{2,1,0:T(8,128)(2,1)S(1)} %pad_maximum_fusion.near_ref), channel_id=1, source_target_pairs={{0,20},{1,21},{2,22},{3,23},{4,16},{5,17},{6,18},{7,19},{8,28},{9,... | collective-permute-start | bytes 368648 | tf_op jit(solution)/shard_map/ppermute | solution.py:704
  27.9 5.0 %copy-start.1 = (bf16[128,2,768]{2,0,1:T(8,128)(2,1)}, bf16[128,2,768]{2,0,1:T(8,128)(2,1)S(1)}, u32[]{:S(2)}) copy-start(bf16[128,2,768]{2,0,1:T(8,128)(2,1)S(1)} %copy.37) | copy-start | bytes 1179652
  32.9 32.6 %copy-start.7 = (s32[8,768]{1,0:T(8,128)S(1)}, s32[8,768]{1,0:T(8,128)}, u32[]{:S(2)}) copy-start(s32[8,768]{1,0:T(8,128)} %constant.16.clone.arrival_ref) | copy-start | bytes 73732
  63.4 5.1 %copy-start = (bf16[8,176,768]{2,1,0:T(8,128)(2,1)}, bf16[8,176,768]{2,1,0:T(8,128)(2,1)S(1)}, u32[]{:S(2)}) copy-start(bf16[8,176,768]{2,1,0:T(8,128)(2,1)S(1)} %all_to_all.35.own_ref) | copy-start | bytes 6488068
  63.4 10.1 %copy-start.6 = (s32[2]{0:T(128)S(1)}, s32[2]{0:T(128)}, u32[]{:S(2)}) copy-start(s32[2]{0:T(128)} %lengths_ref.3) | copy-start | bytes 28
  63.4 2.1 collective-permute-start.4
  68.5 1.1 copy-start.11
  69.6 1.0 copy-start.12
  70.7 0.6 copy-start.15
  71.3 10.4 %copy-start.3 = (bf16[384,1024]{1,0:T(8,128)(2,1)}, bf16[384,1024]{1,0:T(8,128)(2,1)S(1)}, u32[]{:S(2)}) copy-start(bf16[384,1024]{1,0:T(8,128)(2,1)S(1)} %get-tuple-element.43.own_ref) | copy-start | bytes 2359300
  71.3 10.4 %copy-start.13 = (bf16[192,1024]{1,0:T(8,128)(2,1)}, bf16[192,1024]{1,0:T(8,128)(2,1)S(1)}, u32[]{:S(2)}) copy-start(bf16[192,1024]{1,0:T(8,128)(2,1)S(1)} %get-tuple-element.42.q_ref) | copy-start | bytes 1179652
  71.3 2.3 %collective-permute-start.5 = (bf16[384,1024]{1,0:T(8,128)(2,1)S(1)}, bf16[384,1024]{1,0:T(8,128)(2,1)S(1)}, u32[]{:S(2)}, u32[]{:S(2)}) collective-permute-start(bf16[384,1024]{1,0:T(8,128)(2,1)S(1)} %get-tuple-element.43.own_ref), channel_id=1, source_target_pairs={{0,8},{8,0},{16,24},{24,16},{32,40},{40,32},{48,56},{56,48},{64,72... | collective-permute-start | bytes 2359304 | tf_op jit(solution)/shard_map/ppermute | solution.py:741
  73.6 8.1 %copy-start.4 = (bf16[384,1024]{1,0:T(8,128)(2,1)}, bf16[384,1024]{1,0:T(8,128)(2,1)S(1)}, u32[]{:S(2)}) copy-start(bf16[384,1024]{1,0:T(8,128)(2,1)S(1)} %collective-permute-done.5.other_ref) | copy-start | bytes 2359300
  73.6 12.4 %copy-start.21 = (bf16[128,2,768]{2,1,0:T(2,128)(2,1)S(1)}, bf16[128,2,768]{2,1,0:T(2,128)(2,1)}, u32[]{:S(2)}) copy-start(bf16[128,2,768]{2,1,0:T(2,128)(2,1)} %param.27) | copy-start | bytes 1179652
  81.7 29.2 %copy-start.14 = (f32[192,1024]{1,0:T(8,128)}, f32[192,1024]{1,0:T(8,128)S(1)}, u32[]{:S(2)}) copy-start(f32[192,1024]{1,0:T(8,128)S(1)} %get-tuple-element.49.o_ref) | copy-start | bytes 2359300
  81.7 29.2 %copy-start.17 = (f32[3,1024]{1,0:T(4,128)}, f32[3,1024]{1,0:T(4,128)S(1)}, u32[]{:S(2)}) copy-start(f32[3,1024]{1,0:T(4,128)S(1)} %get-tuple-element.50.lse_ref) | copy-start | bytes 36868
  81.7 12.5 %all-to-all-start.1 = ((bf16[8,192,128]{2,1,0:T(8,128)(2,1)}), bf16[8,192,128]{2,1,0:T(8,128)(2,1)S(1)}, u32[]{:S(2)}, u32[]{:S(2)}) async-start(bf16[8,192,128]{2,1,0:T(8,128)(2,1)} %get-tuple-element.44), calls=%async_computation.1 | async-start | bytes 786432 | tf_op jit(solution)/shard_map/all_to_all | solution.py:758
  85.7 97.8 %reduce-scatter.2.cloned.1.call-start = ((), (), s32[]{:S(2)}) async-start(), calls=%async_computation.8 | async-start | bytes 10027008 | tf_op jit(solution)/shard_map/reduce_scatter | solution.py:760
  94.2 0.7 copy-start.22
  110.9 11.7 %all-to-all-start.3 = ((bf16[8,192,128]{2,1,0:T(8,128)(2,1)}), bf16[8,192,128]{2,1,0:T(8,128)(2,1)S(1)}, u32[]{:S(2)}, u32[]{:S(2)}) async-start(bf16[8,192,128]{2,1,0:T(8,128)(2,1)} %get-tuple-element.51), calls=%async_computation.3 | async-start | bytes 786432 | tf_op jit(solution)/shard_map/all_to_all | solution.py:764
  122.7 3.8 %copy-start.23 = (bf16[8,192,128]{2,1,0:T(8,128)(2,1)}, bf16[8,192,128]{2,1,0:T(8,128)(2,1)S(1)}, u32[]{:S(2)}) copy-start(bf16[8,192,128]{2,1,0:T(8,128)(2,1)S(1)} %all-to-all-done.3.da_ref) | copy-start | bytes 1179652
  122.7 20.4 %all-to-all-start.4 = ((bf16[8,96,768]{2,1,0:T(8,128)(2,1)}), bf16[8,96,768]{2,1,0:T(8,128)(2,1)S(1)}, u32[]{:S(2)}, u32[]{:S(2)}) async-start(bf16[8,96,768]{2,1,0:T(8,128)(2,1)} %shard_map.247), calls=%async_computation.4 | async-start | bytes 2359296 | tf_op jit(solution)/shard_map/all_to_all | solution.py:765
  141.8 2.6 %collective-permute-start.6 = (bf16[384,1024]{1,0:T(8,128)(2,1)}, bf16[384,1024]{1,0:T(8,128)(2,1)S(1)}, u32[]{:S(2)}, u32[]{:S(2)}) collective-permute-start(bf16[384,1024]{1,0:T(8,128)(2,1)} %get-tuple-element.54), channel_id=1, source_target_pairs={{0,8},{8,0},{16,24},{24,16},{32,40},{40,32},{48,56},{56,48},{64,72... | collective-permute-start | bytes 2359304 | tf_op jit(solution)/shard_map/ppermute | solution.py:787
  143.1 1.3 copy-start.18
  144.4 0.9 copy-start.24
  154.2 8.3 %collective-permute-start.7 = (bf16[4,2,48,768]{3,2,1,0:T(8,128)(2,1)}, bf16[4,2,48,768]{3,2,1,0:T(8,128)(2,1)S(1)}, u32[]{:S(2)}, u32[]{:S(2)}) collective-permute-start(bf16[4,2,48,768]{3,2,1,0:T(8,128)(2,1)} %get-tuple-element.61), channel_id=1, source_target_pairs={{0,8},{8,0},{16,24},{24,16},{32,40},{40,32},{48,56},{56,48},{64,72... | collective-permute-start | bytes 1769480 | tf_op jit(solution)/shard_map/ppermute | solution.py:800
  154.3 8.2 %copy-start.19 = (bf16[4,2,48,768]{3,2,1,0:T(8,128)(2,1)S(1)}, bf16[4,2,48,768]{3,2,1,0:T(8,128)(2,1)}, u32[]{:S(2)}) copy-start(bf16[4,2,48,768]{3,2,1,0:T(8,128)(2,1)} %get-tuple-element.60) | copy-start | bytes 1769476
  154.3 33.0 %all-to-all-start.5 = ((bf16[8,128,768]{2,1,0:T(8,128)(2,1)}), bf16[8,128,768]{2,1,0:T(8,128)(2,1)S(1)}, u32[]{:S(2)}, u32[]{:S(2)}) async-start(bf16[8,128,768]{2,1,0:T(8,128)(2,1)} %get-tuple-element.59), calls=%async_computation.5 | async-start | bytes 3145728 | tf_op jit(solution)/shard_map/all_to_all | solution.py:808
  162.7 7.6 %collective-permute-start.8 = (bf16[2,48,768]{2,1,0:T(8,128)(2,1)S(1)}, bf16[2,48,768]{2,1,0:T(8,128)(2,1)S(1)}, u32[]{:S(2)}, u32[]{:S(2)}) collective-permute-start(bf16[2,48,768]{2,1,0:T(8,128)(2,1)S(1)} %get-tuple-element.72), channel_id=1, source_target_pairs={{0,1},{1,2},{2,3},{3,0},{4,5},{5,6},{6,7},{7,4},{8,9},{9,10},{10,1... | collective-permute-start | bytes 442376 | tf_op jit(solution)/shard_map/ppermute | solution.py:803
  162.8 11.4 %collective-permute-start.10 = (bf16[2,48,768]{2,1,0:T(8,128)(2,1)S(1)}, bf16[2,48,768]{2,1,0:T(8,128)(2,1)S(1)}, u32[]{:S(2)}, u32[]{:S(2)}) collective-permute-start(bf16[2,48,768]{2,1,0:T(8,128)(2,1)S(1)} %get-tuple-element.73), channel_id=1, source_target_pairs={{0,3},{1,0},{2,1},{3,2},{4,7},{5,4},{6,5},{7,6},{8,11},{9,8},{10,9... | collective-permute-start | bytes 442376 | tf_op jit(solution)/shard_map/ppermute | solution.py:805
  166.0 12.9 %collective-permute-start.9 = (bf16[2,48,768]{2,1,0:T(8,128)(2,1)S(1)}, bf16[2,48,768]{2,1,0:T(8,128)(2,1)S(1)}, u32[]{:S(2)}, u32[]{:S(2)}) collective-permute-start(bf16[2,48,768]{2,1,0:T(8,128)(2,1)S(1)} %get-tuple-element.74), channel_id=1, source_target_pairs={{0,2},{1,3},{2,0},{3,1},{4,6},{5,7},{6,4},{7,5},{8,10},{9,11},{10,... | collective-permute-start | bytes 442376 | tf_op jit(solution)/shard_map/ppermute | solution.py:804
  179.0 4.4 %collective-permute-start.11 = (bf16[48,768]{1,0:T(8,128)(2,1)S(1)}, bf16[48,768]{1,0:T(8,128)(2,1)S(1)}, u32[]{:S(2)}, u32[]{:S(2)}) collective-permute-start(bf16[48,768]{1,0:T(8,128)(2,1)S(1)} %slice_bitcast_fusion.4), channel_id=1, source_target_pairs={{0,20},{1,21},{2,22},{3,23},{4,16},{5,17},{6,18},{7,19},{8,28},{9,... | collective-permute-start | bytes 221192 | tf_op jit(solution)/shard_map/ppermute | solution.py:807
  183.5 1.1 copy-start.5
  185.9 9.1 %copy-start.2 = (bf16[128,2,768]{2,0,1:T(8,128)(2,1)S(1)}, bf16[128,2,768]{2,0,1:T(8,128)(2,1)}, u32[]{:S(2)}) copy-start(bf16[128,2,768]{2,0,1:T(8,128)(2,1)} %copy-done.1) | copy-start | bytes 1179652
  185.9 9.1 %copy-start.10 = (f32[256,768]{1,0:T(8,128)S(1)}, f32[256,768]{1,0:T(8,128)}, u32[]{:S(2)}) copy-start(f32[256,768]{1,0:T(8,128)} %get-tuple-element.48.dfirst_ref) | copy-start | bytes 2359300
  185.9 9.1 %copy-start.16 = (f32[8,768]{1,0:T(8,128)S(1)}, f32[8,768]{1,0:T(8,128)}, u32[]{:S(2)}) copy-start(f32[8,768]{1,0:T(8,128)} %copy-done.15) | copy-start | bytes 73732
  187.3 15.2 %all-to-all-start.6 = ((bf16[8,56,768]{2,1,0:T(8,128)(2,1)}), bf16[8,56,768]{2,1,0:T(8,128)(2,1)S(1)}, u32[]{:S(2)}, u32[]{:S(2)}) async-start(bf16[8,56,768]{2,1,0:T(8,128)(2,1)} %shard_map.250), calls=%async_computation.7 | async-start | bytes 1376256 | tf_op jit(solution)/shard_map/all_to_all | solution.py:824
  195.1 7.5 %copy-start.8 = (s32[1,768]{1,0:T(1,128)S(1)}, s32[1,768]{1,0:T(1,128)}, u32[]{:S(2)}) copy-start(s32[1,768]{1,0:T(1,128)} %constant.13.clone.units_ref) | copy-start | bytes 9220
Sparse Core Ops, SparseCore 0:
  27.8 64.3 all-gather.2
  111.1 70.0 reduce-scatter.1

commit v10 on v9

--- a/solution.py
+++ b/solution.py
@@ -475,10 +475,11 @@
         copy.start()
         departures.append(copy)
 
-    for copy in arrivals[0:4]:
-        copy.wait()
+    arrivals[1].wait()
+    place_ref[...] = places(order_ref[...])
+    for i in (0, 2, 3):
+        arrivals[i].wait()
     gain, bias = gains_ref[2:3], gains_ref[3:4]
-    place_ref[...] = places(order_ref[...])
     natural = [
         jnp.concatenate([att_ref[2 * e + b] for e in range(4)], axis=0).T for b in range(2)
     ]

time: 214 us -> 214 us (level)
  starting transfers between devices: 45.1 us -> 37.1 us
  Pallas kernels: 62.3 us -> 68.6 us
  waiting for transfers between devices: 48.3 us -> 51.1 us
    pallas_call x11, Pallas kernels: 60.2 us -> 66.5 us  [call(): pl.pallas_call(kernel, out_shape=outs, scratch_shapes=list(scratch), cost...]
    all_to_all x1, starting transfers between devices: 8.18 us -> 4.87 us  [body(): back = exchange(part)]
    ppermute x1, waiting for transfers between devices: 0.01 us -> 2.32 us  [body(): lax.ppermute(line[1], 'batch', along_x(1))]
  transfers between devices with their start and end apart: 20 -> 20, of which waited for: 15 -> 15; matrix products, arithmetic and copies ran while one was open for 2% -> 2% of each run, Pallas kernels for 19% -> 22%
where the time goes in v10:
time: 214 us; the launch traced here: 212 us
  Pallas kernels  68.6 us (32%)
  waiting for transfers between devices  51.1 us (24%)
  starting transfers between devices  37.1 us (17%)
  blocking collectives  30.4 us (14%)
  between operations  14.4 us (7%)
  local copies, waits for them, and re-layouts  9.74 us (5%)
    pallas_call x11, Pallas kernels, call(): pl.pallas_call(kernel, out_shape=outs, scratch_shapes=list(scratch), cost...  66.5 us
    all_to_all x1, blocking collectives, body(): own = exchange(sent)  30.4 us
    all_to_all x2, starting transfers between devices, body(): slots = exchange(slots)  9.44 us
    all_to_all x2, waiting for transfers between devices, body(): slots = exchange(slots)  7.97 us
    all_to_all x1, waiting for transfers between devices, body(): att = exchange(o_low)  7.63 us
    ppermute x3, starting transfers between devices, body(): lax.ppermute(raw, 'batch', along_x(step))  5.72 us
    unnamed x51, local copies, waits for them, and re-layouts  5.58 us
    all_to_all x1, waiting for transfers between devices, body(): d_att = exchange(d_att)  5.3 us
  transfers between devices with their start and end apart: 20, of which 15 were waited for; matrix products, arithmetic and copies ran while one was open for 2% of the time, Pallas kernels for 22%

profile of v10, /device:TPU:64, one launch (start us, length us, event | category | flops | bytes accessed | tf_op | source)
XLA Modules:
  0.0 212.4 jit_solution(468304632175695239)
XLA Ops:
  7.2 2.1 shard_map.240
  9.3 5.7 %all-to-all-start.2 = ((bf16[8,56,768]{2,1,0:T(8,128)(2,1)}), bf16[8,56,768]{2,1,0:T(8,128)(2,1)S(1)}, u32[]{:S(2)}, u32[]{:S(2)}) async-start(bf16[8,56,768]{2,1,0:T(8,128)(2,1)} %get-tuple-element.46), calls=%async_computation.2 | async-start | bytes 1376256 | tf_op jit(solution)/shard_map/all_to_all | solution.py:703
  14.9 0.0 all-gather.3.cloned.1.call-start
  15.0 1.6 collective-permute-start.2
  16.5 2.7 %collective-permute-start.1 = (bf16[24,640]{1,0:T(8,128)(2,1)}, bf16[24,640]{1,0:T(8,128)(2,1)S(1)}, u32[]{:S(2)}, u32[]{:S(2)}) collective-permute-start(bf16[24,640]{1,0:T(8,128)(2,1)} %get-tuple-element.41), channel_id=1, source_target_pairs={{0,2},{1,3},{2,0},{3,1},{4,6},{5,7},{6,4},{7,5},{8,10},{9,11},{10,... | collective-permute-start | bytes 92168 | tf_op jit(solution)/shard_map/ppermute | solution.py:704
  19.3 1.4 collective-permute-start
  20.7 1.4 collective-permute-done.1
  22.2 1.2 collective-permute-done
  23.4 0.8 pad_maximum_fusion.near_ref
  24.2 2.0 all-to-all-done.2.slots_ref
  26.2 1.5 shard_map.244
  27.7 0.0 all-gather.3.cloned.1.call-update
  27.7 0.1 collective-permute-start.3
  27.9 4.8 %collective-permute-done.3.far_ref = bf16[4,24,640]{2,1,0:T(8,128)(2,1)S(1)} collective-permute-done((bf16[4,24,640]{2,1,0:T(8,128)(2,1)S(1)}, bf16[4,24,640]{2,1,0:T(8,128)(2,1)S(1)}, u32[]{:S(2)}, u32[]{:S(2)}) %collective-permute-start.3) | collective-permute-done | bytes 122912 | tf_op jit(solution)/shard_map/ppermute | solution.py:705
  32.7 0.2 shard_map.241
  32.9 0.0 copy-start.7
  32.9 30.4 %all_to_all.35.own_ref = bf16[8,176,768]{2,1,0:T(8,128)(2,1)S(1)} all-to-all(bf16[8,176,768]{2,1,0:T(8,128)(2,1)S(1)} %shard_map.241), channel_id=1, replica_groups={{0,16,32,48,64,80,96,112},{8,24,40,56,72,88,104,120},{1,17,33,49,65,81,..., dimensions={0} | all-to-all | bytes 4325376 | tf_op jit(solution)/shard_map/all_to_all | solution.py:727
  63.4 0.1 collective-permute-start.4
  63.5 2.0 collective-permute-done.4.other_ref
  65.5 3.0 %shard_map.242 = (bf16[1024,768]{1,0:T(8,128)(2,1)S(1)}, bf16[576,768]{1,0:T(8,128)(2,1)S(1)}, f32[8,768]{1,0:T(8,128)S(1)}, bf16[192,1024]{1,0:T(8,128)(2,1)S(1)}, bf16[384,1024]{1,0:T(8,128)(2,1)S(1)}) custom-call(bf16[8,176,768]{2,1,0:T(8,128)(2,1)S(1)} %all_to_all.35.own_ref, bf16[8,48,640]{2,1,0:T(8,128)(2,1)S(1)} %collective-permute-done.4.other_ref, ...), custom_call_target="tpu_custom_call" | custom-call | flops 5500000256 | tf_op jit(solution)/shard_map/pallas_call | solution.py:88
  68.5 1.1 copy-done.11
  69.6 1.0 copy-done.12
  70.7 0.6 copy-done.15
  71.3 0.1 collective-permute-start.5
  71.4 2.1 %collective-permute-done.5.other_ref = bf16[384,1024]{1,0:T(8,128)(2,1)S(1)} collective-permute-done((bf16[384,1024]{1,0:T(8,128)(2,1)S(1)}, bf16[384,1024]{1,0:T(8,128)(2,1)S(1)}, u32[]{:S(2)}, u32[]{:S(2)}) %collective-permute-start.5) | collective-permute-done | bytes 786464 | tf_op jit(solution)/shard_map/ppermute | solution.py:742
  73.6 10.2 %shard_map.243 = (f32[192,1024]{1,0:T(8,128)S(1)}, bf16[8,192,128]{2,1,0:T(8,128)(2,1)}, f32[3,1024]{1,0:T(4,128)S(1)}) custom-call(s32[2]{0:T(128)S(1)} %copy-done.6, bf16[192,1024]{1,0:T(8,128)(2,1)S(1)} %get-tuple-element.42.q_ref, bf16[384,1024]{1,0:T(8,128)(2,1)S(1)} %get-tuple-element.43.own_ref, bf16[384,1024]{1,0:T(8,128)(2,1)S(1)} %collective-permute-done.5.other_ref), custom_call_target="tpu_custom_call" | custom-call | flops 13200000000 | tf_op jit(solution)/shard_map/pallas_call | solution.py:88
  83.8 3.5 %all-to-all-start.1 = ((bf16[8,192,128]{2,1,0:T(8,128)(2,1)}), bf16[8,192,128]{2,1,0:T(8,128)(2,1)S(1)}, u32[]{:S(2)}, u32[]{:S(2)}) async-start(bf16[8,192,128]{2,1,0:T(8,128)(2,1)} %get-tuple-element.44), calls=%async_computation.1 | async-start | bytes 786432 | tf_op jit(solution)/shard_map/all_to_all | solution.py:759
  87.3 0.2 reduce-scatter.2.cloned.1.call-start
  87.5 0.8 copy.28
  88.3 7.6 %all-to-all-done.1.att_hbm.att_ref = bf16[8,192,128]{2,1,0:T(8,128)(2,1)S(1)} async-done(((bf16[8,192,128]{2,1,0:T(8,128)(2,1)}), bf16[8,192,128]{2,1,0:T(8,128)(2,1)S(1)}, u32[]{:S(2)}, u32[]{:S(2)}) %all-to-all-start.1) | async-done | bytes 393248 | tf_op jit(solution)/shard_map/all_to_all | solution.py:759
  96.0 0.7 copy-done.22
  96.7 16.0 %shard_map.245 = (bf16[256,768]{1,0:T(8,128)(2,1)}, f32[256,768]{1,0:T(8,128)}, bf16[256,768]{1,0:T(8,128)(2,1)}, bf16[8,192,128]{2,1,0:T(8,128)(2,1)}, f32[8,768]{1,0:T(8,128)}, /*index=5*/bf16[16,384,768]{2,1,0:T(8,128)(2,1)}) custom-call(bf16[8,192,128]{2,1,0:T(8,128)(2,1)} %copy-done.22, s32[1,768]{1,0:T(1,128)} %constant.12.clone.order_hbm, ...), custom_call_target="tpu_custom_call" | custom-call | flops 16499999744 | tf_op jit(solution)/shard_map/pallas_call | solution.py:88
  112.7 0.0 reduce-scatter.2.cloned.1.call-update
  112.7 3.5 %all-to-all-start.3 = ((bf16[8,192,128]{2,1,0:T(8,128)(2,1)}), bf16[8,192,128]{2,1,0:T(8,128)(2,1)S(1)}, u32[]{:S(2)}, u32[]{:S(2)}) async-start(bf16[8,192,128]{2,1,0:T(8,128)(2,1)} %get-tuple-element.51), calls=%async_computation.3 | async-start | bytes 786432 | tf_op jit(solution)/shard_map/all_to_all | solution.py:765
  116.2 2.7 %shard_map.247 = bf16[8,96,768]{2,1,0:T(8,128)(2,1)} custom-call(bf16[8,192,128]{2,1,0:T(8,128)(2,1)} %copy-done.22, bf16[256,768]{1,0:T(8,128)(2,1)} %get-tuple-element.58.low_ref), custom_call_target="tpu_custom_call" | custom-call | flops 2200000000 | tf_op jit(solution)/shard_map/pallas_call | solution.py:88
  118.8 5.3 %all-to-all-done.3.da_ref = bf16[8,192,128]{2,1,0:T(8,128)(2,1)S(1)} async-done(((bf16[8,192,128]{2,1,0:T(8,128)(2,1)}), bf16[8,192,128]{2,1,0:T(8,128)(2,1)S(1)}, u32[]{:S(2)}, u32[]{:S(2)}) %all-to-all-start.3) | async-done | bytes 393248 | tf_op jit(solution)/shard_map/all_to_all | solution.py:765
  124.1 3.8 %all-to-all-start.4 = ((bf16[8,96,768]{2,1,0:T(8,128)(2,1)}), bf16[8,96,768]{2,1,0:T(8,128)(2,1)S(1)}, u32[]{:S(2)}, u32[]{:S(2)}) async-start(bf16[8,96,768]{2,1,0:T(8,128)(2,1)} %shard_map.247), calls=%async_computation.4 | async-start | bytes 2359296 | tf_op jit(solution)/shard_map/all_to_all | solution.py:766
  127.9 19.5 %shard_map.246 = (bf16[192,1024]{1,0:T(8,128)(2,1)}, bf16[384,1024]{1,0:T(8,128)(2,1)}, bf16[384,1024]{1,0:T(8,128)(2,1)}) custom-call(s32[2]{0:T(128)} %lengths_ref.3, bf16[192,1024]{1,0:T(8,128)(2,1)} %copy-done.13, bf16[384,1024]{1,0:T(8,128)(2,1)} %copy-done.3, bf16[384,1024]{1,0:T(8,128)(2,1)} %copy-done.4, f32[192,1024]{1,0:T(8,128)} %copy-done.14, ...), custom_call_target="tpu_custom_call" | custom-call | flops 22000001024 | tf_op jit(solution)/shard_map/pallas_call | solution.py:88
  147.5 2.5 %collective-permute-done.6.partner_ref = bf16[384,1024]{1,0:T(8,128)(2,1)S(1)} collective-permute-done((bf16[384,1024]{1,0:T(8,128)(2,1)}, bf16[384,1024]{1,0:T(8,128)(2,1)S(1)}, u32[]{:S(2)}, u32[]{:S(2)}) %collective-permute-start.6) | collective-permute-done | bytes 786464 | tf_op jit(solution)/shard_map/ppermute | solution.py:788
  149.9 0.9 copy-done.24
  150.8 8.9 %shard_map.248 = (bf16[8,128,768]{2,1,0:T(8,128)(2,1)}, bf16[4,2,48,768]{3,2,1,0:T(8,128)(2,1)}, bf16[4,2,48,768]{3,2,1,0:T(8,128)(2,1)}) custom-call(bf16[8,176,768]{2,1,0:T(8,128)(2,1)} %copy-done, bf16[192,1024]{1,0:T(8,128)(2,1)} %get-tuple-element.52.dq_ref, bf16[384,1024]{1,0:T(8,128)(2,1)} %get-tuple-element.53.dkv_ref, bf16[384,1024]{1,0:T(8,128)(2,1)} %copy-done.24, ...), custom_call_target="tpu_custom_call" | custom-call | flops 7699999744 | tf_op jit(solution)/shard_map/pallas_call | solution.py:88
  159.7 0.1 collective-permute-start.7
  159.9 4.9 %all-to-all-start.5 = ((bf16[8,128,768]{2,1,0:T(8,128)(2,1)}), bf16[8,128,768]{2,1,0:T(8,128)(2,1)S(1)}, u32[]{:S(2)}, u32[]{:S(2)}) async-start(bf16[8,128,768]{2,1,0:T(8,128)(2,1)} %get-tuple-element.59), calls=%async_computation.5 | async-start | bytes 3145728 | tf_op jit(solution)/shard_map/all_to_all | solution.py:809
  164.8 0.1 add_convert_fusion
  165.0 2.1 collective-permute-start.8
  167.1 1.2 collective-permute-start.10
  168.3 2.2 %collective-permute-start.9 = (bf16[2,48,768]{2,1,0:T(8,128)(2,1)S(1)}, bf16[2,48,768]{2,1,0:T(8,128)(2,1)S(1)}, u32[]{:S(2)}, u32[]{:S(2)}) collective-permute-start(bf16[2,48,768]{2,1,0:T(8,128)(2,1)S(1)} %get-tuple-element.74), channel_id=1, source_target_pairs={{0,2},{1,3},{2,0},{3,1},{4,6},{5,7},{6,4},{7,5},{8,10},{9,11},{10,... | collective-permute-start | bytes 442376 | tf_op jit(solution)/shard_map/ppermute | solution.py:805
  170.5 2.3 %collective-permute-done.8 = bf16[2,48,768]{2,1,0:T(8,128)(2,1)S(1)} collective-permute-done((bf16[2,48,768]{2,1,0:T(8,128)(2,1)S(1)}, bf16[2,48,768]{2,1,0:T(8,128)(2,1)S(1)}, u32[]{:S(2)}, u32[]{:S(2)}) %collective-permute-start.8) | collective-permute-done | bytes 147488 | tf_op jit(solution)/shard_map/ppermute | solution.py:804
  172.8 2.4 %collective-permute-done.10 = bf16[2,48,768]{2,1,0:T(8,128)(2,1)S(1)} collective-permute-done((bf16[2,48,768]{2,1,0:T(8,128)(2,1)S(1)}, bf16[2,48,768]{2,1,0:T(8,128)(2,1)S(1)}, u32[]{:S(2)}, u32[]{:S(2)}) %collective-permute-start.10) | collective-permute-done | bytes 147488 | tf_op jit(solution)/shard_map/ppermute | solution.py:806
  175.2 3.9 %collective-permute-done.9 = bf16[2,48,768]{2,1,0:T(8,128)(2,1)S(1)} collective-permute-done((bf16[2,48,768]{2,1,0:T(8,128)(2,1)S(1)}, bf16[2,48,768]{2,1,0:T(8,128)(2,1)S(1)}, u32[]{:S(2)}, u32[]{:S(2)}) %collective-permute-start.9) | collective-permute-done | bytes 147488 | tf_op jit(solution)/shard_map/ppermute | solution.py:805
  179.1 0.1 fusion.2
  179.2 0.1 collective-permute-start.11
  179.3 4.3 %collective-permute-done.11 = bf16[48,768]{1,0:T(8,128)(2,1)S(1)} collective-permute-done((bf16[48,768]{1,0:T(8,128)(2,1)S(1)}, bf16[48,768]{1,0:T(8,128)(2,1)S(1)}, u32[]{:S(2)}, u32[]{:S(2)}) %collective-permute-start.11) | collective-permute-done | bytes 73760 | tf_op jit(solution)/shard_map/ppermute | solution.py:808
  183.6 0.0 reduce-scatter.2.cloned.1.call-done.rest_ref
  183.7 1.1 copy-done.5
  184.7 1.4 shard_map.250
  186.1 3.2 %all-to-all-done.5.got_ref = bf16[8,128,768]{2,1,0:T(8,128)(2,1)S(1)} async-done(((bf16[8,128,768]{2,1,0:T(8,128)(2,1)}), bf16[8,128,768]{2,1,0:T(8,128)(2,1)S(1)}, u32[]{:S(2)}, u32[]{:S(2)}) %all-to-all-start.5) | async-done | bytes 1572896 | tf_op jit(solution)/shard_map/all_to_all | solution.py:809
  189.3 3.8 %all-to-all-start.6 = ((bf16[8,56,768]{2,1,0:T(8,128)(2,1)}), bf16[8,56,768]{2,1,0:T(8,128)(2,1)S(1)}, u32[]{:S(2)}, u32[]{:S(2)}) async-start(bf16[8,56,768]{2,1,0:T(8,128)(2,1)} %shard_map.250), calls=%async_computation.7 | async-start | bytes 1376256 | tf_op jit(solution)/shard_map/all_to_all | solution.py:825
  193.1 2.1 %copy.36 = bf16[2,128,768]{2,0,1:T(2,128)(2,1)} copy(bf16[2,128,768]{2,1,0:T(8,128)(2,1)} %bitcast.52) | data formatting | bytes 786432 | tf_op jit(solution)/shard_map/reshape | solution.py:836
  195.2 0.0 copy-start.8
  195.3 1.3 shard_map.249
  196.6 1.1 copy.35
  197.7 6.0 %all-to-all-done.6.got_ref = bf16[8,56,768]{2,1,0:T(8,128)(2,1)S(1)} async-done(((bf16[8,56,768]{2,1,0:T(8,128)(2,1)}), bf16[8,56,768]{2,1,0:T(8,128)(2,1)S(1)}, u32[]{:S(2)}, u32[]{:S(2)}) %all-to-all-start.6) | async-done | bytes 688160 | tf_op jit(solution)/shard_map/all_to_all | solution.py:825
  203.7 1.9 shard_map.251
  (52 shorter events, 0.2 us)
Async XLA Ops:
  9.3 16.9 %copy-start.9 = (s32[1,512]{1,0:T(1,128)S(1)}, s32[1,512]{1,0:T(1,128)}, u32[]{:S(2)}) copy-start(s32[1,512]{1,0:T(1,128)} %constant.14.clone.order_ref) | copy-start | bytes 6148
  9.3 16.9 %all-to-all-start.2 = ((bf16[8,56,768]{2,1,0:T(8,128)(2,1)}), bf16[8,56,768]{2,1,0:T(8,128)(2,1)S(1)}, u32[]{:S(2)}, u32[]{:S(2)}) async-start(bf16[8,56,768]{2,1,0:T(8,128)(2,1)} %get-tuple-element.46), calls=%async_computation.2 | async-start | bytes 1376256 | tf_op jit(solution)/shard_map/all_to_all | solution.py:703
  14.9 81.0 %all-gather.3.cloned.1.call-start = ((), (), s32[]{:S(2)}) async-start(), calls=%async_computation.9 | async-start | bytes 11280384 | tf_op jit(solution)/shard_map/all_gather | solution.py:716
  15.0 5.7 %collective-permute-start.2 = (bf16[24,640]{1,0:T(8,128)(2,1)}, bf16[24,640]{1,0:T(8,128)(2,1)S(1)}, u32[]{:S(2)}, u32[]{:S(2)}) collective-permute-start(bf16[24,640]{1,0:T(8,128)(2,1)} %get-tuple-element.41), channel_id=1, source_target_pairs={{0,1},{1,2},{2,3},{3,0},{4,5},{5,6},{6,7},{7,4},{8,9},{9,10},{10,1... | collective-permute-start | bytes 92168 | tf_op jit(solution)/shard_map/ppermute | solution.py:704
  16.5 5.6 %collective-permute-start.1 = (bf16[24,640]{1,0:T(8,128)(2,1)}, bf16[24,640]{1,0:T(8,128)(2,1)S(1)}, u32[]{:S(2)}, u32[]{:S(2)}) collective-permute-start(bf16[24,640]{1,0:T(8,128)(2,1)} %get-tuple-element.41), channel_id=1, source_target_pairs={{0,2},{1,3},{2,0},{3,1},{4,6},{5,7},{6,4},{7,5},{8,10},{9,11},{10,... | collective-permute-start | bytes 92168 | tf_op jit(solution)/shard_map/ppermute | solution.py:704
  19.3 4.1 %collective-permute-start = (bf16[24,640]{1,0:T(8,128)(2,1)}, bf16[24,640]{1,0:T(8,128)(2,1)S(1)}, u32[]{:S(2)}, u32[]{:S(2)}) collective-permute-start(bf16[24,640]{1,0:T(8,128)(2,1)} %get-tuple-element.41), channel_id=1, source_target_pairs={{0,3},{1,0},{2,1},{3,2},{4,7},{5,4},{6,5},{7,6},{8,11},{9,8},{10,9... | collective-permute-start | bytes 92168 | tf_op jit(solution)/shard_map/ppermute | solution.py:704
  24.2 3.7 %copy-start.20 = (bf16[128,2,768]{2,1,0:T(2,128)(2,1)S(1)}, bf16[128,2,768]{2,1,0:T(2,128)(2,1)}, u32[]{:S(2)}) copy-start(bf16[128,2,768]{2,1,0:T(2,128)(2,1)} %param.17) | copy-start | bytes 1179652
  27.7 5.0 %collective-permute-start.3 = (bf16[4,24,640]{2,1,0:T(8,128)(2,1)S(1)}, bf16[4,24,640]{2,1,0:T(8,128)(2,1)S(1)}, u32[]{:S(2)}, u32[]{:S(2)}) collective-permute-start(bf16[4,24,640]{2,1,0:T(8,128)(2,1)S(1)} %pad_maximum_fusion.near_ref), channel_id=1, source_target_pairs={{0,20},{1,21},{2,22},{3,23},{4,16},{5,17},{6,18},{7,19},{8,28},{9,... | collective-permute-start | bytes 368648 | tf_op jit(solution)/shard_map/ppermute | solution.py:705
  27.9 5.0 %copy-start.1 = (bf16[128,2,768]{2,0,1:T(8,128)(2,1)}, bf16[128,2,768]{2,0,1:T(8,128)(2,1)S(1)}, u32[]{:S(2)}) copy-start(bf16[128,2,768]{2,0,1:T(8,128)(2,1)S(1)} %copy.37) | copy-start | bytes 1179652
  32.9 32.6 %copy-start.7 = (s32[8,768]{1,0:T(8,128)S(1)}, s32[8,768]{1,0:T(8,128)}, u32[]{:S(2)}) copy-start(s32[8,768]{1,0:T(8,128)} %constant.16.clone.arrival_ref) | copy-start | bytes 73732
  63.4 5.1 %copy-start = (bf16[8,176,768]{2,1,0:T(8,128)(2,1)}, bf16[8,176,768]{2,1,0:T(8,128)(2,1)S(1)}, u32[]{:S(2)}) copy-start(bf16[8,176,768]{2,1,0:T(8,128)(2,1)S(1)} %all_to_all.35.own_ref) | copy-start | bytes 6488068
  63.4 10.1 %copy-start.6 = (s32[2]{0:T(128)S(1)}, s32[2]{0:T(128)}, u32[]{:S(2)}) copy-start(s32[2]{0:T(128)} %lengths_ref.3) | copy-start | bytes 28
  63.4 2.1 collective-permute-start.4
  68.5 1.1 copy-start.11
  69.6 1.0 copy-start.12
  70.7 0.6 copy-start.15
  71.3 12.5 %copy-start.3 = (bf16[384,1024]{1,0:T(8,128)(2,1)}, bf16[384,1024]{1,0:T(8,128)(2,1)S(1)}, u32[]{:S(2)}) copy-start(bf16[384,1024]{1,0:T(8,128)(2,1)S(1)} %get-tuple-element.43.own_ref) | copy-start | bytes 2359300
  71.3 12.5 %copy-start.13 = (bf16[192,1024]{1,0:T(8,128)(2,1)}, bf16[192,1024]{1,0:T(8,128)(2,1)S(1)}, u32[]{:S(2)}) copy-start(bf16[192,1024]{1,0:T(8,128)(2,1)S(1)} %get-tuple-element.42.q_ref) | copy-start | bytes 1179652
  71.3 2.3 %collective-permute-start.5 = (bf16[384,1024]{1,0:T(8,128)(2,1)S(1)}, bf16[384,1024]{1,0:T(8,128)(2,1)S(1)}, u32[]{:S(2)}, u32[]{:S(2)}) collective-permute-start(bf16[384,1024]{1,0:T(8,128)(2,1)S(1)} %get-tuple-element.43.own_ref), channel_id=1, source_target_pairs={{0,8},{8,0},{16,24},{24,16},{32,40},{40,32},{48,56},{56,48},{64,72... | collective-permute-start | bytes 2359304 | tf_op jit(solution)/shard_map/ppermute | solution.py:742
  73.6 10.2 %copy-start.4 = (bf16[384,1024]{1,0:T(8,128)(2,1)}, bf16[384,1024]{1,0:T(8,128)(2,1)S(1)}, u32[]{:S(2)}) copy-start(bf16[384,1024]{1,0:T(8,128)(2,1)S(1)} %collective-permute-done.5.other_ref) | copy-start | bytes 2359300
  73.6 14.0 %copy-start.21 = (bf16[128,2,768]{2,1,0:T(2,128)(2,1)S(1)}, bf16[128,2,768]{2,1,0:T(2,128)(2,1)}, u32[]{:S(2)}) copy-start(bf16[128,2,768]{2,1,0:T(2,128)(2,1)} %param.27) | copy-start | bytes 1179652
  83.8 28.9 %copy-start.14 = (f32[192,1024]{1,0:T(8,128)}, f32[192,1024]{1,0:T(8,128)S(1)}, u32[]{:S(2)}) copy-start(f32[192,1024]{1,0:T(8,128)S(1)} %get-tuple-element.49.o_ref) | copy-start | bytes 2359300
  83.8 28.9 %copy-start.17 = (f32[3,1024]{1,0:T(4,128)}, f32[3,1024]{1,0:T(4,128)S(1)}, u32[]{:S(2)}) copy-start(f32[3,1024]{1,0:T(4,128)S(1)} %get-tuple-element.50.lse_ref) | copy-start | bytes 36868
  83.8 12.1 %all-to-all-start.1 = ((bf16[8,192,128]{2,1,0:T(8,128)(2,1)}), bf16[8,192,128]{2,1,0:T(8,128)(2,1)S(1)}, u32[]{:S(2)}, u32[]{:S(2)}) async-start(bf16[8,192,128]{2,1,0:T(8,128)(2,1)} %get-tuple-element.44), calls=%async_computation.1 | async-start | bytes 786432 | tf_op jit(solution)/shard_map/all_to_all | solution.py:759
  87.3 96.4 %reduce-scatter.2.cloned.1.call-start = ((), (), s32[]{:S(2)}) async-start(), calls=%async_computation.8 | async-start | bytes 10027008 | tf_op jit(solution)/shard_map/reduce_scatter | solution.py:761
  96.0 0.7 copy-start.22
  112.7 11.4 %all-to-all-start.3 = ((bf16[8,192,128]{2,1,0:T(8,128)(2,1)}), bf16[8,192,128]{2,1,0:T(8,128)(2,1)S(1)}, u32[]{:S(2)}, u32[]{:S(2)}) async-start(bf16[8,192,128]{2,1,0:T(8,128)(2,1)} %get-tuple-element.51), calls=%async_computation.3 | async-start | bytes 786432 | tf_op jit(solution)/shard_map/all_to_all | solution.py:765
  124.1 3.8 %copy-start.23 = (bf16[8,192,128]{2,1,0:T(8,128)(2,1)}, bf16[8,192,128]{2,1,0:T(8,128)(2,1)S(1)}, u32[]{:S(2)}) copy-start(bf16[8,192,128]{2,1,0:T(8,128)(2,1)S(1)} %all-to-all-done.3.da_ref) | copy-start | bytes 1179652
  124.1 23.3 %all-to-all-start.4 = ((bf16[8,96,768]{2,1,0:T(8,128)(2,1)}), bf16[8,96,768]{2,1,0:T(8,128)(2,1)S(1)}, u32[]{:S(2)}, u32[]{:S(2)}) async-start(bf16[8,96,768]{2,1,0:T(8,128)(2,1)} %shard_map.247), calls=%async_computation.4 | async-start | bytes 2359296 | tf_op jit(solution)/shard_map/all_to_all | solution.py:766
  147.4 2.5 %collective-permute-start.6 = (bf16[384,1024]{1,0:T(8,128)(2,1)}, bf16[384,1024]{1,0:T(8,128)(2,1)S(1)}, u32[]{:S(2)}, u32[]{:S(2)}) collective-permute-start(bf16[384,1024]{1,0:T(8,128)(2,1)} %get-tuple-element.54), channel_id=1, source_target_pairs={{0,8},{8,0},{16,24},{24,16},{32,40},{40,32},{48,56},{56,48},{64,72... | collective-permute-start | bytes 2359304 | tf_op jit(solution)/shard_map/ppermute | solution.py:788
  147.4 2.5 %copy-start.18 = (bf16[8,96,768]{2,1,0:T(8,128)(2,1)}, bf16[8,96,768]{2,1,0:T(8,128)(2,1)S(1)}, u32[]{:S(2)}) copy-start(bf16[8,96,768]{2,1,0:T(8,128)(2,1)S(1)} %all-to-all-done.4.out_ref) | copy-start | bytes 3538948
  149.9 0.9 copy-start.24
  159.7 5.0 %collective-permute-start.7 = (bf16[4,2,48,768]{3,2,1,0:T(8,128)(2,1)}, bf16[4,2,48,768]{3,2,1,0:T(8,128)(2,1)S(1)}, u32[]{:S(2)}, u32[]{:S(2)}) collective-permute-start(bf16[4,2,48,768]{3,2,1,0:T(8,128)(2,1)} %get-tuple-element.61), channel_id=1, source_target_pairs={{0,8},{8,0},{16,24},{24,16},{32,40},{40,32},{48,56},{56,48},{64,72... | collective-permute-start | bytes 1769480 | tf_op jit(solution)/shard_map/ppermute | solution.py:801
  159.9 4.9 %copy-start.19 = (bf16[4,2,48,768]{3,2,1,0:T(8,128)(2,1)S(1)}, bf16[4,2,48,768]{3,2,1,0:T(8,128)(2,1)}, u32[]{:S(2)}) copy-start(bf16[4,2,48,768]{3,2,1,0:T(8,128)(2,1)} %get-tuple-element.60) | copy-start | bytes 1769476
  159.9 29.4 %all-to-all-start.5 = ((bf16[8,128,768]{2,1,0:T(8,128)(2,1)}), bf16[8,128,768]{2,1,0:T(8,128)(2,1)S(1)}, u32[]{:S(2)}, u32[]{:S(2)}) async-start(bf16[8,128,768]{2,1,0:T(8,128)(2,1)} %get-tuple-element.59), calls=%async_computation.5 | async-start | bytes 3145728 | tf_op jit(solution)/shard_map/all_to_all | solution.py:809
  165.0 7.9 %collective-permute-start.8 = (bf16[2,48,768]{2,1,0:T(8,128)(2,1)S(1)}, bf16[2,48,768]{2,1,0:T(8,128)(2,1)S(1)}, u32[]{:S(2)}, u32[]{:S(2)}) collective-permute-start(bf16[2,48,768]{2,1,0:T(8,128)(2,1)S(1)} %get-tuple-element.72), channel_id=1, source_target_pairs={{0,1},{1,2},{2,3},{3,0},{4,5},{5,6},{6,7},{7,4},{8,9},{9,10},{10,1... | collective-permute-start | bytes 442376 | tf_op jit(solution)/shard_map/ppermute | solution.py:804
  167.1 8.1 %collective-permute-start.10 = (bf16[2,48,768]{2,1,0:T(8,128)(2,1)S(1)}, bf16[2,48,768]{2,1,0:T(8,128)(2,1)S(1)}, u32[]{:S(2)}, u32[]{:S(2)}) collective-permute-start(bf16[2,48,768]{2,1,0:T(8,128)(2,1)S(1)} %get-tuple-element.73), channel_id=1, source_target_pairs={{0,3},{1,0},{2,1},{3,2},{4,7},{5,4},{6,5},{7,6},{8,11},{9,8},{10,9... | collective-permute-start | bytes 442376 | tf_op jit(solution)/shard_map/ppermute | solution.py:806
  168.3 10.8 %collective-permute-start.9 = (bf16[2,48,768]{2,1,0:T(8,128)(2,1)S(1)}, bf16[2,48,768]{2,1,0:T(8,128)(2,1)S(1)}, u32[]{:S(2)}, u32[]{:S(2)}) collective-permute-start(bf16[2,48,768]{2,1,0:T(8,128)(2,1)S(1)} %get-tuple-element.74), channel_id=1, source_target_pairs={{0,2},{1,3},{2,0},{3,1},{4,6},{5,7},{6,4},{7,5},{8,10},{9,11},{10,... | collective-permute-start | bytes 442376 | tf_op jit(solution)/shard_map/ppermute | solution.py:805
  179.2 4.4 %collective-permute-start.11 = (bf16[48,768]{1,0:T(8,128)(2,1)S(1)}, bf16[48,768]{1,0:T(8,128)(2,1)S(1)}, u32[]{:S(2)}, u32[]{:S(2)}) collective-permute-start(bf16[48,768]{1,0:T(8,128)(2,1)S(1)} %slice_bitcast_fusion.4), channel_id=1, source_target_pairs={{0,20},{1,21},{2,22},{3,23},{4,16},{5,17},{6,18},{7,19},{8,28},{9,... | collective-permute-start | bytes 221192 | tf_op jit(solution)/shard_map/ppermute | solution.py:808
  183.7 1.1 copy-start.5
  186.1 9.1 %copy-start.2 = (bf16[128,2,768]{2,0,1:T(8,128)(2,1)S(1)}, bf16[128,2,768]{2,0,1:T(8,128)(2,1)}, u32[]{:S(2)}) copy-start(bf16[128,2,768]{2,0,1:T(8,128)(2,1)} %copy-done.1) | copy-start | bytes 1179652
  186.1 9.1 %copy-start.10 = (f32[256,768]{1,0:T(8,128)S(1)}, f32[256,768]{1,0:T(8,128)}, u32[]{:S(2)}) copy-start(f32[256,768]{1,0:T(8,128)} %get-tuple-element.48.dfirst_ref) | copy-start | bytes 2359300
  186.1 9.1 %copy-start.16 = (f32[8,768]{1,0:T(8,128)S(1)}, f32[8,768]{1,0:T(8,128)}, u32[]{:S(2)}) copy-start(f32[8,768]{1,0:T(8,128)} %copy-done.15) | copy-start | bytes 73732
  189.3 14.4 %all-to-all-start.6 = ((bf16[8,56,768]{2,1,0:T(8,128)(2,1)}), bf16[8,56,768]{2,1,0:T(8,128)(2,1)S(1)}, u32[]{:S(2)}, u32[]{:S(2)}) async-start(bf16[8,56,768]{2,1,0:T(8,128)(2,1)} %shard_map.250), calls=%async_computation.7 | async-start | bytes 1376256 | tf_op jit(solution)/shard_map/all_to_all | solution.py:825
  195.2 8.4 %copy-start.8 = (s32[1,768]{1,0:T(1,128)S(1)}, s32[1,768]{1,0:T(1,128)}, u32[]{:S(2)}) copy-start(s32[1,768]{1,0:T(1,128)} %constant.13.clone.units_ref) | copy-start | bytes 9220
Sparse Core Ops, SparseCore 0:
  27.8 64.3 all-gather.2
  112.8 67.2 reduce-scatter.1
